TPU v7x, 32 devices: a whole 2x2x4 slice. The times are simulated.
32 devices in a mesh: gx: 4 (over y, core), gy: 8 (over z, x).
Axes of the slice: x: 2, y: 2, z: 4, core: 2. Of those that a mesh axis runs over, the one named last changes fastest.
Arguments:
- initial: float32 [3, 24, 24, 384], P(None, 'gx', 'gy'), may hold values from -2.5 to 2.5
- forcing: float32 [3, 24, 24, 384], P(None, 'gx', 'gy'), may hold values from -600 to 600
- modulus: float32 [8, 8, 128], P('gx', 'gy'), may hold values from 0.5 to 2
- solid_list: int32 [4, 8, 192], P('gx', 'gy'), may hold values from 0 to 256, as said below
Outputs:
- displacement: float32 [3, 24, 24, 384], P(None, 'gx', 'gy')
- coarse_iterate: float32 [3, 8, 8, 128], P(None, 'gx', 'gy')
Inputs may be any that keep to these rules, and one draw needn't show every extreme that they name: `solid_list`: each device's row lists distinct local element numbers below 256 first, then padding entries equal to 256; at least 64 entries of a row are live, and in every draw some device's row is live throughout.
All inputs are finite; a program needn't handle non-finite values.
Results may differ from a plain program's by a relative error of at most 0.0003.
Values sent between devices are 32-bit elements; how exact they have to be, the bound alone decides.
No kernel may reach another device: no remote copies, remote signals or barrier semaphores. Data moves between devices by JAX's collectives and lax.ppermute only.
A program may use at most 64 MiB of HBM per device.

v0:
```python
import math

import jax
import jax.numpy as jnp
import numpy as np
from jax import lax
from jax.experimental import pallas as pl
from jax.experimental.pallas import tpu as pltpu
from jax.sharding import PartitionSpec as P

CHEB = 3
EZ = 128

element_span = 20.0
lame_ratio = 4.0
rest_ratio = 1.25
modulus_top = 2.0
spectrum_floor = 0.05
interval_centre = (1.0 + spectrum_floor) / 2.0
interval_radius = (1.0 - spectrum_floor) / 2.0
interval_ratio = interval_centre / interval_radius
inner_anchors = (0.5 - 0.5 / math.sqrt(5.0), 0.5 + 0.5 / math.sqrt(5.0))

BEFORE = 10
PAIRS = 12
PAIR_SLOTS = 16
OWN = BEFORE // 2
FIELD_COLUMNS = 3 * PAIRS * 32

SLOTS = [
    (0, 0, 0), (1, 0, 0), (2, 0, 0), (0, 1, 0), (0, 2, 0), (0, 0, 1), (0, 0, 2), None,
    (0, 1, 1), (0, 1, 2), (0, 2, 1), (0, 2, 2), (1, 0, 1), (1, 0, 2), (2, 0, 1), (2, 0, 2),
    (1, 1, 0), (1, 2, 0), (2, 1, 0), (2, 2, 0), (1, 1, 1), (1, 1, 2), (1, 2, 1), (1, 2, 2),
    (2, 1, 1), (2, 1, 2), (2, 2, 1), (2, 2, 2), None, None, None, None,
]
STIFF_SLOT = 7
GROUPS = [
    ((0, 0, 0), 0), ((0, 0, 0), 1), ((0, 0, 0), 2), ((0, 0, 0), 3),
    ((1, 0, 0), 0), ((1, 0, 0), 1),
    ((0, 1, 0), 0), ((0, 1, 0), 1),
    ((0, 0, 1), 0), ((0, 0, 1), 2),
    ((1, 1, 0), 0), ((1, 0, 1), 0), ((0, 1, 1), 0), ((1, 1, 1), 0),
]
ROWS = 8 * len(GROUPS)
CORNERS = [(a, b, c) for a in range(2) for b in range(2) for c in range(2)]


def gauss_rule(point_count):
    if point_count == 2:
        offset = 1.0 / math.sqrt(3.0)
        points = [-offset, offset]
        weights = [1.0, 1.0]
    else:
        inner = math.sqrt(3.0 / 7.0 - 2.0 / 7.0 * math.sqrt(6.0 / 5.0))
        outer = math.sqrt(3.0 / 7.0 + 2.0 / 7.0 * math.sqrt(6.0 / 5.0))
        heavy = (18.0 + math.sqrt(30.0)) / 36.0
        light = (18.0 - math.sqrt(30.0)) / 36.0
        points = [-outer, -inner, inner, outer]
        weights = [light, heavy, heavy, light]
    return (np.array(points), np.array(weights))


def lagrange_tables(anchors, samples):
    values = np.zeros((len(samples), len(anchors)))
    slopes = np.zeros((len(samples), len(anchors)))
    for sample_index, sample in enumerate(samples):
        for anchor_index, anchor in enumerate(anchors):
            others = [
                location
                for location_index, location in enumerate(anchors)
                if location_index != anchor_index
            ]
            product = 1.0
            for location in others:
                product = product * (sample - location) / (anchor - location)
            values[sample_index, anchor_index] = product
            derivative = 0.0
            for skipped in range(len(others)):
                summand = 1.0 / (anchor - others[skipped])
                for kept_index in range(len(others)):
                    if kept_index != skipped:
                        summand = (
                            summand * (sample - others[kept_index]) / (anchor - others[kept_index])
                        )
                derivative = derivative + summand
            slopes[sample_index, anchor_index] = derivative
    return (values, slopes)


def outer_three(first, second, third):
    return (
        first[:, None, None, :, None, None]
        * second[None, :, None, None, :, None]
        * third[None, None, :, None, None, :]
    )


def build_tables(anchors, point_count):
    raw_points, raw_weights = gauss_rule(point_count)
    samples = (raw_points + 1.0) / 2.0
    weights = raw_weights / 2.0
    basis_values, slopes = lagrange_tables(anchors, samples)
    quad_total = point_count**3
    nodal_count = len(anchors) ** 3
    derivative_one = outer_three(slopes, basis_values, basis_values).reshape(
        quad_total, nodal_count
    )
    derivative_two = outer_three(basis_values, slopes, basis_values).reshape(
        quad_total, nodal_count
    )
    derivative_three = outer_three(basis_values, basis_values, slopes).reshape(
        quad_total, nodal_count
    )
    stacked = np.stack([derivative_one, derivative_two, derivative_three]) / element_span
    volume = (weights[:, None, None] * weights[None, :, None] * weights[None, None, :]).reshape(
        -1
    ) * element_span**3
    forward = stacked.reshape(3 * quad_total, nodal_count)
    backward = (stacked * volume[None, :, None]).reshape(3 * quad_total, nodal_count).T
    weighted = stacked * volume[None, :, None]
    laplace = weighted[0].T @ stacked[0] + weighted[1].T @ stacked[1] + weighted[2].T @ stacked[2]
    matrix = np.zeros((nodal_count, 3, nodal_count, 3))
    for first in range(3):
        for second in range(3):
            block = weighted[second].T @ stacked[first] + (lame_ratio - 1.0) * (
                weighted[first].T @ stacked[second]
            )
            if first == second:
                block = block + laplace
            matrix[:, first, :, second] = block
    matrix = matrix.reshape(3 * nodal_count, 3 * nodal_count)
    vector = 1.5 + np.cos(1.3 * np.arange(3 * nodal_count))
    for repeat in range(200):
        vector = matrix @ vector
        vector = vector / np.sqrt(vector @ vector)
    largest = vector @ (matrix @ vector)
    return (forward, backward, float(4.0 * modulus_top * 1.1 * largest))


def row_nodes():
    nodes = []
    for shift, group in GROUPS:
        for slot in SLOTS[8 * group : 8 * group + 8]:
            if slot is None or any(s and n for s, n in zip(shift, slot)):
                nodes.append(None)
            else:
                a, b, c = (3 * s + n for s, n in zip(shift, slot))
                nodes.append(16 * a + 4 * b + c)
    return nodes


def halves(matrix):
    whole = np.asarray(matrix, np.float32)
    high = whole.astype(jnp.bfloat16)
    low = (whole - high.astype(np.float32)).astype(jnp.bfloat16)
    return high, low


def element_tables():
    forward, backward, bound = build_tables([0.0, inner_anchors[0], inner_anchors[1], 1.0], 4)
    spread = np.zeros((forward.shape[0], ROWS))
    collect = np.zeros((ROWS, backward.shape[1]))
    for row, node in enumerate(row_nodes()):
        if node is not None:
            spread[:, row] = forward[:, node]
            collect[row, :] = backward[node, :]
    spread_high, spread_low = halves(spread)
    collect_high, collect_low = halves(collect)
    return (
        np.concatenate([spread_high, spread_high, spread_low], 1),
        np.concatenate([collect_high, collect_high, collect_low], 1),
        bound,
    )


def transfer_table():
    table = np.zeros((8, 32))
    reach = (0.0, inner_anchors[0], inner_anchors[1])
    for row, corner in enumerate(CORNERS):
        for column, slot in enumerate(SLOTS):
            if slot is not None:
                weight = 1.0
                for side, node in zip(corner, slot):
                    weight = weight * (reach[node] if side else 1.0 - reach[node])
                table[row, column] = weight
    return table.astype(np.float32)


def chebyshev_steps():
    steps = [(0.0, 1.0 / interval_centre)]
    ratio_now = 1.0 / interval_ratio
    for sweep in range(1, CHEB):
        ratio_next = 1.0 / (2.0 * interval_ratio - ratio_now)
        steps.append((ratio_next * ratio_now, 2.0 * ratio_next / interval_radius))
        ratio_now = ratio_next
    return steps


def stack_row(field, component, layer, b):
    return field * 54 + component * 18 + layer * 3 + b


def pack_table():
    table = np.zeros((3, 128, 2, 2, 3, 4, 32), np.float32)
    for field in range(2):
        for x in range(2):
            for component in range(3):
                for column, slot in enumerate(SLOTS):
                    if slot is not None:
                        a, b, c = slot
                        row = stack_row(field, component, 3 * x + a, b)
                        table[c, row, field, x, component, :, column] = 1.0
            table[0, 108 + x, 0, x, 0, :, STIFF_SLOT] = 1.0
    return table.reshape(384, 12 * 128).astype(jnp.bfloat16)


def unpack_table():
    table = np.zeros((2, 128, 3, 128), np.float32)
    for x in range(2):
        for component in range(3):
            for column, slot in enumerate(SLOTS):
                if slot is not None:
                    a, b, c = slot
                    row = stack_row(0, component, 3 * x + a, b)
                    table[x, component * 32 + column, c, row] = 1.0
            table[x, 96 + component, 0, 54 + 2 * component + x] = 1.0
    return table.reshape(256, 384).astype(jnp.bfloat16)


def exact_pick(values, table):
    high = values.astype(jnp.bfloat16)
    rest = values - high.astype(jnp.float32)
    middle = rest.astype(jnp.bfloat16)
    low = (rest - middle.astype(jnp.float32)).astype(jnp.bfloat16)
    parts = [
        jnp.dot(part, table, preferred_element_type=jnp.float32) for part in (high, middle, low)
    ]
    return parts[0] + (parts[1] + parts[2])


def pack_kernel(initial, forcing, modulus, listing, table, out, rows, turned, places):
    devices = out.shape[0]
    own_layers = EZ // devices
    rows[108:128, :] = jnp.zeros((20, 384), jnp.float32)
    for field, source in enumerate((initial, forcing)):
        for component in range(3):
            for layer in range(6):
                at = stack_row(field, component, layer, 0)
                rows[at : at + 3, :] = source[component, layer]
    for part in range(3):
        span = slice(128 * part, 128 * part + 128)
        turned[span, :] = rows[:, span].T
    listed = listing[0].astype(jnp.float32)
    listed = jnp.concatenate([listed, jnp.full((1, 64), 256.0, jnp.float32)], 1)
    listed = jnp.broadcast_to(listed, (128, 256)).T
    lanes = lax.broadcasted_iota(jnp.int32, (256, 128), 1).astype(jnp.float32)
    row_at = lax.broadcasted_iota(jnp.int32, (128, 128), 0)
    stiff = jnp.zeros((128, 128), jnp.float32)
    for x in range(2):
        hit = jnp.max(jnp.where(listed == lanes + 128.0 * x, 1.0, 0.0), axis=0, keepdims=True)
        stiff = jnp.where(row_at == 108 + x, hit * modulus[x], stiff)
    picked = [turned[pl.ds(c, 128, stride=3), :] for c in range(3)]
    picked[0] = picked[0] + stiff.T
    wide = exact_pick(jnp.concatenate(picked, 1), table[...])
    group = lax.broadcasted_iota(jnp.int32, (128, 128), 1) // 32
    for block in range(12):
        here = wide[:, 128 * block : 128 * block + 128]
        shifted = here
        for ahead in range(1, 4):
            shifted = jnp.where(group == ahead, pltpu.roll(here, 128 - 2 * ahead, 0), shifted)
        places[block, 16:144, :] = shifted
        places[block, 0:16, :] = shifted[112:128]
        places[block, 144:160, :] = shifted[0:16]
    for field in range(2):
        for x in range(2):
            for component in range(3):
                block = (field * 2 + x) * 3 + component
                for parity in range(2):
                    for chunk in range(PAIRS // 4):
                        first = 16 - BEFORE + 8 * chunk + parity
                        at = component * 32 * PAIRS + 128 * chunk
                        out[:, field * 4 + x * 2 + parity, at : at + 128] = places[
                            block, pl.ds(first, devices, stride=own_layers), :
                        ]


def unpack_kernel(arrived, table, out, coarse_out, layers, turned):
    devices = arrived.shape[0]
    own_layers = EZ // devices
    for x in range(2):
        for layer in range(own_layers):
            row = (layer // 2) * 4 + x * 2 + layer % 2
            layers[x, pl.ds(layer, devices, stride=own_layers), :] = arrived[:, row, :]
    wide = exact_pick(jnp.concatenate([layers[0], layers[1]], 1), table[...])
    for c in range(3):
        turned[pl.ds(c, 128, stride=3), :] = wide[:, 128 * c : 128 * c + 128]
    for part in range(3):
        span = slice(128 * part, 128 * part + 128)
        back = turned[span, :].T
        for component in range(3):
            for layer in range(6):
                at = stack_row(0, component, layer, 0)
                out[component, layer, :, span] = back[at : at + 3, :]
    back = wide[:, 0:128].T
    for component in range(3):
        for x in range(2):
            at = 54 + 2 * component + x
            coarse_out[component, x] = back[at : at + 1, :]


def cofactor_rows(deform):
    return [
        [
            deform[(row_at + 1) % 3][(column + 1) % 3] * deform[(row_at + 2) % 3][(column + 2) % 3]
            - deform[(row_at + 1) % 3][(column + 2) % 3]
            * deform[(row_at + 2) % 3][(column + 1) % 3]
            for column in range(3)
        ]
        for row_at in range(3)
    ]


def point_stress(deform, stiffness, stiffness_four):
    cofactors = cofactor_rows(deform)
    jacobian = (
        deform[0][0] * cofactors[0][0]
        + deform[0][1] * cofactors[0][1]
        + deform[0][2] * cofactors[0][2]
    )
    pressure = stiffness_four * (jacobian - rest_ratio)
    return [
        [stiffness * deform[i][d] + pressure * cofactors[i][d] for d in range(3)] for i in range(3)
    ]


def split_rows(values):
    high = values.astype(jnp.bfloat16)
    low = (values - high.astype(jnp.float32)).astype(jnp.bfloat16)
    return jnp.concatenate([high, low, high], 0)


def make_cycle_kernel(width, across, own_layers, fine_bound, coarse_bound):
    steps = chebyshev_steps()
    y_step = 2 * across

    def cycle_kernel(
        arrived, spread, collect, transfer, transfer_back, out, u, f, d, shares, raised
    ):
        def lane_of(rows):
            return lax.broadcasted_iota(jnp.int32, (rows, width), 1)

        def masks(rows):
            lane = lane_of(rows)
            x = (lane // 2) % across
            return x == 0, x == across - 1, lane % 2 == 0

        def next_x(v, top):
            return jnp.where(top, 0.0, pltpu.roll(v, width - 2, 1))

        def next_y(v):
            return pltpu.roll(v, width - y_step, 1)

        def onto_x(v, bottom):
            return jnp.where(bottom, 0.0, pltpu.roll(v, 2, 1))

        def onto_y(v):
            return pltpu.roll(v, y_step, 1)

        bottom8, top8, even8 = masks(8)
        bottom16, top16, even16 = masks(16)
        row32 = lax.broadcasted_iota(jnp.int32, (32, width), 0)
        on_face = (row32 == 0) | ((row32 >= 3) & (row32 <= 6)) | ((row32 >= 8) & (row32 <= 11))
        keep = jnp.where(on_face & masks(32)[0], 0.0, 1.0)

        u[:, PAIRS:, :, :] = jnp.zeros((3, PAIR_SLOTS - PAIRS, 32, width), jnp.float32)
        lower = lax.broadcasted_iota(jnp.int32, (width // 8, 8, 128), 1) < 4
        for component in range(3):
            for chunk in range(PAIRS // 4):
                at = component * 32 * PAIRS + 128 * chunk
                first = arrived[:, 0, :, at : at + 128]
                second = arrived[:, 1, :, at : at + 128]
                value = jnp.where(lower, first, pltpu.roll(second, 4, 1))
                load = jnp.where(lower, pltpu.roll(first, 4, 1), second)
                value = value.reshape(width, 128).T
                load = load.reshape(width, 128).T
                for q in range(4):
                    u[component, 4 * chunk + q] = value[32 * q : 32 * q + 32] * keep
                    f[component, 4 * chunk + q] = load[32 * q : 32 * q + 32]

        def gather(component, pair):
            here = u[component, pair]
            ahead = u[component, pair + 1]
            g0, g1, g2 = here[0:8], here[8:16], here[16:24]
            z0 = jnp.where(
                even8, pltpu.roll(g0, width - 1, 1), pltpu.roll(ahead[0:8], 1, 1)
            )
            z2 = jnp.where(
                even8, pltpu.roll(g2, width - 1, 1), pltpu.roll(ahead[16:24], 1, 1)
            )
            y0, y1 = next_y(g0), next_y(g1)
            yz = next_y(z0)
            return jnp.concatenate(
                [
                    here,
                    next_x(g0, top8),
                    next_x(g1, top8),
                    y0,
                    y1,
                    z0,
                    z2,
                    next_x(y0, top8),
                    next_x(z0, top8),
                    yz,
                    next_x(yz, top8),
                ],
                0,
            )

        def scatter(part, behind):
            g = [part[8 * n : 8 * n + 8] for n in range(len(GROUPS))]
            yz = g[12] + onto_x(g[13], bottom8)
            z0 = g[8] + onto_x(g[11], bottom8) + onto_y(yz)
            y0 = g[6] + onto_x(g[10], bottom8)
            z2 = g[9]
            own0 = g[0] + onto_x(g[4], bottom8) + onto_y(y0)
            own1 = g[1] + onto_x(g[5], bottom8) + onto_y(g[7])
            own0 = own0 + jnp.where(even8, behind[0], pltpu.roll(z0, 1, 1))
            own2 = g[2] + jnp.where(even8, behind[1], pltpu.roll(z2, 1, 1))
            moved = (pltpu.roll(z0, width - 1, 1), pltpu.roll(z2, width - 1, 1))
            return jnp.concatenate([own0, own1, own2, g[3]], 0), moved

        def apply(first, count, finish):
            def step(index, carry):
                pair = first + 2 * index
                blocks = [gather(i, pair + q) for i in range(3) for q in range(2)]
                gradient = jnp.dot(
                    spread[...],
                    split_rows(jnp.concatenate(blocks, 1)),
                    preferred_element_type=jnp.float32,
                )
                stiffness = jnp.concatenate(
                    [u[0, pair + q, STIFF_SLOT : STIFF_SLOT + 1, :] for q in range(2)], 1
                )
                deform = [
                    [
                        gradient[64 * e : 64 * e + 64, 2 * width * i : 2 * width * (i + 1)]
                        + (1.0 if i == e else 0.0)
                        for e in range(3)
                    ]
                    for i in range(3)
                ]
                stress = point_stress(deform, stiffness, lame_ratio * stiffness)
                stress = jnp.concatenate(
                    [jnp.concatenate([stress[i][e] for i in range(3)], 1) for e in range(3)], 0
                )
                force = jnp.dot(
                    collect[...], split_rows(stress), preferred_element_type=jnp.float32
                )
                carry = list(carry)
                totals = [[], []]
                for q in range(2):
                    for i in range(3):
                        at = (2 * i + q) * width
                        total, carry[i] = scatter(force[:, at : at + width], carry[i])
                        totals[q].append(total)
                for q in range(2):
                    finish(pair + q, totals[q])
                return tuple(carry)

            none = jnp.zeros((8, width), jnp.float32)
            lax.fori_loop(0, (count + 1) // 2, step, tuple((none, none) for i in range(3)))

        def smooth(starts):
            for (first, count), (held, added) in zip(starts, steps):

                def finish(pair, forces, held=held, added=added):
                    for i in range(3):
                        z = (added / fine_bound) * keep * (f[i, pair] - forces[i])
                        move = held * d[i, pair] + z if held else z
                        d[i, pair] = move
                        u[i, pair] = u[i, pair] + move

                apply(first, count, finish)

        reach = [BEFORE - 9, BEFORE - 8, BEFORE - 7, BEFORE - 6, BEFORE - 3, BEFORE - 2, BEFORE - 1]
        ends = [BEFORE + own_layers + n for n in (8, 7, 6, 5, 2, 1, 0)]
        spans = [(lo // 2, (hi + 1) // 2 - lo // 2) for lo, hi in zip(reach, ends)]

        smooth(spans[0:3])

        shares[...] = jnp.zeros(shares.shape, jnp.float32)

        def restrict(pair, forces):
            rest = jnp.concatenate([keep * (f[i, pair] - forces[i]) for i in range(3)], 1)
            corner = jnp.dot(
                transfer[...],
                rest,
                preferred_element_type=jnp.float32,
                precision=lax.Precision.HIGHEST,
            )
            for i in range(3):
                shares[i, pair] = corner[:, width * i : width * (i + 1)]

        apply(spans[3][0], spans[3][1], restrict)

        def next_z(v):
            return jnp.where(
                even16,
                pltpu.roll(v, width - 1, 1),
                pltpu.roll(pltpu.roll(v, 1, 1), PAIR_SLOTS - 1, 0),
            )

        def onto_z(v):
            return jnp.where(
                even16, pltpu.roll(pltpu.roll(v, width - 1, 1), 1, 0), pltpu.roll(v, 1, 1)
            )

        def corners_of(v):
            found = {}
            found[0, 0, 0] = v
            found[0, 0, 1] = next_z(v)
            for c in range(2):
                found[0, 1, c] = next_y(found[0, 0, c])
            for b in range(2):
                for c in range(2):
                    found[1, b, c] = next_x(found[0, b, c], top16)
            return found

        def assemble(part):
            line = {
                (a, b): part[a, b, 0] + onto_z(part[a, b, 1]) for a in range(2) for b in range(2)
            }
            face = [line[a, 0] + onto_y(line[a, 1]) for a in range(2)]
            return face[0] + onto_x(face[1], bottom16)

        samples = [0.5 - 0.5 / math.sqrt(3.0), 0.5 + 0.5 / math.sqrt(3.0)]
        two = range(2)

        def at_points(low, high):
            change = high - low
            return [low + s * change for s in samples], change * (1.0 / element_span)

        def coarse_force(values, stiffness):
            grads = []
            for i in range(3):
                v = corners_of(values[i])
                vz, sz = {}, {}
                for a in two:
                    for b in two:
                        vz[a, b], sz[a, b] = at_points(v[a, b, 0], v[a, b, 1])
                vv, vs, sv = {}, {}, {}
                for a in two:
                    for k in two:
                        vv[a, k], vs[a, k] = at_points(vz[a, 0][k], vz[a, 1][k])
                    sv[a], unused = at_points(sz[a, 0], sz[a, 1])
                dx, dy, dz = {}, {}, {}
                for k in two:
                    for j in two:
                        dx[j, k] = (vv[1, k][j] - vv[0, k][j]) * (1.0 / element_span)
                    line, unused = at_points(vs[0, k], vs[1, k])
                    for h in two:
                        dy[h, k] = line[h]
                for j in two:
                    line, unused = at_points(sv[0][j], sv[1][j])
                    for h in two:
                        dz[h, j] = line[h]
                grads.append((dx, dy, dz))
            weight = element_span**2 / 8.0
            scaled = weight * stiffness
            scaled_four = lame_ratio * scaled
            sums = [({}, {}, {}) for i in range(3)]

            def add(table, key, value):
                table[key] = table[key] + value if key in table else value

            for h in two:
                for j in two:
                    for k in two:
                        deform = [
                            [grads[i][0][j, k], grads[i][1][h, k], grads[i][2][h, j]]
                            for i in range(3)
                        ]
                        for i in range(3):
                            deform[i][i] = deform[i][i] + 1.0
                        stress = point_stress(deform, scaled, scaled_four)
                        for i in range(3):
                            add(sums[i][0], (j, k), stress[i][0])
                            add(sums[i][1], (h, k), stress[i][1])
                            add(sums[i][2], (h, j), stress[i][2])

            def ends_of(first, second):
                high = samples[0] * first + samples[1] * second
                return [first + second - high, high]

            forces = []
            for i in range(3):
                part = {}
                qx, qy, qz = sums[i]
                along_z = [ends_of(qx[j, 0], qx[j, 1]) for j in two]
                for c in two:
                    line = ends_of(along_z[0][c], along_z[1][c])
                    for b in two:
                        part[0, b, c] = -line[b]
                        part[1, b, c] = line[b]
                along_z = [ends_of(qy[h, 0], qy[h, 1]) for h in two]
                for c in two:
                    line = ends_of(along_z[0][c], along_z[1][c])
                    for a in two:
                        part[a, 0, c] = part[a, 0, c] - line[a]
                        part[a, 1, c] = part[a, 1, c] + line[a]
                along_y = [ends_of(qz[h, 0], qz[h, 1]) for h in two]
                for b in two:
                    line = ends_of(along_y[0][b], along_y[1][b])
                    for a in two:
                        part[a, b, 0] = part[a, b, 0] - line[a]
                        part[a, b, 1] = part[a, b, 1] + line[a]
                forces.append(assemble(part))
            return forces

        stiffness = u[0, :, STIFF_SLOT, :]
        keep_coarse = jnp.where(bottom16, 0.0, 1.0)
        start = [u[i, :, 0, :] for i in range(3)]
        restricted = [
            assemble({corner: shares[i, :, n, :] for n, corner in enumerate(CORNERS)})
            for i in range(3)
        ]
        before = coarse_force(start, stiffness)
        move = [(steps[0][1] / coarse_bound) * keep_coarse * restricted[i] for i in range(3)]
        level = [start[i] + move[i] for i in range(3)]
        for held, added in steps[1:]:
            force = coarse_force(level, stiffness)
            for i in range(3):
                z = keep_coarse * (restricted[i] + before[i] - force[i])
                move[i] = held * move[i] + (added / coarse_bound) * z
                level[i] = level[i] + move[i]

        for i in range(3):
            change = corners_of(level[i] - start[i])
            for n, corner in enumerate(CORNERS):
                raised[i, :, n, :] = change[corner]
        for pair in range(spans[4][0], spans[4][0] + spans[4][1] + 2):
            lift = jnp.dot(
                transfer_back[...],
                jnp.concatenate([raised[i, pair] for i in range(3)], 1),
                preferred_element_type=jnp.float32,
                precision=lax.Precision.HIGHEST,
            )
            for i in range(3):
                u[i, pair] = u[i, pair] + lift[:, width * i : width * (i + 1)]

        smooth(spans[4:7])

        sides = []
        blank = jnp.zeros((29, width), jnp.float32)
        for q in range(2):
            ends_here = jnp.concatenate(
                [u[i, OWN + q] for i in range(3)]
                + [level[i][OWN + q : OWN + q + 1] for i in range(3)]
                + [blank],
                0,
            )
            sides.append(ends_here.T.reshape(width // 8, 8, 128))
        out[:, 0] = jnp.where(lower, sides[0], pltpu.roll(sides[1], 4, 1))
        out[:, 1] = jnp.where(lower, pltpu.roll(sides[0], 4, 1), sides[1])

    return cycle_kernel


def solution(mesh):
    rows_of, columns_of = mesh.shape["gx"], mesh.shape["gy"]
    devices = rows_of * columns_of
    own_layers = EZ // devices
    width = 4 * devices
    spread, collect, fine_bound = element_tables()
    coarse_bound = build_tables([0.0, 1.0], 2)[2]
    transfer = transfer_table()
    limit = pltpu.CompilerParams(vmem_limit_bytes=48 * 1024 * 1024)
    f32 = jnp.float32

    pack = pl.pallas_call(
        pack_kernel,
        out_shape=jax.ShapeDtypeStruct((devices, 8, FIELD_COLUMNS), f32),
        scratch_shapes=[
            pltpu.VMEM((128, 384), f32),
            pltpu.VMEM((384, 128), f32),
            pltpu.VMEM((12, 160, 128), f32),
        ],
        compiler_params=limit,
    )
    cycle = pl.pallas_call(
        make_cycle_kernel(width, 2 * rows_of, own_layers, fine_bound, coarse_bound),
        out_shape=jax.ShapeDtypeStruct((devices // 2, 2, 8, 128), f32),
        scratch_shapes=[
            pltpu.VMEM((3, PAIR_SLOTS, 32, width), f32),
            pltpu.VMEM((3, PAIR_SLOTS, 32, width), f32),
            pltpu.VMEM((3, PAIR_SLOTS, 32, width), f32),
            pltpu.VMEM((3, PAIR_SLOTS, 8, width), f32),
            pltpu.VMEM((3, PAIR_SLOTS, 8, width), f32),
        ],
        compiler_params=limit,
    )
    unpack = pl.pallas_call(
        unpack_kernel,
        out_shape=(
            jax.ShapeDtypeStruct((3, 6, 3, 384), f32),
            jax.ShapeDtypeStruct((3, 2, 1, EZ), f32),
        ),
        scratch_shapes=[pltpu.VMEM((2, 128, 128), f32), pltpu.VMEM((384, 128), f32)],
        compiler_params=limit,
    )
    everyone = ("gy", "gx")

    def body(initial, forcing, modulus, solid_list):
        sent = pack(initial, forcing, modulus, solid_list, jnp.asarray(pack_table()))
        arrived = lax.all_to_all(sent, everyone, 0, 0, tiled=True)
        result = cycle(
            arrived.reshape(devices // 2, 2, 8, FIELD_COLUMNS),
            jnp.asarray(spread),
            jnp.asarray(collect),
            jnp.asarray(transfer),
            jnp.asarray(transfer.T.copy()),
        )
        back = lax.all_to_all(result.reshape(devices, 8, 128), everyone, 0, 0, tiled=True)
        return unpack(back, jnp.asarray(unpack_table()))

    placed = (
        P(None, "gx", "gy", None),
        P(None, "gx", "gy", None),
        P("gx", "gy", None),
        P("gx", "gy", None),
    )
    return jax.shard_map(
        body,
        mesh=mesh,
        in_specs=placed,
        out_specs=(P(None, "gx", "gy", None), P(None, "gx", "gy", None)),
        check_vma=False,
    )
```

profile of v0, /device:TPU:0, one launch (start us, length us, event | category | flops | bytes accessed | tf_op | source)
XLA Modules:
  0.0 95.1 jit_solution(17657513946126790007)
XLA Ops:
  0.6 0.0 copy-start
  0.6 1.3 %copy-done = bf16[384,1536]{1,0:T(8,128)(2,1)S(1)} copy-done((bf16[384,1536]{1,0:T(8,128)(2,1)S(1)}, bf16[384,1536]{1,0:T(8,128)(2,1)}, u32[]{:S(2)}) %copy-start) | copy-done | bytes 1179672
  1.9 0.0 copy-start.4
  1.9 0.9 copy-done.4
  2.8 0.0 copy-start.5
  2.8 0.9 copy-done.5
  3.7 0.0 copy-start.8
  3.7 0.7 copy-done.8
  4.4 0.0 copy-start.9
  4.4 0.7 copy-done.9
  5.1 1.7 %shard_map.113 = f32[32,8,1152]{2,1,0:T(8,128)S(1)} custom-call(f32[3,6,3,384]{3,2,1,0:T(4,128)S(1)} %copy-done.4, f32[3,6,3,384]{3,2,1,0:T(4,128)S(1)} %copy-done.5, f32[2,1,128]{2,1,0:T(1,128)S(1)} %copy-done.8, s32[1,1,192]{2,1,0:T(1,128)S(1)} %copy-done.9, bf16[384,1536]{1,0:T(8,128)(2,1)S(1)} %copy-done), custom_call_target="tpu_custom_call" | custom-call | tf_op jit(solution)/shard_map/pallas_call | solution.py:714
  6.8 0.0 copy-start.2
  6.8 0.0 copy-start.3
  6.8 0.0 copy-start.6
  6.8 0.0 copy-start.7
  6.8 37.8 %all_to_all.10 = f32[32,8,1152]{2,1,0:T(8,128)S(1)} all-to-all(f32[32,8,1152]{2,1,0:T(8,128)S(1)} %shard_map.113), channel_id=1, replica_groups=mesh['gx'=4,'gy'=8] {'gy','gx'}, dimensions={0} | all-to-all | bytes 2359296 | tf_op jit(solution)/shard_map/all_to_all | solution.py:715
  44.6 0.0 copy-start.1
  44.6 0.0 copy-done.2
  44.6 0.0 copy-done.3
  44.6 0.0 copy-done.6
  44.6 0.0 copy-done.7
  44.6 39.3 %shard_map.114 = f32[16,2,8,128]{3,2,1,0:T(8,128)S(1)} custom-call(f32[16,2,8,1152]{3,2,1,0:T(8,128)S(1)} %bitcast.2, bf16[192,336]{1,0:T(8,128)(2,1)S(1)} %copy-done.2, bf16[112,576]{1,0:T(8,128)(2,1)S(1)} %copy-done.3, f32[8,32]{1,0:T(8,128)S(1)} %copy-done.7, f32[32,8]{1,0:T(8,128)S(1)} %copy-done.6), custom_call_target="tpu_custom_call" | custom-call | tf_op jit(solution)/shard_map/pallas_call | solution.py:716
  84.0 10.1 %all_to_all.11.arrived = f32[32,8,128]{2,1,0:T(8,128)S(1)} all-to-all(f32[32,8,128]{2,1,0:T(8,128)S(1)} %bitcast.3), channel_id=1, replica_groups=mesh['gx'=4,'gy'=8] {'gy','gx'}, dimensions={0} | all-to-all | bytes 262144 | tf_op jit(solution)/shard_map/all_to_all | solution.py:723
  94.0 0.0 copy-done.1
  94.0 1.1 %shard_map.115 = (f32[3,6,3,384]{3,2,1,0:T(4,128)}, f32[3,2,1,128]{3,2,1,0:T(1,128)}) custom-call(f32[32,8,128]{2,1,0:T(8,128)S(1)} %all_to_all.11.arrived, bf16[256,384]{1,0:T(8,128)(2,1)S(1)} %copy-done.1), custom_call_target="tpu_custom_call" | custom-call | tf_op jit(solution)/shard_map/pallas_call | solution.py:724
Async XLA Ops:
  0.6 1.3 %copy-start = (bf16[384,1536]{1,0:T(8,128)(2,1)S(1)}, bf16[384,1536]{1,0:T(8,128)(2,1)}, u32[]{:S(2)}) copy-start(bf16[384,1536]{1,0:T(8,128)(2,1)} %constant.12.clone.table) | copy-start | bytes 3538948
  1.9 0.9 copy-start.4
  2.8 0.9 copy-start.5
  3.7 0.7 copy-start.8
  4.4 0.7 copy-start.9
  6.8 37.8 %copy-start.2 = (bf16[192,336]{1,0:T(8,128)(2,1)S(1)}, bf16[192,336]{1,0:T(8,128)(2,1)}, u32[]{:S(2)}) copy-start(bf16[192,336]{1,0:T(8,128)(2,1)} %constant.13.clone.spread) | copy-start | bytes 387076
  6.8 37.8 %copy-start.3 = (bf16[112,576]{1,0:T(8,128)(2,1)S(1)}, bf16[112,576]{1,0:T(8,128)(2,1)}, u32[]{:S(2)}) copy-start(bf16[112,576]{1,0:T(8,128)(2,1)} %constant.14.clone.collect) | copy-start | bytes 387076
  6.8 37.8 %copy-start.6 = (f32[32,8]{1,0:T(8,128)S(1)}, f32[32,8]{1,0:T(8,128)}, u32[]{:S(2)}) copy-start(f32[32,8]{1,0:T(8,128)} %constant.16.clone.transfer_back) | copy-start | bytes 3076
  6.8 37.8 %copy-start.7 = (f32[8,32]{1,0:T(8,128)S(1)}, f32[8,32]{1,0:T(8,128)}, u32[]{:S(2)}) copy-start(f32[8,32]{1,0:T(8,128)} %constant.15.clone.transfer) | copy-start | bytes 3076
  44.6 49.4 %copy-start.1 = (bf16[256,384]{1,0:T(8,128)(2,1)S(1)}, bf16[256,384]{1,0:T(8,128)(2,1)}, u32[]{:S(2)}) copy-start(bf16[256,384]{1,0:T(8,128)(2,1)} %constant.17.clone.table) | copy-start | bytes 589828
where the time goes:
time: 95.4 us; the launch traced here: 95.1 us
  blocking collectives  47.8 us (50%)
  Pallas kernels  42.1 us (44%)
  local copies, waits for them, and re-layouts  4.45 us (5%)
    pallas_call x1, Pallas kernels, body(): cycle(arrived.reshape(devices // 2, 2, 8, FIELD_COLUMNS), jnp.asarray(spr...  39.3 us
    all_to_all x1, blocking collectives, body(): arrived = lax.all_to_all(sent, everyone, 0, 0, tiled=True)  37.8 us
    all_to_all x1, blocking collectives, body(): lax.all_to_all(result.reshape(devices, 8, 128), everyone, 0, 0, tiled=True)  10.1 us
    unnamed x20, local copies, waits for them, and re-layouts  4.45 us

commit v1 on v0

v1 whole, which is shorter than its diff:
```python
import math

import jax
import jax.numpy as jnp
import numpy as np
from jax import lax
from jax.experimental import pallas as pl
from jax.experimental.pallas import tpu as pltpu
from jax.sharding import PartitionSpec as P

CHEB = 3
EZ = 128

element_span = 20.0
lame_ratio = 4.0
rest_ratio = 1.25
modulus_top = 2.0
spectrum_floor = 0.05
interval_centre = (1.0 + spectrum_floor) / 2.0
interval_radius = (1.0 - spectrum_floor) / 2.0
interval_ratio = interval_centre / interval_radius
inner_anchors = (0.5 - 0.5 / math.sqrt(5.0), 0.5 + 0.5 / math.sqrt(5.0))

BEFORE = 4
PAIRS = 6
BEFORE_B = 6
PAIRS_B = 8
BLOCK = 84
SENT = 512

SLOTS = [
    (0, 0, 0), (1, 0, 0), (2, 0, 0), (0, 1, 0), (0, 2, 0), (0, 0, 1), (0, 0, 2), None,
    (0, 1, 1), (0, 1, 2), (0, 2, 1), (0, 2, 2), (1, 0, 1), (1, 0, 2), (2, 0, 1), (2, 0, 2),
    (1, 1, 0), (1, 2, 0), (2, 1, 0), (2, 2, 0), (1, 1, 1), (1, 1, 2), (1, 2, 1), (1, 2, 2),
    None, None, None, None, (2, 1, 1), (2, 1, 2), (2, 2, 1), (2, 2, 2),
]
TWIN = 7
RESTRICTED_SLOT = 24
STIFF_SLOT = 25
OWN_SHIFT, SHIFT_X, SHIFT_Y, SHIFT_Z = (0, 0, 0), (1, 0, 0), (0, 1, 0), (0, 0, 1)
ELEMENT_ROWS = (
    [(slot, OWN_SHIFT) for slot in range(24)]
    + [(slot, SHIFT_Z) for slot in range(16, 20)]
    + [(slot, OWN_SHIFT) for slot in range(28, 32)]
    + [(slot, SHIFT_X) for slot in range(7)] + [None]
    + [(slot, SHIFT_Y) for slot in range(7)] + [(0, (0, 1, 1))]
    + [(slot, SHIFT_Z) for slot in range(7)] + [(0, (1, 0, 1))]
    + [(slot, SHIFT_X) for slot in range(8, 12)] + [(slot, SHIFT_Y) for slot in range(12, 16)]
    + [(0, (1, 1, 1)), (1, (0, 1, 1)), (2, (0, 1, 1)), (3, (1, 0, 1)), (4, (1, 0, 1))]
    + [(5, (1, 1, 0)), (6, (1, 1, 0)), (0, (1, 1, 0))]
)
ROWS = len(ELEMENT_ROWS)
DEPTH = 80
CORNERS = [(a, b, c) for a in range(2) for b in range(2) for c in range(2)]


def gauss_rule(point_count):
    if point_count == 2:
        offset = 1.0 / math.sqrt(3.0)
        points = [-offset, offset]
        weights = [1.0, 1.0]
    else:
        inner = math.sqrt(3.0 / 7.0 - 2.0 / 7.0 * math.sqrt(6.0 / 5.0))
        outer = math.sqrt(3.0 / 7.0 + 2.0 / 7.0 * math.sqrt(6.0 / 5.0))
        heavy = (18.0 + math.sqrt(30.0)) / 36.0
        light = (18.0 - math.sqrt(30.0)) / 36.0
        points = [-outer, -inner, inner, outer]
        weights = [light, heavy, heavy, light]
    return (np.array(points), np.array(weights))


def lagrange_tables(anchors, samples):
    values = np.zeros((len(samples), len(anchors)))
    slopes = np.zeros((len(samples), len(anchors)))
    for sample_index, sample in enumerate(samples):
        for anchor_index, anchor in enumerate(anchors):
            others = [
                location
                for location_index, location in enumerate(anchors)
                if location_index != anchor_index
            ]
            product = 1.0
            for location in others:
                product = product * (sample - location) / (anchor - location)
            values[sample_index, anchor_index] = product
            derivative = 0.0
            for skipped in range(len(others)):
                summand = 1.0 / (anchor - others[skipped])
                for kept_index in range(len(others)):
                    if kept_index != skipped:
                        summand = (
                            summand * (sample - others[kept_index]) / (anchor - others[kept_index])
                        )
                derivative = derivative + summand
            slopes[sample_index, anchor_index] = derivative
    return (values, slopes)


def outer_three(first, second, third):
    return (
        first[:, None, None, :, None, None]
        * second[None, :, None, None, :, None]
        * third[None, None, :, None, None, :]
    )


def build_tables(anchors, point_count):
    raw_points, raw_weights = gauss_rule(point_count)
    samples = (raw_points + 1.0) / 2.0
    weights = raw_weights / 2.0
    basis_values, slopes = lagrange_tables(anchors, samples)
    quad_total = point_count**3
    nodal_count = len(anchors) ** 3
    derivative_one = outer_three(slopes, basis_values, basis_values).reshape(
        quad_total, nodal_count
    )
    derivative_two = outer_three(basis_values, slopes, basis_values).reshape(
        quad_total, nodal_count
    )
    derivative_three = outer_three(basis_values, basis_values, slopes).reshape(
        quad_total, nodal_count
    )
    stacked = np.stack([derivative_one, derivative_two, derivative_three]) / element_span
    volume = (weights[:, None, None] * weights[None, :, None] * weights[None, None, :]).reshape(
        -1
    ) * element_span**3
    forward = stacked.reshape(3 * quad_total, nodal_count)
    backward = (stacked * volume[None, :, None]).reshape(3 * quad_total, nodal_count).T
    weighted = stacked * volume[None, :, None]
    laplace = weighted[0].T @ stacked[0] + weighted[1].T @ stacked[1] + weighted[2].T @ stacked[2]
    matrix = np.zeros((nodal_count, 3, nodal_count, 3))
    for first in range(3):
        for second in range(3):
            block = weighted[second].T @ stacked[first] + (lame_ratio - 1.0) * (
                weighted[first].T @ stacked[second]
            )
            if first == second:
                block = block + laplace
            matrix[:, first, :, second] = block
    matrix = matrix.reshape(3 * nodal_count, 3 * nodal_count)
    vector = 1.5 + np.cos(1.3 * np.arange(3 * nodal_count))
    for repeat in range(200):
        vector = matrix @ vector
        vector = vector / np.sqrt(vector @ vector)
    largest = vector @ (matrix @ vector)
    return (forward, backward, float(4.0 * modulus_top * 1.1 * largest))


def row_nodes():
    nodes = []
    for entry in ELEMENT_ROWS:
        slot = SLOTS[entry[0]] if entry else None
        if slot is None or any(s and n for s, n in zip(entry[1], slot)):
            nodes.append(None)
        else:
            a, b, c = (3 * s + n for s, n in zip(entry[1], slot))
            nodes.append(16 * a + 4 * b + c)
    return nodes


def halves(matrix):
    whole = np.asarray(matrix, np.float32)
    high = whole.astype(jnp.bfloat16)
    low = (whole - high.astype(np.float32)).astype(jnp.bfloat16)
    return high, low


def element_tables():
    forward, backward, bound = build_tables([0.0, inner_anchors[0], inner_anchors[1], 1.0], 4)
    spread = np.zeros((forward.shape[0], DEPTH))
    collect = np.zeros((ROWS, backward.shape[1]))
    for row, node in enumerate(row_nodes()):
        if node is not None:
            spread[:, row] = forward[:, node]
            collect[row, :] = backward[node, :]
    spread_high, spread_low = halves(spread)
    collect_high, collect_low = halves(collect)
    return (
        np.concatenate([spread_high, spread_high, spread_low], 1),
        np.concatenate([collect_high, collect_low], 0),
        bound,
    )


def transfer_table():
    table = np.zeros((8, 32))
    reach = (0.0, inner_anchors[0], inner_anchors[1])
    for row, corner in enumerate(CORNERS):
        for column, slot in enumerate(SLOTS):
            if slot is not None:
                weight = 1.0
                for side, node in zip(corner, slot):
                    weight = weight * (reach[node] if side else 1.0 - reach[node])
                table[row, column] = weight
    back = table.T.copy()
    back[TWIN] = back[0]
    return table.astype(np.float32), back.astype(np.float32)


def chebyshev_steps():
    steps = [(0.0, 1.0 / interval_centre)]
    ratio_now = 1.0 / interval_ratio
    for sweep in range(1, CHEB):
        ratio_next = 1.0 / (2.0 * interval_ratio - ratio_now)
        steps.append((ratio_next * ratio_now, 2.0 * ratio_next / interval_radius))
        ratio_now = ratio_next
    return steps


def stack_row(field, component, layer, b):
    return field * 54 + component * 18 + layer * 3 + b


def block_column(component, slot):
    return 72 + 4 * component + slot - 28 if slot >= 24 else 24 * component + slot


def pack_table():
    table = np.zeros((3, 128, 2, 2, 128), np.float32)
    for field in range(2):
        for x in range(2):
            for component in range(3):
                for column, slot in enumerate(SLOTS):
                    if slot is not None:
                        a, b, c = slot
                        row = stack_row(field, component, 3 * x + a, b)
                        table[c, row, field, x, block_column(component, column)] = 1.0
            table[0, 108 + x, 0, x, TWIN] = 1.0
    return table.reshape(384, 512).astype(jnp.bfloat16)


def unpack_table():
    table = np.zeros((2, 128, 3, 128), np.float32)
    for x in range(2):
        for component in range(3):
            for column, slot in enumerate(SLOTS):
                if slot is not None:
                    a, b, c = slot
                    row = stack_row(0, component, 3 * x + a, b)
                    table[x, component * 32 + column, c, row] = 1.0
            table[x, 96 + component, 0, 54 + 2 * component + x] = 1.0
    return table.reshape(256, 384).astype(jnp.bfloat16)


def exact_pick(values, table):
    high = values.astype(jnp.bfloat16)
    rest = values - high.astype(jnp.float32)
    middle = rest.astype(jnp.bfloat16)
    low = (rest - middle.astype(jnp.float32)).astype(jnp.bfloat16)
    count = values.shape[0]
    parts = jnp.dot(
        jnp.concatenate([high, middle, low], 0), table, preferred_element_type=jnp.float32
    )
    return parts[:count] + (parts[count : 2 * count] + parts[2 * count :])


def pack_kernel(
    initial_at, forcing_at, modulus_at, listing_at, table_at, out,
    initial, forcing, modulus, listing, table, rows, turned, places, ready,
):
    devices = out.shape[0]
    own_layers = EZ // devices
    sources = (listing_at, modulus_at, initial_at, forcing_at, table_at)
    copies = [
        pltpu.make_async_copy(source, here, ready.at[n])
        for n, (source, here) in enumerate(
            zip(sources, (listing, modulus, initial, forcing, table))
        )
    ]
    for copy in copies:
        copy.start()
    rows[108:128, :] = jnp.zeros((20, 384), jnp.float32)
    copies[0].wait()
    copies[1].wait()
    listed = listing[0].astype(jnp.float32)
    listed = jnp.concatenate([listed, jnp.full((1, 64), 256.0, jnp.float32)], 1)
    listed = jnp.broadcast_to(listed, (128, 256)).T
    lanes = lax.broadcasted_iota(jnp.int32, (256, 128), 1).astype(jnp.float32)
    row_at = lax.broadcasted_iota(jnp.int32, (128, 128), 0)
    stiff = jnp.zeros((128, 128), jnp.float32)
    for x in range(2):
        hit = jnp.max(jnp.where(listed == lanes + 128.0 * x, 1.0, 0.0), axis=0, keepdims=True)
        stiff = jnp.where(row_at == 108 + x, hit * modulus[x], stiff)
    copies[2].wait()
    copies[3].wait()
    for field, source in enumerate((initial, forcing)):
        for component in range(3):
            for layer in range(6):
                at = stack_row(field, component, layer, 0)
                rows[at : at + 3, :] = source[component, layer]
    for part in range(3):
        span = slice(128 * part, 128 * part + 128)
        turned[span, :] = rows[:, span].T
    picked = [turned[pl.ds(c, 128, stride=3), :] for c in range(3)]
    picked[0] = picked[0] + stiff.T
    copies[4].wait()
    wide = exact_pick(jnp.concatenate(picked, 1), table[...])
    lane = lax.broadcasted_iota(jnp.int32, (128, 128), 1)
    for block in range(4):
        here = wide[:, 128 * block : 128 * block + 128]
        tiles = [None] * (SENT // 128)
        for pair in range(PAIRS):
            first = BLOCK * pair
            moved = here if pair == 0 else pltpu.roll(here, 128 - 2 * pair, 0)
            if first % 128:
                moved = pltpu.roll(moved, first % 128, 1)
            for tile in range(first // 128, (first + BLOCK - 1) // 128 + 1):
                before = tiles[tile]
                if before is None:
                    tiles[tile] = moved
                else:
                    tiles[tile] = jnp.where(lane >= first - 128 * tile, moved, before)
        for tile in range(SENT // 128):
            at = 4 * block + tile
            places[at, 16:144, :] = tiles[tile]
            places[at, 0:16, :] = tiles[tile][112:128]
            places[at, 144:160, :] = tiles[tile][0:16]
    for block in range(4):
        for parity in range(2):
            for tile in range(SENT // 128):
                out[:, 2 * block + parity, 128 * tile : 128 * tile + 128] = places[
                    4 * block + tile, pl.ds(16 - BEFORE + parity, devices, stride=own_layers), :
                ]


def unpack_kernel(arrived, table, out, coarse_out, layers, turned):
    devices = arrived.shape[0]
    own_layers = EZ // devices
    for x in range(2):
        for layer in range(own_layers):
            row = (layer // 2) * 4 + x * 2 + layer % 2
            layers[x, pl.ds(layer, devices, stride=own_layers), :] = arrived[:, row, :]
    wide = exact_pick(jnp.concatenate([layers[0], layers[1]], 1), table[...])
    for c in range(3):
        turned[pl.ds(c, 128, stride=3), :] = wide[:, 128 * c : 128 * c + 128]
    for part in range(3):
        span = slice(128 * part, 128 * part + 128)
        back = turned[span, :].T
        for component in range(3):
            for layer in range(6):
                at = stack_row(0, component, layer, 0)
                out[component, layer, :, span] = back[at : at + 3, :]
    back = wide[:, 0:128].T
    for component in range(3):
        for x in range(2):
            at = 54 + 2 * component + x
            coarse_out[component, x] = back[at : at + 1, :]


def cofactor_rows(deform):
    return [
        [
            deform[(row_at + 1) % 3][(column + 1) % 3] * deform[(row_at + 2) % 3][(column + 2) % 3]
            - deform[(row_at + 1) % 3][(column + 2) % 3]
            * deform[(row_at + 2) % 3][(column + 1) % 3]
            for column in range(3)
        ]
        for row_at in range(3)
    ]


def point_stress(deform, stiffness, stiffness_four):
    cofactors = cofactor_rows(deform)
    jacobian = (
        deform[0][0] * cofactors[0][0]
        + deform[0][1] * cofactors[0][1]
        + deform[0][2] * cofactors[0][2]
    )
    pressure = stiffness_four * (jacobian - rest_ratio)
    return [
        [stiffness * deform[i][d] + pressure * cofactors[i][d] for d in range(3)] for i in range(3)
    ]


coarse_samples = [0.5 - 0.5 / math.sqrt(3.0), 0.5 + 0.5 / math.sqrt(3.0)]
two = range(2)


def at_points(low, high):
    change = high - low
    return [low + s * change for s in coarse_samples], change * (1.0 / element_span)


def ends_of(first, second):
    high = coarse_samples[0] * first + coarse_samples[1] * second
    return [first + second - high, high]


def high_low(values):
    high = values.astype(jnp.bfloat16)
    return high, (values - high.astype(jnp.float32)).astype(jnp.bfloat16)


class Slab:
    def __init__(self, width, across):
        self.width = width
        self.y_step = 2 * across
        lane = lax.broadcasted_iota(jnp.int32, (8, width), 1)
        x = (lane // 2) % across
        self.bottom, self.top, self.even = x == 0, x == across - 1, lane % 2 == 0
        self.row = lax.broadcasted_iota(jnp.int32, (8, width), 0)
        row = lax.broadcasted_iota(jnp.int32, (32, width), 0)
        lane = lax.broadcasted_iota(jnp.int32, (32, width), 1)
        on_face = (row == 0) | ((row >= 3) & (row <= 11))
        self.keep = jnp.where(on_face & ((lane // 2) % across == 0), 0.0, 1.0)

    def lanes(self, v, step):
        return pltpu.roll(v, step % self.width, 1)

    def next_x(self, v):
        return jnp.where(self.top, 0.0, self.lanes(v, -2))

    def next_y(self, v):
        return self.lanes(v, -self.y_step)

    def next_z(self, v, ahead):
        return jnp.where(self.even, self.lanes(v, -1), self.lanes(ahead, 1))

    def onto_x(self, v):
        return jnp.where(self.bottom, 0.0, self.lanes(v, 2))

    def onto_y(self, v):
        return self.lanes(v, self.y_step)

    def gather(self, here, ahead):
        row = self.row
        g0, g1, g2, g3 = here[0:8], here[8:16], here[16:24], here[24:32]
        z0 = self.next_z(g0, ahead[0:8])
        z2 = self.next_z(g2, ahead[16:24])
        y0 = self.next_y(g0)
        yz, xz, xy = self.next_y(z0), self.next_x(z0), self.next_x(y0)
        edges = jnp.where(row <= 2, yz, jnp.where(row <= 4, xz, xy))
        return jnp.concatenate(
            [
                g0,
                g1,
                g2,
                jnp.where(row < 4, z2, g3),
                self.next_x(g0),
                jnp.where(row == 7, yz, y0),
                jnp.where(row == 7, xz, z0),
                jnp.where(row < 4, self.next_x(g1), self.next_y(g1)),
                jnp.where(row == 0, self.next_x(yz), edges),
                jnp.zeros_like(g0),
            ],
            0,
        )

    def scatter(self, part, behind):
        row = self.row
        g0, g1, g2, g3, x0, y0, z0, sides, edges = (part[8 * n : 8 * n + 8] for n in range(9))
        edges_x = self.onto_x(edges)
        yz = jnp.where(row == 0, edges_x, jnp.where(row == 7, y0, edges))
        yz = jnp.where((row <= 2) | (row == 7), yz, 0.0)
        z0 = jnp.where(row == 7, self.onto_x(z0), z0)
        z0 = z0 + jnp.where((row == 3) | (row == 4), edges_x, 0.0) + self.onto_y(yz)
        y0 = jnp.where(row == 7, edges_x, y0 + jnp.where(row >= 5, edges_x, 0.0))
        z2 = g3
        own0 = g0 + self.onto_x(x0) + self.onto_y(y0)
        own0 = own0 + jnp.where(self.even, behind[0], self.lanes(z0, 1))
        own1 = g1 + jnp.where(row < 4, self.onto_x(sides), self.onto_y(sides))
        share2 = jnp.where(self.even, behind[1], self.lanes(z2, 1))
        own2 = g2 + jnp.where(row < 4, share2, 0.0)
        own3 = jnp.where(row < 4, 0.0, g3)
        own0 = own0 + jnp.where(row == 0, pltpu.roll(own0, 1, 0), 0.0)
        own0 = jnp.where(row == 7, pltpu.roll(own0, 7, 0), own0)
        moved = (self.lanes(z0, -1), self.lanes(z2, -1))
        return jnp.concatenate([own0, own1, own2, own3], 0), moved

    def apply(self, u, stiff, spread, collect, first, count, finish):
        width = self.width

        def step(index, carry):
            pair = first + 2 * index
            blocks = [
                self.gather(u[i, pair + q], u[i, pair + q + 1])
                for i in range(3)
                for q in range(2)
            ]
            high, low = high_low(jnp.concatenate(blocks, 1))
            gradient = jnp.dot(
                spread[...],
                jnp.concatenate([high, low, high], 0),
                preferred_element_type=jnp.float32,
            )
            stiffness = jnp.concatenate([stiff[pl.ds(pair + q, 1), :] for q in range(2)], 1)
            deform = [
                [
                    gradient[64 * e : 64 * e + 64, 2 * width * i : 2 * width * (i + 1)]
                    + (1.0 if i == e else 0.0)
                    for e in range(3)
                ]
                for i in range(3)
            ]
            stress = point_stress(deform, stiffness, lame_ratio * stiffness)
            stress = jnp.concatenate(
                [jnp.concatenate([stress[i][e] for i in range(3)], 1) for e in range(3)], 0
            )
            high, low = high_low(stress)
            force = jnp.dot(collect[...], high, preferred_element_type=jnp.float32)
            force = force[0:ROWS] + (
                force[ROWS:] + jnp.dot(collect[0:ROWS], low, preferred_element_type=jnp.float32)
            )
            carry = list(carry)
            totals = [[], []]
            for q in range(2):
                for i in range(3):
                    at = (2 * i + q) * width
                    total, carry[i] = self.scatter(force[:, at : at + width], carry[i])
                    totals[q].append(total)
            for q in range(2):
                finish(pair + q, totals[q])
            return tuple(carry)

        none = jnp.zeros((8, width), jnp.float32)
        lax.fori_loop(0, (count + 1) // 2, step, tuple((none, none) for i in range(3)))

    def smooth(self, u, f, f_shift, d, stiff, spread, collect, spans, bound):
        for (first, count), (held, added) in zip(spans, chebyshev_steps()):

            def finish(pair, forces, held=held, added=added):
                for i in range(3):
                    z = (added / bound) * self.keep * (f[i, pair + f_shift] - forces[i])
                    move = held * d[i, pair] + z if held else z
                    d[i, pair] = move
                    u[i, pair] = u[i, pair] + move

            self.apply(u, stiff, spread, collect, first, count, finish)

    def coarse_next_z(self, v):
        return self.next_z(v, pltpu.roll(v, 7, 0))

    def coarse_onto_z(self, v):
        return jnp.where(self.even, pltpu.roll(self.lanes(v, -1), 1, 0), self.lanes(v, 1))

    def corners_of(self, v):
        found = {(0, 0, 0): v, (0, 0, 1): self.coarse_next_z(v)}
        for c in range(2):
            found[0, 1, c] = self.next_y(found[0, 0, c])
        for b in range(2):
            for c in range(2):
                found[1, b, c] = self.next_x(found[0, b, c])
        return found

    def assemble(self, part):
        line = {
            (a, b): part[a, b, 0] + self.coarse_onto_z(part[a, b, 1])
            for a in range(2)
            for b in range(2)
        }
        face = [line[a, 0] + self.onto_y(line[a, 1]) for a in range(2)]
        return face[0] + self.onto_x(face[1])

    def coarse_force(self, values, stiffness):
        grads = []
        for i in range(3):
            v = self.corners_of(values[i])
            vz, sz = {}, {}
            for a in two:
                for b in two:
                    vz[a, b], sz[a, b] = at_points(v[a, b, 0], v[a, b, 1])
            vv, vs, sv = {}, {}, {}
            for a in two:
                for k in two:
                    vv[a, k], vs[a, k] = at_points(vz[a, 0][k], vz[a, 1][k])
                sv[a], unused = at_points(sz[a, 0], sz[a, 1])
            dx, dy, dz = {}, {}, {}
            for k in two:
                for j in two:
                    dx[j, k] = (vv[1, k][j] - vv[0, k][j]) * (1.0 / element_span)
                line, unused = at_points(vs[0, k], vs[1, k])
                for h in two:
                    dy[h, k] = line[h]
            for j in two:
                line, unused = at_points(sv[0][j], sv[1][j])
                for h in two:
                    dz[h, j] = line[h]
            grads.append((dx, dy, dz))
        weight = element_span**2 / 8.0
        scaled = weight * stiffness
        scaled_four = lame_ratio * scaled
        sums = [({}, {}, {}) for i in range(3)]

        def add(table, key, value):
            table[key] = table[key] + value if key in table else value

        for h in two:
            for j in two:
                for k in two:
                    deform = [
                        [grads[i][0][j, k], grads[i][1][h, k], grads[i][2][h, j]]
                        for i in range(3)
                    ]
                    for i in range(3):
                        deform[i][i] = deform[i][i] + 1.0
                    stress = point_stress(deform, scaled, scaled_four)
                    for i in range(3):
                        add(sums[i][0], (j, k), stress[i][0])
                        add(sums[i][1], (h, k), stress[i][1])
                        add(sums[i][2], (h, j), stress[i][2])

        forces = []
        for i in range(3):
            part = {}
            qx, qy, qz = sums[i]
            along_z = [ends_of(qx[j, 0], qx[j, 1]) for j in two]
            for c in two:
                line = ends_of(along_z[0][c], along_z[1][c])
                for b in two:
                    part[0, b, c] = -line[b]
                    part[1, b, c] = line[b]
            along_z = [ends_of(qy[h, 0], qy[h, 1]) for h in two]
            for c in two:
                line = ends_of(along_z[0][c], along_z[1][c])
                for a in two:
                    part[a, 0, c] = part[a, 0, c] - line[a]
                    part[a, 1, c] = part[a, 1, c] + line[a]
            along_y = [ends_of(qz[h, 0], qz[h, 1]) for h in two]
            for b in two:
                line = ends_of(along_y[0][b], along_y[1][b])
                for a in two:
                    part[a, b, 0] = part[a, b, 0] - line[a]
                    part[a, b, 1] = part[a, b, 1] + line[a]
            forces.append(self.assemble(part))
        return forces


def make_first_kernel(width, across, own_layers, fine_bound):
    own = BEFORE // 2
    own_pairs = (own_layers + 1) // 2
    spans = []
    for n in (4, 3, 2, 1):
        low, high = BEFORE - n, BEFORE + own_layers + n - 1
        spans.append((low // 2, (high + 1) // 2 - low // 2))

    def first_kernel(
        arrived, spread, collect, transfer, message, edge, f, u, d, stiff, shares, turned
    ):
        slab = Slab(width, across)
        row = slab.row
        u[...] = jnp.zeros(u.shape, jnp.float32)
        f[...] = jnp.zeros(f.shape, jnp.float32)
        shares[...] = jnp.zeros(shares.shape, jnp.float32)
        stiff[...] = jnp.zeros(stiff.shape, jnp.float32)
        lower = lax.broadcasted_iota(jnp.int32, (width // 8, 8, 128), 1) < 4
        for tile in range(SENT // 128):
            span = slice(128 * tile, 128 * tile + 128)
            first, second = arrived[:, 0, :, span], arrived[:, 1, :, span]
            value = jnp.where(lower, first, pltpu.roll(second, 4, 1))
            load = jnp.where(lower, pltpu.roll(first, 4, 1), second)
            turned[0, span, :] = value.reshape(width, 128).T
            turned[1, span, :] = load.reshape(width, 128).T
        for field, target in enumerate((u, f)):
            for pair in range(PAIRS):
                base = BLOCK * pair
                for i in range(3):
                    parts = [
                        turned[field, base + 24 * i + 8 * n : base + 24 * i + 8 * n + 8, :]
                        for n in range(3)
                    ]
                    inner = turned[field, base + 68 + 4 * i : base + 76 + 4 * i, :]
                    if field == 0 and i == 0:
                        stiff[pair : pair + 1, :] = parts[0][TWIN : TWIN + 1]
                    parts[0] = jnp.where(row == TWIN, pltpu.roll(parts[0], TWIN, 0), parts[0])
                    parts.append(jnp.where(row < 4, 0.0, inner))
                    whole = jnp.concatenate(parts, 0)
                    target[i, pair] = whole * slab.keep if field == 0 else whole

        slab.smooth(u, f, 0, d, stiff, spread, collect, spans[0:3], fine_bound)

        def restrict(pair, forces):
            rest = jnp.concatenate([slab.keep * (f[i, pair] - forces[i]) for i in range(3)], 1)
            corner = jnp.dot(
                transfer[...],
                rest,
                preferred_element_type=jnp.float32,
                precision=lax.Precision.HIGHEST,
            )
            for i in range(3):
                shares[i, pair] = corner[:, width * i : width * (i + 1)]

        slab.apply(u, stiff, spread, collect, *spans[3], restrict)

        restricted = [
            slab.assemble({corner: shares[i, :, n, :] for n, corner in enumerate(CORNERS)})
            for i in range(3)
        ]
        for q in range(own_pairs):
            hard = stiff[own + q : own + q + 1, :]
            for i in range(3):
                message[i, q] = u[i, own + q]
                message[i, q, RESTRICTED_SLOT : RESTRICTED_SLOT + 1, :] = restricted[i][
                    own + q : own + q + 1
                ]
                edge[q, i : i + 1, :] = u[i, own + q, 0:1, :]
                edge[q, 3 + i : 4 + i, :] = restricted[i][own + q : own + q + 1]
            message[0, q, STIFF_SLOT : STIFF_SLOT + 1, :] = hard
            edge[q, 6:8, :] = jnp.broadcast_to(hard, (2, width))

    return first_kernel


def full_reach(own_layers):
    return -(-3 // own_layers)


def coarse_reach(own_layers):
    return -(-5 // own_layers)


def make_second_kernel(width, across, own_layers, fine_bound, coarse_bound):
    own = BEFORE_B // 2
    own_pairs = (own_layers + 1) // 2
    shift = (BEFORE - BEFORE_B) // 2
    near, far = full_reach(own_layers), coarse_reach(own_layers)
    steps = chebyshev_steps()
    spans = []
    for n in (3, 2, 1):
        low, high = BEFORE_B - n, BEFORE_B + own_layers + n - 1
        spans.append((low // 2, (high + 1) // 2 - low // 2))

    def second_kernel(*refs):
        messages = dict(zip(range(-near, near + 1), refs[: 2 * near + 1]))
        refs = refs[2 * near + 1 :]
        outer = [n for n in range(-far, far + 1) if abs(n) > near]
        edges = dict(zip(outer, refs[: len(outer)]))
        f, spread, collect, transfer_back, out, u, d, stiff, coarse, raised = refs[len(outer) :]
        slab = Slab(width, across)

        def pair_of(pair, fetch):
            found = []
            for parity in range(2):
                layer = 2 * pair - BEFORE_B + parity
                device = layer // own_layers
                layer = layer - device * own_layers
                found.append((device, layer // 2, layer % 2))
            values = [fetch(device, q) for device, q, parity in found]
            if found[0][:2] == found[1][:2] or (values[0] is None and values[1] is None):
                return values[0]
            for parity in range(2):
                if values[parity] is None:
                    values[parity] = jnp.zeros_like(values[1 - parity])
                elif found[parity][2] != parity:
                    values[parity] = slab.lanes(values[parity], 2 * parity - 1)
            lane = lax.broadcasted_iota(jnp.int32, values[0].shape, 1)
            return jnp.where(lane % 2 == 0, values[0], values[1])

        u[...] = jnp.zeros(u.shape, jnp.float32)
        coarse[...] = jnp.zeros(coarse.shape, jnp.float32)
        d[...] = jnp.zeros(d.shape, jnp.float32)
        for pair in range(PAIRS_B):
            for i in range(3):
                whole = pair_of(pair, lambda n, q: messages[n][i, q] if n in messages else None)
                if whole is not None:
                    u[i, pair] = whole
            for n in range(7):

                def fetch(device, q, n=n):
                    if device in messages:
                        i, slot = ((n, 0), (n - 3, RESTRICTED_SLOT), (0, STIFF_SLOT))[n // 3]
                        return messages[device][i, q, slot : slot + 1, :]
                    return edges[device][q, n : n + 1, :] if device in edges else None

                line = pair_of(pair, fetch)
                if line is not None:
                    coarse[n, pair : pair + 1, :] = line
        stiff[...] = coarse[6]

        stiffness = coarse[6]
        keep_coarse = jnp.where(slab.bottom, 0.0, 1.0)
        start = [coarse[i] for i in range(3)]
        restricted = [coarse[3 + i] for i in range(3)]
        before = slab.coarse_force(start, stiffness)
        move = [(steps[0][1] / coarse_bound) * keep_coarse * restricted[i] for i in range(3)]
        level = [start[i] + move[i] for i in range(3)]
        for held, added in steps[1:]:
            force = slab.coarse_force(level, stiffness)
            for i in range(3):
                z = keep_coarse * (restricted[i] + before[i] - force[i])
                move[i] = held * move[i] + (added / coarse_bound) * z
                level[i] = level[i] + move[i]

        for i in range(3):
            change = slab.corners_of(level[i] - start[i])
            for n, corner in enumerate(CORNERS):
                raised[i, :, n, :] = change[corner]
        for pair in range(spans[0][0], min(spans[0][0] + spans[0][1] + 1, PAIRS_B)):
            lift = jnp.dot(
                transfer_back[...],
                jnp.concatenate([raised[i, pair] for i in range(3)], 1),
                preferred_element_type=jnp.float32,
                precision=lax.Precision.HIGHEST,
            )
            for i in range(3):
                u[i, pair] = u[i, pair] + lift[:, width * i : width * (i + 1)]

        slab.smooth(u, f, shift, d, stiff, spread, collect, spans, fine_bound)

        lower = lax.broadcasted_iota(jnp.int32, (width // 8, 8, 128), 1) < 4
        sides = []
        blank = jnp.zeros((29, width), jnp.float32)
        for q in range(2):
            ends_here = jnp.concatenate(
                [u[i, own + q] for i in range(3)]
                + [level[i][own + q : own + q + 1] for i in range(3)]
                + [blank],
                0,
            )
            sides.append(ends_here.T.reshape(width // 8, 8, 128))
        out[:, 0] = jnp.where(lower, sides[0], pltpu.roll(sides[1], 4, 1))
        out[:, 1] = jnp.where(lower, pltpu.roll(sides[0], 4, 1), sides[1])

    return second_kernel


def solution(mesh):
    rows_of, columns_of = mesh.shape["gx"], mesh.shape["gy"]
    devices = rows_of * columns_of
    own_layers = EZ // devices
    own_pairs = (own_layers + 1) // 2
    width = 4 * devices
    across = 2 * rows_of
    near, far = full_reach(own_layers), coarse_reach(own_layers)
    spread, collect, fine_bound = element_tables()
    coarse_bound = build_tables([0.0, 1.0], 2)[2]
    transfer, transfer_back = transfer_table()
    wide = pltpu.CompilerParams(vmem_limit_bytes=60 * 1024 * 1024)
    limit = pltpu.CompilerParams(vmem_limit_bytes=48 * 1024 * 1024)
    f32 = jnp.float32

    pack = pl.pallas_call(
        pack_kernel,
        out_shape=jax.ShapeDtypeStruct((devices, 8, SENT), f32),
        in_specs=[pl.BlockSpec(memory_space=pl.ANY)] * 5,
        out_specs=pl.BlockSpec(memory_space=pltpu.VMEM),
        scratch_shapes=[
            pltpu.VMEM((3, 6, 3, 384), f32),
            pltpu.VMEM((3, 6, 3, 384), f32),
            pltpu.VMEM((2, 1, EZ), f32),
            pltpu.VMEM((1, 1, 192), jnp.int32),
            pltpu.VMEM((384, 512), jnp.bfloat16),
            pltpu.VMEM((128, 384), f32),
            pltpu.VMEM((384, 128), f32),
            pltpu.VMEM((16, 160, 128), f32),
            pltpu.SemaphoreType.DMA((5,)),
        ],
        compiler_params=wide,
    )
    first = pl.pallas_call(
        make_first_kernel(width, across, own_layers, fine_bound),
        out_shape=(
            jax.ShapeDtypeStruct((3, own_pairs, 32, width), f32),
            jax.ShapeDtypeStruct((own_pairs, 8, width), f32),
            jax.ShapeDtypeStruct((3, PAIRS, 32, width), f32),
        ),
        scratch_shapes=[
            pltpu.VMEM((3, 8, 32, width), f32),
            pltpu.VMEM((3, 8, 32, width), f32),
            pltpu.VMEM((8, width), f32),
            pltpu.VMEM((3, 8, 8, width), f32),
            pltpu.VMEM((2, SENT, width), f32),
        ],
        compiler_params=limit,
    )
    second = pl.pallas_call(
        make_second_kernel(width, across, own_layers, fine_bound, coarse_bound),
        out_shape=jax.ShapeDtypeStruct((devices // 2, 2, 8, 128), f32),
        scratch_shapes=[
            pltpu.VMEM((3, PAIRS_B + 2, 32, width), f32),
            pltpu.VMEM((3, PAIRS_B, 32, width), f32),
            pltpu.VMEM((PAIRS_B, width), f32),
            pltpu.VMEM((7, PAIRS_B, width), f32),
            pltpu.VMEM((3, PAIRS_B, 8, width), f32),
        ],
        compiler_params=limit,
    )
    unpack = pl.pallas_call(
        unpack_kernel,
        out_shape=(
            jax.ShapeDtypeStruct((3, 6, 3, 384), f32),
            jax.ShapeDtypeStruct((3, 2, 1, EZ), f32),
        ),
        scratch_shapes=[pltpu.VMEM((2, 128, 128), f32), pltpu.VMEM((384, 128), f32)],
        compiler_params=limit,
    )
    everyone = ("gy", "gx")

    def from_device(block, distance):
        place = [k % rows_of * columns_of + k // rows_of for k in range(devices)]
        route = [(place[(k + distance) % devices], place[k]) for k in range(devices)]
        return lax.ppermute(block, ("gx", "gy"), route)

    def body(initial, forcing, modulus, solid_list):
        sent = pack(initial, forcing, modulus, solid_list, jnp.asarray(pack_table()))
        arrived = lax.all_to_all(sent, everyone, 0, 0, tiled=True)
        message, edge, load = first(
            arrived.reshape(devices // 2, 2, 8, SENT),
            jnp.asarray(spread),
            jnp.asarray(collect),
            jnp.asarray(transfer),
        )
        messages = [
            from_device(message, n) if n else message for n in range(-near, near + 1)
        ]
        edges = [from_device(edge, n) for n in range(-far, far + 1) if abs(n) > near]
        result = second(
            *messages,
            *edges,
            load,
            jnp.asarray(spread),
            jnp.asarray(collect),
            jnp.asarray(transfer_back),
        )
        back = lax.all_to_all(result.reshape(devices, 8, 128), everyone, 0, 0, tiled=True)
        return unpack(back, jnp.asarray(unpack_table()))

    placed = (
        P(None, "gx", "gy", None),
        P(None, "gx", "gy", None),
        P("gx", "gy", None),
        P("gx", "gy", None),
    )
    return jax.shard_map(
        body,
        mesh=mesh,
        in_specs=placed,
        out_specs=(P(None, "gx", "gy", None), P(None, "gx", "gy", None)),
        check_vma=False,
    )
```

time: 95.4 us -> 71.6 us (0.75)
  Pallas kernels: 42.1 us -> 25.8 us
  blocking collectives: 47.8 us -> 34.3 us
  waiting for transfers between devices: 0 us -> 6.49 us
  local copies, waits for them, and re-layouts: 4.45 us -> 0.03 us
  starting transfers between devices: 0 us -> 4 us
    pallas_call x1 -> x2, Pallas kernels: 39.3 us -> 21.8 us  [the longest x1 12 us: body(): first(arrived.reshape(devices // 2, 2, 8, SENT), jnp.asarray(spread), jnp...]
    all_to_all x1, blocking collectives: 37.8 us -> 22.9 us  [body(): arrived = lax.all_to_all(sent, everyone, 0, 0, tiled=True)]
    ppermute x0 -> x4, waiting for transfers between devices: none -> 6.49 us  [from_device(): return lax.ppermute(block, ('gx', 'gy'), route)]
    unnamed x20 -> x10, local copies, waits for them, and re-layouts: 4.45 us -> 0.03 us
    ppermute x0 -> x4, starting transfers between devices: none -> 4 us  [from_device(): return lax.ppermute(block, ('gx', 'gy'), route)]
    all_to_all x1, blocking collectives: 10.1 us -> 11.4 us  [body(): lax.all_to_all(result.reshape(devices, 8, 128), everyone, 0, 0, tiled=True)]
    pallas_call x1, Pallas kernels: 1.71 us -> 2.95 us  [body(): pack(initial, forcing, modulus, solid_list, jnp.asarray(pack_table()))]
  transfers between devices with their start and end apart: 0 -> 4, of which waited for: 0 -> 2; matrix products, arithmetic and copies ran while one was open for 0% -> 0% of each run, Pallas kernels for 0% -> 0%
where the time goes in v1:
time: 71.6 us; the launch traced here: 71.3 us
  blocking collectives  34.3 us (48%)
  Pallas kernels  25.8 us (36%)
  waiting for transfers between devices  6.49 us (9%)
  starting transfers between devices  4 us (6%)
    all_to_all x1, blocking collectives, body(): arrived = lax.all_to_all(sent, everyone, 0, 0, tiled=True)  22.9 us
    pallas_call x1, Pallas kernels, body(): first(arrived.reshape(devices // 2, 2, 8, SENT), jnp.asarray(spread), jnp...  12 us
    all_to_all x1, blocking collectives, body(): lax.all_to_all(result.reshape(devices, 8, 128), everyone, 0, 0, tiled=True)  11.4 us
    pallas_call x1, Pallas kernels, body(): second(*messages, *edges, load, jnp.asarray(spread), jnp.asarray(collect)...  9.82 us
    ppermute x4, waiting for transfers between devices, from_device(): return lax.ppermute(block, ('gx', 'gy'), route)  6.49 us
    ppermute x4, starting transfers between devices, from_device(): return lax.ppermute(block, ('gx', 'gy'), route)  4 us
    pallas_call x1, Pallas kernels, body(): pack(initial, forcing, modulus, solid_list, jnp.asarray(pack_table()))  2.95 us
  transfers between devices with their start and end apart: 4, of which 2 were waited for; matrix products, arithmetic and copies ran while one was open for 0% of the time, Pallas kernels for 0%

profile of v1, /device:TPU:0, one launch (start us, length us, event | category | flops | bytes accessed | tf_op | source)
XLA Modules:
  0.0 71.3 jit_solution(10669252417048021958)
XLA Ops:
  0.6 3.0 %shard_map.113 = f32[32,8,512]{2,1,0:T(8,128)} custom-call(f32[3,6,3,384]{3,2,1,0:T(4,128)} %initial_at.1, f32[3,6,3,384]{3,2,1,0:T(4,128)} %forcing_at.1, f32[2,1,128]{2,1,0:T(1,128)} %modulus_at.1, s32[1,1,192]{2,1,0:T(1,128)} %listing_at.1, bf16[384,512]{1,0:T(8,128)(2,1)} %constant.12.clone.table_at), custom_call_target="tpu_custom_call" | custom-call | tf_op jit(solution)/shard_map/pallas_call | solution.py:894
  3.6 0.0 copy-start
  3.6 0.0 copy-start.1
  3.6 0.0 copy-start.4
  3.6 22.9 %all_to_all.10 = f32[32,8,512]{2,1,0:T(8,128)S(1)} all-to-all(f32[32,8,512]{2,1,0:T(8,128)} %shard_map.113), channel_id=1, replica_groups=mesh['gx'=4,'gy'=8] {'gy','gx'}, dimensions={0} | all-to-all | bytes 1048576 | tf_op jit(solution)/shard_map/all_to_all | solution.py:895
  26.5 0.0 copy-done
  26.5 0.0 copy-done.1
  26.5 0.0 copy-done.4
  26.5 0.0 copy-start.3
  26.5 12.0 %shard_map.114 = (f32[3,2,32,128]{3,2,1,0:T(8,128)S(1)}, f32[2,8,128]{2,1,0:T(8,128)S(1)}, f32[3,6,32,128]{3,2,1,0:T(8,128)S(1)}) custom-call(f32[16,2,8,512]{3,2,1,0:T(8,128)S(1)} %bitcast.2, bf16[192,240]{1,0:T(8,128)(2,1)S(1)} %copy-done, bf16[144,192]{1,0:T(8,128)(2,1)S(1)} %copy-done.1, f32[8,32]{1,0:T(8,128)S(1)} %copy-done.4), custom_call_target="tpu_custom_call" | custom-call | tf_op jit(solution)/shard_map/pallas_call | solution.py:896
  38.5 2.0 %collective-permute-start.1 = (f32[3,2,32,128]{3,2,1,0:T(8,128)S(1)}, f32[3,2,32,128]{3,2,1,0:T(8,128)S(1)}, u32[]{:S(2)}, u32[]{:S(2)}) collective-permute-start(f32[3,2,32,128]{3,2,1,0:T(8,128)S(1)} %get-tuple-element.5.refs_1_), channel_id=1, source_target_pairs={{8,0},{16,8},{24,16},{1,24},{9,1},{17,9},{25,17},{2,25},{10,2},{18... | collective-permute-start | bytes 294920 | tf_op jit(solution)/shard_map/ppermute | solution.py:891
  40.4 0.0 collective-permute-start
  40.4 1.3 %collective-permute-start.3 = (f32[2,8,128]{2,1,0:T(8,128)S(1)}, f32[2,8,128]{2,1,0:T(8,128)S(1)}, u32[]{:S(2)}, u32[]{:S(2)}) collective-permute-start(f32[2,8,128]{2,1,0:T(8,128)S(1)} %get-tuple-element.6), channel_id=1, source_target_pairs={{16,0},{24,8},{1,16},{9,24},{17,1},{25,9},{2,17},{10,25},{18,2},{2... | collective-permute-start | bytes 24584 | tf_op jit(solution)/shard_map/ppermute | solution.py:891
  41.7 0.8 %collective-permute-start.2 = (f32[2,8,128]{2,1,0:T(8,128)S(1)}, f32[2,8,128]{2,1,0:T(8,128)S(1)}, u32[]{:S(2)}, u32[]{:S(2)}) collective-permute-start(f32[2,8,128]{2,1,0:T(8,128)S(1)} %get-tuple-element.6), channel_id=1, source_target_pairs={{23,0},{31,8},{0,16},{8,24},{16,1},{24,9},{1,17},{9,25},{17,2},{25... | collective-permute-start | bytes 24584 | tf_op jit(solution)/shard_map/ppermute | solution.py:891
  42.5 1.6 %collective-permute-done.3.refs_4_ = f32[2,8,128]{2,1,0:T(8,128)S(1)} collective-permute-done((f32[2,8,128]{2,1,0:T(8,128)S(1)}, f32[2,8,128]{2,1,0:T(8,128)S(1)}, u32[]{:S(2)}, u32[]{:S(2)}) %collective-permute-start.3) | collective-permute-done | bytes 8224 | tf_op jit(solution)/shard_map/ppermute | solution.py:891
  44.1 4.9 %collective-permute-done.2.refs_3_ = f32[2,8,128]{2,1,0:T(8,128)S(1)} collective-permute-done((f32[2,8,128]{2,1,0:T(8,128)S(1)}, f32[2,8,128]{2,1,0:T(8,128)S(1)}, u32[]{:S(2)}, u32[]{:S(2)}) %collective-permute-start.2) | collective-permute-done | bytes 8224 | tf_op jit(solution)/shard_map/ppermute | solution.py:891
  49.0 0.0 collective-permute-done.1.refs_2_
  49.0 0.0 collective-permute-done.refs_0_
  49.0 0.0 copy-done.3
  49.0 9.8 %shard_map.115 = f32[16,2,8,128]{3,2,1,0:T(8,128)S(1)} custom-call(f32[3,2,32,128]{3,2,1,0:T(8,128)S(1)} %collective-permute-done.refs_0_, f32[3,2,32,128]{3,2,1,0:T(8,128)S(1)} %get-tuple-element.5.refs_1_, f32[3,2,32,128]{3,2,1,0:T(8,128)S(1)} %collective-permute-done.1.refs_2_, f32[2,8,128]{2,1,0:T(8,128)S(1)} %collective-permute-done.2.refs_3_, ...), custom_call_target="tpu_custom_call" | custom-call | tf_op jit(solution)/shard_map/pallas_call | solution.py:906
  58.8 0.0 copy-start.2
  58.8 11.4 %all_to_all.11.arrived = f32[32,8,128]{2,1,0:T(8,128)S(1)} all-to-all(f32[32,8,128]{2,1,0:T(8,128)S(1)} %bitcast.3), channel_id=1, replica_groups=mesh['gx'=4,'gy'=8] {'gy','gx'}, dimensions={0} | all-to-all | bytes 262144 | tf_op jit(solution)/shard_map/all_to_all | solution.py:914
  70.3 0.0 copy-done.2
  70.3 1.1 %shard_map.116 = (f32[3,6,3,384]{3,2,1,0:T(4,128)}, f32[3,2,1,128]{3,2,1,0:T(1,128)}) custom-call(f32[32,8,128]{2,1,0:T(8,128)S(1)} %all_to_all.11.arrived, bf16[256,384]{1,0:T(8,128)(2,1)S(1)} %copy-done.2), custom_call_target="tpu_custom_call" | custom-call | tf_op jit(solution)/shard_map/pallas_call | solution.py:915
Async XLA Ops:
  3.6 22.9 %copy-start = (bf16[192,240]{1,0:T(8,128)(2,1)S(1)}, bf16[192,240]{1,0:T(8,128)(2,1)}, u32[]{:S(2)}) copy-start(bf16[192,240]{1,0:T(8,128)(2,1)} %constant.13.clone.spread.refs_6_) | copy-start | bytes 276484
  3.6 22.9 %copy-start.1 = (bf16[144,192]{1,0:T(8,128)(2,1)S(1)}, bf16[144,192]{1,0:T(8,128)(2,1)}, u32[]{:S(2)}) copy-start(bf16[144,192]{1,0:T(8,128)(2,1)} %constant.14.clone.collect.refs_7_) | copy-start | bytes 165892
  3.6 22.9 %copy-start.4 = (f32[8,32]{1,0:T(8,128)S(1)}, f32[8,32]{1,0:T(8,128)}, u32[]{:S(2)}) copy-start(f32[8,32]{1,0:T(8,128)} %constant.15.clone.transfer) | copy-start | bytes 3076
  26.5 22.5 %copy-start.3 = (f32[32,8]{1,0:T(8,128)S(1)}, f32[32,8]{1,0:T(8,128)}, u32[]{:S(2)}) copy-start(f32[32,8]{1,0:T(8,128)} %constant.16.clone.refs_8_) | copy-start | bytes 3076
  38.5 10.5 %collective-permute-start.1 = (f32[3,2,32,128]{3,2,1,0:T(8,128)S(1)}, f32[3,2,32,128]{3,2,1,0:T(8,128)S(1)}, u32[]{:S(2)}, u32[]{:S(2)}) collective-permute-start(f32[3,2,32,128]{3,2,1,0:T(8,128)S(1)} %get-tuple-element.5.refs_1_), channel_id=1, source_target_pairs={{8,0},{16,8},{24,16},{1,24},{9,1},{17,9},{25,17},{2,25},{10,2},{18... | collective-permute-start | bytes 294920 | tf_op jit(solution)/shard_map/ppermute | solution.py:891
  40.4 8.5 %collective-permute-start = (f32[3,2,32,128]{3,2,1,0:T(8,128)S(1)}, f32[3,2,32,128]{3,2,1,0:T(8,128)S(1)}, u32[]{:S(2)}, u32[]{:S(2)}) collective-permute-start(f32[3,2,32,128]{3,2,1,0:T(8,128)S(1)} %get-tuple-element.5.refs_1_), channel_id=1, source_target_pairs={{31,0},{0,8},{8,16},{16,24},{24,1},{1,9},{9,17},{17,25},{25,2},{2,... | collective-permute-start | bytes 294920 | tf_op jit(solution)/shard_map/ppermute | solution.py:891
  40.4 3.7 %collective-permute-start.3 = (f32[2,8,128]{2,1,0:T(8,128)S(1)}, f32[2,8,128]{2,1,0:T(8,128)S(1)}, u32[]{:S(2)}, u32[]{:S(2)}) collective-permute-start(f32[2,8,128]{2,1,0:T(8,128)S(1)} %get-tuple-element.6), channel_id=1, source_target_pairs={{16,0},{24,8},{1,16},{9,24},{17,1},{25,9},{2,17},{10,25},{18,2},{2... | collective-permute-start | bytes 24584 | tf_op jit(solution)/shard_map/ppermute | solution.py:891
  41.7 7.2 %collective-permute-start.2 = (f32[2,8,128]{2,1,0:T(8,128)S(1)}, f32[2,8,128]{2,1,0:T(8,128)S(1)}, u32[]{:S(2)}, u32[]{:S(2)}) collective-permute-start(f32[2,8,128]{2,1,0:T(8,128)S(1)} %get-tuple-element.6), channel_id=1, source_target_pairs={{23,0},{31,8},{0,16},{8,24},{16,1},{24,9},{1,17},{9,25},{17,2},{25... | collective-permute-start | bytes 24584 | tf_op jit(solution)/shard_map/ppermute | solution.py:891
  58.8 11.5 %copy-start.2 = (bf16[256,384]{1,0:T(8,128)(2,1)S(1)}, bf16[256,384]{1,0:T(8,128)(2,1)}, u32[]{:S(2)}) copy-start(bf16[256,384]{1,0:T(8,128)(2,1)} %constant.17.clone.table) | copy-start | bytes 589828

commit v2 on v1

--- a/solution.py
+++ b/solution.py
@@ -194,7 +194,7 @@
                 table[row, column] = weight
     back = table.T.copy()
     back[TWIN] = back[0]
-    return table.astype(np.float32), back.astype(np.float32)
+    return table.T.astype(np.float32), back.astype(np.float32)
 
 
 def chebyshev_steps():
@@ -668,21 +668,20 @@
 
         slab.smooth(u, f, 0, d, stiff, spread, collect, spans[0:3], fine_bound)
 
+        weights = [jnp.broadcast_to(transfer[:, n : n + 1], (32, width)) for n in range(8)]
+
         def restrict(pair, forces):
-            rest = jnp.concatenate([slab.keep * (f[i, pair] - forces[i]) for i in range(3)], 1)
-            corner = jnp.dot(
-                transfer[...],
-                rest,
-                preferred_element_type=jnp.float32,
-                precision=lax.Precision.HIGHEST,
-            )
             for i in range(3):
-                shares[i, pair] = corner[:, width * i : width * (i + 1)]
+                rest = slab.keep * (f[i, pair] - forces[i])
+                for n in range(8):
+                    part = rest * weights[n]
+                    part = (part[0:8] + part[8:16]) + (part[16:24] + part[24:32])
+                    shares[i, n, pl.ds(pair, 1), :] = jnp.sum(part, axis=0, keepdims=True)
 
         slab.apply(u, stiff, spread, collect, *spans[3], restrict)
 
         restricted = [
-            slab.assemble({corner: shares[i, :, n, :] for n, corner in enumerate(CORNERS)})
+            slab.assemble({corner: shares[i, n] for n, corner in enumerate(CORNERS)})
             for i in range(3)
         ]
         for q in range(own_pairs):
@@ -724,7 +723,7 @@
         refs = refs[2 * near + 1 :]
         outer = [n for n in range(-far, far + 1) if abs(n) > near]
         edges = dict(zip(outer, refs[: len(outer)]))
-        f, spread, collect, transfer_back, out, u, d, stiff, coarse, raised = refs[len(outer) :]
+        f, spread, collect, transfer_back, out, u, d, stiff, coarse = refs[len(outer) :]
         slab = Slab(width, across)
 
         def pair_of(pair, fetch):
@@ -780,19 +779,14 @@
                 move[i] = held * move[i] + (added / coarse_bound) * z
                 level[i] = level[i] + move[i]
 
+        weights = [jnp.broadcast_to(transfer_back[:, n : n + 1], (32, width)) for n in range(8)]
         for i in range(3):
             change = slab.corners_of(level[i] - start[i])
-            for n, corner in enumerate(CORNERS):
-                raised[i, :, n, :] = change[corner]
-        for pair in range(spans[0][0], min(spans[0][0] + spans[0][1] + 1, PAIRS_B)):
-            lift = jnp.dot(
-                transfer_back[...],
-                jnp.concatenate([raised[i, pair] for i in range(3)], 1),
-                preferred_element_type=jnp.float32,
-                precision=lax.Precision.HIGHEST,
-            )
-            for i in range(3):
-                u[i, pair] = u[i, pair] + lift[:, width * i : width * (i + 1)]
+            for pair in range(spans[0][0], min(spans[0][0] + spans[0][1] + 1, PAIRS_B)):
+                lift = u[i, pair]
+                for n, corner in enumerate(CORNERS):
+                    lift = lift + weights[n] * change[corner][pair : pair + 1]
+                u[i, pair] = lift
 
         slab.smooth(u, f, shift, d, stiff, spread, collect, spans, fine_bound)
 
@@ -870,7 +864,6 @@
             pltpu.VMEM((3, PAIRS_B, 32, width), f32),
             pltpu.VMEM((PAIRS_B, width), f32),
             pltpu.VMEM((7, PAIRS_B, width), f32),
-            pltpu.VMEM((3, PAIRS_B, 8, width), f32),
         ],
         compiler_params=limit,
     )

time: 71.6 us -> 71.1 us (level)
  no operation moved by 1% of the time
where the time goes in v2:
time: 71.1 us; the launch traced here: 70.9 us
  blocking collectives  34.3 us (48%)
  Pallas kernels  25.3 us (36%)
  waiting for transfers between devices  6.49 us (9%)
  starting transfers between devices  3.99 us (6%)
    all_to_all x1, blocking collectives, body(): arrived = lax.all_to_all(sent, everyone, 0, 0, tiled=True)  22.9 us
    pallas_call x1, Pallas kernels, body(): first(arrived.reshape(devices // 2, 2, 8, SENT), jnp.asarray(spread), jnp...  11.9 us
    all_to_all x1, blocking collectives, body(): lax.all_to_all(result.reshape(devices, 8, 128), everyone, 0, 0, tiled=True)  11.4 us
    pallas_call x1, Pallas kernels, body(): second(*messages, *edges, load, jnp.asarray(spread), jnp.asarray(collect)...  9.45 us
    ppermute x4, waiting for transfers between devices, from_device(): return lax.ppermute(block, ('gx', 'gy'), route)  6.49 us
    ppermute x4, starting transfers between devices, from_device(): return lax.ppermute(block, ('gx', 'gy'), route)  3.99 us
    pallas_call x1, Pallas kernels, body(): pack(initial, forcing, modulus, solid_list, jnp.asarray(pack_table()))  2.95 us
  transfers between devices with their start and end apart: 4, of which 2 were waited for; matrix products, arithmetic and copies ran while one was open for 0% of the time, Pallas kernels for 0%

profile of v2, /device:TPU:0, one launch (start us, length us, event | category | flops | bytes accessed | tf_op | source)
XLA Modules:
  0.0 70.9 jit_solution(15220192104434111496)
XLA Ops:
  0.6 3.0 %shard_map.113 = f32[32,8,512]{2,1,0:T(8,128)} custom-call(f32[3,6,3,384]{3,2,1,0:T(4,128)} %initial_at.1, f32[3,6,3,384]{3,2,1,0:T(4,128)} %forcing_at.1, f32[2,1,128]{2,1,0:T(1,128)} %modulus_at.1, s32[1,1,192]{2,1,0:T(1,128)} %listing_at.1, bf16[384,512]{1,0:T(8,128)(2,1)} %constant.12.clone.table_at), custom_call_target="tpu_custom_call" | custom-call | tf_op jit(solution)/shard_map/pallas_call | solution.py:887
  3.6 0.0 copy-start
  3.6 0.0 copy-start.1
  3.6 0.0 copy-start.4
  3.6 22.9 %all_to_all.10 = f32[32,8,512]{2,1,0:T(8,128)S(1)} all-to-all(f32[32,8,512]{2,1,0:T(8,128)} %shard_map.113), channel_id=1, replica_groups=mesh['gx'=4,'gy'=8] {'gy','gx'}, dimensions={0} | all-to-all | bytes 1048576 | tf_op jit(solution)/shard_map/all_to_all | solution.py:888
  26.5 0.0 copy-done
  26.5 0.0 copy-done.1
  26.5 0.0 copy-done.4
  26.5 0.0 copy-start.3
  26.5 11.9 %shard_map.114 = (f32[3,2,32,128]{3,2,1,0:T(8,128)S(1)}, f32[2,8,128]{2,1,0:T(8,128)S(1)}, f32[3,6,32,128]{3,2,1,0:T(8,128)S(1)}) custom-call(f32[16,2,8,512]{3,2,1,0:T(8,128)S(1)} %bitcast.2, bf16[192,240]{1,0:T(8,128)(2,1)S(1)} %copy-done, bf16[144,192]{1,0:T(8,128)(2,1)S(1)} %copy-done.1, f32[32,8]{1,0:T(8,128)S(1)} %copy-done.4), custom_call_target="tpu_custom_call" | custom-call | tf_op jit(solution)/shard_map/pallas_call | solution.py:889
  38.4 2.0 %collective-permute-start.1 = (f32[3,2,32,128]{3,2,1,0:T(8,128)S(1)}, f32[3,2,32,128]{3,2,1,0:T(8,128)S(1)}, u32[]{:S(2)}, u32[]{:S(2)}) collective-permute-start(f32[3,2,32,128]{3,2,1,0:T(8,128)S(1)} %get-tuple-element.5.refs_1_), channel_id=1, source_target_pairs={{8,0},{16,8},{24,16},{1,24},{9,1},{17,9},{25,17},{2,25},{10,2},{18... | collective-permute-start | bytes 294920 | tf_op jit(solution)/shard_map/ppermute | solution.py:884
  40.3 0.0 collective-permute-start
  40.3 1.3 %collective-permute-start.3 = (f32[2,8,128]{2,1,0:T(8,128)S(1)}, f32[2,8,128]{2,1,0:T(8,128)S(1)}, u32[]{:S(2)}, u32[]{:S(2)}) collective-permute-start(f32[2,8,128]{2,1,0:T(8,128)S(1)} %get-tuple-element.6), channel_id=1, source_target_pairs={{16,0},{24,8},{1,16},{9,24},{17,1},{25,9},{2,17},{10,25},{18,2},{2... | collective-permute-start | bytes 24584 | tf_op jit(solution)/shard_map/ppermute | solution.py:884
  41.6 0.8 %collective-permute-start.2 = (f32[2,8,128]{2,1,0:T(8,128)S(1)}, f32[2,8,128]{2,1,0:T(8,128)S(1)}, u32[]{:S(2)}, u32[]{:S(2)}) collective-permute-start(f32[2,8,128]{2,1,0:T(8,128)S(1)} %get-tuple-element.6), channel_id=1, source_target_pairs={{23,0},{31,8},{0,16},{8,24},{16,1},{24,9},{1,17},{9,25},{17,2},{25... | collective-permute-start | bytes 24584 | tf_op jit(solution)/shard_map/ppermute | solution.py:884
  42.4 1.6 %collective-permute-done.3.refs_4_ = f32[2,8,128]{2,1,0:T(8,128)S(1)} collective-permute-done((f32[2,8,128]{2,1,0:T(8,128)S(1)}, f32[2,8,128]{2,1,0:T(8,128)S(1)}, u32[]{:S(2)}, u32[]{:S(2)}) %collective-permute-start.3) | collective-permute-done | bytes 8224 | tf_op jit(solution)/shard_map/ppermute | solution.py:884
  44.0 4.9 %collective-permute-done.2.refs_3_ = f32[2,8,128]{2,1,0:T(8,128)S(1)} collective-permute-done((f32[2,8,128]{2,1,0:T(8,128)S(1)}, f32[2,8,128]{2,1,0:T(8,128)S(1)}, u32[]{:S(2)}, u32[]{:S(2)}) %collective-permute-start.2) | collective-permute-done | bytes 8224 | tf_op jit(solution)/shard_map/ppermute | solution.py:884
  48.8 0.0 collective-permute-done.1.refs_2_
  48.8 0.0 collective-permute-done.refs_0_
  48.8 0.0 copy-done.3
  48.9 9.4 %shard_map.115 = f32[16,2,8,128]{3,2,1,0:T(8,128)S(1)} custom-call(f32[3,2,32,128]{3,2,1,0:T(8,128)S(1)} %collective-permute-done.refs_0_, f32[3,2,32,128]{3,2,1,0:T(8,128)S(1)} %get-tuple-element.5.refs_1_, f32[3,2,32,128]{3,2,1,0:T(8,128)S(1)} %collective-permute-done.1.refs_2_, f32[2,8,128]{2,1,0:T(8,128)S(1)} %collective-permute-done.2.refs_3_, ...), custom_call_target="tpu_custom_call" | custom-call | tf_op jit(solution)/shard_map/pallas_call | solution.py:899
  58.3 0.0 copy-start.2
  58.3 11.4 %all_to_all.11.arrived = f32[32,8,128]{2,1,0:T(8,128)S(1)} all-to-all(f32[32,8,128]{2,1,0:T(8,128)S(1)} %bitcast.3), channel_id=1, replica_groups=mesh['gx'=4,'gy'=8] {'gy','gx'}, dimensions={0} | all-to-all | bytes 262144 | tf_op jit(solution)/shard_map/all_to_all | solution.py:907
  69.8 0.0 copy-done.2
  69.8 1.1 %shard_map.116 = (f32[3,6,3,384]{3,2,1,0:T(4,128)}, f32[3,2,1,128]{3,2,1,0:T(1,128)}) custom-call(f32[32,8,128]{2,1,0:T(8,128)S(1)} %all_to_all.11.arrived, bf16[256,384]{1,0:T(8,128)(2,1)S(1)} %copy-done.2), custom_call_target="tpu_custom_call" | custom-call | tf_op jit(solution)/shard_map/pallas_call | solution.py:908
Async XLA Ops:
  3.6 22.9 %copy-start = (bf16[192,240]{1,0:T(8,128)(2,1)S(1)}, bf16[192,240]{1,0:T(8,128)(2,1)}, u32[]{:S(2)}) copy-start(bf16[192,240]{1,0:T(8,128)(2,1)} %constant.13.clone.spread.refs_6_) | copy-start | bytes 276484
  3.6 22.9 %copy-start.1 = (bf16[144,192]{1,0:T(8,128)(2,1)S(1)}, bf16[144,192]{1,0:T(8,128)(2,1)}, u32[]{:S(2)}) copy-start(bf16[144,192]{1,0:T(8,128)(2,1)} %constant.14.clone.collect.refs_7_) | copy-start | bytes 165892
  3.6 22.9 %copy-start.4 = (f32[32,8]{1,0:T(8,128)S(1)}, f32[32,8]{1,0:T(8,128)}, u32[]{:S(2)}) copy-start(f32[32,8]{1,0:T(8,128)} %constant.15.clone.transfer) | copy-start | bytes 3076
  26.5 22.3 %copy-start.3 = (f32[32,8]{1,0:T(8,128)S(1)}, f32[32,8]{1,0:T(8,128)}, u32[]{:S(2)}) copy-start(f32[32,8]{1,0:T(8,128)} %constant.16.clone.refs_8_) | copy-start | bytes 3076
  38.4 10.5 %collective-permute-start.1 = (f32[3,2,32,128]{3,2,1,0:T(8,128)S(1)}, f32[3,2,32,128]{3,2,1,0:T(8,128)S(1)}, u32[]{:S(2)}, u32[]{:S(2)}) collective-permute-start(f32[3,2,32,128]{3,2,1,0:T(8,128)S(1)} %get-tuple-element.5.refs_1_), channel_id=1, source_target_pairs={{8,0},{16,8},{24,16},{1,24},{9,1},{17,9},{25,17},{2,25},{10,2},{18... | collective-permute-start | bytes 294920 | tf_op jit(solution)/shard_map/ppermute | solution.py:884
  40.3 8.5 %collective-permute-start = (f32[3,2,32,128]{3,2,1,0:T(8,128)S(1)}, f32[3,2,32,128]{3,2,1,0:T(8,128)S(1)}, u32[]{:S(2)}, u32[]{:S(2)}) collective-permute-start(f32[3,2,32,128]{3,2,1,0:T(8,128)S(1)} %get-tuple-element.5.refs_1_), channel_id=1, source_target_pairs={{31,0},{0,8},{8,16},{16,24},{24,1},{1,9},{9,17},{17,25},{25,2},{2,... | collective-permute-start | bytes 294920 | tf_op jit(solution)/shard_map/ppermute | solution.py:884
  40.3 3.7 %collective-permute-start.3 = (f32[2,8,128]{2,1,0:T(8,128)S(1)}, f32[2,8,128]{2,1,0:T(8,128)S(1)}, u32[]{:S(2)}, u32[]{:S(2)}) collective-permute-start(f32[2,8,128]{2,1,0:T(8,128)S(1)} %get-tuple-element.6), channel_id=1, source_target_pairs={{16,0},{24,8},{1,16},{9,24},{17,1},{25,9},{2,17},{10,25},{18,2},{2... | collective-permute-start | bytes 24584 | tf_op jit(solution)/shard_map/ppermute | solution.py:884
  41.6 7.2 %collective-permute-start.2 = (f32[2,8,128]{2,1,0:T(8,128)S(1)}, f32[2,8,128]{2,1,0:T(8,128)S(1)}, u32[]{:S(2)}, u32[]{:S(2)}) collective-permute-start(f32[2,8,128]{2,1,0:T(8,128)S(1)} %get-tuple-element.6), channel_id=1, source_target_pairs={{23,0},{31,8},{0,16},{8,24},{16,1},{24,9},{1,17},{9,25},{17,2},{25... | collective-permute-start | bytes 24584 | tf_op jit(solution)/shard_map/ppermute | solution.py:884
  58.3 11.5 %copy-start.2 = (bf16[256,384]{1,0:T(8,128)(2,1)S(1)}, bf16[256,384]{1,0:T(8,128)(2,1)}, u32[]{:S(2)}) copy-start(bf16[256,384]{1,0:T(8,128)(2,1)} %constant.17.clone.table) | copy-start | bytes 589828

commit v3 on v2

--- a/solution.py
+++ b/solution.py
@@ -1,3 +1,4 @@
+import functools
 import math
 
 import jax
@@ -254,7 +255,24 @@
     return parts[:count] + (parts[count : 2 * count] + parts[2 * count :])
 
 
+def ring_order(rows_of, columns_of):
+    if (rows_of, columns_of) != (4, 8):
+        return list(range(rows_of * columns_of))
+    order = []
+    for z in range(4):
+        for x in range(2):
+            for y in range(2):
+                chip = (z, 7 - z, 15 - z, 8 + z)[2 * x + y]
+                order += [2 * chip, 2 * chip + 1]
+    return order
+
+
+def region_shift(own_layers):
+    return 2 if own_layers == 4 else 0
+
+
 def pack_kernel(
+    order,
     initial_at, forcing_at, modulus_at, listing_at, table_at, out,
     initial, forcing, modulus, listing, table, rows, turned, places, ready,
 ):
@@ -318,18 +336,32 @@
     for block in range(4):
         for parity in range(2):
             for tile in range(SENT // 128):
-                out[:, 2 * block + parity, 128 * tile : 128 * tile + 128] = places[
-                    4 * block + tile, pl.ds(16 - BEFORE + parity, devices, stride=own_layers), :
-                ]
-
-
-def unpack_kernel(arrived, table, out, coarse_out, layers, turned):
+                at, span = 4 * block + tile, slice(128 * tile, 128 * tile + 128)
+                first = 16 - BEFORE + parity
+                if order == sorted(order):
+                    out[:, 2 * block + parity, span] = places[
+                        at, pl.ds(first, devices, stride=own_layers), :
+                    ]
+                    continue
+                for device, k in enumerate(order):
+                    row = first + own_layers * k
+                    out[device, 2 * block + parity : 2 * block + parity + 1, span] = places[
+                        at, row : row + 1, :
+                    ]
+
+
+def unpack_kernel(order, arrived, table, out, coarse_out, layers, turned):
     devices = arrived.shape[0]
     own_layers = EZ // devices
     for x in range(2):
         for layer in range(own_layers):
             row = (layer // 2) * 4 + x * 2 + layer % 2
-            layers[x, pl.ds(layer, devices, stride=own_layers), :] = arrived[:, row, :]
+            if order == sorted(order):
+                layers[x, pl.ds(layer, devices, stride=own_layers), :] = arrived[:, row, :]
+                continue
+            for device, k in enumerate(order):
+                at = (region_shift(own_layers) + own_layers * k + layer) % EZ
+                layers[x, at : at + 1, :] = arrived[device, row : row + 1, :]
     wide = exact_pick(jnp.concatenate([layers[0], layers[1]], 1), table[...])
     for c in range(3):
         turned[pl.ds(c, 128, stride=3), :] = wide[:, 128 * c : 128 * c + 128]
@@ -699,19 +731,19 @@
     return first_kernel
 
 
-def full_reach(own_layers):
-    return -(-3 // own_layers)
-
-
-def coarse_reach(own_layers):
-    return -(-5 // own_layers)
+def sources_of(own_layers):
+    shift = region_shift(own_layers)
+    whole = range((shift - 3) // own_layers, (shift + own_layers + 2) // own_layers + 1)
+    coarse = range((shift - 5) // own_layers, (shift + own_layers + 4) // own_layers + 1)
+    return list(whole), [n for n in coarse if n not in whole]
 
 
 def make_second_kernel(width, across, own_layers, fine_bound, coarse_bound):
     own = BEFORE_B // 2
     own_pairs = (own_layers + 1) // 2
-    shift = (BEFORE - BEFORE_B) // 2
-    near, far = full_reach(own_layers), coarse_reach(own_layers)
+    first_layer = region_shift(own_layers) - BEFORE_B
+    shift = (BEFORE + first_layer) // 2
+    whole, outer = sources_of(own_layers)
     steps = chebyshev_steps()
     spans = []
     for n in (3, 2, 1):
@@ -719,17 +751,16 @@
         spans.append((low // 2, (high + 1) // 2 - low // 2))
 
     def second_kernel(*refs):
-        messages = dict(zip(range(-near, near + 1), refs[: 2 * near + 1]))
-        refs = refs[2 * near + 1 :]
-        outer = [n for n in range(-far, far + 1) if abs(n) > near]
-        edges = dict(zip(outer, refs[: len(outer)]))
+        messages = dict(zip(whole, refs))
+        refs = refs[len(whole) :]
+        edges = dict(zip(outer, refs))
         f, spread, collect, transfer_back, out, u, d, stiff, coarse = refs[len(outer) :]
         slab = Slab(width, across)
 
         def pair_of(pair, fetch):
             found = []
             for parity in range(2):
-                layer = 2 * pair - BEFORE_B + parity
+                layer = 2 * pair + first_layer + parity
                 device = layer // own_layers
                 layer = layer - device * own_layers
                 found.append((device, layer // 2, layer % 2))
@@ -749,9 +780,9 @@
         d[...] = jnp.zeros(d.shape, jnp.float32)
         for pair in range(PAIRS_B):
             for i in range(3):
-                whole = pair_of(pair, lambda n, q: messages[n][i, q] if n in messages else None)
-                if whole is not None:
-                    u[i, pair] = whole
+                block = pair_of(pair, lambda n, q: messages[n][i, q] if n in messages else None)
+                if block is not None:
+                    u[i, pair] = block
             for n in range(7):
 
                 def fetch(device, q, n=n):
@@ -810,11 +841,12 @@
 def solution(mesh):
     rows_of, columns_of = mesh.shape["gx"], mesh.shape["gy"]
     devices = rows_of * columns_of
+    order = ring_order(rows_of, columns_of)
     own_layers = EZ // devices
     own_pairs = (own_layers + 1) // 2
     width = 4 * devices
     across = 2 * rows_of
-    near, far = full_reach(own_layers), coarse_reach(own_layers)
+    whole, outer = sources_of(own_layers)
     spread, collect, fine_bound = element_tables()
     coarse_bound = build_tables([0.0, 1.0], 2)[2]
     transfer, transfer_back = transfer_table()
@@ -823,7 +855,7 @@
     f32 = jnp.float32
 
     pack = pl.pallas_call(
-        pack_kernel,
+        functools.partial(pack_kernel, order),
         out_shape=jax.ShapeDtypeStruct((devices, 8, SENT), f32),
         in_specs=[pl.BlockSpec(memory_space=pl.ANY)] * 5,
         out_specs=pl.BlockSpec(memory_space=pltpu.VMEM),
@@ -845,7 +877,7 @@
         out_shape=(
             jax.ShapeDtypeStruct((3, own_pairs, 32, width), f32),
             jax.ShapeDtypeStruct((own_pairs, 8, width), f32),
-            jax.ShapeDtypeStruct((3, PAIRS, 32, width), f32),
+            jax.ShapeDtypeStruct((3, PAIRS_B, 32, width), f32),
         ),
         scratch_shapes=[
             pltpu.VMEM((3, 8, 32, width), f32),
@@ -868,7 +900,7 @@
         compiler_params=limit,
     )
     unpack = pl.pallas_call(
-        unpack_kernel,
+        functools.partial(unpack_kernel, order),
         out_shape=(
             jax.ShapeDtypeStruct((3, 6, 3, 384), f32),
             jax.ShapeDtypeStruct((3, 2, 1, EZ), f32),
@@ -879,7 +911,7 @@
     everyone = ("gy", "gx")
 
     def from_device(block, distance):
-        place = [k % rows_of * columns_of + k // rows_of for k in range(devices)]
+        place = {k: m % rows_of * columns_of + m // rows_of for m, k in enumerate(order)}
         route = [(place[(k + distance) % devices], place[k]) for k in range(devices)]
         return lax.ppermute(block, ("gx", "gy"), route)
 
@@ -892,10 +924,8 @@
             jnp.asarray(collect),
             jnp.asarray(transfer),
         )
-        messages = [
-            from_device(message, n) if n else message for n in range(-near, near + 1)
-        ]
-        edges = [from_device(edge, n) for n in range(-far, far + 1) if abs(n) > near]
+        messages = [from_device(message, n) if n else message for n in whole]
+        edges = [from_device(edge, n) for n in outer]
         result = second(
             *messages,
             *edges,

time: 71.1 us -> 65.8 us (0.925)
  waiting for transfers between devices: 6.49 us -> 3.53 us
  starting transfers between devices: 3.99 us -> 1.75 us
    ppermute x4 -> x3, waiting for transfers between devices: 6.49 us -> 3.53 us  [from_device(): return lax.ppermute(block, ('gx', 'gy'), route)]
    ppermute x4 -> x3, starting transfers between devices: 3.99 us -> 1.75 us  [from_device(): return lax.ppermute(block, ('gx', 'gy'), route)]
  transfers between devices with their start and end apart: 4 -> 3, of which waited for: 2 -> 2; matrix products, arithmetic and copies ran while one was open for 0% -> 0% of each run, Pallas kernels for 0% -> 0%
where the time goes in v3:
time: 65.8 us; the launch traced here: 65.6 us
  blocking collectives  33.8 us (51%)
  Pallas kernels  25.8 us (39%)
  waiting for transfers between devices  3.53 us (5%)
  starting transfers between devices  1.75 us (3%)
  between operations  0.7 us (1%)
    all_to_all x1, blocking collectives, body(): arrived = lax.all_to_all(sent, everyone, 0, 0, tiled=True)  22.9 us
    pallas_call x1, Pallas kernels, body(): first(arrived.reshape(devices // 2, 2, 8, SENT), jnp.asarray(spread), jnp...  12.4 us
    all_to_all x1, blocking collectives, body(): lax.all_to_all(result.reshape(devices, 8, 128), everyone, 0, 0, tiled=True)  10.9 us
    pallas_call x1, Pallas kernels, body(): second(*messages, *edges, load, jnp.asarray(spread), jnp.asarray(collect)...  9.42 us
    ppermute x3, waiting for transfers between devices, from_device(): return lax.ppermute(block, ('gx', 'gy'), route)  3.53 us
    pallas_call x1, Pallas kernels, body(): pack(initial, forcing, modulus, solid_list, jnp.asarray(pack_table()))  2.87 us
    ppermute x3, starting transfers between devices, from_device(): return lax.ppermute(block, ('gx', 'gy'), route)  1.75 us
  transfers between devices with their start and end apart: 3, of which 2 were waited for; matrix products, arithmetic and copies ran while one was open for 0% of the time, Pallas kernels for 0%

profile of v3, /device:TPU:0, one launch (start us, length us, event | category | flops | bytes accessed | tf_op | source)
XLA Modules:
  0.0 65.6 jit_solution(12196732933623197505)
XLA Ops:
  0.6 2.9 %shard_map.113 = f32[32,8,512]{2,1,0:T(8,128)} custom-call(f32[3,6,3,384]{3,2,1,0:T(4,128)} %initial_at.1, f32[3,6,3,384]{3,2,1,0:T(4,128)} %forcing_at.1, f32[2,1,128]{2,1,0:T(1,128)} %modulus_at.1, s32[1,1,192]{2,1,0:T(1,128)} %listing_at.1, bf16[384,512]{1,0:T(8,128)(2,1)} %constant.12.clone.table_at), custom_call_target="tpu_custom_call" | custom-call | tf_op jit(solution)/shard_map/pallas_call | solution.py:919
  3.5 0.0 copy-start
  3.5 0.0 copy-start.1
  3.5 0.0 copy-start.4
  3.5 22.9 %all_to_all.10 = f32[32,8,512]{2,1,0:T(8,128)S(1)} all-to-all(f32[32,8,512]{2,1,0:T(8,128)} %shard_map.113), channel_id=1, replica_groups=mesh['gx'=4,'gy'=8] {'gy','gx'}, dimensions={0} | all-to-all | bytes 1048576 | tf_op jit(solution)/shard_map/all_to_all | solution.py:920
  26.4 0.0 copy-done
  26.4 0.0 copy-done.1
  26.4 0.0 copy-done.4
  26.4 0.0 copy-start.3
  26.4 12.4 %shard_map.114 = (f32[3,2,32,128]{3,2,1,0:T(8,128)S(1)}, f32[2,8,128]{2,1,0:T(8,128)}, f32[3,8,32,128]{3,2,1,0:T(8,128)S(1)}) custom-call(f32[16,2,8,512]{3,2,1,0:T(8,128)S(1)} %bitcast.2, bf16[192,240]{1,0:T(8,128)(2,1)S(1)} %copy-done, bf16[144,192]{1,0:T(8,128)(2,1)S(1)} %copy-done.1, f32[32,8]{1,0:T(8,128)S(1)} %copy-done.4), custom_call_target="tpu_custom_call" | custom-call | tf_op jit(solution)/shard_map/pallas_call | solution.py:921
  38.9 1.2 %collective-permute-start.2 = (f32[3,2,32,128]{3,2,1,0:T(8,128)S(1)}, f32[3,2,32,128]{3,2,1,0:T(8,128)S(1)}, u32[]{:S(2)}, u32[]{:S(2)}) collective-permute-start(f32[3,2,32,128]{3,2,1,0:T(8,128)S(1)} %get-tuple-element.4.refs_1_), channel_id=1, source_target_pairs={{2,0},{10,8},{4,2},{12,10},{6,4},{14,12},{22,6},{30,14},{20,22},{2... | collective-permute-start | bytes 294920 | tf_op jit(solution)/shard_map/ppermute | solution.py:916
  40.1 0.0 collective-permute-start.1
  40.1 0.5 collective-permute-start
  40.6 2.9 %collective-permute-done.2.refs_3_ = f32[3,2,32,128]{3,2,1,0:T(8,128)S(1)} collective-permute-done((f32[3,2,32,128]{3,2,1,0:T(8,128)S(1)}, f32[3,2,32,128]{3,2,1,0:T(8,128)S(1)}, u32[]{:S(2)}, u32[]{:S(2)}) %collective-permute-start.2) | collective-permute-done | bytes 98336 | tf_op jit(solution)/shard_map/ppermute | solution.py:916
  43.5 0.0 collective-permute-done.1.refs_2_
  43.5 0.7 %collective-permute-done.refs_0_ = f32[3,2,32,128]{3,2,1,0:T(8,128)S(1)} collective-permute-done((f32[3,2,32,128]{3,2,1,0:T(8,128)S(1)}, f32[3,2,32,128]{3,2,1,0:T(8,128)S(1)}, u32[]{:S(2)}, u32[]{:S(2)}) %collective-permute-start) | collective-permute-done | bytes 98336 | tf_op jit(solution)/shard_map/ppermute | solution.py:916
  44.2 0.0 copy-done.3
  44.2 9.4 %shard_map.115 = f32[16,2,8,128]{3,2,1,0:T(8,128)S(1)} custom-call(f32[3,2,32,128]{3,2,1,0:T(8,128)S(1)} %collective-permute-done.refs_0_, f32[3,2,32,128]{3,2,1,0:T(8,128)S(1)} %get-tuple-element.4.refs_1_, f32[3,2,32,128]{3,2,1,0:T(8,128)S(1)} %collective-permute-done.1.refs_2_, f32[3,2,32,128]{3,2,1,0:T(8,128)S(1)} %collective-permute-done.2.refs_3_, ...), custom_call_target="tpu_custom_call" | custom-call | tf_op jit(solution)/shard_map/pallas_call | solution.py:929
  53.6 0.0 copy-start.2
  53.6 10.9 %all_to_all.11.arrived = f32[32,8,128]{2,1,0:T(8,128)S(1)} all-to-all(f32[32,8,128]{2,1,0:T(8,128)S(1)} %bitcast.3), channel_id=1, replica_groups=mesh['gx'=4,'gy'=8] {'gy','gx'}, dimensions={0} | all-to-all | bytes 262144 | tf_op jit(solution)/shard_map/all_to_all | solution.py:937
  64.5 0.0 copy-done.2
  64.5 1.0 %shard_map.116 = (f32[3,6,3,384]{3,2,1,0:T(4,128)}, f32[3,2,1,128]{3,2,1,0:T(1,128)}) custom-call(f32[32,8,128]{2,1,0:T(8,128)S(1)} %all_to_all.11.arrived, bf16[256,384]{1,0:T(8,128)(2,1)S(1)} %copy-done.2), custom_call_target="tpu_custom_call" | custom-call | tf_op jit(solution)/shard_map/pallas_call | solution.py:938
Async XLA Ops:
  3.5 22.9 %copy-start = (bf16[192,240]{1,0:T(8,128)(2,1)S(1)}, bf16[192,240]{1,0:T(8,128)(2,1)}, u32[]{:S(2)}) copy-start(bf16[192,240]{1,0:T(8,128)(2,1)} %constant.13.clone.spread.refs_5_) | copy-start | bytes 276484
  3.5 22.9 %copy-start.1 = (bf16[144,192]{1,0:T(8,128)(2,1)S(1)}, bf16[144,192]{1,0:T(8,128)(2,1)}, u32[]{:S(2)}) copy-start(bf16[144,192]{1,0:T(8,128)(2,1)} %constant.14.clone.collect.refs_6_) | copy-start | bytes 165892
  3.5 22.9 %copy-start.4 = (f32[32,8]{1,0:T(8,128)S(1)}, f32[32,8]{1,0:T(8,128)}, u32[]{:S(2)}) copy-start(f32[32,8]{1,0:T(8,128)} %constant.15.clone.transfer) | copy-start | bytes 3076
  26.4 17.7 %copy-start.3 = (f32[32,8]{1,0:T(8,128)S(1)}, f32[32,8]{1,0:T(8,128)}, u32[]{:S(2)}) copy-start(f32[32,8]{1,0:T(8,128)} %constant.16.clone.refs_7_) | copy-start | bytes 3076
  38.9 4.6 %collective-permute-start.2 = (f32[3,2,32,128]{3,2,1,0:T(8,128)S(1)}, f32[3,2,32,128]{3,2,1,0:T(8,128)S(1)}, u32[]{:S(2)}, u32[]{:S(2)}) collective-permute-start(f32[3,2,32,128]{3,2,1,0:T(8,128)S(1)} %get-tuple-element.4.refs_1_), channel_id=1, source_target_pairs={{2,0},{10,8},{4,2},{12,10},{6,4},{14,12},{22,6},{30,14},{20,22},{2... | collective-permute-start | bytes 294920 | tf_op jit(solution)/shard_map/ppermute | solution.py:916
  40.1 3.4 %collective-permute-start.1 = (f32[3,2,32,128]{3,2,1,0:T(8,128)S(1)}, f32[3,2,32,128]{3,2,1,0:T(8,128)S(1)}, u32[]{:S(2)}, u32[]{:S(2)}) collective-permute-start(f32[3,2,32,128]{3,2,1,0:T(8,128)S(1)} %get-tuple-element.4.refs_1_), channel_id=1, source_target_pairs={{8,0},{2,8},{10,2},{4,10},{12,4},{6,12},{14,6},{22,14},{30,22},{20... | collective-permute-start | bytes 294920 | tf_op jit(solution)/shard_map/ppermute | solution.py:916
  40.1 4.0 %collective-permute-start = (f32[3,2,32,128]{3,2,1,0:T(8,128)S(1)}, f32[3,2,32,128]{3,2,1,0:T(8,128)S(1)}, u32[]{:S(2)}, u32[]{:S(2)}) collective-permute-start(f32[3,2,32,128]{3,2,1,0:T(8,128)S(1)} %get-tuple-element.4.refs_1_), channel_id=1, source_target_pairs={{9,0},{0,8},{8,2},{2,10},{10,4},{4,12},{12,6},{6,14},{14,22},{22,3... | collective-permute-start | bytes 294920 | tf_op jit(solution)/shard_map/ppermute | solution.py:916
  53.6 10.9 %copy-start.2 = (bf16[256,384]{1,0:T(8,128)(2,1)S(1)}, bf16[256,384]{1,0:T(8,128)(2,1)}, u32[]{:S(2)}) copy-start(bf16[256,384]{1,0:T(8,128)(2,1)} %constant.17.clone.table) | copy-start | bytes 589828

commit v4 on v3

--- a/solution.py
+++ b/solution.py
@@ -499,41 +499,49 @@
         moved = (self.lanes(z0, -1), self.lanes(z2, -1))
         return jnp.concatenate([own0, own1, own2, own3], 0), moved
 
+    def gradient(self, u, spread, pair):
+        blocks = [
+            self.gather(u[i, pair + q], u[i, pair + q + 1]) for i in range(3) for q in range(2)
+        ]
+        high, low = high_low(jnp.concatenate(blocks, 1))
+        return jnp.dot(
+            spread[...],
+            jnp.concatenate([high, low, high], 0),
+            preferred_element_type=jnp.float32,
+        )
+
+    def force(self, gradient, stiff, collect, pair):
+        width = 2 * self.width
+        stiffness = jnp.concatenate([stiff[pair + q : pair + q + 1, :] for q in range(2)], 1)
+        deform = [
+            [
+                gradient[64 * e : 64 * e + 64, width * i : width * (i + 1)]
+                + (1.0 if i == e else 0.0)
+                for e in range(3)
+            ]
+            for i in range(3)
+        ]
+        stress = point_stress(deform, stiffness, lame_ratio * stiffness)
+        stress = jnp.concatenate(
+            [jnp.concatenate([stress[i][e] for i in range(3)], 1) for e in range(3)], 0
+        )
+        high, low = high_low(stress)
+        force = jnp.dot(collect[...], high, preferred_element_type=jnp.float32)
+        return force[0:ROWS] + (
+            force[ROWS:] + jnp.dot(collect[0:ROWS], low, preferred_element_type=jnp.float32)
+        )
+
     def apply(self, u, stiff, spread, collect, first, count, finish):
         width = self.width
-
-        def step(index, carry):
-            pair = first + 2 * index
-            blocks = [
-                self.gather(u[i, pair + q], u[i, pair + q + 1])
-                for i in range(3)
-                for q in range(2)
-            ]
-            high, low = high_low(jnp.concatenate(blocks, 1))
-            gradient = jnp.dot(
-                spread[...],
-                jnp.concatenate([high, low, high], 0),
-                preferred_element_type=jnp.float32,
-            )
-            stiffness = jnp.concatenate([stiff[pl.ds(pair + q, 1), :] for q in range(2)], 1)
-            deform = [
-                [
-                    gradient[64 * e : 64 * e + 64, 2 * width * i : 2 * width * (i + 1)]
-                    + (1.0 if i == e else 0.0)
-                    for e in range(3)
-                ]
-                for i in range(3)
-            ]
-            stress = point_stress(deform, stiffness, lame_ratio * stiffness)
-            stress = jnp.concatenate(
-                [jnp.concatenate([stress[i][e] for i in range(3)], 1) for e in range(3)], 0
-            )
-            high, low = high_low(stress)
-            force = jnp.dot(collect[...], high, preferred_element_type=jnp.float32)
-            force = force[0:ROWS] + (
-                force[ROWS:] + jnp.dot(collect[0:ROWS], low, preferred_element_type=jnp.float32)
-            )
-            carry = list(carry)
+        none = jnp.zeros((8, width), jnp.float32)
+        carry = [(none, none) for i in range(3)]
+        last = first + 2 * ((count + 1) // 2)
+        ahead = self.gradient(u, spread, first)
+        for pair in range(first, last, 2):
+            gradient = ahead
+            if pair + 2 < last:
+                ahead = self.gradient(u, spread, pair + 2)
+            force = self.force(gradient, stiff, collect, pair)
             totals = [[], []]
             for q in range(2):
                 for i in range(3):
@@ -542,10 +550,6 @@
                     totals[q].append(total)
             for q in range(2):
                 finish(pair + q, totals[q])
-            return tuple(carry)
-
-        none = jnp.zeros((8, width), jnp.float32)
-        lax.fori_loop(0, (count + 1) // 2, step, tuple((none, none) for i in range(3)))
 
     def smooth(self, u, f, f_shift, d, stiff, spread, collect, spans, bound):
         for (first, count), (held, added) in zip(spans, chebyshev_steps()):

time: 65.8 us -> 57.7 us (0.88)
  Pallas kernels: 25.8 us -> 17.7 us
    pallas_call x1, Pallas kernels: 12.4 us -> 7.58 us  [body(): first(arrived.reshape(devices // 2, 2, 8, SENT), jnp.asarray(spread), jnp...]
    pallas_call x1, Pallas kernels: 9.42 us -> 6.17 us  [body(): second(*messages, *edges, load, jnp.asarray(spread), jnp.asarray(collect)...]
where the time goes in v4:
time: 57.7 us; the launch traced here: 57.5 us
  blocking collectives  33.8 us (59%)
  Pallas kernels  17.7 us (31%)
  waiting for transfers between devices  3.53 us (6%)
  starting transfers between devices  1.76 us (3%)
  between operations  0.7 us (1%)
    all_to_all x1, blocking collectives, body(): arrived = lax.all_to_all(sent, everyone, 0, 0, tiled=True)  22.9 us
    all_to_all x1, blocking collectives, body(): lax.all_to_all(result.reshape(devices, 8, 128), everyone, 0, 0, tiled=True)  10.9 us
    pallas_call x1, Pallas kernels, body(): first(arrived.reshape(devices // 2, 2, 8, SENT), jnp.asarray(spread), jnp...  7.58 us
    pallas_call x1, Pallas kernels, body(): second(*messages, *edges, load, jnp.asarray(spread), jnp.asarray(collect)...  6.17 us
    ppermute x3, waiting for transfers between devices, from_device(): return lax.ppermute(block, ('gx', 'gy'), route)  3.53 us
    pallas_call x1, Pallas kernels, body(): pack(initial, forcing, modulus, solid_list, jnp.asarray(pack_table()))  2.87 us
    ppermute x3, starting transfers between devices, from_device(): return lax.ppermute(block, ('gx', 'gy'), route)  1.76 us
  transfers between devices with their start and end apart: 3, of which 2 were waited for; matrix products, arithmetic and copies ran while one was open for 0% of the time, Pallas kernels for 0%

profile of v4, /device:TPU:0, one launch (start us, length us, event | category | flops | bytes accessed | tf_op | source)
XLA Modules:
  0.0 57.5 jit_solution(2622328313367795091)
XLA Ops:
  0.6 2.9 %shard_map.113 = f32[32,8,512]{2,1,0:T(8,128)} custom-call(f32[3,6,3,384]{3,2,1,0:T(4,128)} %initial_at.1, f32[3,6,3,384]{3,2,1,0:T(4,128)} %forcing_at.1, f32[2,1,128]{2,1,0:T(1,128)} %modulus_at.1, s32[1,1,192]{2,1,0:T(1,128)} %listing_at.1, bf16[384,512]{1,0:T(8,128)(2,1)} %constant.12.clone.table_at), custom_call_target="tpu_custom_call" | custom-call | tf_op jit(solution)/shard_map/pallas_call | solution.py:923
  3.5 0.0 copy-start
  3.5 0.0 copy-start.1
  3.5 0.0 copy-start.4
  3.5 22.9 %all_to_all.10 = f32[32,8,512]{2,1,0:T(8,128)S(1)} all-to-all(f32[32,8,512]{2,1,0:T(8,128)} %shard_map.113), channel_id=1, replica_groups=mesh['gx'=4,'gy'=8] {'gy','gx'}, dimensions={0} | all-to-all | bytes 1048576 | tf_op jit(solution)/shard_map/all_to_all | solution.py:924
  26.4 0.0 copy-done
  26.4 0.0 copy-done.1
  26.4 0.0 copy-done.4
  26.4 0.0 copy-start.3
  26.4 7.6 %shard_map.114 = (f32[3,2,32,128]{3,2,1,0:T(8,128)S(1)}, f32[2,8,128]{2,1,0:T(8,128)}, f32[3,8,32,128]{3,2,1,0:T(8,128)S(1)}) custom-call(f32[16,2,8,512]{3,2,1,0:T(8,128)S(1)} %bitcast.2, bf16[192,240]{1,0:T(8,128)(2,1)S(1)} %copy-done, bf16[144,192]{1,0:T(8,128)(2,1)S(1)} %copy-done.1, f32[32,8]{1,0:T(8,128)S(1)} %copy-done.4), custom_call_target="tpu_custom_call" | custom-call | tf_op jit(solution)/shard_map/pallas_call | solution.py:925
  34.0 1.2 %collective-permute-start.2 = (f32[3,2,32,128]{3,2,1,0:T(8,128)S(1)}, f32[3,2,32,128]{3,2,1,0:T(8,128)S(1)}, u32[]{:S(2)}, u32[]{:S(2)}) collective-permute-start(f32[3,2,32,128]{3,2,1,0:T(8,128)S(1)} %get-tuple-element.4.refs_1_), channel_id=1, source_target_pairs={{2,0},{10,8},{4,2},{12,10},{6,4},{14,12},{22,6},{30,14},{20,22},{2... | collective-permute-start | bytes 294920 | tf_op jit(solution)/shard_map/ppermute | solution.py:920
  35.3 0.0 collective-permute-start.1
  35.3 0.5 collective-permute-start
  35.8 2.9 %collective-permute-done.2.refs_3_ = f32[3,2,32,128]{3,2,1,0:T(8,128)S(1)} collective-permute-done((f32[3,2,32,128]{3,2,1,0:T(8,128)S(1)}, f32[3,2,32,128]{3,2,1,0:T(8,128)S(1)}, u32[]{:S(2)}, u32[]{:S(2)}) %collective-permute-start.2) | collective-permute-done | bytes 98336 | tf_op jit(solution)/shard_map/ppermute | solution.py:920
  38.6 0.0 collective-permute-done.1.refs_2_
  38.6 0.7 %collective-permute-done.refs_0_ = f32[3,2,32,128]{3,2,1,0:T(8,128)S(1)} collective-permute-done((f32[3,2,32,128]{3,2,1,0:T(8,128)S(1)}, f32[3,2,32,128]{3,2,1,0:T(8,128)S(1)}, u32[]{:S(2)}, u32[]{:S(2)}) %collective-permute-start) | collective-permute-done | bytes 98336 | tf_op jit(solution)/shard_map/ppermute | solution.py:920
  39.3 0.0 copy-done.3
  39.3 6.2 %shard_map.115 = f32[16,2,8,128]{3,2,1,0:T(8,128)S(1)} custom-call(f32[3,2,32,128]{3,2,1,0:T(8,128)S(1)} %collective-permute-done.refs_0_, f32[3,2,32,128]{3,2,1,0:T(8,128)S(1)} %get-tuple-element.4.refs_1_, f32[3,2,32,128]{3,2,1,0:T(8,128)S(1)} %collective-permute-done.1.refs_2_, f32[3,2,32,128]{3,2,1,0:T(8,128)S(1)} %collective-permute-done.2.refs_3_, ...), custom_call_target="tpu_custom_call" | custom-call | tf_op jit(solution)/shard_map/pallas_call | solution.py:933
  45.5 0.0 copy-start.2
  45.5 10.9 %all_to_all.11.arrived = f32[32,8,128]{2,1,0:T(8,128)S(1)} all-to-all(f32[32,8,128]{2,1,0:T(8,128)S(1)} %bitcast.3), channel_id=1, replica_groups=mesh['gx'=4,'gy'=8] {'gy','gx'}, dimensions={0} | all-to-all | bytes 262144 | tf_op jit(solution)/shard_map/all_to_all | solution.py:941
  56.4 0.0 copy-done.2
  56.4 1.0 %shard_map.116 = (f32[3,6,3,384]{3,2,1,0:T(4,128)}, f32[3,2,1,128]{3,2,1,0:T(1,128)}) custom-call(f32[32,8,128]{2,1,0:T(8,128)S(1)} %all_to_all.11.arrived, bf16[256,384]{1,0:T(8,128)(2,1)S(1)} %copy-done.2), custom_call_target="tpu_custom_call" | custom-call | tf_op jit(solution)/shard_map/pallas_call | solution.py:942
Async XLA Ops:
  3.5 22.9 %copy-start = (bf16[192,240]{1,0:T(8,128)(2,1)S(1)}, bf16[192,240]{1,0:T(8,128)(2,1)}, u32[]{:S(2)}) copy-start(bf16[192,240]{1,0:T(8,128)(2,1)} %constant.13.clone.spread.refs_5_) | copy-start | bytes 276484
  3.5 22.9 %copy-start.1 = (bf16[144,192]{1,0:T(8,128)(2,1)S(1)}, bf16[144,192]{1,0:T(8,128)(2,1)}, u32[]{:S(2)}) copy-start(bf16[144,192]{1,0:T(8,128)(2,1)} %constant.14.clone.collect.refs_6_) | copy-start | bytes 165892
  3.5 22.9 %copy-start.4 = (f32[32,8]{1,0:T(8,128)S(1)}, f32[32,8]{1,0:T(8,128)}, u32[]{:S(2)}) copy-start(f32[32,8]{1,0:T(8,128)} %constant.15.clone.transfer) | copy-start | bytes 3076
  26.4 12.9 %copy-start.3 = (f32[32,8]{1,0:T(8,128)S(1)}, f32[32,8]{1,0:T(8,128)}, u32[]{:S(2)}) copy-start(f32[32,8]{1,0:T(8,128)} %constant.16.clone.refs_7_) | copy-start | bytes 3076
  34.0 4.6 %collective-permute-start.2 = (f32[3,2,32,128]{3,2,1,0:T(8,128)S(1)}, f32[3,2,32,128]{3,2,1,0:T(8,128)S(1)}, u32[]{:S(2)}, u32[]{:S(2)}) collective-permute-start(f32[3,2,32,128]{3,2,1,0:T(8,128)S(1)} %get-tuple-element.4.refs_1_), channel_id=1, source_target_pairs={{2,0},{10,8},{4,2},{12,10},{6,4},{14,12},{22,6},{30,14},{20,22},{2... | collective-permute-start | bytes 294920 | tf_op jit(solution)/shard_map/ppermute | solution.py:920
  35.3 3.4 %collective-permute-start.1 = (f32[3,2,32,128]{3,2,1,0:T(8,128)S(1)}, f32[3,2,32,128]{3,2,1,0:T(8,128)S(1)}, u32[]{:S(2)}, u32[]{:S(2)}) collective-permute-start(f32[3,2,32,128]{3,2,1,0:T(8,128)S(1)} %get-tuple-element.4.refs_1_), channel_id=1, source_target_pairs={{8,0},{2,8},{10,2},{4,10},{12,4},{6,12},{14,6},{22,14},{30,22},{20... | collective-permute-start | bytes 294920 | tf_op jit(solution)/shard_map/ppermute | solution.py:920
  35.3 4.0 %collective-permute-start = (f32[3,2,32,128]{3,2,1,0:T(8,128)S(1)}, f32[3,2,32,128]{3,2,1,0:T(8,128)S(1)}, u32[]{:S(2)}, u32[]{:S(2)}) collective-permute-start(f32[3,2,32,128]{3,2,1,0:T(8,128)S(1)} %get-tuple-element.4.refs_1_), channel_id=1, source_target_pairs={{9,0},{0,8},{8,2},{2,10},{10,4},{4,12},{12,6},{6,14},{14,22},{22,3... | collective-permute-start | bytes 294920 | tf_op jit(solution)/shard_map/ppermute | solution.py:920
  45.5 10.9 %copy-start.2 = (bf16[256,384]{1,0:T(8,128)(2,1)S(1)}, bf16[256,384]{1,0:T(8,128)(2,1)}, u32[]{:S(2)}) copy-start(bf16[256,384]{1,0:T(8,128)(2,1)} %constant.17.clone.table) | copy-start | bytes 589828

commit v5 on v4

--- a/solution.py
+++ b/solution.py
@@ -27,7 +27,7 @@
 BEFORE_B = 6
 PAIRS_B = 8
 BLOCK = 84
-SENT = 512
+SENT = 384
 
 SLOTS = [
     (0, 0, 0), (1, 0, 0), (2, 0, 0), (0, 1, 0), (0, 2, 0), (0, 0, 1), (0, 0, 2), None,
@@ -276,8 +276,7 @@
     initial_at, forcing_at, modulus_at, listing_at, table_at, out,
     initial, forcing, modulus, listing, table, rows, turned, places, ready,
 ):
-    devices = out.shape[0]
-    own_layers = EZ // devices
+    own_layers = EZ // len(order)
     sources = (listing_at, modulus_at, initial_at, forcing_at, table_at)
     copies = [
         pltpu.make_async_copy(source, here, ready.at[n])
@@ -314,12 +313,14 @@
     copies[4].wait()
     wide = exact_pick(jnp.concatenate(picked, 1), table[...])
     lane = lax.broadcasted_iota(jnp.int32, (128, 128), 1)
-    for block in range(4):
-        here = wide[:, 128 * block : 128 * block + 128]
+    for x in range(2):
         tiles = [None] * (SENT // 128)
-        for pair in range(PAIRS):
-            first = BLOCK * pair
-            moved = here if pair == 0 else pltpu.roll(here, 128 - 2 * pair, 0)
+        for n in range(4):
+            pair, field = n // 2, n % 2
+            moved = wide[:, 128 * (2 * field + x) : 128 * (2 * field + x) + 128]
+            first = BLOCK * n
+            if pair:
+                moved = pltpu.roll(moved, 128 - 2 * pair, 0)
             if first % 128:
                 moved = pltpu.roll(moved, first % 128, 1)
             for tile in range(first // 128, (first + BLOCK - 1) // 128 + 1):
@@ -329,25 +330,15 @@
                 else:
                     tiles[tile] = jnp.where(lane >= first - 128 * tile, moved, before)
         for tile in range(SENT // 128):
-            at = 4 * block + tile
-            places[at, 16:144, :] = tiles[tile]
-            places[at, 0:16, :] = tiles[tile][112:128]
-            places[at, 144:160, :] = tiles[tile][0:16]
-    for block in range(4):
-        for parity in range(2):
-            for tile in range(SENT // 128):
-                at, span = 4 * block + tile, slice(128 * tile, 128 * tile + 128)
-                first = 16 - BEFORE + parity
-                if order == sorted(order):
-                    out[:, 2 * block + parity, span] = places[
-                        at, pl.ds(first, devices, stride=own_layers), :
-                    ]
-                    continue
-                for device, k in enumerate(order):
-                    row = first + own_layers * k
-                    out[device, 2 * block + parity : 2 * block + parity + 1, span] = places[
-                        at, row : row + 1, :
-                    ]
+            places[3 * x + tile, 0:128, :] = tiles[tile]
+            places[3 * x + tile, 128:136, :] = jnp.zeros((8, 128), jnp.float32)
+    for device, k in enumerate(order):
+        for tile in range(SENT // 128):
+            for x in range(2):
+                at = 12 * device + 4 * tile + 2 * x
+                out[at : at + 2, :] = places[
+                    3 * x + tile, own_layers * k : own_layers * k + 2, :
+                ]
 
 
 def unpack_kernel(order, arrived, table, out, coarse_out, layers, turned):
@@ -661,6 +652,29 @@
         return forces
 
 
+def window_pair(slab, first_layer, own_layers, fetch):
+    found = []
+    for parity in range(2):
+        layer = first_layer + parity
+        device = layer // own_layers
+        layer = layer - device * own_layers
+        found.append((device, layer // 2, layer % 2))
+    values = [fetch(device, q) for device, q, parity in found]
+    if found[0][:2] == found[1][:2] or (values[0] is None and values[1] is None):
+        return values[0]
+    for parity in range(2):
+        if values[parity] is None:
+            values[parity] = jnp.zeros_like(values[1 - parity])
+        elif found[parity][2] != parity:
+            values[parity] = slab.lanes(values[parity], 2 * parity - 1)
+    lane = lax.broadcasted_iota(jnp.int32, values[0].shape, 1)
+    return jnp.where(lane % 2 == 0, values[0], values[1])
+
+
+def first_sources(own_layers):
+    return list(range(-BEFORE // own_layers, (own_layers + BEFORE - 1) // own_layers + 1))
+
+
 def make_first_kernel(width, across, own_layers, fine_bound):
     own = BEFORE // 2
     own_pairs = (own_layers + 1) // 2
@@ -669,36 +683,44 @@
         low, high = BEFORE - n, BEFORE + own_layers + n - 1
         spans.append((low // 2, (high + 1) // 2 - low // 2))
 
-    def first_kernel(
-        arrived, spread, collect, transfer, message, edge, f, u, d, stiff, shares, turned
-    ):
+    sources = first_sources(own_layers)
+
+    def first_kernel(*refs):
+        arrived = refs[: len(sources)]
+        refs = refs[len(sources) :]
+        spread, collect, transfer, message, edge, f, u, d, stiff, shares, mixed, turned = refs
         slab = Slab(width, across)
         row = slab.row
         u[...] = jnp.zeros(u.shape, jnp.float32)
         f[...] = jnp.zeros(f.shape, jnp.float32)
         shares[...] = jnp.zeros(shares.shape, jnp.float32)
         stiff[...] = jnp.zeros(stiff.shape, jnp.float32)
-        lower = lax.broadcasted_iota(jnp.int32, (width // 8, 8, 128), 1) < 4
-        for tile in range(SENT // 128):
-            span = slice(128 * tile, 128 * tile + 128)
-            first, second = arrived[:, 0, :, span], arrived[:, 1, :, span]
-            value = jnp.where(lower, first, pltpu.roll(second, 4, 1))
-            load = jnp.where(lower, pltpu.roll(first, 4, 1), second)
-            turned[0, span, :] = value.reshape(width, 128).T
-            turned[1, span, :] = load.reshape(width, 128).T
+        for n in range(len(sources)):
+            for tile in range(SENT // 128):
+                at = n * (SENT // 128) + tile
+                for m in range(width // 4):
+                    first = 12 * m + 4 * tile
+                    mixed[at, 4 * m : 4 * m + 4, :] = arrived[n][first : first + 4, :]
+                turned[n, 128 * tile : 128 * tile + 128, :] = mixed[at].T
         for field, target in enumerate((u, f)):
             for pair in range(PAIRS):
-                base = BLOCK * pair
+
+                def rows(start, field=field, pair=pair):
+                    def fetch(device, q):
+                        if device not in sources:
+                            return None
+                        at = BLOCK * (2 * q + field) + start
+                        return turned[device - sources[0], at : at + 8, :]
+
+                    value = window_pair(slab, 2 * pair - BEFORE, own_layers, fetch)
+                    return jnp.zeros((8, width), jnp.float32) if value is None else value
+
                 for i in range(3):
-                    parts = [
-                        turned[field, base + 24 * i + 8 * n : base + 24 * i + 8 * n + 8, :]
-                        for n in range(3)
-                    ]
-                    inner = turned[field, base + 68 + 4 * i : base + 76 + 4 * i, :]
+                    parts = [rows(24 * i + 8 * n) for n in range(3)]
                     if field == 0 and i == 0:
                         stiff[pair : pair + 1, :] = parts[0][TWIN : TWIN + 1]
                     parts[0] = jnp.where(row == TWIN, pltpu.roll(parts[0], TWIN, 0), parts[0])
-                    parts.append(jnp.where(row < 4, 0.0, inner))
+                    parts.append(jnp.where(row < 4, 0.0, rows(68 + 4 * i)))
                     whole = jnp.concatenate(parts, 0)
                     target[i, pair] = whole * slab.keep if field == 0 else whole
 
@@ -762,22 +784,7 @@
         slab = Slab(width, across)
 
         def pair_of(pair, fetch):
-            found = []
-            for parity in range(2):
-                layer = 2 * pair + first_layer + parity
-                device = layer // own_layers
-                layer = layer - device * own_layers
-                found.append((device, layer // 2, layer % 2))
-            values = [fetch(device, q) for device, q, parity in found]
-            if found[0][:2] == found[1][:2] or (values[0] is None and values[1] is None):
-                return values[0]
-            for parity in range(2):
-                if values[parity] is None:
-                    values[parity] = jnp.zeros_like(values[1 - parity])
-                elif found[parity][2] != parity:
-                    values[parity] = slab.lanes(values[parity], 2 * parity - 1)
-            lane = lax.broadcasted_iota(jnp.int32, values[0].shape, 1)
-            return jnp.where(lane % 2 == 0, values[0], values[1])
+            return window_pair(slab, first_layer + 2 * pair, own_layers, fetch)
 
         u[...] = jnp.zeros(u.shape, jnp.float32)
         coarse[...] = jnp.zeros(coarse.shape, jnp.float32)
@@ -850,6 +857,7 @@
     own_pairs = (own_layers + 1) // 2
     width = 4 * devices
     across = 2 * rows_of
+    near = first_sources(own_layers)
     whole, outer = sources_of(own_layers)
     spread, collect, fine_bound = element_tables()
     coarse_bound = build_tables([0.0, 1.0], 2)[2]
@@ -860,7 +868,7 @@
 
     pack = pl.pallas_call(
         functools.partial(pack_kernel, order),
-        out_shape=jax.ShapeDtypeStruct((devices, 8, SENT), f32),
+        out_shape=jax.ShapeDtypeStruct((devices * 12, 128), f32),
         in_specs=[pl.BlockSpec(memory_space=pl.ANY)] * 5,
         out_specs=pl.BlockSpec(memory_space=pltpu.VMEM),
         scratch_shapes=[
@@ -871,7 +879,7 @@
             pltpu.VMEM((384, 512), jnp.bfloat16),
             pltpu.VMEM((128, 384), f32),
             pltpu.VMEM((384, 128), f32),
-            pltpu.VMEM((16, 160, 128), f32),
+            pltpu.VMEM((6, 136, 128), f32),
             pltpu.SemaphoreType.DMA((5,)),
         ],
         compiler_params=wide,
@@ -888,7 +896,8 @@
             pltpu.VMEM((3, 8, 32, width), f32),
             pltpu.VMEM((8, width), f32),
             pltpu.VMEM((3, 8, 8, width), f32),
-            pltpu.VMEM((2, SENT, width), f32),
+            pltpu.VMEM((len(near) * (SENT // 128), width, 128), f32),
+            pltpu.VMEM((len(near), SENT, width), f32),
         ],
         compiler_params=limit,
     )
@@ -921,9 +930,10 @@
 
     def body(initial, forcing, modulus, solid_list):
         sent = pack(initial, forcing, modulus, solid_list, jnp.asarray(pack_table()))
-        arrived = lax.all_to_all(sent, everyone, 0, 0, tiled=True)
+        sent = sent.reshape(devices, SENT // 128, 4, 128)
+        arrived = lax.all_to_all(sent, everyone, 0, 0, tiled=True).reshape(devices * 12, 128)
         message, edge, load = first(
-            arrived.reshape(devices // 2, 2, 8, SENT),
+            *[from_device(arrived, n) if n else arrived for n in near],
             jnp.asarray(spread),
             jnp.asarray(collect),
             jnp.asarray(transfer),

time: 57.7 us -> 56 us (0.971)
  blocking collectives: 33.8 us -> 27.2 us
  waiting for transfers between devices: 3.53 us -> 8.37 us
    all_to_all x1, blocking collectives: 22.9 us -> 16.2 us  [body(): lax.all_to_all(sent, everyone, 0, 0, tiled=True).reshape(devices * 12, 128)]
    ppermute x3 -> x5, waiting for transfers between devices: 3.53 us -> 8.37 us  [from_device(): return lax.ppermute(block, ('gx', 'gy'), route)]
    ppermute x3 -> x5, starting transfers between devices: 1.76 us -> 2.03 us  [from_device(): return lax.ppermute(block, ('gx', 'gy'), route)]
  transfers between devices with their start and end apart: 3 -> 5, of which waited for: 2 -> 3; matrix products, arithmetic and copies ran while one was open for 0% -> 0% of each run, Pallas kernels for 0% -> 0%
where the time goes in v5:
time: 56 us; the launch traced here: 55.7 us
  blocking collectives  27.2 us (49%)
  Pallas kernels  17.4 us (31%)
  waiting for transfers between devices  8.37 us (15%)
  starting transfers between devices  2.03 us (4%)
  between operations  0.69 us (1%)
    all_to_all x1, blocking collectives, body(): lax.all_to_all(sent, everyone, 0, 0, tiled=True).reshape(devices * 12, 128)  16.2 us
    all_to_all x1, blocking collectives, body(): lax.all_to_all(result.reshape(devices, 8, 128), everyone, 0, 0, tiled=True)  11 us
    ppermute x5, waiting for transfers between devices, from_device(): return lax.ppermute(block, ('gx', 'gy'), route)  8.37 us
    pallas_call x1, Pallas kernels, body(): first(*[from_device(arrived, n) if n else arrived for n in near], jnp.asa...  7.77 us
    pallas_call x1, Pallas kernels, body(): second(*messages, *edges, load, jnp.asarray(spread), jnp.asarray(collect)...  6.17 us
    pallas_call x1, Pallas kernels, body(): pack(initial, forcing, modulus, solid_list, jnp.asarray(pack_table()))  2.43 us
    ppermute x5, starting transfers between devices, from_device(): return lax.ppermute(block, ('gx', 'gy'), route)  2.03 us
  transfers between devices with their start and end apart: 5, of which 3 were waited for; matrix products, arithmetic and copies ran while one was open for 0% of the time, Pallas kernels for 0%

profile of v5, /device:TPU:0, one launch (start us, length us, event | category | flops | bytes accessed | tf_op | source)
XLA Modules:
  0.0 55.7 jit_solution(17979559696593201943)
XLA Ops:
  0.6 2.4 %shard_map.113 = f32[384,128]{1,0:T(8,128)} custom-call(f32[3,6,3,384]{3,2,1,0:T(4,128)} %initial_at.1, f32[3,6,3,384]{3,2,1,0:T(4,128)} %forcing_at.1, f32[2,1,128]{2,1,0:T(1,128)} %modulus_at.1, s32[1,1,192]{2,1,0:T(1,128)} %listing_at.1, bf16[384,512]{1,0:T(8,128)(2,1)} %constant.12.clone.table_at), custom_call_target="tpu_custom_call" | custom-call | tf_op jit(solution)/shard_map/pallas_call | solution.py:932
  3.1 0.0 copy-start
  3.1 0.0 copy-start.1
  3.1 0.0 copy-start.4
  3.1 16.2 %all_to_all.10 = f32[32,3,4,128]{3,2,1,0:T(4,128)S(1)} all-to-all(f32[32,3,4,128]{3,2,1,0:T(4,128)} %bitcast.7), channel_id=1, replica_groups=mesh['gx'=4,'gy'=8] {'gy','gx'}, dimensions={0} | all-to-all | bytes 393216 | tf_op jit(solution)/shard_map/all_to_all | solution.py:934
  19.3 0.0 copy-start.3
  19.3 0.2 collective-permute-start.1
  19.5 0.4 collective-permute-start
  19.9 2.8 %collective-permute-done.1.refs_2_ = f32[384,128]{1,0:T(8,128)S(1)} collective-permute-done((f32[384,128]{1,0:T(8,128)S(1)}, f32[384,128]{1,0:T(8,128)S(1)}, u32[]{:S(2)}, u32[]{:S(2)}) %collective-permute-start.1) | collective-permute-done | bytes 196640 | tf_op jit(solution)/shard_map/ppermute | solution.py:929
  22.7 1.9 %collective-permute-done.refs_0_ = f32[384,128]{1,0:T(8,128)S(1)} collective-permute-done((f32[384,128]{1,0:T(8,128)S(1)}, f32[384,128]{1,0:T(8,128)S(1)}, u32[]{:S(2)}, u32[]{:S(2)}) %collective-permute-start) | collective-permute-done | bytes 196640 | tf_op jit(solution)/shard_map/ppermute | solution.py:929
  24.6 0.0 copy-done
  24.6 0.0 copy-done.1
  24.6 0.0 copy-done.4
  24.6 7.8 %shard_map.114 = (f32[3,2,32,128]{3,2,1,0:T(8,128)S(1)}, f32[2,8,128]{2,1,0:T(8,128)}, f32[3,8,32,128]{3,2,1,0:T(8,128)S(1)}) custom-call(f32[384,128]{1,0:T(8,128)S(1)} %collective-permute-done.refs_0_, f32[384,128]{1,0:T(8,128)S(1)} %bitcast.5, f32[384,128]{1,0:T(8,128)S(1)} %collective-permute-done.1.refs_2_, bf16[192,240]{1,0:T(8,128)(2,1)S(1)} %copy-done, ...), custom_call_target="tpu_custom_call" | custom-call | tf_op jit(solution)/shard_map/pallas_call | solution.py:935
  32.4 0.9 %collective-permute-start.4 = (f32[3,2,32,128]{3,2,1,0:T(8,128)S(1)}, f32[3,2,32,128]{3,2,1,0:T(8,128)S(1)}, u32[]{:S(2)}, u32[]{:S(2)}) collective-permute-start(f32[3,2,32,128]{3,2,1,0:T(8,128)S(1)} %get-tuple-element.4.refs_1_), channel_id=1, source_target_pairs={{2,0},{10,8},{4,2},{12,10},{6,4},{14,12},{22,6},{30,14},{20,22},{2... | collective-permute-start | bytes 294920 | tf_op jit(solution)/shard_map/ppermute | solution.py:929
  33.3 0.0 collective-permute-start.3
  33.4 0.5 collective-permute-start.2
  33.8 3.7 %collective-permute-done.4.refs_3_ = f32[3,2,32,128]{3,2,1,0:T(8,128)S(1)} collective-permute-done((f32[3,2,32,128]{3,2,1,0:T(8,128)S(1)}, f32[3,2,32,128]{3,2,1,0:T(8,128)S(1)}, u32[]{:S(2)}, u32[]{:S(2)}) %collective-permute-start.4) | collective-permute-done | bytes 98336 | tf_op jit(solution)/shard_map/ppermute | solution.py:929
  37.5 0.0 collective-permute-done.3.refs_2_
  37.5 0.0 collective-permute-done.2.refs_0_
  37.5 0.0 copy-done.3
  37.5 6.2 %shard_map.115 = f32[16,2,8,128]{3,2,1,0:T(8,128)S(1)} custom-call(f32[3,2,32,128]{3,2,1,0:T(8,128)S(1)} %collective-permute-done.2.refs_0_, f32[3,2,32,128]{3,2,1,0:T(8,128)S(1)} %get-tuple-element.4.refs_1_, f32[3,2,32,128]{3,2,1,0:T(8,128)S(1)} %collective-permute-done.3.refs_2_, f32[3,2,32,128]{3,2,1,0:T(8,128)S(1)} %collective-permute-done.4.refs_3_, ...), custom_call_target="tpu_custom_call" | custom-call | tf_op jit(solution)/shard_map/pallas_call | solution.py:943
  43.7 0.0 copy-start.2
  43.7 11.0 %all_to_all.11.arrived = f32[32,8,128]{2,1,0:T(8,128)S(1)} all-to-all(f32[32,8,128]{2,1,0:T(8,128)S(1)} %bitcast.6), channel_id=1, replica_groups=mesh['gx'=4,'gy'=8] {'gy','gx'}, dimensions={0} | all-to-all | bytes 262144 | tf_op jit(solution)/shard_map/all_to_all | solution.py:951
  54.7 0.0 copy-done.2
  54.7 1.0 %shard_map.116 = (f32[3,6,3,384]{3,2,1,0:T(4,128)}, f32[3,2,1,128]{3,2,1,0:T(1,128)}) custom-call(f32[32,8,128]{2,1,0:T(8,128)S(1)} %all_to_all.11.arrived, bf16[256,384]{1,0:T(8,128)(2,1)S(1)} %copy-done.2), custom_call_target="tpu_custom_call" | custom-call | tf_op jit(solution)/shard_map/pallas_call | solution.py:952
Async XLA Ops:
  3.1 21.5 %copy-start = (bf16[192,240]{1,0:T(8,128)(2,1)S(1)}, bf16[192,240]{1,0:T(8,128)(2,1)}, u32[]{:S(2)}) copy-start(bf16[192,240]{1,0:T(8,128)(2,1)} %constant.13.clone.refs_3_.refs_5_) | copy-start | bytes 276484
  3.1 21.5 %copy-start.1 = (bf16[144,192]{1,0:T(8,128)(2,1)S(1)}, bf16[144,192]{1,0:T(8,128)(2,1)}, u32[]{:S(2)}) copy-start(bf16[144,192]{1,0:T(8,128)(2,1)} %constant.14.clone.refs_4_.refs_6_) | copy-start | bytes 165892
  3.1 21.5 %copy-start.4 = (f32[32,8]{1,0:T(8,128)S(1)}, f32[32,8]{1,0:T(8,128)}, u32[]{:S(2)}) copy-start(f32[32,8]{1,0:T(8,128)} %constant.15.clone.refs_5_) | copy-start | bytes 3076
  19.3 18.2 %copy-start.3 = (f32[32,8]{1,0:T(8,128)S(1)}, f32[32,8]{1,0:T(8,128)}, u32[]{:S(2)}) copy-start(f32[32,8]{1,0:T(8,128)} %constant.16.clone.refs_7_) | copy-start | bytes 3076
  19.3 3.4 %collective-permute-start.1 = (f32[384,128]{1,0:T(8,128)S(1)}, f32[384,128]{1,0:T(8,128)S(1)}, u32[]{:S(2)}, u32[]{:S(2)}) collective-permute-start(f32[384,128]{1,0:T(8,128)S(1)} %bitcast.3), channel_id=1, source_target_pairs={{8,0},{2,8},{10,2},{4,10},{12,4},{6,12},{14,6},{22,14},{30,22},{20... | collective-permute-start | bytes 589832 | tf_op jit(solution)/shard_map/ppermute | solution.py:929
  19.5 5.1 %collective-permute-start = (f32[384,128]{1,0:T(8,128)S(1)}, f32[384,128]{1,0:T(8,128)S(1)}, u32[]{:S(2)}, u32[]{:S(2)}) collective-permute-start(f32[384,128]{1,0:T(8,128)S(1)} %bitcast.4), channel_id=1, source_target_pairs={{9,0},{0,8},{8,2},{2,10},{10,4},{4,12},{12,6},{6,14},{14,22},{22,3... | collective-permute-start | bytes 589832 | tf_op jit(solution)/shard_map/ppermute | solution.py:929
  32.4 5.1 %collective-permute-start.4 = (f32[3,2,32,128]{3,2,1,0:T(8,128)S(1)}, f32[3,2,32,128]{3,2,1,0:T(8,128)S(1)}, u32[]{:S(2)}, u32[]{:S(2)}) collective-permute-start(f32[3,2,32,128]{3,2,1,0:T(8,128)S(1)} %get-tuple-element.4.refs_1_), channel_id=1, source_target_pairs={{2,0},{10,8},{4,2},{12,10},{6,4},{14,12},{22,6},{30,14},{20,22},{2... | collective-permute-start | bytes 294920 | tf_op jit(solution)/shard_map/ppermute | solution.py:929
  33.3 4.2 %collective-permute-start.3 = (f32[3,2,32,128]{3,2,1,0:T(8,128)S(1)}, f32[3,2,32,128]{3,2,1,0:T(8,128)S(1)}, u32[]{:S(2)}, u32[]{:S(2)}) collective-permute-start(f32[3,2,32,128]{3,2,1,0:T(8,128)S(1)} %get-tuple-element.4.refs_1_), channel_id=1, source_target_pairs={{8,0},{2,8},{10,2},{4,10},{12,4},{6,12},{14,6},{22,14},{30,22},{20... | collective-permute-start | bytes 294920 | tf_op jit(solution)/shard_map/ppermute | solution.py:929
  33.4 4.1 %collective-permute-start.2 = (f32[3,2,32,128]{3,2,1,0:T(8,128)S(1)}, f32[3,2,32,128]{3,2,1,0:T(8,128)S(1)}, u32[]{:S(2)}, u32[]{:S(2)}) collective-permute-start(f32[3,2,32,128]{3,2,1,0:T(8,128)S(1)} %get-tuple-element.4.refs_1_), channel_id=1, source_target_pairs={{9,0},{0,8},{8,2},{2,10},{10,4},{4,12},{12,6},{6,14},{14,22},{22,3... | collective-permute-start | bytes 294920 | tf_op jit(solution)/shard_map/ppermute | solution.py:929
  43.7 11.0 %copy-start.2 = (bf16[256,384]{1,0:T(8,128)(2,1)S(1)}, bf16[256,384]{1,0:T(8,128)(2,1)}, u32[]{:S(2)}) copy-start(bf16[256,384]{1,0:T(8,128)(2,1)} %constant.17.clone.table) | copy-start | bytes 589828

commit v6 on v5

--- a/solution.py
+++ b/solution.py
@@ -243,16 +243,12 @@
     return table.reshape(256, 384).astype(jnp.bfloat16)
 
 
-def exact_pick(values, table):
-    high = values.astype(jnp.bfloat16)
-    rest = values - high.astype(jnp.float32)
-    middle = rest.astype(jnp.bfloat16)
-    low = (rest - middle.astype(jnp.float32)).astype(jnp.bfloat16)
+def pick(values, table):
     count = values.shape[0]
     parts = jnp.dot(
-        jnp.concatenate([high, middle, low], 0), table, preferred_element_type=jnp.float32
-    )
-    return parts[:count] + (parts[count : 2 * count] + parts[2 * count :])
+        jnp.concatenate(high_low(values), 0), table, preferred_element_type=jnp.float32
+    )
+    return parts[:count] + parts[count:]
 
 
 def ring_order(rows_of, columns_of):
@@ -265,10 +261,6 @@
                 chip = (z, 7 - z, 15 - z, 8 + z)[2 * x + y]
                 order += [2 * chip, 2 * chip + 1]
     return order
-
-
-def region_shift(own_layers):
-    return 2 if own_layers == 4 else 0
 
 
 def pack_kernel(
@@ -311,7 +303,7 @@
     picked = [turned[pl.ds(c, 128, stride=3), :] for c in range(3)]
     picked[0] = picked[0] + stiff.T
     copies[4].wait()
-    wide = exact_pick(jnp.concatenate(picked, 1), table[...])
+    wide = pick(jnp.concatenate(picked, 1), table[...])
     lane = lax.broadcasted_iota(jnp.int32, (128, 128), 1)
     for x in range(2):
         tiles = [None] * (SENT // 128)
@@ -351,9 +343,9 @@
                 layers[x, pl.ds(layer, devices, stride=own_layers), :] = arrived[:, row, :]
                 continue
             for device, k in enumerate(order):
-                at = (region_shift(own_layers) + own_layers * k + layer) % EZ
+                at = own_layers * k + layer
                 layers[x, at : at + 1, :] = arrived[device, row : row + 1, :]
-    wide = exact_pick(jnp.concatenate([layers[0], layers[1]], 1), table[...])
+    wide = pick(jnp.concatenate([layers[0], layers[1]], 1), table[...])
     for c in range(3):
         turned[pl.ds(c, 128, stride=3), :] = wide[:, 128 * c : 128 * c + 128]
     for part in range(3):
@@ -490,10 +482,8 @@
         moved = (self.lanes(z0, -1), self.lanes(z2, -1))
         return jnp.concatenate([own0, own1, own2, own3], 0), moved
 
-    def gradient(self, u, spread, pair):
-        blocks = [
-            self.gather(u[i, pair + q], u[i, pair + q + 1]) for i in range(3) for q in range(2)
-        ]
+    def gradient(self, u, spread, pairs):
+        blocks = [self.gather(u[i, pair], u[i, pair + 1]) for i in range(3) for pair in pairs]
         high, low = high_low(jnp.concatenate(blocks, 1))
         return jnp.dot(
             spread[...],
@@ -501,9 +491,9 @@
             preferred_element_type=jnp.float32,
         )
 
-    def force(self, gradient, stiff, collect, pair):
-        width = 2 * self.width
-        stiffness = jnp.concatenate([stiff[pair + q : pair + q + 1, :] for q in range(2)], 1)
+    def force(self, gradient, stiff, collect, pairs):
+        width = len(pairs) * self.width
+        stiffness = jnp.concatenate([stiff[pair : pair + 1, :] for pair in pairs], 1)
         deform = [
             [
                 gradient[64 * e : 64 * e + 64, width * i : width * (i + 1)]
@@ -526,21 +516,22 @@
         width = self.width
         none = jnp.zeros((8, width), jnp.float32)
         carry = [(none, none) for i in range(3)]
-        last = first + 2 * ((count + 1) // 2)
-        ahead = self.gradient(u, spread, first)
-        for pair in range(first, last, 2):
+        last = first + count
+        steps = [list(range(at, min(at + 2, last))) for at in range(first, last, 2)]
+        ahead = self.gradient(u, spread, steps[0])
+        for n, pairs in enumerate(steps):
             gradient = ahead
-            if pair + 2 < last:
-                ahead = self.gradient(u, spread, pair + 2)
-            force = self.force(gradient, stiff, collect, pair)
-            totals = [[], []]
-            for q in range(2):
+            if n + 1 < len(steps):
+                ahead = self.gradient(u, spread, steps[n + 1])
+            force = self.force(gradient, stiff, collect, pairs)
+            totals = [[] for pair in pairs]
+            for q in range(len(pairs)):
                 for i in range(3):
-                    at = (2 * i + q) * width
+                    at = (len(pairs) * i + q) * width
                     total, carry[i] = self.scatter(force[:, at : at + width], carry[i])
                     totals[q].append(total)
-            for q in range(2):
-                finish(pair + q, totals[q])
+            for pair, total in zip(pairs, totals):
+                finish(pair, total)
 
     def smooth(self, u, f, f_shift, d, stiff, spread, collect, spans, bound):
         for (first, count), (held, added) in zip(spans, chebyshev_steps()):
@@ -758,17 +749,15 @@
 
 
 def sources_of(own_layers):
-    shift = region_shift(own_layers)
-    whole = range((shift - 3) // own_layers, (shift + own_layers + 2) // own_layers + 1)
-    coarse = range((shift - 5) // own_layers, (shift + own_layers + 4) // own_layers + 1)
+    whole = range(-3 // own_layers, (own_layers + 2) // own_layers + 1)
+    coarse = range(-5 // own_layers, (own_layers + 4) // own_layers + 1)
     return list(whole), [n for n in coarse if n not in whole]
 
 
 def make_second_kernel(width, across, own_layers, fine_bound, coarse_bound):
     own = BEFORE_B // 2
     own_pairs = (own_layers + 1) // 2
-    first_layer = region_shift(own_layers) - BEFORE_B
-    shift = (BEFORE + first_layer) // 2
+    shift = (BEFORE - BEFORE_B) // 2
     whole, outer = sources_of(own_layers)
     steps = chebyshev_steps()
     spans = []
@@ -784,7 +773,7 @@
         slab = Slab(width, across)
 
         def pair_of(pair, fetch):
-            return window_pair(slab, first_layer + 2 * pair, own_layers, fetch)
+            return window_pair(slab, 2 * pair - BEFORE_B, own_layers, fetch)
 
         u[...] = jnp.zeros(u.shape, jnp.float32)
         coarse[...] = jnp.zeros(coarse.shape, jnp.float32)
@@ -889,7 +878,7 @@
         out_shape=(
             jax.ShapeDtypeStruct((3, own_pairs, 32, width), f32),
             jax.ShapeDtypeStruct((own_pairs, 8, width), f32),
-            jax.ShapeDtypeStruct((3, PAIRS_B, 32, width), f32),
+            jax.ShapeDtypeStruct((3, PAIRS, 32, width), f32),
         ),
         scratch_shapes=[
             pltpu.VMEM((3, 8, 32, width), f32),

time: 56 us -> 54.5 us (0.973)
  Pallas kernels: 17.4 us -> 15.8 us
  starting transfers between devices: 2.03 us -> 3.15 us
  waiting for transfers between devices: 8.37 us -> 7.25 us
    ppermute x5 -> x6, starting transfers between devices: 2.03 us -> 3.15 us  [from_device(): return lax.ppermute(block, ('gx', 'gy'), route)]
    ppermute x5 -> x6, waiting for transfers between devices: 8.37 us -> 7.25 us  [from_device(): return lax.ppermute(block, ('gx', 'gy'), route)]
    pallas_call x1, Pallas kernels: 7.77 us -> 6.72 us  [body(): first(*[from_device(arrived, n) if n else arrived for n in near], jnp.asa...]
  transfers between devices with their start and end apart: 5 -> 6, of which waited for: 3 -> 4; matrix products, arithmetic and copies ran while one was open for 0% -> 0% of each run, Pallas kernels for 0% -> 0%
where the time goes in v6:
time: 54.5 us; the launch traced here: 54.3 us
  blocking collectives  27.3 us (50%)
  Pallas kernels  15.8 us (29%)
  waiting for transfers between devices  7.25 us (13%)
  starting transfers between devices  3.15 us (6%)
  between operations  0.7 us (1%)
    all_to_all x1, blocking collectives, body(): lax.all_to_all(sent, everyone, 0, 0, tiled=True).reshape(devices * 12, 128)  16.2 us
    all_to_all x1, blocking collectives, body(): lax.all_to_all(result.reshape(devices, 8, 128), everyone, 0, 0, tiled=True)  11.1 us
    ppermute x6, waiting for transfers between devices, from_device(): return lax.ppermute(block, ('gx', 'gy'), route)  7.25 us
    pallas_call x1, Pallas kernels, body(): first(*[from_device(arrived, n) if n else arrived for n in near], jnp.asa...  6.72 us
    pallas_call x1, Pallas kernels, body(): second(*messages, *edges, load, jnp.asarray(spread), jnp.asarray(collect)...  5.73 us
    ppermute x6, starting transfers between devices, from_device(): return lax.ppermute(block, ('gx', 'gy'), route)  3.15 us
    pallas_call x1, Pallas kernels, body(): pack(initial, forcing, modulus, solid_list, jnp.asarray(pack_table()))  2.37 us
  transfers between devices with their start and end apart: 6, of which 4 were waited for; matrix products, arithmetic and copies ran while one was open for 0% of the time, Pallas kernels for 0%

profile of v6, /device:TPU:0, one launch (start us, length us, event | category | flops | bytes accessed | tf_op | source)
XLA Modules:
  0.0 54.3 jit_solution(13587309295698521131)
XLA Ops:
  0.6 2.4 %shard_map.113 = f32[384,128]{1,0:T(8,128)} custom-call(f32[3,6,3,384]{3,2,1,0:T(4,128)} %initial_at.1, f32[3,6,3,384]{3,2,1,0:T(4,128)} %forcing_at.1, f32[2,1,128]{2,1,0:T(1,128)} %modulus_at.1, s32[1,1,192]{2,1,0:T(1,128)} %listing_at.1, bf16[384,512]{1,0:T(8,128)(2,1)} %constant.12.clone.table_at), custom_call_target="tpu_custom_call" | custom-call | tf_op jit(solution)/shard_map/pallas_call | solution.py:921
  3.0 0.0 copy-start
  3.0 0.0 copy-start.1
  3.0 0.0 copy-start.4
  3.0 16.2 %all_to_all.10 = f32[32,3,4,128]{3,2,1,0:T(4,128)S(1)} all-to-all(f32[32,3,4,128]{3,2,1,0:T(4,128)} %bitcast.7), channel_id=1, replica_groups=mesh['gx'=4,'gy'=8] {'gy','gx'}, dimensions={0} | all-to-all | bytes 393216 | tf_op jit(solution)/shard_map/all_to_all | solution.py:923
  19.2 0.2 collective-permute-start.1
  19.5 0.4 collective-permute-start
  19.8 2.8 %collective-permute-done.1.refs_2_ = f32[384,128]{1,0:T(8,128)S(1)} collective-permute-done((f32[384,128]{1,0:T(8,128)S(1)}, f32[384,128]{1,0:T(8,128)S(1)}, u32[]{:S(2)}, u32[]{:S(2)}) %collective-permute-start.1) | collective-permute-done | bytes 196640 | tf_op jit(solution)/shard_map/ppermute | solution.py:918
  22.6 1.9 %collective-permute-done.refs_0_ = f32[384,128]{1,0:T(8,128)S(1)} collective-permute-done((f32[384,128]{1,0:T(8,128)S(1)}, f32[384,128]{1,0:T(8,128)S(1)}, u32[]{:S(2)}, u32[]{:S(2)}) %collective-permute-start) | collective-permute-done | bytes 196640 | tf_op jit(solution)/shard_map/ppermute | solution.py:918
  24.6 0.0 copy-done
  24.6 0.0 copy-done.1
  24.6 0.0 copy-done.4
  24.6 0.0 copy-start.3
  24.6 6.7 %shard_map.114 = (f32[3,2,32,128]{3,2,1,0:T(8,128)S(1)}, f32[2,8,128]{2,1,0:T(8,128)S(1)}, f32[3,6,32,128]{3,2,1,0:T(8,128)S(1)}) custom-call(f32[384,128]{1,0:T(8,128)S(1)} %collective-permute-done.refs_0_, f32[384,128]{1,0:T(8,128)S(1)} %bitcast.5, f32[384,128]{1,0:T(8,128)S(1)} %collective-permute-done.1.refs_2_, bf16[192,240]{1,0:T(8,128)(2,1)S(1)} %copy-done, ...), custom_call_target="tpu_custom_call" | custom-call | tf_op jit(solution)/shard_map/pallas_call | solution.py:924
  31.3 0.3 collective-permute-start.3
  31.6 0.2 collective-permute-start.2
  31.8 0.9 %collective-permute-start.5 = (f32[2,8,128]{2,1,0:T(8,128)S(1)}, f32[2,8,128]{2,1,0:T(8,128)S(1)}, u32[]{:S(2)}, u32[]{:S(2)}) collective-permute-start(f32[2,8,128]{2,1,0:T(8,128)S(1)} %get-tuple-element.6), channel_id=1, source_target_pairs={{2,0},{10,8},{4,2},{12,10},{6,4},{14,12},{22,6},{30,14},{20,22},{2... | collective-permute-start | bytes 24584 | tf_op jit(solution)/shard_map/ppermute | solution.py:918
  32.7 1.1 %collective-permute-start.4 = (f32[2,8,128]{2,1,0:T(8,128)S(1)}, f32[2,8,128]{2,1,0:T(8,128)S(1)}, u32[]{:S(2)}, u32[]{:S(2)}) collective-permute-start(f32[2,8,128]{2,1,0:T(8,128)S(1)} %get-tuple-element.6), channel_id=1, source_target_pairs={{1,0},{9,8},{0,2},{8,10},{2,4},{10,12},{4,6},{12,14},{6,22},{14,30... | collective-permute-start | bytes 24584 | tf_op jit(solution)/shard_map/ppermute | solution.py:918
  33.9 2.2 %collective-permute-done.5.refs_4_ = f32[2,8,128]{2,1,0:T(8,128)S(1)} collective-permute-done((f32[2,8,128]{2,1,0:T(8,128)S(1)}, f32[2,8,128]{2,1,0:T(8,128)S(1)}, u32[]{:S(2)}, u32[]{:S(2)}) %collective-permute-start.5) | collective-permute-done | bytes 8224 | tf_op jit(solution)/shard_map/ppermute | solution.py:918
  36.0 0.4 collective-permute-done.4.refs_3_
  36.4 0.0 collective-permute-done.3.refs_2_
  36.4 0.0 collective-permute-done.2.refs_0_
  36.4 0.0 copy-done.3
  36.4 5.7 %shard_map.115 = f32[16,2,8,128]{3,2,1,0:T(8,128)S(1)} custom-call(f32[3,2,32,128]{3,2,1,0:T(8,128)S(1)} %collective-permute-done.2.refs_0_, f32[3,2,32,128]{3,2,1,0:T(8,128)S(1)} %get-tuple-element.5.refs_1_, f32[3,2,32,128]{3,2,1,0:T(8,128)S(1)} %collective-permute-done.3.refs_2_, f32[2,8,128]{2,1,0:T(8,128)S(1)} %collective-permute-done.4.refs_3_, ...), custom_call_target="tpu_custom_call" | custom-call | tf_op jit(solution)/shard_map/pallas_call | solution.py:932
  42.1 0.0 copy-start.2
  42.2 11.1 %all_to_all.11.arrived = f32[32,8,128]{2,1,0:T(8,128)S(1)} all-to-all(f32[32,8,128]{2,1,0:T(8,128)S(1)} %bitcast.6), channel_id=1, replica_groups=mesh['gx'=4,'gy'=8] {'gy','gx'}, dimensions={0} | all-to-all | bytes 262144 | tf_op jit(solution)/shard_map/all_to_all | solution.py:940
  53.3 0.0 copy-done.2
  53.3 1.0 %shard_map.116 = (f32[3,6,3,384]{3,2,1,0:T(4,128)}, f32[3,2,1,128]{3,2,1,0:T(1,128)}) custom-call(f32[32,8,128]{2,1,0:T(8,128)S(1)} %all_to_all.11.arrived, bf16[256,384]{1,0:T(8,128)(2,1)S(1)} %copy-done.2), custom_call_target="tpu_custom_call" | custom-call | tf_op jit(solution)/shard_map/pallas_call | solution.py:941
Async XLA Ops:
  3.0 21.5 %copy-start = (bf16[192,240]{1,0:T(8,128)(2,1)S(1)}, bf16[192,240]{1,0:T(8,128)(2,1)}, u32[]{:S(2)}) copy-start(bf16[192,240]{1,0:T(8,128)(2,1)} %constant.13.clone.refs_3_.refs_6_) | copy-start | bytes 276484
  3.0 21.5 %copy-start.1 = (bf16[144,192]{1,0:T(8,128)(2,1)S(1)}, bf16[144,192]{1,0:T(8,128)(2,1)}, u32[]{:S(2)}) copy-start(bf16[144,192]{1,0:T(8,128)(2,1)} %constant.14.clone.refs_4_.refs_7_) | copy-start | bytes 165892
  3.0 21.5 %copy-start.4 = (f32[32,8]{1,0:T(8,128)S(1)}, f32[32,8]{1,0:T(8,128)}, u32[]{:S(2)}) copy-start(f32[32,8]{1,0:T(8,128)} %constant.15.clone.refs_5_) | copy-start | bytes 3076
  19.2 3.4 %collective-permute-start.1 = (f32[384,128]{1,0:T(8,128)S(1)}, f32[384,128]{1,0:T(8,128)S(1)}, u32[]{:S(2)}, u32[]{:S(2)}) collective-permute-start(f32[384,128]{1,0:T(8,128)S(1)} %bitcast.3), channel_id=1, source_target_pairs={{8,0},{2,8},{10,2},{4,10},{12,4},{6,12},{14,6},{22,14},{30,22},{20... | collective-permute-start | bytes 589832 | tf_op jit(solution)/shard_map/ppermute | solution.py:918
  19.5 5.1 %collective-permute-start = (f32[384,128]{1,0:T(8,128)S(1)}, f32[384,128]{1,0:T(8,128)S(1)}, u32[]{:S(2)}, u32[]{:S(2)}) collective-permute-start(f32[384,128]{1,0:T(8,128)S(1)} %bitcast.4), channel_id=1, source_target_pairs={{9,0},{0,8},{8,2},{2,10},{10,4},{4,12},{12,6},{6,14},{14,22},{22,3... | collective-permute-start | bytes 589832 | tf_op jit(solution)/shard_map/ppermute | solution.py:918
  24.6 11.8 %copy-start.3 = (f32[32,8]{1,0:T(8,128)S(1)}, f32[32,8]{1,0:T(8,128)}, u32[]{:S(2)}) copy-start(f32[32,8]{1,0:T(8,128)} %constant.16.clone.refs_8_) | copy-start | bytes 3076
  31.3 5.1 %collective-permute-start.3 = (f32[3,2,32,128]{3,2,1,0:T(8,128)S(1)}, f32[3,2,32,128]{3,2,1,0:T(8,128)S(1)}, u32[]{:S(2)}, u32[]{:S(2)}) collective-permute-start(f32[3,2,32,128]{3,2,1,0:T(8,128)S(1)} %get-tuple-element.5.refs_1_), channel_id=1, source_target_pairs={{8,0},{2,8},{10,2},{4,10},{12,4},{6,12},{14,6},{22,14},{30,22},{20... | collective-permute-start | bytes 294920 | tf_op jit(solution)/shard_map/ppermute | solution.py:918
  31.6 4.8 %collective-permute-start.2 = (f32[3,2,32,128]{3,2,1,0:T(8,128)S(1)}, f32[3,2,32,128]{3,2,1,0:T(8,128)S(1)}, u32[]{:S(2)}, u32[]{:S(2)}) collective-permute-start(f32[3,2,32,128]{3,2,1,0:T(8,128)S(1)} %get-tuple-element.5.refs_1_), channel_id=1, source_target_pairs={{9,0},{0,8},{8,2},{2,10},{10,4},{4,12},{12,6},{6,14},{14,22},{22,3... | collective-permute-start | bytes 294920 | tf_op jit(solution)/shard_map/ppermute | solution.py:918
  31.8 4.2 %collective-permute-start.5 = (f32[2,8,128]{2,1,0:T(8,128)S(1)}, f32[2,8,128]{2,1,0:T(8,128)S(1)}, u32[]{:S(2)}, u32[]{:S(2)}) collective-permute-start(f32[2,8,128]{2,1,0:T(8,128)S(1)} %get-tuple-element.6), channel_id=1, source_target_pairs={{2,0},{10,8},{4,2},{12,10},{6,4},{14,12},{22,6},{30,14},{20,22},{2... | collective-permute-start | bytes 24584 | tf_op jit(solution)/shard_map/ppermute | solution.py:918
  32.7 3.7 %collective-permute-start.4 = (f32[2,8,128]{2,1,0:T(8,128)S(1)}, f32[2,8,128]{2,1,0:T(8,128)S(1)}, u32[]{:S(2)}, u32[]{:S(2)}) collective-permute-start(f32[2,8,128]{2,1,0:T(8,128)S(1)} %get-tuple-element.6), channel_id=1, source_target_pairs={{1,0},{9,8},{0,2},{8,10},{2,4},{10,12},{4,6},{12,14},{6,22},{14,30... | collective-permute-start | bytes 24584 | tf_op jit(solution)/shard_map/ppermute | solution.py:918
  42.1 11.1 %copy-start.2 = (bf16[256,384]{1,0:T(8,128)(2,1)S(1)}, bf16[256,384]{1,0:T(8,128)(2,1)}, u32[]{:S(2)}) copy-start(bf16[256,384]{1,0:T(8,128)(2,1)} %constant.17.clone.table) | copy-start | bytes 589828

commit v7 on v6

--- a/solution.py
+++ b/solution.py
@@ -231,7 +231,7 @@
 
 
 def unpack_table():
-    table = np.zeros((2, 128, 3, 128), np.float32)
+    table = np.zeros((2, 128, 4, 128), np.float32)
     for x in range(2):
         for component in range(3):
             for column, slot in enumerate(SLOTS):
@@ -239,8 +239,14 @@
                     a, b, c = slot
                     row = stack_row(0, component, 3 * x + a, b)
                     table[x, component * 32 + column, c, row] = 1.0
-            table[x, 96 + component, 0, 54 + 2 * component + x] = 1.0
-    return table.reshape(256, 384).astype(jnp.bfloat16)
+                    if column < 5:
+                        table[x, 96 + 8 * component + column, 3, row] = 1.0
+                    if column == 0:
+                        table[x, 96 + 8 * component + TWIN, 3, row] = 1.0
+                    if 16 <= column < 20:
+                        table[x, component * 32 + column + 8, 3, row] = 1.0
+            table[x, 120 + component, 0, 54 + 2 * component + x] = 1.0
+    return table.reshape(256, 512).astype(jnp.bfloat16)
 
 
 def pick(values, table):
@@ -346,7 +352,9 @@
                 at = own_layers * k + layer
                 layers[x, at : at + 1, :] = arrived[device, row : row + 1, :]
     wide = pick(jnp.concatenate([layers[0], layers[1]], 1), table[...])
-    for c in range(3):
+    shares = pltpu.roll(wide[:, 384:512], own_layers, 0)
+    turned[pl.ds(0, 128, stride=3), :] = wide[:, 0:128] + shares
+    for c in range(1, 3):
         turned[pl.ds(c, 128, stride=3), :] = wide[:, 128 * c : 128 * c + 128]
     for part in range(3):
         span = slice(128 * part, 128 * part + 128)
@@ -532,6 +540,7 @@
                     totals[q].append(total)
             for pair, total in zip(pairs, totals):
                 finish(pair, total)
+        return carry
 
     def smooth(self, u, f, f_shift, d, stiff, spread, collect, spans, bound):
         for (first, count), (held, added) in zip(spans, chebyshev_steps()):
@@ -543,7 +552,13 @@
                     d[i, pair] = move
                     u[i, pair] = u[i, pair] + move
 
-            self.apply(u, stiff, spread, collect, first, count, finish)
+            rest = self.apply(u, stiff, spread, collect, first, count, finish)
+        owed = []
+        for low, high in rest:
+            low = jnp.where(self.even, low, 0.0) * self.keep[0:8]
+            high = jnp.where(self.even, high, 0.0) * self.keep[16:24]
+            owed.append((-(added / bound) * low, -(added / bound) * high))
+        return owed
 
     def coarse_next_z(self, v):
         return self.next_z(v, pltpu.roll(v, 7, 0))
@@ -748,9 +763,14 @@
     return first_kernel
 
 
+def shares_sent(own_layers):
+    return own_layers % 2 == 0
+
+
 def sources_of(own_layers):
-    whole = range(-3 // own_layers, (own_layers + 2) // own_layers + 1)
-    coarse = range(-5 // own_layers, (own_layers + 4) // own_layers + 1)
+    below = 2 if shares_sent(own_layers) else 3
+    whole = range(-below // own_layers, (own_layers + 2) // own_layers + 1)
+    coarse = range(-(below + 2) // own_layers, (own_layers + 4) // own_layers + 1)
     return list(whole), [n for n in coarse if n not in whole]
 
 
@@ -762,7 +782,7 @@
     steps = chebyshev_steps()
     spans = []
     for n in (3, 2, 1):
-        low, high = BEFORE_B - n, BEFORE_B + own_layers + n - 1
+        low, high = BEFORE_B - n + shares_sent(own_layers), BEFORE_B + own_layers + n - 1
         spans.append((low // 2, (high + 1) // 2 - low // 2))
 
     def second_kernel(*refs):
@@ -819,19 +839,21 @@
                     lift = lift + weights[n] * change[corner][pair : pair + 1]
                 u[i, pair] = lift
 
-        slab.smooth(u, f, shift, d, stiff, spread, collect, spans, fine_bound)
+        owed = slab.smooth(u, f, shift, d, stiff, spread, collect, spans, fine_bound)
 
         lower = lax.broadcasted_iota(jnp.int32, (width // 8, 8, 128), 1) < 4
+        nothing = jnp.zeros((8, width), jnp.float32)
         sides = []
-        blank = jnp.zeros((29, width), jnp.float32)
         for q in range(2):
-            ends_here = jnp.concatenate(
-                [u[i, own + q] for i in range(3)]
-                + [level[i][own + q : own + q + 1] for i in range(3)]
-                + [blank],
-                0,
-            )
-            sides.append(ends_here.T.reshape(width // 8, 8, 128))
+            if q or not shares_sent(own_layers):
+                owed = [(nothing, nothing)] * 3
+            rows = []
+            for i in range(3):
+                value = u[i, own + q]
+                rows += [value[0:24], jnp.where(slab.row < 4, owed[i][1], value[24:32])]
+            rows += [owed[i][0] for i in range(3)]
+            rows += [level[i][own + q : own + q + 1] for i in range(3)] + [nothing[0:5]]
+            sides.append(jnp.concatenate(rows, 0).T.reshape(width // 8, 8, 128))
         out[:, 0] = jnp.where(lower, sides[0], pltpu.roll(sides[1], 4, 1))
         out[:, 1] = jnp.where(lower, pltpu.roll(sides[0], 4, 1), sides[1])
 

time: 54.5 us -> 53 us (0.972)
  starting transfers between devices: 3.15 us -> 2.07 us
  blocking collectives: 27.3 us -> 26.5 us
  waiting for transfers between devices: 7.25 us -> 7.96 us
    ppermute x6 -> x5, starting transfers between devices: 3.15 us -> 2.07 us  [from_device(): return lax.ppermute(block, ('gx', 'gy'), route)]
    all_to_all x1, blocking collectives: 11.1 us -> 10.3 us  [body(): lax.all_to_all(result.reshape(devices, 8, 128), everyone, 0, 0, tiled=True)]
    ppermute x6 -> x5, waiting for transfers between devices: 7.25 us -> 7.96 us  [from_device(): return lax.ppermute(block, ('gx', 'gy'), route)]
  transfers between devices with their start and end apart: 6 -> 5, of which waited for: 4 -> 3; matrix products, arithmetic and copies ran while one was open for 0% -> 0% of each run, Pallas kernels for 0% -> 0%
where the time goes in v7:
time: 53 us; the launch traced here: 52.7 us
  blocking collectives  26.5 us (50%)
  Pallas kernels  15.5 us (29%)
  waiting for transfers between devices  7.96 us (15%)
  starting transfers between devices  2.07 us (4%)
  between operations  0.7 us (1%)
    all_to_all x1, blocking collectives, body(): lax.all_to_all(sent, everyone, 0, 0, tiled=True).reshape(devices * 12, 128)  16.2 us
    all_to_all x1, blocking collectives, body(): lax.all_to_all(result.reshape(devices, 8, 128), everyone, 0, 0, tiled=True)  10.3 us
    ppermute x5, waiting for transfers between devices, from_device(): return lax.ppermute(block, ('gx', 'gy'), route)  7.96 us
    pallas_call x1, Pallas kernels, body(): first(*[from_device(arrived, n) if n else arrived for n in near], jnp.asa...  6.71 us
    pallas_call x1, Pallas kernels, body(): second(*messages, *edges, load, jnp.asarray(spread), jnp.asarray(collect)...  5.38 us
    pallas_call x1, Pallas kernels, body(): pack(initial, forcing, modulus, solid_list, jnp.asarray(pack_table()))  2.36 us
    ppermute x5, starting transfers between devices, from_device(): return lax.ppermute(block, ('gx', 'gy'), route)  2.07 us
  transfers between devices with their start and end apart: 5, of which 3 were waited for; matrix products, arithmetic and copies ran while one was open for 0% of the time, Pallas kernels for 0%

profile of v7, /device:TPU:0, one launch (start us, length us, event | category | flops | bytes accessed | tf_op | source)
XLA Modules:
  0.0 52.7 jit_solution(14733395925541516217)
XLA Ops:
  0.6 2.4 %shard_map.113 = f32[384,128]{1,0:T(8,128)} custom-call(f32[3,6,3,384]{3,2,1,0:T(4,128)} %initial_at.1, f32[3,6,3,384]{3,2,1,0:T(4,128)} %forcing_at.1, f32[2,1,128]{2,1,0:T(1,128)} %modulus_at.1, s32[1,1,192]{2,1,0:T(1,128)} %listing_at.1, bf16[384,512]{1,0:T(8,128)(2,1)} %constant.12.clone.table_at), custom_call_target="tpu_custom_call" | custom-call | tf_op jit(solution)/shard_map/pallas_call | solution.py:943
  3.0 0.0 copy-start
  3.0 0.0 copy-start.1
  3.0 0.0 copy-start.4
  3.0 16.2 %all_to_all.10 = f32[32,3,4,128]{3,2,1,0:T(4,128)S(1)} all-to-all(f32[32,3,4,128]{3,2,1,0:T(4,128)} %bitcast.7), channel_id=1, replica_groups=mesh['gx'=4,'gy'=8] {'gy','gx'}, dimensions={0} | all-to-all | bytes 393216 | tf_op jit(solution)/shard_map/all_to_all | solution.py:945
  19.2 0.2 collective-permute-start.1
  19.5 0.4 collective-permute-start
  19.8 2.8 %collective-permute-done.1.refs_2_ = f32[384,128]{1,0:T(8,128)S(1)} collective-permute-done((f32[384,128]{1,0:T(8,128)S(1)}, f32[384,128]{1,0:T(8,128)S(1)}, u32[]{:S(2)}, u32[]{:S(2)}) %collective-permute-start.1) | collective-permute-done | bytes 196640 | tf_op jit(solution)/shard_map/ppermute | solution.py:940
  22.6 1.9 %collective-permute-done.refs_0_ = f32[384,128]{1,0:T(8,128)S(1)} collective-permute-done((f32[384,128]{1,0:T(8,128)S(1)}, f32[384,128]{1,0:T(8,128)S(1)}, u32[]{:S(2)}, u32[]{:S(2)}) %collective-permute-start) | collective-permute-done | bytes 196640 | tf_op jit(solution)/shard_map/ppermute | solution.py:940
  24.5 0.0 copy-done
  24.6 0.0 copy-done.1
  24.6 0.0 copy-done.4
  24.6 0.0 copy-start.3
  24.6 6.7 %shard_map.114 = (f32[3,2,32,128]{3,2,1,0:T(8,128)S(1)}, f32[2,8,128]{2,1,0:T(8,128)S(1)}, f32[3,6,32,128]{3,2,1,0:T(8,128)S(1)}) custom-call(f32[384,128]{1,0:T(8,128)S(1)} %collective-permute-done.refs_0_, f32[384,128]{1,0:T(8,128)S(1)} %bitcast.5, f32[384,128]{1,0:T(8,128)S(1)} %collective-permute-done.1.refs_2_, bf16[192,240]{1,0:T(8,128)(2,1)S(1)} %copy-done, ...), custom_call_target="tpu_custom_call" | custom-call | tf_op jit(solution)/shard_map/pallas_call | solution.py:946
  31.3 0.3 collective-permute-start.3
  31.6 0.2 collective-permute-start.2
  31.8 0.9 %collective-permute-start.4 = (f32[2,8,128]{2,1,0:T(8,128)S(1)}, f32[2,8,128]{2,1,0:T(8,128)S(1)}, u32[]{:S(2)}, u32[]{:S(2)}) collective-permute-start(f32[2,8,128]{2,1,0:T(8,128)S(1)} %get-tuple-element.6), channel_id=1, source_target_pairs={{2,0},{10,8},{4,2},{12,10},{6,4},{14,12},{22,6},{30,14},{20,22},{2... | collective-permute-start | bytes 24584 | tf_op jit(solution)/shard_map/ppermute | solution.py:940
  32.8 3.2 %collective-permute-done.4.refs_3_ = f32[2,8,128]{2,1,0:T(8,128)S(1)} collective-permute-done((f32[2,8,128]{2,1,0:T(8,128)S(1)}, f32[2,8,128]{2,1,0:T(8,128)S(1)}, u32[]{:S(2)}, u32[]{:S(2)}) %collective-permute-start.4) | collective-permute-done | bytes 8224 | tf_op jit(solution)/shard_map/ppermute | solution.py:940
  36.0 0.0 collective-permute-done.3.refs_2_
  36.0 0.0 collective-permute-done.2.refs_0_
  36.0 0.0 copy-done.3
  36.0 5.4 %shard_map.115 = f32[16,2,8,128]{3,2,1,0:T(8,128)S(1)} custom-call(f32[3,2,32,128]{3,2,1,0:T(8,128)S(1)} %collective-permute-done.2.refs_0_, f32[3,2,32,128]{3,2,1,0:T(8,128)S(1)} %get-tuple-element.5.refs_1_, f32[3,2,32,128]{3,2,1,0:T(8,128)S(1)} %collective-permute-done.3.refs_2_, f32[2,8,128]{2,1,0:T(8,128)S(1)} %collective-permute-done.4.refs_3_, ...), custom_call_target="tpu_custom_call" | custom-call | tf_op jit(solution)/shard_map/pallas_call | solution.py:954
  41.4 0.0 copy-start.2
  41.4 10.3 %all_to_all.11.arrived = f32[32,8,128]{2,1,0:T(8,128)S(1)} all-to-all(f32[32,8,128]{2,1,0:T(8,128)S(1)} %bitcast.6), channel_id=1, replica_groups=mesh['gx'=4,'gy'=8] {'gy','gx'}, dimensions={0} | all-to-all | bytes 262144 | tf_op jit(solution)/shard_map/all_to_all | solution.py:962
  51.7 0.0 copy-done.2
  51.7 1.0 %shard_map.116 = (f32[3,6,3,384]{3,2,1,0:T(4,128)}, f32[3,2,1,128]{3,2,1,0:T(1,128)}) custom-call(f32[32,8,128]{2,1,0:T(8,128)S(1)} %all_to_all.11.arrived, bf16[256,512]{1,0:T(8,128)(2,1)S(1)} %copy-done.2), custom_call_target="tpu_custom_call" | custom-call | tf_op jit(solution)/shard_map/pallas_call | solution.py:963
Async XLA Ops:
  3.0 21.5 %copy-start = (bf16[192,240]{1,0:T(8,128)(2,1)S(1)}, bf16[192,240]{1,0:T(8,128)(2,1)}, u32[]{:S(2)}) copy-start(bf16[192,240]{1,0:T(8,128)(2,1)} %constant.13.clone.refs_3_.refs_5_) | copy-start | bytes 276484
  3.0 21.5 %copy-start.1 = (bf16[144,192]{1,0:T(8,128)(2,1)S(1)}, bf16[144,192]{1,0:T(8,128)(2,1)}, u32[]{:S(2)}) copy-start(bf16[144,192]{1,0:T(8,128)(2,1)} %constant.14.clone.refs_4_.refs_6_) | copy-start | bytes 165892
  3.0 21.5 %copy-start.4 = (f32[32,8]{1,0:T(8,128)S(1)}, f32[32,8]{1,0:T(8,128)}, u32[]{:S(2)}) copy-start(f32[32,8]{1,0:T(8,128)} %constant.15.clone.refs_5_) | copy-start | bytes 3076
  19.2 3.4 %collective-permute-start.1 = (f32[384,128]{1,0:T(8,128)S(1)}, f32[384,128]{1,0:T(8,128)S(1)}, u32[]{:S(2)}, u32[]{:S(2)}) collective-permute-start(f32[384,128]{1,0:T(8,128)S(1)} %bitcast.3), channel_id=1, source_target_pairs={{8,0},{2,8},{10,2},{4,10},{12,4},{6,12},{14,6},{22,14},{30,22},{20... | collective-permute-start | bytes 589832 | tf_op jit(solution)/shard_map/ppermute | solution.py:940
  19.5 5.1 %collective-permute-start = (f32[384,128]{1,0:T(8,128)S(1)}, f32[384,128]{1,0:T(8,128)S(1)}, u32[]{:S(2)}, u32[]{:S(2)}) collective-permute-start(f32[384,128]{1,0:T(8,128)S(1)} %bitcast.4), channel_id=1, source_target_pairs={{9,0},{0,8},{8,2},{2,10},{10,4},{4,12},{12,6},{6,14},{14,22},{22,3... | collective-permute-start | bytes 589832 | tf_op jit(solution)/shard_map/ppermute | solution.py:940
  24.6 11.4 %copy-start.3 = (f32[32,8]{1,0:T(8,128)S(1)}, f32[32,8]{1,0:T(8,128)}, u32[]{:S(2)}) copy-start(f32[32,8]{1,0:T(8,128)} %constant.16.clone.refs_7_) | copy-start | bytes 3076
  31.3 4.7 %collective-permute-start.3 = (f32[3,2,32,128]{3,2,1,0:T(8,128)S(1)}, f32[3,2,32,128]{3,2,1,0:T(8,128)S(1)}, u32[]{:S(2)}, u32[]{:S(2)}) collective-permute-start(f32[3,2,32,128]{3,2,1,0:T(8,128)S(1)} %get-tuple-element.5.refs_1_), channel_id=1, source_target_pairs={{8,0},{2,8},{10,2},{4,10},{12,4},{6,12},{14,6},{22,14},{30,22},{20... | collective-permute-start | bytes 294920 | tf_op jit(solution)/shard_map/ppermute | solution.py:940
  31.6 4.4 %collective-permute-start.2 = (f32[3,2,32,128]{3,2,1,0:T(8,128)S(1)}, f32[3,2,32,128]{3,2,1,0:T(8,128)S(1)}, u32[]{:S(2)}, u32[]{:S(2)}) collective-permute-start(f32[3,2,32,128]{3,2,1,0:T(8,128)S(1)} %get-tuple-element.5.refs_1_), channel_id=1, source_target_pairs={{9,0},{0,8},{8,2},{2,10},{10,4},{4,12},{12,6},{6,14},{14,22},{22,3... | collective-permute-start | bytes 294920 | tf_op jit(solution)/shard_map/ppermute | solution.py:940
  31.8 4.2 %collective-permute-start.4 = (f32[2,8,128]{2,1,0:T(8,128)S(1)}, f32[2,8,128]{2,1,0:T(8,128)S(1)}, u32[]{:S(2)}, u32[]{:S(2)}) collective-permute-start(f32[2,8,128]{2,1,0:T(8,128)S(1)} %get-tuple-element.6), channel_id=1, source_target_pairs={{2,0},{10,8},{4,2},{12,10},{6,4},{14,12},{22,6},{30,14},{20,22},{2... | collective-permute-start | bytes 24584 | tf_op jit(solution)/shard_map/ppermute | solution.py:940
  41.4 10.3 %copy-start.2 = (bf16[256,512]{1,0:T(8,128)(2,1)S(1)}, bf16[256,512]{1,0:T(8,128)(2,1)}, u32[]{:S(2)}) copy-start(bf16[256,512]{1,0:T(8,128)(2,1)} %constant.17.clone.table) | copy-start | bytes 786436

commit v8 on v7

--- a/solution.py
+++ b/solution.py
@@ -414,6 +414,23 @@
     return high, (values - high.astype(jnp.float32)).astype(jnp.bfloat16)
 
 
+def reads(pairs):
+    return set(range(pairs[0], pairs[-1] + 2))
+
+
+def plan_steps(spans):
+    plan = []
+    for first, count in spans:
+        pairs = list(range(first, first + count))
+        plan.append([pairs[n : n + 2] for n in range(0, count, 2)])
+    for now, later in zip(plan, plan[1:]):
+        if reads(later[0]) & set(now[-1]) and len(now[-1]) == 2:
+            now[-1:] = [now[-1][:1], now[-1][1:]]
+        if reads(later[0]) & set(now[-1]) and len(later[0]) == 2:
+            later[:1] = [later[0][:1], later[0][1:]]
+    return plan
+
+
 class Slab:
     def __init__(self, width, across):
         self.width = width
@@ -430,40 +447,41 @@
     def lanes(self, v, step):
         return pltpu.roll(v, step % self.width, 1)
 
-    def next_x(self, v):
-        return jnp.where(self.top, 0.0, self.lanes(v, -2))
-
-    def next_y(self, v):
-        return self.lanes(v, -self.y_step)
-
-    def next_z(self, v, ahead):
-        return jnp.where(self.even, self.lanes(v, -1), self.lanes(ahead, 1))
-
-    def onto_x(self, v):
-        return jnp.where(self.bottom, 0.0, self.lanes(v, 2))
-
-    def onto_y(self, v):
-        return self.lanes(v, self.y_step)
+    def from_next(self, v, x, y):
+        if x or y:
+            v = self.lanes(v, -2 * x - self.y_step * y)
+        return jnp.where(self.top, 0.0, v) if x else v
+
+    def from_next_z(self, v, ahead, x, y):
+        step = -2 * x - self.y_step * y
+        v = jnp.where(self.even, self.lanes(v, step - 1), self.lanes(ahead, step + 1))
+        return jnp.where(self.top, 0.0, v) if x else v
+
+    def onto_next(self, v, x, y, z=0):
+        if x or y or z:
+            v = self.lanes(v, 2 * x + self.y_step * y + z)
+        return jnp.where(self.bottom, 0.0, v) if x else v
 
     def gather(self, here, ahead):
         row = self.row
         g0, g1, g2, g3 = here[0:8], here[8:16], here[16:24], here[24:32]
-        z0 = self.next_z(g0, ahead[0:8])
-        z2 = self.next_z(g2, ahead[16:24])
-        y0 = self.next_y(g0)
-        yz, xz, xy = self.next_y(z0), self.next_x(z0), self.next_x(y0)
-        edges = jnp.where(row <= 2, yz, jnp.where(row <= 4, xz, xy))
+        a0 = ahead[0:8]
+        z0, xz = self.from_next_z(g0, a0, 0, 0), self.from_next_z(g0, a0, 1, 0)
+        yz, xyz = self.from_next_z(g0, a0, 0, 1), self.from_next_z(g0, a0, 1, 1)
+        z2 = self.from_next_z(g2, ahead[16:24], 0, 0)
+        edges = jnp.where(row <= 4, xz, self.from_next(g0, 1, 1))
+        edges = jnp.where(row == 0, xyz, jnp.where(row <= 2, yz, edges))
         return jnp.concatenate(
             [
                 g0,
                 g1,
                 g2,
                 jnp.where(row < 4, z2, g3),
-                self.next_x(g0),
-                jnp.where(row == 7, yz, y0),
+                self.from_next(g0, 1, 0),
+                jnp.where(row == 7, yz, self.from_next(g0, 0, 1)),
                 jnp.where(row == 7, xz, z0),
-                jnp.where(row < 4, self.next_x(g1), self.next_y(g1)),
-                jnp.where(row == 0, self.next_x(yz), edges),
+                jnp.where(row < 4, self.from_next(g1, 1, 0), self.from_next(g1, 0, 1)),
+                edges,
                 jnp.zeros_like(g0),
             ],
             0,
@@ -472,22 +490,31 @@
     def scatter(self, part, behind):
         row = self.row
         g0, g1, g2, g3, x0, y0, z0, sides, edges = (part[8 * n : 8 * n + 8] for n in range(9))
-        edges_x = self.onto_x(edges)
-        yz = jnp.where(row == 0, edges_x, jnp.where(row == 7, y0, edges))
-        yz = jnp.where((row <= 2) | (row == 7), yz, 0.0)
-        z0 = jnp.where(row == 7, self.onto_x(z0), z0)
-        z0 = z0 + jnp.where((row == 3) | (row == 4), edges_x, 0.0) + self.onto_y(yz)
-        y0 = jnp.where(row == 7, edges_x, y0 + jnp.where(row >= 5, edges_x, 0.0))
-        z2 = g3
-        own0 = g0 + self.onto_x(x0) + self.onto_y(y0)
-        own0 = own0 + jnp.where(self.even, behind[0], self.lanes(z0, 1))
-        own1 = g1 + jnp.where(row < 4, self.onto_x(sides), self.onto_y(sides))
-        share2 = jnp.where(self.even, behind[1], self.lanes(z2, 1))
+        last = row == 7
+        for_z = jnp.where(last, 0.0, z0)
+        for_xz = jnp.where(last, z0, jnp.where((row == 3) | (row == 4), edges, 0.0))
+        for_yz = jnp.where(last, y0, jnp.where((row == 1) | (row == 2), edges, 0.0))
+        for_xyz = jnp.where(row == 0, edges, 0.0)
+        for_xy = jnp.where(row >= 5, edges, 0.0)
+
+        def above(z):
+            return (
+                self.onto_next(for_z, 0, 0, z)
+                + self.onto_next(for_yz, 0, 1, z)
+                + self.onto_next(for_xz, 1, 0, z)
+                + self.onto_next(for_xyz, 1, 1, z)
+            )
+
+        own0 = g0 + self.onto_next(x0, 1, 0) + self.onto_next(jnp.where(last, 0.0, y0), 0, 1)
+        own0 = own0 + self.onto_next(for_xy, 1, 1)
+        own0 = own0 + jnp.where(self.even, behind[0], above(1))
+        own1 = g1 + jnp.where(row < 4, self.onto_next(sides, 1, 0), self.onto_next(sides, 0, 1))
+        share2 = jnp.where(self.even, behind[1], self.onto_next(g3, 0, 0, 1))
         own2 = g2 + jnp.where(row < 4, share2, 0.0)
         own3 = jnp.where(row < 4, 0.0, g3)
-        own0 = own0 + jnp.where(row == 0, pltpu.roll(own0, 1, 0), 0.0)
-        own0 = jnp.where(row == 7, pltpu.roll(own0, 7, 0), own0)
-        moved = (self.lanes(z0, -1), self.lanes(z2, -1))
+        twins = jnp.where(last, pltpu.roll(own0, 7, 0), 0.0)
+        own0 = own0 + jnp.where(row == 0, pltpu.roll(own0, 1, 0), twins)
+        moved = (above(-1), self.onto_next(g3, 0, 0, -1))
         return jnp.concatenate([own0, own1, own2, own3], 0), moved
 
     def gradient(self, u, spread, pairs):
@@ -520,29 +547,33 @@
             force[ROWS:] + jnp.dot(collect[0:ROWS], low, preferred_element_type=jnp.float32)
         )
 
-    def apply(self, u, stiff, spread, collect, first, count, finish):
-        width = self.width
-        none = jnp.zeros((8, width), jnp.float32)
-        carry = [(none, none) for i in range(3)]
-        last = first + count
-        steps = [list(range(at, min(at + 2, last))) for at in range(first, last, 2)]
-        ahead = self.gradient(u, spread, steps[0])
-        for n, pairs in enumerate(steps):
-            gradient = ahead
-            if n + 1 < len(steps):
-                ahead = self.gradient(u, spread, steps[n + 1])
+    def run(self, u, stiff, spread, collect, jobs):
+        plan = plan_steps([job[:2] for job in jobs])
+        steps = [(pairs, n) for n, chunks in enumerate(plan) for pairs in chunks]
+        none = jnp.zeros((8, self.width), jnp.float32)
+        ahead, carry, job = None, None, None
+        for at, (pairs, n) in enumerate(steps):
+            gradient = self.gradient(u, spread, pairs) if ahead is None else ahead
+            ahead = None
+            if at + 1 < len(steps):
+                later, later_job = steps[at + 1]
+                if later_job == n or not reads(later) & set(pairs):
+                    ahead = self.gradient(u, spread, later)
+            if job != n:
+                carry, job = [(none, none) for i in range(3)], n
             force = self.force(gradient, stiff, collect, pairs)
             totals = [[] for pair in pairs]
             for q in range(len(pairs)):
                 for i in range(3):
-                    at = (len(pairs) * i + q) * width
-                    total, carry[i] = self.scatter(force[:, at : at + width], carry[i])
+                    lane = (len(pairs) * i + q) * self.width
+                    total, carry[i] = self.scatter(force[:, lane : lane + self.width], carry[i])
                     totals[q].append(total)
             for pair, total in zip(pairs, totals):
-                finish(pair, total)
+                jobs[n][2](pair, total)
         return carry
 
-    def smooth(self, u, f, f_shift, d, stiff, spread, collect, spans, bound):
+    def smoothing(self, u, f, f_shift, d, spans, bound):
+        jobs = []
         for (first, count), (held, added) in zip(spans, chebyshev_steps()):
 
             def finish(pair, forces, held=held, added=added):
@@ -552,37 +583,36 @@
                     d[i, pair] = move
                     u[i, pair] = u[i, pair] + move
 
-            rest = self.apply(u, stiff, spread, collect, first, count, finish)
-        owed = []
-        for low, high in rest:
-            low = jnp.where(self.even, low, 0.0) * self.keep[0:8]
-            high = jnp.where(self.even, high, 0.0) * self.keep[16:24]
-            owed.append((-(added / bound) * low, -(added / bound) * high))
-        return owed
-
-    def coarse_next_z(self, v):
-        return self.next_z(v, pltpu.roll(v, 7, 0))
-
-    def coarse_onto_z(self, v):
-        return jnp.where(self.even, pltpu.roll(self.lanes(v, -1), 1, 0), self.lanes(v, 1))
+            jobs.append((first, count, finish))
+        return jobs
+
+    def owed(self, carry, bound):
+        scale = -chebyshev_steps()[-1][1] / bound
+        return [
+            (
+                scale * jnp.where(self.even, low, 0.0) * self.keep[0:8],
+                scale * jnp.where(self.even, high, 0.0) * self.keep[16:24],
+            )
+            for low, high in carry
+        ]
 
     def corners_of(self, v):
-        found = {(0, 0, 0): v, (0, 0, 1): self.coarse_next_z(v)}
-        for c in range(2):
-            found[0, 1, c] = self.next_y(found[0, 0, c])
-        for b in range(2):
-            for c in range(2):
-                found[1, b, c] = self.next_x(found[0, b, c])
+        ahead = pltpu.roll(v, 7, 0)
+        found = {}
+        for a in range(2):
+            for b in range(2):
+                found[a, b, 0] = self.from_next(v, a, b)
+                found[a, b, 1] = self.from_next_z(v, ahead, a, b)
         return found
 
     def assemble(self, part):
-        line = {
-            (a, b): part[a, b, 0] + self.coarse_onto_z(part[a, b, 1])
-            for a in range(2)
-            for b in range(2)
-        }
-        face = [line[a, 0] + self.onto_y(line[a, 1]) for a in range(2)]
-        return face[0] + self.onto_x(face[1])
+        here, odd, even = 0.0, 0.0, 0.0
+        for a in range(2):
+            for b in range(2):
+                here = here + self.onto_next(part[a, b, 0], a, b)
+                odd = odd + self.onto_next(part[a, b, 1], a, b, 1)
+                even = even + self.onto_next(part[a, b, 1], a, b, -1)
+        return here + jnp.where(self.even, pltpu.roll(even, 1, 0), odd)
 
     def coarse_force(self, values, stiffness):
         grads = []
@@ -730,8 +760,6 @@
                     whole = jnp.concatenate(parts, 0)
                     target[i, pair] = whole * slab.keep if field == 0 else whole
 
-        slab.smooth(u, f, 0, d, stiff, spread, collect, spans[0:3], fine_bound)
-
         weights = [jnp.broadcast_to(transfer[:, n : n + 1], (32, width)) for n in range(8)]
 
         def restrict(pair, forces):
@@ -742,7 +770,8 @@
                     part = (part[0:8] + part[8:16]) + (part[16:24] + part[24:32])
                     shares[i, n, pl.ds(pair, 1), :] = jnp.sum(part, axis=0, keepdims=True)
 
-        slab.apply(u, stiff, spread, collect, *spans[3], restrict)
+        jobs = slab.smoothing(u, f, 0, d, spans[0:3], fine_bound)
+        slab.run(u, stiff, spread, collect, jobs + [(*spans[3], restrict)])
 
         restricted = [
             slab.assemble({corner: shares[i, n] for n, corner in enumerate(CORNERS)})
@@ -839,7 +868,8 @@
                     lift = lift + weights[n] * change[corner][pair : pair + 1]
                 u[i, pair] = lift
 
-        owed = slab.smooth(u, f, shift, d, stiff, spread, collect, spans, fine_bound)
+        jobs = slab.smoothing(u, f, shift, d, spans, fine_bound)
+        owed = slab.owed(slab.run(u, stiff, spread, collect, jobs), fine_bound)
 
         lower = lax.broadcasted_iota(jnp.int32, (width // 8, 8, 128), 1) < 4
         nothing = jnp.zeros((8, width), jnp.float32)

time: 53 us -> 50.8 us (0.958)
  Pallas kernels: 15.5 us -> 13.3 us
    pallas_call x1, Pallas kernels: 6.71 us -> 5.52 us  [body(): first(*[from_device(arrived, n) if n else arrived for n in near], jnp.asa...]
    pallas_call x1, Pallas kernels: 5.38 us -> 4.41 us  [body(): second(*messages, *edges, load, jnp.asarray(spread), jnp.asarray(collect)...]
where the time goes in v8:
time: 50.8 us; the launch traced here: 50.6 us
  blocking collectives  26.4 us (52%)
  Pallas kernels  13.3 us (26%)
  waiting for transfers between devices  8 us (16%)
  starting transfers between devices  2.06 us (4%)
  between operations  0.7 us (1%)
    all_to_all x1, blocking collectives, body(): lax.all_to_all(sent, everyone, 0, 0, tiled=True).reshape(devices * 12, 128)  16.2 us
    all_to_all x1, blocking collectives, body(): lax.all_to_all(result.reshape(devices, 8, 128), everyone, 0, 0, tiled=True)  10.2 us
    ppermute x5, waiting for transfers between devices, from_device(): return lax.ppermute(block, ('gx', 'gy'), route)  8 us
    pallas_call x1, Pallas kernels, body(): first(*[from_device(arrived, n) if n else arrived for n in near], jnp.asa...  5.52 us
    pallas_call x1, Pallas kernels, body(): second(*messages, *edges, load, jnp.asarray(spread), jnp.asarray(collect)...  4.41 us
    pallas_call x1, Pallas kernels, body(): pack(initial, forcing, modulus, solid_list, jnp.asarray(pack_table()))  2.36 us
    ppermute x5, starting transfers between devices, from_device(): return lax.ppermute(block, ('gx', 'gy'), route)  2.06 us
    pallas_call x1, Pallas kernels, body(): return unpack(back, jnp.asarray(unpack_table()))  1.02 us
  transfers between devices with their start and end apart: 5, of which 3 were waited for; matrix products, arithmetic and copies ran while one was open for 0% of the time, Pallas kernels for 0%

profile of v8, /device:TPU:0, one launch (start us, length us, event | category | flops | bytes accessed | tf_op | source)
XLA Modules:
  0.0 50.6 jit_solution(131936104776482609)
XLA Ops:
  0.6 2.4 %shard_map.113 = f32[384,128]{1,0:T(8,128)} custom-call(f32[3,6,3,384]{3,2,1,0:T(4,128)} %initial_at.1, f32[3,6,3,384]{3,2,1,0:T(4,128)} %forcing_at.1, f32[2,1,128]{2,1,0:T(1,128)} %modulus_at.1, s32[1,1,192]{2,1,0:T(1,128)} %listing_at.1, bf16[384,512]{1,0:T(8,128)(2,1)} %constant.12.clone.table_at), custom_call_target="tpu_custom_call" | custom-call | tf_op jit(solution)/shard_map/pallas_call | solution.py:973
  3.0 0.0 copy-start
  3.0 0.0 copy-start.1
  3.0 0.0 copy-start.4
  3.0 16.2 %all_to_all.10 = f32[32,3,4,128]{3,2,1,0:T(4,128)S(1)} all-to-all(f32[32,3,4,128]{3,2,1,0:T(4,128)} %bitcast.7), channel_id=1, replica_groups=mesh['gx'=4,'gy'=8] {'gy','gx'}, dimensions={0} | all-to-all | bytes 393216 | tf_op jit(solution)/shard_map/all_to_all | solution.py:975
  19.2 0.2 collective-permute-start.1
  19.5 0.4 collective-permute-start
  19.8 2.8 %collective-permute-done.1.refs_2_ = f32[384,128]{1,0:T(8,128)S(1)} collective-permute-done((f32[384,128]{1,0:T(8,128)S(1)}, f32[384,128]{1,0:T(8,128)S(1)}, u32[]{:S(2)}, u32[]{:S(2)}) %collective-permute-start.1) | collective-permute-done | bytes 196640 | tf_op jit(solution)/shard_map/ppermute | solution.py:970
  22.6 1.9 %collective-permute-done.refs_0_ = f32[384,128]{1,0:T(8,128)S(1)} collective-permute-done((f32[384,128]{1,0:T(8,128)S(1)}, f32[384,128]{1,0:T(8,128)S(1)}, u32[]{:S(2)}, u32[]{:S(2)}) %collective-permute-start) | collective-permute-done | bytes 196640 | tf_op jit(solution)/shard_map/ppermute | solution.py:970
  24.5 0.0 copy-done
  24.6 0.0 copy-done.1
  24.6 0.0 copy-done.4
  24.6 0.0 copy-start.3
  24.6 5.5 %shard_map.114 = (f32[3,2,32,128]{3,2,1,0:T(8,128)S(1)}, f32[2,8,128]{2,1,0:T(8,128)S(1)}, f32[3,6,32,128]{3,2,1,0:T(8,128)S(1)}) custom-call(f32[384,128]{1,0:T(8,128)S(1)} %collective-permute-done.refs_0_, f32[384,128]{1,0:T(8,128)S(1)} %bitcast.5, f32[384,128]{1,0:T(8,128)S(1)} %collective-permute-done.1.refs_2_, bf16[192,240]{1,0:T(8,128)(2,1)S(1)} %copy-done, ...), custom_call_target="tpu_custom_call" | custom-call | tf_op jit(solution)/shard_map/pallas_call | solution.py:976
  30.1 0.4 collective-permute-start.3
  30.5 0.2 collective-permute-start.2
  30.7 0.9 %collective-permute-start.4 = (f32[2,8,128]{2,1,0:T(8,128)S(1)}, f32[2,8,128]{2,1,0:T(8,128)S(1)}, u32[]{:S(2)}, u32[]{:S(2)}) collective-permute-start(f32[2,8,128]{2,1,0:T(8,128)S(1)} %get-tuple-element.6), channel_id=1, source_target_pairs={{2,0},{10,8},{4,2},{12,10},{6,4},{14,12},{22,6},{30,14},{20,22},{2... | collective-permute-start | bytes 24584 | tf_op jit(solution)/shard_map/ppermute | solution.py:970
  31.6 3.3 %collective-permute-done.4.refs_3_ = f32[2,8,128]{2,1,0:T(8,128)S(1)} collective-permute-done((f32[2,8,128]{2,1,0:T(8,128)S(1)}, f32[2,8,128]{2,1,0:T(8,128)S(1)}, u32[]{:S(2)}, u32[]{:S(2)}) %collective-permute-start.4) | collective-permute-done | bytes 8224 | tf_op jit(solution)/shard_map/ppermute | solution.py:970
  34.8 0.0 collective-permute-done.3.refs_2_
  34.8 0.0 collective-permute-done.2.refs_0_
  34.9 0.0 copy-done.3
  34.9 4.4 %shard_map.115 = f32[16,2,8,128]{3,2,1,0:T(8,128)S(1)} custom-call(f32[3,2,32,128]{3,2,1,0:T(8,128)S(1)} %collective-permute-done.2.refs_0_, f32[3,2,32,128]{3,2,1,0:T(8,128)S(1)} %get-tuple-element.5.refs_1_, f32[3,2,32,128]{3,2,1,0:T(8,128)S(1)} %collective-permute-done.3.refs_2_, f32[2,8,128]{2,1,0:T(8,128)S(1)} %collective-permute-done.4.refs_3_, ...), custom_call_target="tpu_custom_call" | custom-call | tf_op jit(solution)/shard_map/pallas_call | solution.py:984
  39.3 0.0 copy-start.2
  39.3 10.2 %all_to_all.11.arrived = f32[32,8,128]{2,1,0:T(8,128)S(1)} all-to-all(f32[32,8,128]{2,1,0:T(8,128)S(1)} %bitcast.6), channel_id=1, replica_groups=mesh['gx'=4,'gy'=8] {'gy','gx'}, dimensions={0} | all-to-all | bytes 262144 | tf_op jit(solution)/shard_map/all_to_all | solution.py:992
  49.5 0.0 copy-done.2
  49.5 1.0 %shard_map.116 = (f32[3,6,3,384]{3,2,1,0:T(4,128)}, f32[3,2,1,128]{3,2,1,0:T(1,128)}) custom-call(f32[32,8,128]{2,1,0:T(8,128)S(1)} %all_to_all.11.arrived, bf16[256,512]{1,0:T(8,128)(2,1)S(1)} %copy-done.2), custom_call_target="tpu_custom_call" | custom-call | tf_op jit(solution)/shard_map/pallas_call | solution.py:993
Async XLA Ops:
  3.0 21.5 %copy-start = (bf16[192,240]{1,0:T(8,128)(2,1)S(1)}, bf16[192,240]{1,0:T(8,128)(2,1)}, u32[]{:S(2)}) copy-start(bf16[192,240]{1,0:T(8,128)(2,1)} %constant.13.clone.refs_3_.refs_5_) | copy-start | bytes 276484
  3.0 21.5 %copy-start.1 = (bf16[144,192]{1,0:T(8,128)(2,1)S(1)}, bf16[144,192]{1,0:T(8,128)(2,1)}, u32[]{:S(2)}) copy-start(bf16[144,192]{1,0:T(8,128)(2,1)} %constant.14.clone.refs_4_.refs_6_) | copy-start | bytes 165892
  3.0 21.5 %copy-start.4 = (f32[32,8]{1,0:T(8,128)S(1)}, f32[32,8]{1,0:T(8,128)}, u32[]{:S(2)}) copy-start(f32[32,8]{1,0:T(8,128)} %constant.15.clone.refs_5_) | copy-start | bytes 3076
  19.2 3.4 %collective-permute-start.1 = (f32[384,128]{1,0:T(8,128)S(1)}, f32[384,128]{1,0:T(8,128)S(1)}, u32[]{:S(2)}, u32[]{:S(2)}) collective-permute-start(f32[384,128]{1,0:T(8,128)S(1)} %bitcast.3), channel_id=1, source_target_pairs={{8,0},{2,8},{10,2},{4,10},{12,4},{6,12},{14,6},{22,14},{30,22},{20... | collective-permute-start | bytes 589832 | tf_op jit(solution)/shard_map/ppermute | solution.py:970
  19.5 5.1 %collective-permute-start = (f32[384,128]{1,0:T(8,128)S(1)}, f32[384,128]{1,0:T(8,128)S(1)}, u32[]{:S(2)}, u32[]{:S(2)}) collective-permute-start(f32[384,128]{1,0:T(8,128)S(1)} %bitcast.4), channel_id=1, source_target_pairs={{9,0},{0,8},{8,2},{2,10},{10,4},{4,12},{12,6},{6,14},{14,22},{22,3... | collective-permute-start | bytes 589832 | tf_op jit(solution)/shard_map/ppermute | solution.py:970
  24.6 10.3 %copy-start.3 = (f32[32,8]{1,0:T(8,128)S(1)}, f32[32,8]{1,0:T(8,128)}, u32[]{:S(2)}) copy-start(f32[32,8]{1,0:T(8,128)} %constant.16.clone.refs_7_) | copy-start | bytes 3076
  30.1 4.8 %collective-permute-start.3 = (f32[3,2,32,128]{3,2,1,0:T(8,128)S(1)}, f32[3,2,32,128]{3,2,1,0:T(8,128)S(1)}, u32[]{:S(2)}, u32[]{:S(2)}) collective-permute-start(f32[3,2,32,128]{3,2,1,0:T(8,128)S(1)} %get-tuple-element.5.refs_1_), channel_id=1, source_target_pairs={{8,0},{2,8},{10,2},{4,10},{12,4},{6,12},{14,6},{22,14},{30,22},{20... | collective-permute-start | bytes 294920 | tf_op jit(solution)/shard_map/ppermute | solution.py:970
  30.5 4.4 %collective-permute-start.2 = (f32[3,2,32,128]{3,2,1,0:T(8,128)S(1)}, f32[3,2,32,128]{3,2,1,0:T(8,128)S(1)}, u32[]{:S(2)}, u32[]{:S(2)}) collective-permute-start(f32[3,2,32,128]{3,2,1,0:T(8,128)S(1)} %get-tuple-element.5.refs_1_), channel_id=1, source_target_pairs={{9,0},{0,8},{8,2},{2,10},{10,4},{4,12},{12,6},{6,14},{14,22},{22,3... | collective-permute-start | bytes 294920 | tf_op jit(solution)/shard_map/ppermute | solution.py:970
  30.7 4.2 %collective-permute-start.4 = (f32[2,8,128]{2,1,0:T(8,128)S(1)}, f32[2,8,128]{2,1,0:T(8,128)S(1)}, u32[]{:S(2)}, u32[]{:S(2)}) collective-permute-start(f32[2,8,128]{2,1,0:T(8,128)S(1)} %get-tuple-element.6), channel_id=1, source_target_pairs={{2,0},{10,8},{4,2},{12,10},{6,4},{14,12},{22,6},{30,14},{20,22},{2... | collective-permute-start | bytes 24584 | tf_op jit(solution)/shard_map/ppermute | solution.py:970
  39.3 10.3 %copy-start.2 = (bf16[256,512]{1,0:T(8,128)(2,1)S(1)}, bf16[256,512]{1,0:T(8,128)(2,1)}, u32[]{:S(2)}) copy-start(bf16[256,512]{1,0:T(8,128)(2,1)} %constant.17.clone.table) | copy-start | bytes 786436

commit v9 on v8

--- a/solution.py
+++ b/solution.py
@@ -36,6 +36,8 @@
     None, None, None, None, (2, 1, 1), (2, 1, 2), (2, 2, 1), (2, 2, 2),
 ]
 TWIN = 7
+NEXT_SLOTS = [0, 1, 2, 3, 4, 5, 6, 7, 16, 17, 18, 19]
+NEXT_COLUMN = 4 * BLOCK
 RESTRICTED_SLOT = 24
 STIFF_SLOT = 25
 OWN_SHIFT, SHIFT_X, SHIFT_Y, SHIFT_Z = (0, 0, 0), (1, 0, 0), (0, 1, 0), (0, 0, 1)
@@ -226,6 +228,9 @@
                         a, b, c = slot
                         row = stack_row(field, component, 3 * x + a, b)
                         table[c, row, field, x, block_column(component, column)] = 1.0
+                        if field == 0 and column in NEXT_SLOTS:
+                            at = BLOCK + 12 * component + NEXT_SLOTS.index(column)
+                            table[c, row, 1, x, at] = 1.0
             table[0, 108 + x, 0, x, TWIN] = 1.0
     return table.reshape(384, 512).astype(jnp.bfloat16)
 
@@ -327,6 +332,9 @@
                     tiles[tile] = moved
                 else:
                     tiles[tile] = jnp.where(lane >= first - 128 * tile, moved, before)
+        above = wide[:, 128 * (2 + x) : 128 * (2 + x) + 128]
+        above = pltpu.roll(pltpu.roll(above, 128 - own_layers, 0), (NEXT_COLUMN - BLOCK) % 128, 1)
+        tiles[-1] = jnp.where(lane >= NEXT_COLUMN % 128, above, tiles[-1])
         for tile in range(SENT // 128):
             places[3 * x + tile, 0:128, :] = tiles[tile]
             places[3 * x + tile, 128:136, :] = jnp.zeros((8, 128), jnp.float32)
@@ -512,10 +520,19 @@
         share2 = jnp.where(self.even, behind[1], self.onto_next(g3, 0, 0, 1))
         own2 = g2 + jnp.where(row < 4, share2, 0.0)
         own3 = jnp.where(row < 4, 0.0, g3)
-        twins = jnp.where(last, pltpu.roll(own0, 7, 0), 0.0)
-        own0 = own0 + jnp.where(row == 0, pltpu.roll(own0, 1, 0), twins)
         moved = (above(-1), self.onto_next(g3, 0, 0, -1))
-        return jnp.concatenate([own0, own1, own2, own3], 0), moved
+        return jnp.concatenate([self.twinned(own0), own1, own2, own3], 0), moved
+
+    def twinned(self, v):
+        twins = jnp.where(self.row == 7, pltpu.roll(v, 7, 0), 0.0)
+        return v + jnp.where(self.row == 0, pltpu.roll(v, 1, 0), twins)
+
+    def absorb(self, total, behind):
+        low = self.twinned(jnp.where(self.even, behind[0], 0.0))
+        high = jnp.where(self.even & (self.row < 4), behind[1], 0.0)
+        return jnp.concatenate(
+            [total[0:8] + low, total[8:16], total[16:24] + high, total[24:32]], 0
+        )
 
     def gradient(self, u, spread, pairs):
         blocks = [self.gather(u[i, pair], u[i, pair + 1]) for i in range(3) for pair in pairs]
@@ -547,20 +564,34 @@
             force[ROWS:] + jnp.dot(collect[0:ROWS], low, preferred_element_type=jnp.float32)
         )
 
-    def run(self, u, stiff, spread, collect, jobs):
+    def run(self, u, stiff, spread, collect, jobs, given=None):
         plan = plan_steps([job[:2] for job in jobs])
         steps = [(pairs, n) for n, chunks in enumerate(plan) for pairs in chunks]
         none = jnp.zeros((8, self.width), jnp.float32)
         ahead, carry, job = None, None, None
         for at, (pairs, n) in enumerate(steps):
-            gradient = self.gradient(u, spread, pairs) if ahead is None else ahead
-            ahead = None
-            if at + 1 < len(steps):
+            ready = given is not None and n == 0 and pairs == given[0]
+            gradient = ahead
+            if ahead is None and not ready:
+                gradient = self.gradient(u, spread, pairs)
+            if not ready:
+                ahead = None
+            if ahead is None and at + 1 < len(steps):
                 later, later_job = steps[at + 1]
+                if given is not None and later_job == 0 and later == given[0]:
+                    later, later_job = steps[at + 2]
                 if later_job == n or not reads(later) & set(pairs):
                     ahead = self.gradient(u, spread, later)
             if job != n:
                 carry, job = [(none, none) for i in range(3)], n
+            if ready:
+                for q, pair in enumerate(pairs):
+                    total = given[1][q]
+                    if q == 0:
+                        total = [self.absorb(total[i], carry[i]) for i in range(3)]
+                    jobs[n][2](pair, total)
+                carry = list(given[2])
+                continue
             force = self.force(gradient, stiff, collect, pairs)
             totals = [[] for pair in pairs]
             for q in range(len(pairs)):
@@ -711,6 +742,67 @@
     return list(range(-BEFORE // own_layers, (own_layers + BEFORE - 1) // own_layers + 1))
 
 
+def turn_rows(block, mixed, turned, width, at):
+    for tile in range(SENT // 128):
+        n = at * (SENT // 128) + tile
+        for m in range(width // 4):
+            first = 12 * m + 4 * tile
+            mixed[n, 4 * m : 4 * m + 4, :] = block[first : first + 4, :]
+        turned[at, 128 * tile : 128 * tile + 128, :] = mixed[n].T
+
+
+def regroup(slab, field, rows):
+    values, hard = [], None
+    for i in range(3):
+        parts = [rows(24 * i + 8 * n) for n in range(3)]
+        if field == 0 and i == 0:
+            hard = parts[0][TWIN : TWIN + 1]
+        parts[0] = jnp.where(slab.row == TWIN, pltpu.roll(parts[0], TWIN, 0), parts[0])
+        parts.append(jnp.where(slab.row < 4, 0.0, rows(68 + 4 * i)))
+        whole = jnp.concatenate(parts, 0)
+        values.append(whole * slab.keep if field == 0 else whole)
+    return values, hard
+
+
+def make_own_kernel(width, across, own_layers):
+    own_pairs = own_layers // 2
+    pairs = list(range(own_pairs))
+
+    def own_kernel(block, spread, collect, u, f, stiff, forces, moved, mixed, turned):
+        slab = Slab(width, across)
+        turn_rows(block, mixed, turned, width, 0)
+        for pair in pairs:
+            for field, target in enumerate((u, f)):
+
+                def rows(start, field=field, pair=pair):
+                    at = BLOCK * (2 * pair + field) + start
+                    return turned[0, at : at + 8, :]
+
+                values, hard = regroup(slab, field, rows)
+                for i in range(3):
+                    target[i, pair] = values[i]
+                if field == 0:
+                    stiff[pair : pair + 1, :] = hard
+        for i in range(3):
+            low = turned[0, NEXT_COLUMN + 12 * i : NEXT_COLUMN + 12 * i + 8, :]
+            high = turned[0, NEXT_COLUMN + 12 * i + 4 : NEXT_COLUMN + 12 * i + 12, :]
+            high = jnp.where(slab.row < 4, pltpu.roll(high, 4, 0), 0.0)
+            low = jnp.where(slab.row == TWIN, pltpu.roll(low, TWIN, 0), low)
+            nothing = jnp.zeros((8, width), jnp.float32)
+            u[i, own_pairs] = jnp.concatenate([low, nothing, high, nothing], 0) * slab.keep
+
+        def finish(pair, total):
+            for i in range(3):
+                forces[i, pair] = total[i]
+
+        carry = slab.run(u, stiff, spread, collect, [(0, own_pairs, finish)])
+        for i in range(3):
+            moved[i, 0] = carry[i][0]
+            moved[i, 1] = carry[i][1]
+
+    return own_kernel
+
+
 def make_first_kernel(width, across, own_layers, fine_bound):
     own = BEFORE // 2
     own_pairs = (own_layers + 1) // 2
@@ -718,47 +810,55 @@
     for n in (4, 3, 2, 1):
         low, high = BEFORE - n, BEFORE + own_layers + n - 1
         spans.append((low // 2, (high + 1) // 2 - low // 2))
-
-    sources = first_sources(own_layers)
+    prepared = own_layers == 4
+    sources = [n for n in first_sources(own_layers) if n or not prepared]
 
     def first_kernel(*refs):
         arrived = refs[: len(sources)]
         refs = refs[len(sources) :]
+        if prepared:
+            own_u, own_f, own_stiff, own_forces, own_moved = refs[:5]
+            refs = refs[5:]
         spread, collect, transfer, message, edge, f, u, d, stiff, shares, mixed, turned = refs
         slab = Slab(width, across)
-        row = slab.row
         u[...] = jnp.zeros(u.shape, jnp.float32)
-        f[...] = jnp.zeros(f.shape, jnp.float32)
+        if not prepared:
+            f[...] = jnp.zeros(f.shape, jnp.float32)
         shares[...] = jnp.zeros(shares.shape, jnp.float32)
         stiff[...] = jnp.zeros(stiff.shape, jnp.float32)
         for n in range(len(sources)):
-            for tile in range(SENT // 128):
-                at = n * (SENT // 128) + tile
-                for m in range(width // 4):
-                    first = 12 * m + 4 * tile
-                    mixed[at, 4 * m : 4 * m + 4, :] = arrived[n][first : first + 4, :]
-                turned[n, 128 * tile : 128 * tile + 128, :] = mixed[at].T
-        for field, target in enumerate((u, f)):
-            for pair in range(PAIRS):
+            turn_rows(arrived[n], mixed, turned, width, n)
+        for pair in range(PAIRS):
+            if prepared and own <= pair < own + own_pairs:
+                for i in range(3):
+                    u[i, pair] = own_u[i, pair - own]
+                    f[i, pair] = own_f[i, pair - own]
+                stiff[pair : pair + 1, :] = own_stiff[pair - own : pair - own + 1, :]
+                continue
+            for field, target in enumerate((u, f)):
 
                 def rows(start, field=field, pair=pair):
                     def fetch(device, q):
                         if device not in sources:
                             return None
                         at = BLOCK * (2 * q + field) + start
-                        return turned[device - sources[0], at : at + 8, :]
+                        return turned[sources.index(device), at : at + 8, :]
 
                     value = window_pair(slab, 2 * pair - BEFORE, own_layers, fetch)
                     return jnp.zeros((8, width), jnp.float32) if value is None else value
 
+                values, hard = regroup(slab, field, rows)
                 for i in range(3):
-                    parts = [rows(24 * i + 8 * n) for n in range(3)]
-                    if field == 0 and i == 0:
-                        stiff[pair : pair + 1, :] = parts[0][TWIN : TWIN + 1]
-                    parts[0] = jnp.where(row == TWIN, pltpu.roll(parts[0], TWIN, 0), parts[0])
-                    parts.append(jnp.where(row < 4, 0.0, rows(68 + 4 * i)))
-                    whole = jnp.concatenate(parts, 0)
-                    target[i, pair] = whole * slab.keep if field == 0 else whole
+                    target[i, pair] = values[i]
+                if field == 0:
+                    stiff[pair : pair + 1, :] = hard
+        given = None
+        if prepared:
+            given = (
+                list(range(own, own + own_pairs)),
+                [[own_forces[i, q] for i in range(3)] for q in range(own_pairs)],
+                [(own_moved[i, 0], own_moved[i, 1]) for i in range(3)],
+            )
 
         weights = [jnp.broadcast_to(transfer[:, n : n + 1], (32, width)) for n in range(8)]
 
@@ -771,7 +871,7 @@
                     shares[i, n, pl.ds(pair, 1), :] = jnp.sum(part, axis=0, keepdims=True)
 
         jobs = slab.smoothing(u, f, 0, d, spans[0:3], fine_bound)
-        slab.run(u, stiff, spread, collect, jobs + [(*spans[3], restrict)])
+        slab.run(u, stiff, spread, collect, jobs + [(*spans[3], restrict)], given)
 
         restricted = [
             slab.assemble({corner: shares[i, n] for n, corner in enumerate(CORNERS)})
@@ -899,6 +999,7 @@
     width = 4 * devices
     across = 2 * rows_of
     near = first_sources(own_layers)
+    prepared = own_layers == 4
     whole, outer = sources_of(own_layers)
     spread, collect, fine_bound = element_tables()
     coarse_bound = build_tables([0.0, 1.0], 2)[2]
@@ -925,6 +1026,22 @@
         ],
         compiler_params=wide,
     )
+    own = pl.pallas_call(
+        make_own_kernel(width, across, own_layers),
+        out_shape=(
+            jax.ShapeDtypeStruct((3, own_pairs + 1, 32, width), f32),
+            jax.ShapeDtypeStruct((3, own_pairs, 32, width), f32),
+            jax.ShapeDtypeStruct((own_pairs, width), f32),
+            jax.ShapeDtypeStruct((3, own_pairs, 32, width), f32),
+            jax.ShapeDtypeStruct((3, 2, 8, width), f32),
+        ),
+        scratch_shapes=[
+            pltpu.VMEM((SENT // 128, width, 128), f32),
+            pltpu.VMEM((1, SENT, width), f32),
+        ],
+        compiler_params=limit,
+        cost_estimate=pl.CostEstimate(flops=400_000_000, bytes_accessed=1_000_000, transcendentals=0),
+    )
     first = pl.pallas_call(
         make_first_kernel(width, across, own_layers, fine_bound),
         out_shape=(
@@ -973,8 +1090,12 @@
         sent = pack(initial, forcing, modulus, solid_list, jnp.asarray(pack_table()))
         sent = sent.reshape(devices, SENT // 128, 4, 128)
         arrived = lax.all_to_all(sent, everyone, 0, 0, tiled=True).reshape(devices * 12, 128)
+        blocks = [from_device(arrived, n) if n else arrived for n in near]
+        if prepared:
+            blocks = [block for n, block in zip(near, blocks) if n]
+            blocks += own(arrived, jnp.asarray(spread), jnp.asarray(collect))
         message, edge, load = first(
-            *[from_device(arrived, n) if n else arrived for n in near],
+            *blocks,
             jnp.asarray(spread),
             jnp.asarray(collect),
             jnp.asarray(transfer),

time: 50.8 us -> 50.6 us (level)
  waiting for transfers between devices: 8 us -> 6.93 us
  Pallas kernels: 13.3 us -> 14.1 us
    ppermute x5, waiting for transfers between devices: 8 us -> 6.93 us  [from_device(): return lax.ppermute(block, ('gx', 'gy'), route)]
    pallas_call x1 -> x2, Pallas kernels: 5.52 us -> 6.25 us  [the longest x1 5.22 us: body(): first(*blocks, jnp.asarray(spread), jnp.asarray(collect), jnp.asarray(tra...]
  transfers between devices with their start and end apart: 5 -> 5, of which waited for: 3 -> 3; matrix products, arithmetic and copies ran while one was open for 0% -> 0% of each run, Pallas kernels for 0% -> 2%
where the time goes in v9:
time: 50.6 us; the launch traced here: 50.4 us
  blocking collectives  26.5 us (52%)
  Pallas kernels  14.1 us (28%)
  waiting for transfers between devices  6.93 us (14%)
  starting transfers between devices  2.08 us (4%)
  between operations  0.7 us (1%)
    all_to_all x1, blocking collectives, body(): lax.all_to_all(sent, everyone, 0, 0, tiled=True).reshape(devices * 12, 128)  16.2 us
    all_to_all x1, blocking collectives, body(): lax.all_to_all(result.reshape(devices, 8, 128), everyone, 0, 0, tiled=True)  10.3 us
    ppermute x5, waiting for transfers between devices, from_device(): return lax.ppermute(block, ('gx', 'gy'), route)  6.93 us
    pallas_call x1, Pallas kernels, body(): first(*blocks, jnp.asarray(spread), jnp.asarray(collect), jnp.asarray(tra...  5.22 us
    pallas_call x1, Pallas kernels, body(): second(*messages, *edges, load, jnp.asarray(spread), jnp.asarray(collect)...  4.46 us
    pallas_call x1, Pallas kernels, body(): pack(initial, forcing, modulus, solid_list, jnp.asarray(pack_table()))  2.42 us
    ppermute x5, starting transfers between devices, from_device(): return lax.ppermute(block, ('gx', 'gy'), route)  2.08 us
    pallas_call x1, Pallas kernels, body(): blocks += own(arrived, jnp.asarray(spread), jnp.asarray(collect))  1.03 us
  transfers between devices with their start and end apart: 5, of which 3 were waited for; matrix products, arithmetic and copies ran while one was open for 0% of the time, Pallas kernels for 2%

profile of v9, /device:TPU:0, one launch (start us, length us, event | category | flops | bytes accessed | tf_op | source)
XLA Modules:
  0.0 50.4 jit_solution(2768077873715254083)
XLA Ops:
  0.6 2.4 %shard_map.113 = f32[384,128]{1,0:T(8,128)} custom-call(f32[3,6,3,384]{3,2,1,0:T(4,128)} %initial_at.1, f32[3,6,3,384]{3,2,1,0:T(4,128)} %forcing_at.1, f32[2,1,128]{2,1,0:T(1,128)} %modulus_at.1, s32[1,1,192]{2,1,0:T(1,128)} %listing_at.1, bf16[384,512]{1,0:T(8,128)(2,1)} %constant.12.clone.table_at), custom_call_target="tpu_custom_call" | custom-call | tf_op jit(solution)/shard_map/pallas_call | solution.py:1090
  3.1 0.0 copy-start
  3.1 0.0 copy-start.1
  3.1 16.2 %all_to_all.10 = f32[32,3,4,128]{3,2,1,0:T(4,128)S(1)} all-to-all(f32[32,3,4,128]{3,2,1,0:T(4,128)} %bitcast.7), channel_id=1, replica_groups=mesh['gx'=4,'gy'=8] {'gy','gx'}, dimensions={0} | all-to-all | bytes 393216 | tf_op jit(solution)/shard_map/all_to_all | solution.py:1092
  19.3 0.2 collective-permute-start.1
  19.5 0.4 collective-permute-start
  19.9 0.0 copy-done
  19.9 0.0 copy-done.1
  19.9 0.0 copy-start.4
  19.9 1.0 %shard_map.114 = (f32[3,3,32,128]{3,2,1,0:T(8,128)S(1)}, f32[3,2,32,128]{3,2,1,0:T(8,128)S(1)}, f32[2,128]{1,0:T(2,128)S(1)}, f32[3,2,32,128]{3,2,1,0:T(8,128)S(1)}, f32[3,2,8,128]{3,2,1,0:T(8,128)S(1)}) custom-call(f32[384,128]{1,0:T(8,128)S(1)} %bitcast.6, bf16[192,240]{1,0:T(8,128)(2,1)S(1)} %copy-done, bf16[144,192]{1,0:T(8,128)(2,1)S(1)} %copy-done.1), custom_call_target="tpu_custom_call" | custom-call | flops 400000000 | bytes 1000000 | tf_op jit(solution)/shard_map/pallas_call | solution.py:1096
  20.9 1.8 %collective-permute-done.1.refs_1_ = f32[384,128]{1,0:T(8,128)S(1)} collective-permute-done((f32[384,128]{1,0:T(8,128)S(1)}, f32[384,128]{1,0:T(8,128)S(1)}, u32[]{:S(2)}, u32[]{:S(2)}) %collective-permute-start.1) | collective-permute-done | bytes 196640 | tf_op jit(solution)/shard_map/ppermute | solution.py:1087
  22.7 1.9 %collective-permute-done.refs_0_ = f32[384,128]{1,0:T(8,128)S(1)} collective-permute-done((f32[384,128]{1,0:T(8,128)S(1)}, f32[384,128]{1,0:T(8,128)S(1)}, u32[]{:S(2)}, u32[]{:S(2)}) %collective-permute-start) | collective-permute-done | bytes 196640 | tf_op jit(solution)/shard_map/ppermute | solution.py:1087
  24.6 0.0 copy-done.4
  24.6 0.0 copy-start.3
  24.6 5.2 %shard_map.115 = (f32[3,2,32,128]{3,2,1,0:T(8,128)S(1)}, f32[2,8,128]{2,1,0:T(8,128)S(1)}, f32[3,6,32,128]{3,2,1,0:T(8,128)S(1)}) custom-call(f32[384,128]{1,0:T(8,128)S(1)} %collective-permute-done.refs_0_, f32[384,128]{1,0:T(8,128)S(1)} %collective-permute-done.1.refs_1_, f32[3,3,32,128]{3,2,1,0:T(8,128)S(1)} %get-tuple-element.10.refs_2_, ...), custom_call_target="tpu_custom_call" | custom-call | tf_op jit(solution)/shard_map/pallas_call | solution.py:1097
  29.8 0.3 collective-permute-start.3
  30.2 0.2 collective-permute-start.2
  30.4 0.9 %collective-permute-start.4 = (f32[2,8,128]{2,1,0:T(8,128)S(1)}, f32[2,8,128]{2,1,0:T(8,128)S(1)}, u32[]{:S(2)}, u32[]{:S(2)}) collective-permute-start(f32[2,8,128]{2,1,0:T(8,128)S(1)} %get-tuple-element.16), channel_id=1, source_target_pairs={{2,0},{10,8},{4,2},{12,10},{6,4},{14,12},{22,6},{30,14},{20,22},{2... | collective-permute-start | bytes 24584 | tf_op jit(solution)/shard_map/ppermute | solution.py:1087
  31.3 3.3 %collective-permute-done.4.refs_3_ = f32[2,8,128]{2,1,0:T(8,128)S(1)} collective-permute-done((f32[2,8,128]{2,1,0:T(8,128)S(1)}, f32[2,8,128]{2,1,0:T(8,128)S(1)}, u32[]{:S(2)}, u32[]{:S(2)}) %collective-permute-start.4) | collective-permute-done | bytes 8224 | tf_op jit(solution)/shard_map/ppermute | solution.py:1087
  34.6 0.0 collective-permute-done.3.refs_2_
  34.6 0.0 collective-permute-done.2.refs_0_
  34.6 0.0 copy-done.3
  34.6 4.5 %shard_map.116 = f32[16,2,8,128]{3,2,1,0:T(8,128)S(1)} custom-call(f32[3,2,32,128]{3,2,1,0:T(8,128)S(1)} %collective-permute-done.2.refs_0_, f32[3,2,32,128]{3,2,1,0:T(8,128)S(1)} %get-tuple-element.15.refs_1_, f32[3,2,32,128]{3,2,1,0:T(8,128)S(1)} %collective-permute-done.3.refs_2_, f32[2,8,128]{2,1,0:T(8,128)S(1)} %collective-permute-done.4.refs_3_, ...), custom_call_target="tpu_custom_call" | custom-call | tf_op jit(solution)/shard_map/pallas_call | solution.py:1105
  39.1 0.0 copy-start.2
  39.1 10.3 %all_to_all.11.arrived = f32[32,8,128]{2,1,0:T(8,128)S(1)} all-to-all(f32[32,8,128]{2,1,0:T(8,128)S(1)} %bitcast.3), channel_id=1, replica_groups=mesh['gx'=4,'gy'=8] {'gy','gx'}, dimensions={0} | all-to-all | bytes 262144 | tf_op jit(solution)/shard_map/all_to_all | solution.py:1113
  49.4 0.0 copy-done.2
  49.4 1.0 %shard_map.117 = (f32[3,6,3,384]{3,2,1,0:T(4,128)}, f32[3,2,1,128]{3,2,1,0:T(1,128)}) custom-call(f32[32,8,128]{2,1,0:T(8,128)S(1)} %all_to_all.11.arrived, bf16[256,512]{1,0:T(8,128)(2,1)S(1)} %copy-done.2), custom_call_target="tpu_custom_call" | custom-call | tf_op jit(solution)/shard_map/pallas_call | solution.py:1114
Async XLA Ops:
  3.1 16.8 %copy-start = (bf16[192,240]{1,0:T(8,128)(2,1)S(1)}, bf16[192,240]{1,0:T(8,128)(2,1)}, u32[]{:S(2)}) copy-start(bf16[192,240]{1,0:T(8,128)(2,1)} %constant.13.clone.spread.refs_7_.refs_5_) | copy-start | bytes 276484
  3.1 16.8 %copy-start.1 = (bf16[144,192]{1,0:T(8,128)(2,1)S(1)}, bf16[144,192]{1,0:T(8,128)(2,1)}, u32[]{:S(2)}) copy-start(bf16[144,192]{1,0:T(8,128)(2,1)} %constant.14.clone.collect.refs_8_.refs_6_) | copy-start | bytes 165892
  19.3 3.4 %collective-permute-start.1 = (f32[384,128]{1,0:T(8,128)S(1)}, f32[384,128]{1,0:T(8,128)S(1)}, u32[]{:S(2)}, u32[]{:S(2)}) collective-permute-start(f32[384,128]{1,0:T(8,128)S(1)} %bitcast.4), channel_id=1, source_target_pairs={{8,0},{2,8},{10,2},{4,10},{12,4},{6,12},{14,6},{22,14},{30,22},{20... | collective-permute-start | bytes 589832 | tf_op jit(solution)/shard_map/ppermute | solution.py:1087
  19.5 5.1 %collective-permute-start = (f32[384,128]{1,0:T(8,128)S(1)}, f32[384,128]{1,0:T(8,128)S(1)}, u32[]{:S(2)}, u32[]{:S(2)}) collective-permute-start(f32[384,128]{1,0:T(8,128)S(1)} %bitcast.5), channel_id=1, source_target_pairs={{9,0},{0,8},{8,2},{2,10},{10,4},{4,12},{12,6},{6,14},{14,22},{22,3... | collective-permute-start | bytes 589832 | tf_op jit(solution)/shard_map/ppermute | solution.py:1087
  19.9 4.7 %copy-start.4 = (f32[32,8]{1,0:T(8,128)S(1)}, f32[32,8]{1,0:T(8,128)}, u32[]{:S(2)}) copy-start(f32[32,8]{1,0:T(8,128)} %constant.15.clone.refs_9_) | copy-start | bytes 3076
  24.6 10.0 %copy-start.3 = (f32[32,8]{1,0:T(8,128)S(1)}, f32[32,8]{1,0:T(8,128)}, u32[]{:S(2)}) copy-start(f32[32,8]{1,0:T(8,128)} %constant.16.clone.refs_7_) | copy-start | bytes 3076
  29.8 4.8 %collective-permute-start.3 = (f32[3,2,32,128]{3,2,1,0:T(8,128)S(1)}, f32[3,2,32,128]{3,2,1,0:T(8,128)S(1)}, u32[]{:S(2)}, u32[]{:S(2)}) collective-permute-start(f32[3,2,32,128]{3,2,1,0:T(8,128)S(1)} %get-tuple-element.15.refs_1_), channel_id=1, source_target_pairs={{8,0},{2,8},{10,2},{4,10},{12,4},{6,12},{14,6},{22,14},{30,22},{20... | collective-permute-start | bytes 294920 | tf_op jit(solution)/shard_map/ppermute | solution.py:1087
  30.2 4.4 %collective-permute-start.2 = (f32[3,2,32,128]{3,2,1,0:T(8,128)S(1)}, f32[3,2,32,128]{3,2,1,0:T(8,128)S(1)}, u32[]{:S(2)}, u32[]{:S(2)}) collective-permute-start(f32[3,2,32,128]{3,2,1,0:T(8,128)S(1)} %get-tuple-element.15.refs_1_), channel_id=1, source_target_pairs={{9,0},{0,8},{8,2},{2,10},{10,4},{4,12},{12,6},{6,14},{14,22},{22,3... | collective-permute-start | bytes 294920 | tf_op jit(solution)/shard_map/ppermute | solution.py:1087
  30.4 4.2 %collective-permute-start.4 = (f32[2,8,128]{2,1,0:T(8,128)S(1)}, f32[2,8,128]{2,1,0:T(8,128)S(1)}, u32[]{:S(2)}, u32[]{:S(2)}) collective-permute-start(f32[2,8,128]{2,1,0:T(8,128)S(1)} %get-tuple-element.16), channel_id=1, source_target_pairs={{2,0},{10,8},{4,2},{12,10},{6,4},{14,12},{22,6},{30,14},{20,22},{2... | collective-permute-start | bytes 24584 | tf_op jit(solution)/shard_map/ppermute | solution.py:1087
  39.1 10.3 %copy-start.2 = (bf16[256,512]{1,0:T(8,128)(2,1)S(1)}, bf16[256,512]{1,0:T(8,128)(2,1)}, u32[]{:S(2)}) copy-start(bf16[256,512]{1,0:T(8,128)(2,1)} %constant.17.clone.table) | copy-start | bytes 786436

commit v10 on v9

--- a/solution.py
+++ b/solution.py
@@ -742,6 +742,10 @@
     return list(range(-BEFORE // own_layers, (own_layers + BEFORE - 1) // own_layers + 1))
 
 
+def whole_pairs(own_layers):
+    return own_layers == 4
+
+
 def turn_rows(block, mixed, turned, width, at):
     for tile in range(SENT // 128):
         n = at * (SENT // 128) + tile
@@ -764,6 +768,15 @@
     return values, hard
 
 
+def layer_above(slab, turned, at, i):
+    first = NEXT_COLUMN + 12 * i
+    low, high = turned[at, first : first + 8, :], turned[at, first + 4 : first + 12, :]
+    high = jnp.where(slab.row < 4, pltpu.roll(high, 4, 0), 0.0)
+    low = jnp.where(slab.row == TWIN, pltpu.roll(low, TWIN, 0), low)
+    nothing = jnp.zeros_like(low)
+    return jnp.concatenate([low, nothing, high, nothing], 0) * slab.keep
+
+
 def make_own_kernel(width, across, own_layers):
     own_pairs = own_layers // 2
     pairs = list(range(own_pairs))
@@ -784,12 +797,7 @@
                 if field == 0:
                     stiff[pair : pair + 1, :] = hard
         for i in range(3):
-            low = turned[0, NEXT_COLUMN + 12 * i : NEXT_COLUMN + 12 * i + 8, :]
-            high = turned[0, NEXT_COLUMN + 12 * i + 4 : NEXT_COLUMN + 12 * i + 12, :]
-            high = jnp.where(slab.row < 4, pltpu.roll(high, 4, 0), 0.0)
-            low = jnp.where(slab.row == TWIN, pltpu.roll(low, TWIN, 0), low)
-            nothing = jnp.zeros((8, width), jnp.float32)
-            u[i, own_pairs] = jnp.concatenate([low, nothing, high, nothing], 0) * slab.keep
+            u[i, own_pairs] = layer_above(slab, turned, 0, i)
 
         def finish(pair, total):
             for i in range(3):
@@ -807,10 +815,10 @@
     own = BEFORE // 2
     own_pairs = (own_layers + 1) // 2
     spans = []
+    prepared = whole_pairs(own_layers)
     for n in (4, 3, 2, 1):
-        low, high = BEFORE - n, BEFORE + own_layers + n - 1
+        low, high = BEFORE - n, BEFORE + own_layers + n - 1 + prepared
         spans.append((low // 2, (high + 1) // 2 - low // 2))
-    prepared = own_layers == 4
     sources = [n for n in first_sources(own_layers) if n or not prepared]
 
     def first_kernel(*refs):
@@ -819,7 +827,7 @@
         if prepared:
             own_u, own_f, own_stiff, own_forces, own_moved = refs[:5]
             refs = refs[5:]
-        spread, collect, transfer, message, edge, f, u, d, stiff, shares, mixed, turned = refs
+        spread, collect, transfer, message, *sent, f, u, d, stiff, shares, mixed, turned = refs
         slab = Slab(width, across)
         u[...] = jnp.zeros(u.shape, jnp.float32)
         if not prepared:
@@ -854,6 +862,8 @@
                     stiff[pair : pair + 1, :] = hard
         given = None
         if prepared:
+            for i in range(3):
+                u[i, PAIRS] = layer_above(slab, turned, sources.index(1), i)
             given = (
                 list(range(own, own + own_pairs)),
                 [[own_forces[i, q] for i in range(3)] for q in range(own_pairs)],
@@ -877,17 +887,40 @@
             slab.assemble({corner: shares[i, n] for n, corner in enumerate(CORNERS)})
             for i in range(3)
         ]
+        def line(rows, q):
+            return rows[own + q : own + q + 1]
+
         for q in range(own_pairs):
-            hard = stiff[own + q : own + q + 1, :]
             for i in range(3):
                 message[i, q] = u[i, own + q]
-                message[i, q, RESTRICTED_SLOT : RESTRICTED_SLOT + 1, :] = restricted[i][
-                    own + q : own + q + 1
-                ]
+                message[i, q, RESTRICTED_SLOT : RESTRICTED_SLOT + 1, :] = line(restricted[i], q)
+            message[0, q, STIFF_SLOT : STIFF_SLOT + 1, :] = line(stiff, q)
+        if prepared:
+            down, up = sent
+            for i in range(3):
+                down[i, 0:32] = u[i, own]
+                down[i, 32:40] = u[i, own + 1, 0:8, :]
+                down[i, 40:48] = u[i, own + 1, 16:24, :]
+                up[i] = u[i, own + 1]
+                for n, row in enumerate(
+                    (line(restricted[i], 0), line(restricted[i], 1), u[i, own + 2, 0:1, :])
+                    + (line(restricted[i], 2),)
+                ):
+                    down[i, 24 + n : 25 + n, :] = row
+                for n, row in enumerate(
+                    (line(restricted[i], 1), line(restricted[i], 0), u[i, own, 0:1, :])
+                ):
+                    up[i, 24 + n : 25 + n, :] = row
+            for q in range(own_pairs):
+                down[q, 32 + TWIN : 33 + TWIN, :] = line(stiff, q)
+                up[q, TWIN : TWIN + 1, :] = line(stiff, q)
+            return
+        edge = sent[0]
+        for q in range(own_pairs):
+            for i in range(3):
                 edge[q, i : i + 1, :] = u[i, own + q, 0:1, :]
-                edge[q, 3 + i : 4 + i, :] = restricted[i][own + q : own + q + 1]
-            message[0, q, STIFF_SLOT : STIFF_SLOT + 1, :] = hard
-            edge[q, 6:8, :] = jnp.broadcast_to(hard, (2, width))
+                edge[q, 3 + i : 4 + i, :] = line(restricted[i], q)
+            edge[q, 6:8, :] = jnp.broadcast_to(line(stiff, q), (2, width))
 
     return first_kernel
 
@@ -901,6 +934,48 @@
     whole = range(-below // own_layers, (own_layers + 2) // own_layers + 1)
     coarse = range(-(below + 2) // own_layers, (own_layers + 4) // own_layers + 1)
     return list(whole), [n for n in coarse if n not in whole]
+
+
+def message_line(message, q, n):
+    i, slot = ((n, 0), (n - 3, RESTRICTED_SLOT), (0, STIFF_SLOT))[n // 3]
+    return message[i, q, slot : slot + 1, :]
+
+
+def sent_readers(slab, up, message, down):
+    def block_of(device, q, i):
+        if device == 0:
+            return message[i, q]
+        if (device, q) == (1, 0):
+            whole = down[i, 0:32]
+        elif (device, q) == (1, 1):
+            low, high = down[i, 32:40], down[i, 40:48]
+            low = jnp.where(slab.row == TWIN, pltpu.roll(low, TWIN, 0), low)
+            whole = jnp.concatenate([low, jnp.zeros_like(low), high, jnp.zeros_like(low)], 0)
+        elif (device, q) == (-1, 1):
+            low = up[i, 0:8]
+            low = jnp.where(slab.row == TWIN, pltpu.roll(low, TWIN, 0), low)
+            whole = jnp.concatenate([low, up[i, 8:32]], 0)
+        else:
+            return None
+        return whole
+
+    def line_of(device, q, n):
+        if device == 0:
+            return message_line(message, q, n)
+        kind, i = n // 3, n % 3
+        if device == 1:
+            row = ((0, 24), (32, 25))[q][kind] if kind < 2 else 32 + TWIN
+            i = i if kind < 2 else q
+            return down[i, row : row + 1, :]
+        if device == -1:
+            row = ((26, 25), (0, 24))[q][kind] if kind < 2 else TWIN
+            i = i if kind < 2 else q
+            return up[i, row : row + 1, :]
+        if (device, q) == (2, 0) and kind < 2:
+            return down[i, 26 + kind : 27 + kind, :]
+        return None
+
+    return block_of, line_of
 
 
 def make_second_kernel(width, across, own_layers, fine_bound, coarse_bound):
@@ -915,11 +990,25 @@
         spans.append((low // 2, (high + 1) // 2 - low // 2))
 
     def second_kernel(*refs):
-        messages = dict(zip(whole, refs))
-        refs = refs[len(whole) :]
-        edges = dict(zip(outer, refs))
-        f, spread, collect, transfer_back, out, u, d, stiff, coarse = refs[len(outer) :]
         slab = Slab(width, across)
+        if whole_pairs(own_layers):
+            up, message, down = refs[:3]
+            refs = refs[3:]
+            block_of, line_of = sent_readers(slab, up, message, down)
+        else:
+            messages = dict(zip(whole, refs))
+            edges = dict(zip(outer, refs[len(whole) :]))
+            refs = refs[len(whole) + len(outer) :]
+
+            def block_of(device, q, i):
+                return messages[device][i, q] if device in messages else None
+
+            def line_of(device, q, n):
+                if device in messages:
+                    return message_line(messages[device], q, n)
+                return edges[device][q, n : n + 1, :] if device in edges else None
+
+        f, spread, collect, transfer_back, out, u, d, stiff, coarse = refs
 
         def pair_of(pair, fetch):
             return window_pair(slab, 2 * pair - BEFORE_B, own_layers, fetch)
@@ -929,18 +1018,11 @@
         d[...] = jnp.zeros(d.shape, jnp.float32)
         for pair in range(PAIRS_B):
             for i in range(3):
-                block = pair_of(pair, lambda n, q: messages[n][i, q] if n in messages else None)
+                block = pair_of(pair, lambda device, q: block_of(device, q, i))
                 if block is not None:
                     u[i, pair] = block
             for n in range(7):
-
-                def fetch(device, q, n=n):
-                    if device in messages:
-                        i, slot = ((n, 0), (n - 3, RESTRICTED_SLOT), (0, STIFF_SLOT))[n // 3]
-                        return messages[device][i, q, slot : slot + 1, :]
-                    return edges[device][q, n : n + 1, :] if device in edges else None
-
-                line = pair_of(pair, fetch)
+                line = pair_of(pair, lambda device, q: line_of(device, q, n))
                 if line is not None:
                     coarse[n, pair : pair + 1, :] = line
         stiff[...] = coarse[6]
@@ -999,7 +1081,7 @@
     width = 4 * devices
     across = 2 * rows_of
     near = first_sources(own_layers)
-    prepared = own_layers == 4
+    prepared = whole_pairs(own_layers)
     whole, outer = sources_of(own_layers)
     spread, collect, fine_bound = element_tables()
     coarse_bound = build_tables([0.0, 1.0], 2)[2]
@@ -1042,11 +1124,14 @@
         compiler_params=limit,
         cost_estimate=pl.CostEstimate(flops=400_000_000, bytes_accessed=1_000_000, transcendentals=0),
     )
+    sent = [jax.ShapeDtypeStruct((own_pairs, 8, width), f32)]
+    if prepared:
+        sent = [jax.ShapeDtypeStruct((3, rows, width), f32) for rows in (48, 32)]
     first = pl.pallas_call(
         make_first_kernel(width, across, own_layers, fine_bound),
         out_shape=(
             jax.ShapeDtypeStruct((3, own_pairs, 32, width), f32),
-            jax.ShapeDtypeStruct((own_pairs, 8, width), f32),
+            *sent,
             jax.ShapeDtypeStruct((3, PAIRS, 32, width), f32),
         ),
         scratch_shapes=[
@@ -1094,17 +1179,20 @@
         if prepared:
             blocks = [block for n, block in zip(near, blocks) if n]
             blocks += own(arrived, jnp.asarray(spread), jnp.asarray(collect))
-        message, edge, load = first(
+        message, *edges, load = first(
             *blocks,
             jnp.asarray(spread),
             jnp.asarray(collect),
             jnp.asarray(transfer),
         )
-        messages = [from_device(message, n) if n else message for n in whole]
-        edges = [from_device(edge, n) for n in outer]
+        if prepared:
+            down, up = edges
+            messages = [from_device(up, -1), message, from_device(down, 1)]
+        else:
+            messages = [from_device(message, n) if n else message for n in whole]
+            messages += [from_device(edges[0], n) for n in outer]
         result = second(
             *messages,
-            *edges,
             load,
             jnp.asarray(spread),
             jnp.asarray(collect),

time: 50.6 us -> 50.4 us (level)
  starting transfers between devices: 2.08 us -> 1.16 us
    ppermute x5 -> x4, starting transfers between devices: 2.08 us -> 1.16 us  [from_device(): return lax.ppermute(block, ('gx', 'gy'), route)]
    ppermute x5 -> x4, waiting for transfers between devices: 6.93 us -> 6.98 us  [from_device(): return lax.ppermute(block, ('gx', 'gy'), route)]
  transfers between devices with their start and end apart: 5 -> 4, of which waited for: 3 -> 3; matrix products, arithmetic and copies ran while one was open for 0% -> 0% of each run, Pallas kernels for 2% -> 2%
where the time goes in v10:
time: 50.4 us; the launch traced here: 50.2 us
  blocking collectives  26.8 us (53%)
  Pallas kernels  14.5 us (29%)
  waiting for transfers between devices  6.98 us (14%)
  starting transfers between devices  1.16 us (2%)
  between operations  0.69 us (1%)
    all_to_all x1, blocking collectives, body(): lax.all_to_all(sent, everyone, 0, 0, tiled=True).reshape(devices * 12, 128)  16.2 us
    all_to_all x1, blocking collectives, body(): lax.all_to_all(result.reshape(devices, 8, 128), everyone, 0, 0, tiled=True)  10.6 us
    ppermute x4, waiting for transfers between devices, from_device(): return lax.ppermute(block, ('gx', 'gy'), route)  6.98 us
    pallas_call x1, Pallas kernels, body(): first(*blocks, jnp.asarray(spread), jnp.asarray(collect), jnp.asarray(tra...  5.58 us
    pallas_call x1, Pallas kernels, body(): second(*messages, load, jnp.asarray(spread), jnp.asarray(collect), jnp.as...  4.46 us
    pallas_call x1, Pallas kernels, body(): pack(initial, forcing, modulus, solid_list, jnp.asarray(pack_table()))  2.42 us
    ppermute x4, starting transfers between devices, from_device(): return lax.ppermute(block, ('gx', 'gy'), route)  1.16 us
    pallas_call x1, Pallas kernels, body(): blocks += own(arrived, jnp.asarray(spread), jnp.asarray(collect))  1.03 us
  transfers between devices with their start and end apart: 4, of which 3 were waited for; matrix products, arithmetic and copies ran while one was open for 0% of the time, Pallas kernels for 2%

profile of v10, /device:TPU:0, one launch (start us, length us, event | category | flops | bytes accessed | tf_op | source)
XLA Modules:
  0.0 50.2 jit_solution(2458319333726780840)
XLA Ops:
  0.6 2.4 %shard_map.113 = f32[384,128]{1,0:T(8,128)} custom-call(f32[3,6,3,384]{3,2,1,0:T(4,128)} %initial_at.1, f32[3,6,3,384]{3,2,1,0:T(4,128)} %forcing_at.1, f32[2,1,128]{2,1,0:T(1,128)} %modulus_at.1, s32[1,1,192]{2,1,0:T(1,128)} %listing_at.1, bf16[384,512]{1,0:T(8,128)(2,1)} %constant.12.clone.table_at), custom_call_target="tpu_custom_call" | custom-call | tf_op jit(solution)/shard_map/pallas_call | solution.py:1175
  3.1 0.0 copy-start
  3.1 0.0 copy-start.1
  3.1 16.2 %all_to_all.10 = f32[32,3,4,128]{3,2,1,0:T(4,128)S(1)} all-to-all(f32[32,3,4,128]{3,2,1,0:T(4,128)} %bitcast.7), channel_id=1, replica_groups=mesh['gx'=4,'gy'=8] {'gy','gx'}, dimensions={0} | all-to-all | bytes 393216 | tf_op jit(solution)/shard_map/all_to_all | solution.py:1177
  19.3 0.2 collective-permute-start.1
  19.5 0.4 collective-permute-start
  19.9 0.0 copy-done
  19.9 0.0 copy-done.1
  19.9 0.0 copy-start.3
  19.9 1.0 %shard_map.114 = (f32[3,3,32,128]{3,2,1,0:T(8,128)S(1)}, f32[3,2,32,128]{3,2,1,0:T(8,128)S(1)}, f32[2,128]{1,0:T(2,128)S(1)}, f32[3,2,32,128]{3,2,1,0:T(8,128)S(1)}, f32[3,2,8,128]{3,2,1,0:T(8,128)S(1)}) custom-call(f32[384,128]{1,0:T(8,128)S(1)} %bitcast.6, bf16[192,240]{1,0:T(8,128)(2,1)S(1)} %copy-done, bf16[144,192]{1,0:T(8,128)(2,1)S(1)} %copy-done.1), custom_call_target="tpu_custom_call" | custom-call | flops 400000000 | bytes 1000000 | tf_op jit(solution)/shard_map/pallas_call | solution.py:1181
  20.9 1.8 %collective-permute-done.1.refs_1_ = f32[384,128]{1,0:T(8,128)S(1)} collective-permute-done((f32[384,128]{1,0:T(8,128)S(1)}, f32[384,128]{1,0:T(8,128)S(1)}, u32[]{:S(2)}, u32[]{:S(2)}) %collective-permute-start.1) | collective-permute-done | bytes 196640 | tf_op jit(solution)/shard_map/ppermute | solution.py:1172
  22.7 1.9 %collective-permute-done.refs_0_ = f32[384,128]{1,0:T(8,128)S(1)} collective-permute-done((f32[384,128]{1,0:T(8,128)S(1)}, f32[384,128]{1,0:T(8,128)S(1)}, u32[]{:S(2)}, u32[]{:S(2)}) %collective-permute-start) | collective-permute-done | bytes 196640 | tf_op jit(solution)/shard_map/ppermute | solution.py:1172
  24.6 0.0 copy-done.3
  24.6 0.0 copy-start.4
  24.6 5.6 %shard_map.115 = (f32[3,2,32,128]{3,2,1,0:T(8,128)S(1)}, f32[3,48,128]{2,1,0:T(8,128)S(1)}, f32[3,32,128]{2,1,0:T(8,128)S(1)}, f32[3,6,32,128]{3,2,1,0:T(8,128)S(1)}) custom-call(f32[384,128]{1,0:T(8,128)S(1)} %collective-permute-done.refs_0_, f32[384,128]{1,0:T(8,128)S(1)} %collective-permute-done.1.refs_1_, ...), custom_call_target="tpu_custom_call" | custom-call | tf_op jit(solution)/shard_map/pallas_call | solution.py:1182
  30.2 0.4 collective-permute-start.3
  30.5 0.2 collective-permute-start.2
  30.7 3.3 %collective-permute-done.2.refs_0_ = f32[3,32,128]{2,1,0:T(8,128)S(1)} collective-permute-done((f32[3,32,128]{2,1,0:T(8,128)S(1)}, f32[3,32,128]{2,1,0:T(8,128)S(1)}, u32[]{:S(2)}, u32[]{:S(2)}) %collective-permute-start.2) | collective-permute-done | bytes 49184 | tf_op jit(solution)/shard_map/ppermute | solution.py:1172
  34.0 0.0 collective-permute-done.3.refs_2_
  34.0 0.0 copy-done.4
  34.1 4.5 %shard_map.116 = f32[16,2,8,128]{3,2,1,0:T(8,128)S(1)} custom-call(f32[3,32,128]{2,1,0:T(8,128)S(1)} %collective-permute-done.2.refs_0_, f32[3,2,32,128]{3,2,1,0:T(8,128)S(1)} %get-tuple-element.17.refs_1_, f32[3,48,128]{2,1,0:T(8,128)S(1)} %collective-permute-done.3.refs_2_, f32[3,6,32,128]{3,2,1,0:T(8,128)S(1)} %get-tuple-element.19.refs_3_, ...), custom_call_target="tpu_custom_call" | custom-call | tf_op jit(solution)/shard_map/pallas_call | solution.py:1194
  38.5 0.0 copy-start.2
  38.5 10.6 %all_to_all.11.arrived = f32[32,8,128]{2,1,0:T(8,128)S(1)} all-to-all(f32[32,8,128]{2,1,0:T(8,128)S(1)} %bitcast.3), channel_id=1, replica_groups=mesh['gx'=4,'gy'=8] {'gy','gx'}, dimensions={0} | all-to-all | bytes 262144 | tf_op jit(solution)/shard_map/all_to_all | solution.py:1201
  49.1 0.0 copy-done.2
  49.1 1.0 %shard_map.117 = (f32[3,6,3,384]{3,2,1,0:T(4,128)}, f32[3,2,1,128]{3,2,1,0:T(1,128)}) custom-call(f32[32,8,128]{2,1,0:T(8,128)S(1)} %all_to_all.11.arrived, bf16[256,512]{1,0:T(8,128)(2,1)S(1)} %copy-done.2), custom_call_target="tpu_custom_call" | custom-call | tf_op jit(solution)/shard_map/pallas_call | solution.py:1202
Async XLA Ops:
  3.1 16.8 %copy-start = (bf16[192,240]{1,0:T(8,128)(2,1)S(1)}, bf16[192,240]{1,0:T(8,128)(2,1)}, u32[]{:S(2)}) copy-start(bf16[192,240]{1,0:T(8,128)(2,1)} %constant.13.clone.spread.refs_7_.refs_4_) | copy-start | bytes 276484
  3.1 16.8 %copy-start.1 = (bf16[144,192]{1,0:T(8,128)(2,1)S(1)}, bf16[144,192]{1,0:T(8,128)(2,1)}, u32[]{:S(2)}) copy-start(bf16[144,192]{1,0:T(8,128)(2,1)} %constant.14.clone.collect.refs_8_.refs_5_) | copy-start | bytes 165892
  19.3 3.4 %collective-permute-start.1 = (f32[384,128]{1,0:T(8,128)S(1)}, f32[384,128]{1,0:T(8,128)S(1)}, u32[]{:S(2)}, u32[]{:S(2)}) collective-permute-start(f32[384,128]{1,0:T(8,128)S(1)} %bitcast.4), channel_id=1, source_target_pairs={{8,0},{2,8},{10,2},{4,10},{12,4},{6,12},{14,6},{22,14},{30,22},{20... | collective-permute-start | bytes 589832 | tf_op jit(solution)/shard_map/ppermute | solution.py:1172
  19.5 5.1 %collective-permute-start = (f32[384,128]{1,0:T(8,128)S(1)}, f32[384,128]{1,0:T(8,128)S(1)}, u32[]{:S(2)}, u32[]{:S(2)}) collective-permute-start(f32[384,128]{1,0:T(8,128)S(1)} %bitcast.5), channel_id=1, source_target_pairs={{9,0},{0,8},{8,2},{2,10},{10,4},{4,12},{12,6},{6,14},{14,22},{22,3... | collective-permute-start | bytes 589832 | tf_op jit(solution)/shard_map/ppermute | solution.py:1172
  19.9 4.7 %copy-start.3 = (f32[32,8]{1,0:T(8,128)S(1)}, f32[32,8]{1,0:T(8,128)}, u32[]{:S(2)}) copy-start(f32[32,8]{1,0:T(8,128)} %constant.15.clone.refs_9_) | copy-start | bytes 3076
  24.6 9.5 %copy-start.4 = (f32[32,8]{1,0:T(8,128)S(1)}, f32[32,8]{1,0:T(8,128)}, u32[]{:S(2)}) copy-start(f32[32,8]{1,0:T(8,128)} %constant.16.clone.refs_6_) | copy-start | bytes 3076
  30.2 3.9 %collective-permute-start.3 = (f32[3,48,128]{2,1,0:T(8,128)S(1)}, f32[3,48,128]{2,1,0:T(8,128)S(1)}, u32[]{:S(2)}, u32[]{:S(2)}) collective-permute-start(f32[3,48,128]{2,1,0:T(8,128)S(1)} %get-tuple-element.18), channel_id=1, source_target_pairs={{8,0},{2,8},{10,2},{4,10},{12,4},{6,12},{14,6},{22,14},{30,22},{20... | collective-permute-start | bytes 221192 | tf_op jit(solution)/shard_map/ppermute | solution.py:1172
  30.5 3.5 %collective-permute-start.2 = (f32[3,32,128]{2,1,0:T(8,128)S(1)}, f32[3,32,128]{2,1,0:T(8,128)S(1)}, u32[]{:S(2)}, u32[]{:S(2)}) collective-permute-start(f32[3,32,128]{2,1,0:T(8,128)S(1)} %get-tuple-element.16), channel_id=1, source_target_pairs={{9,0},{0,8},{8,2},{2,10},{10,4},{4,12},{12,6},{6,14},{14,22},{22,3... | collective-permute-start | bytes 147464 | tf_op jit(solution)/shard_map/ppermute | solution.py:1172
  38.5 10.6 %copy-start.2 = (bf16[256,512]{1,0:T(8,128)(2,1)S(1)}, bf16[256,512]{1,0:T(8,128)(2,1)}, u32[]{:S(2)}) copy-start(bf16[256,512]{1,0:T(8,128)(2,1)} %constant.17.clone.table) | copy-start | bytes 786436

commit v11 on v10

--- a/solution.py
+++ b/solution.py
@@ -169,7 +169,17 @@
 
 
 def element_tables():
-    forward, backward, bound = build_tables([0.0, inner_anchors[0], inner_anchors[1], 1.0], 4)
+    anchors = [0.0, inner_anchors[0], inner_anchors[1], 1.0]
+    bound = build_tables(anchors, 4)[2]
+    raw_points, raw_weights = gauss_rule(4)
+    weights = raw_weights / 2.0
+    values, slopes = lagrange_tables(anchors, (raw_points + 1.0) / 2.0)
+    both = [outer_three(values, values, each).reshape(64, 64) for each in (values, slopes)]
+    forward = np.concatenate([both[0], both[1] / element_span], 0)
+    volume = (weights[:, None, None] * weights[None, :, None] * weights[None, None, :]).reshape(
+        -1
+    ) * element_span**3
+    backward = (forward * np.concatenate([volume, volume])[:, None]).T
     spread = np.zeros((forward.shape[0], DEPTH))
     collect = np.zeros((ROWS, backward.shape[1]))
     for row, node in enumerate(row_nodes()):
@@ -180,9 +190,55 @@
     collect_high, collect_low = halves(collect)
     return (
         np.concatenate([spread_high, spread_high, spread_low], 1),
-        np.concatenate([collect_high, collect_low], 0),
+        np.concatenate(
+            [
+                np.concatenate([collect_high, collect_high], 1),
+                np.concatenate([collect_low, np.zeros_like(collect_low)], 1),
+            ],
+            0,
+        ),
         bound,
     )
+
+
+def slope_tables(transposed):
+    raw_points, weights = gauss_rule(4)
+    samples = (raw_points + 1.0) / 2.0
+    slopes = lagrange_tables(list(samples), samples)[1] / element_span
+    if transposed:
+        slopes = slopes.T * weights[None, :] / weights[:, None]
+    from_even = [[(slopes[i, j] + slopes[i, 3 - j]) / 2.0 for j in range(2)] for i in range(2)]
+    from_odd = [[(slopes[i, j] - slopes[i, 3 - j]) / 2.0 for j in range(2)] for i in range(2)]
+    return (
+        [[float(c) for c in row] for row in from_even],
+        [[float(c) for c in row] for row in from_odd],
+    )
+
+
+def slopes_x(v, tables):
+    from_even, from_odd = tables
+    v = [v[16 * n : 16 * n + 16] for n in range(4)]
+    even, odd = [v[0] + v[3], v[1] + v[2]], [v[0] - v[3], v[1] - v[2]]
+    t = [from_even[i][0] * even[0] + from_even[i][1] * even[1] for i in range(2)]
+    s = [from_odd[i][0] * odd[0] + from_odd[i][1] * odd[1] for i in range(2)]
+    return jnp.concatenate([s[0] + t[0], s[1] + t[1], s[1] - t[1], s[0] - t[0]], 0)
+
+
+def slopes_y(v, tables):
+    lower = lax.broadcasted_iota(jnp.int32, (8, v.shape[1]), 0) < 4
+
+    def both(first, second):
+        return jnp.where(lower, first, second)
+
+    (e, o) = tables
+    parts = []
+    for n in range(4):
+        here, there = v[16 * n : 16 * n + 8], pltpu.roll(v[16 * n + 8 : 16 * n + 16], 4, 0)
+        even, odd = here + there, here - there
+        t = both(e[0][0], e[1][1]) * even + both(e[0][1], e[1][0]) * pltpu.roll(even, 4, 0)
+        s = both(o[0][0], o[1][1]) * odd + both(o[0][1], o[1][0]) * pltpu.roll(odd, 4, 0)
+        parts += [s + t, pltpu.roll(s - t, 4, 0)]
+    return jnp.concatenate(parts, 0)
 
 
 def transfer_table():
@@ -546,23 +602,23 @@
     def force(self, gradient, stiff, collect, pairs):
         width = len(pairs) * self.width
         stiffness = jnp.concatenate([stiff[pair : pair + 1, :] for pair in pairs], 1)
-        deform = [
-            [
-                gradient[64 * e : 64 * e + 64, width * i : width * (i + 1)]
-                + (1.0 if i == e else 0.0)
-                for e in range(3)
-            ]
-            for i in range(3)
-        ]
+        tables, tables_back = slope_tables(False), slope_tables(True)
+        deform = []
+        for i in range(3):
+            span = slice(width * i, width * (i + 1))
+            values = gradient[0:64, span]
+            deform.append([slopes_x(values, tables), slopes_y(values, tables), gradient[64:, span]])
+            deform[i][i] = deform[i][i] + 1.0
         stress = point_stress(deform, stiffness, lame_ratio * stiffness)
-        stress = jnp.concatenate(
-            [jnp.concatenate([stress[i][e] for i in range(3)], 1) for e in range(3)], 0
+        parts = []
+        for i in range(3):
+            plane = slopes_x(stress[i][0], tables_back) + slopes_y(stress[i][1], tables_back)
+            parts.append(jnp.concatenate([plane, stress[i][2]], 0))
+        high, low = high_low(jnp.concatenate(parts, 1))
+        force = jnp.dot(
+            collect[...], jnp.concatenate([high, low], 0), preferred_element_type=jnp.float32
         )
-        high, low = high_low(stress)
-        force = jnp.dot(collect[...], high, preferred_element_type=jnp.float32)
-        return force[0:ROWS] + (
-            force[ROWS:] + jnp.dot(collect[0:ROWS], low, preferred_element_type=jnp.float32)
-        )
+        return force[0:ROWS] + force[ROWS:]
 
     def run(self, u, stiff, spread, collect, jobs, given=None):
         plan = plan_steps([job[:2] for job in jobs])

time: 50.4 us -> 51.2 us (1.016)
  Pallas kernels: 14.5 us -> 15.4 us
    pallas_call x1, Pallas kernels: 5.58 us -> 6.11 us  [body(): first(*blocks, jnp.asarray(spread), jnp.asarray(collect), jnp.asarray(tra...]
where the time goes in v11:
time: 51.2 us; the launch traced here: 51 us
  blocking collectives  26.8 us (52%)
  Pallas kernels  15.4 us (30%)
  waiting for transfers between devices  6.94 us (14%)
  starting transfers between devices  1.16 us (2%)
  between operations  0.69 us (1%)
    all_to_all x1, blocking collectives, body(): lax.all_to_all(sent, everyone, 0, 0, tiled=True).reshape(devices * 12, 128)  16.2 us
    all_to_all x1, blocking collectives, body(): lax.all_to_all(result.reshape(devices, 8, 128), everyone, 0, 0, tiled=True)  10.6 us
    ppermute x4, waiting for transfers between devices, from_device(): return lax.ppermute(block, ('gx', 'gy'), route)  6.94 us
    pallas_call x1, Pallas kernels, body(): first(*blocks, jnp.asarray(spread), jnp.asarray(collect), jnp.asarray(tra...  6.11 us
    pallas_call x1, Pallas kernels, body(): second(*messages, load, jnp.asarray(spread), jnp.asarray(collect), jnp.as...  4.74 us
    pallas_call x1, Pallas kernels, body(): pack(initial, forcing, modulus, solid_list, jnp.asarray(pack_table()))  2.42 us
    ppermute x4, starting transfers between devices, from_device(): return lax.ppermute(block, ('gx', 'gy'), route)  1.16 us
    pallas_call x1, Pallas kernels, body(): blocks += own(arrived, jnp.asarray(spread), jnp.asarray(collect))  1.07 us
  transfers between devices with their start and end apart: 4, of which 3 were waited for; matrix products, arithmetic and copies ran while one was open for 0% of the time, Pallas kernels for 2%

profile of v11, /device:TPU:0, one launch (start us, length us, event | category | flops | bytes accessed | tf_op | source)
XLA Modules:
  0.0 51.0 jit_solution(5416259444721558504)
XLA Ops:
  0.6 2.4 %shard_map.113 = f32[384,128]{1,0:T(8,128)} custom-call(f32[3,6,3,384]{3,2,1,0:T(4,128)} %initial_at.1, f32[3,6,3,384]{3,2,1,0:T(4,128)} %forcing_at.1, f32[2,1,128]{2,1,0:T(1,128)} %modulus_at.1, s32[1,1,192]{2,1,0:T(1,128)} %listing_at.1, bf16[384,512]{1,0:T(8,128)(2,1)} %constant.12.clone.table_at), custom_call_target="tpu_custom_call" | custom-call | tf_op jit(solution)/shard_map/pallas_call | solution.py:1231
  3.1 0.0 copy-start
  3.1 0.0 copy-start.1
  3.1 16.2 %all_to_all.10 = f32[32,3,4,128]{3,2,1,0:T(4,128)S(1)} all-to-all(f32[32,3,4,128]{3,2,1,0:T(4,128)} %bitcast.7), channel_id=1, replica_groups=mesh['gx'=4,'gy'=8] {'gy','gx'}, dimensions={0} | all-to-all | bytes 393216 | tf_op jit(solution)/shard_map/all_to_all | solution.py:1233
  19.3 0.2 collective-permute-start.1
  19.5 0.4 collective-permute-start
  19.9 0.0 copy-done
  19.9 0.0 copy-done.1
  19.9 0.0 copy-start.3
  19.9 1.1 %shard_map.114 = (f32[3,3,32,128]{3,2,1,0:T(8,128)S(1)}, f32[3,2,32,128]{3,2,1,0:T(8,128)S(1)}, f32[2,128]{1,0:T(2,128)S(1)}, f32[3,2,32,128]{3,2,1,0:T(8,128)S(1)}, f32[3,2,8,128]{3,2,1,0:T(8,128)S(1)}) custom-call(f32[384,128]{1,0:T(8,128)S(1)} %bitcast.6, bf16[128,240]{1,0:T(8,128)(2,1)S(1)} %copy-done.1, bf16[144,256]{1,0:T(8,128)(2,1)S(1)} %copy-done), custom_call_target="tpu_custom_call" | custom-call | flops 400000000 | bytes 1000000 | tf_op jit(solution)/shard_map/pallas_call | solution.py:1237
  21.0 1.7 %collective-permute-done.1.refs_1_ = f32[384,128]{1,0:T(8,128)S(1)} collective-permute-done((f32[384,128]{1,0:T(8,128)S(1)}, f32[384,128]{1,0:T(8,128)S(1)}, u32[]{:S(2)}, u32[]{:S(2)}) %collective-permute-start.1) | collective-permute-done | bytes 196640 | tf_op jit(solution)/shard_map/ppermute | solution.py:1228
  22.7 1.9 %collective-permute-done.refs_0_ = f32[384,128]{1,0:T(8,128)S(1)} collective-permute-done((f32[384,128]{1,0:T(8,128)S(1)}, f32[384,128]{1,0:T(8,128)S(1)}, u32[]{:S(2)}, u32[]{:S(2)}) %collective-permute-start) | collective-permute-done | bytes 196640 | tf_op jit(solution)/shard_map/ppermute | solution.py:1228
  24.6 0.0 copy-done.3
  24.6 0.0 copy-start.4
  24.6 6.1 %shard_map.115 = (f32[3,2,32,128]{3,2,1,0:T(8,128)S(1)}, f32[3,48,128]{2,1,0:T(8,128)S(1)}, f32[3,32,128]{2,1,0:T(8,128)S(1)}, f32[3,6,32,128]{3,2,1,0:T(8,128)S(1)}) custom-call(f32[384,128]{1,0:T(8,128)S(1)} %collective-permute-done.refs_0_, f32[384,128]{1,0:T(8,128)S(1)} %collective-permute-done.1.refs_1_, ...), custom_call_target="tpu_custom_call" | custom-call | tf_op jit(solution)/shard_map/pallas_call | solution.py:1238
  30.7 0.4 collective-permute-start.3
  31.1 0.2 collective-permute-start.2
  31.3 3.3 %collective-permute-done.2.refs_0_ = f32[3,32,128]{2,1,0:T(8,128)S(1)} collective-permute-done((f32[3,32,128]{2,1,0:T(8,128)S(1)}, f32[3,32,128]{2,1,0:T(8,128)S(1)}, u32[]{:S(2)}, u32[]{:S(2)}) %collective-permute-start.2) | collective-permute-done | bytes 49184 | tf_op jit(solution)/shard_map/ppermute | solution.py:1228
  34.6 0.0 collective-permute-done.3.refs_2_
  34.6 0.0 copy-done.4
  34.6 4.7 %shard_map.116 = f32[16,2,8,128]{3,2,1,0:T(8,128)S(1)} custom-call(f32[3,32,128]{2,1,0:T(8,128)S(1)} %collective-permute-done.2.refs_0_, f32[3,2,32,128]{3,2,1,0:T(8,128)S(1)} %get-tuple-element.17.refs_1_, f32[3,48,128]{2,1,0:T(8,128)S(1)} %collective-permute-done.3.refs_2_, f32[3,6,32,128]{3,2,1,0:T(8,128)S(1)} %get-tuple-element.19.refs_3_, ...), custom_call_target="tpu_custom_call" | custom-call | tf_op jit(solution)/shard_map/pallas_call | solution.py:1250
  39.3 0.0 copy-start.2
  39.3 10.6 %all_to_all.11.arrived = f32[32,8,128]{2,1,0:T(8,128)S(1)} all-to-all(f32[32,8,128]{2,1,0:T(8,128)S(1)} %bitcast.3), channel_id=1, replica_groups=mesh['gx'=4,'gy'=8] {'gy','gx'}, dimensions={0} | all-to-all | bytes 262144 | tf_op jit(solution)/shard_map/all_to_all | solution.py:1257
  50.0 0.0 copy-done.2
  50.0 1.0 %shard_map.117 = (f32[3,6,3,384]{3,2,1,0:T(4,128)}, f32[3,2,1,128]{3,2,1,0:T(1,128)}) custom-call(f32[32,8,128]{2,1,0:T(8,128)S(1)} %all_to_all.11.arrived, bf16[256,512]{1,0:T(8,128)(2,1)S(1)} %copy-done.2), custom_call_target="tpu_custom_call" | custom-call | tf_op jit(solution)/shard_map/pallas_call | solution.py:1258
Async XLA Ops:
  3.1 16.8 %copy-start = (bf16[144,256]{1,0:T(8,128)(2,1)S(1)}, bf16[144,256]{1,0:T(8,128)(2,1)}, u32[]{:S(2)}) copy-start(bf16[144,256]{1,0:T(8,128)(2,1)} %constant.14.clone.collect.refs_8_.refs_5_) | copy-start | bytes 221188
  3.1 16.8 %copy-start.1 = (bf16[128,240]{1,0:T(8,128)(2,1)S(1)}, bf16[128,240]{1,0:T(8,128)(2,1)}, u32[]{:S(2)}) copy-start(bf16[128,240]{1,0:T(8,128)(2,1)} %constant.13.clone.spread.refs_7_.refs_4_) | copy-start | bytes 184324
  19.3 3.4 %collective-permute-start.1 = (f32[384,128]{1,0:T(8,128)S(1)}, f32[384,128]{1,0:T(8,128)S(1)}, u32[]{:S(2)}, u32[]{:S(2)}) collective-permute-start(f32[384,128]{1,0:T(8,128)S(1)} %bitcast.4), channel_id=1, source_target_pairs={{8,0},{2,8},{10,2},{4,10},{12,4},{6,12},{14,6},{22,14},{30,22},{20... | collective-permute-start | bytes 589832 | tf_op jit(solution)/shard_map/ppermute | solution.py:1228
  19.5 5.1 %collective-permute-start = (f32[384,128]{1,0:T(8,128)S(1)}, f32[384,128]{1,0:T(8,128)S(1)}, u32[]{:S(2)}, u32[]{:S(2)}) collective-permute-start(f32[384,128]{1,0:T(8,128)S(1)} %bitcast.5), channel_id=1, source_target_pairs={{9,0},{0,8},{8,2},{2,10},{10,4},{4,12},{12,6},{6,14},{14,22},{22,3... | collective-permute-start | bytes 589832 | tf_op jit(solution)/shard_map/ppermute | solution.py:1228
  19.9 4.7 %copy-start.3 = (f32[32,8]{1,0:T(8,128)S(1)}, f32[32,8]{1,0:T(8,128)}, u32[]{:S(2)}) copy-start(f32[32,8]{1,0:T(8,128)} %constant.15.clone.refs_9_) | copy-start | bytes 3076
  24.6 10.0 %copy-start.4 = (f32[32,8]{1,0:T(8,128)S(1)}, f32[32,8]{1,0:T(8,128)}, u32[]{:S(2)}) copy-start(f32[32,8]{1,0:T(8,128)} %constant.16.clone.refs_6_) | copy-start | bytes 3076
  30.7 3.9 %collective-permute-start.3 = (f32[3,48,128]{2,1,0:T(8,128)S(1)}, f32[3,48,128]{2,1,0:T(8,128)S(1)}, u32[]{:S(2)}, u32[]{:S(2)}) collective-permute-start(f32[3,48,128]{2,1,0:T(8,128)S(1)} %get-tuple-element.18), channel_id=1, source_target_pairs={{8,0},{2,8},{10,2},{4,10},{12,4},{6,12},{14,6},{22,14},{30,22},{20... | collective-permute-start | bytes 221192 | tf_op jit(solution)/shard_map/ppermute | solution.py:1228
  31.1 3.5 %collective-permute-start.2 = (f32[3,32,128]{2,1,0:T(8,128)S(1)}, f32[3,32,128]{2,1,0:T(8,128)S(1)}, u32[]{:S(2)}, u32[]{:S(2)}) collective-permute-start(f32[3,32,128]{2,1,0:T(8,128)S(1)} %get-tuple-element.16), channel_id=1, source_target_pairs={{9,0},{0,8},{8,2},{2,10},{10,4},{4,12},{12,6},{6,14},{14,22},{22,3... | collective-permute-start | bytes 147464 | tf_op jit(solution)/shard_map/ppermute | solution.py:1228
  39.3 10.6 %copy-start.2 = (bf16[256,512]{1,0:T(8,128)(2,1)S(1)}, bf16[256,512]{1,0:T(8,128)(2,1)}, u32[]{:S(2)}) copy-start(bf16[256,512]{1,0:T(8,128)(2,1)} %constant.17.clone.table) | copy-start | bytes 786436

commit v12 on v10

--- a/solution.py
+++ b/solution.py
@@ -390,16 +390,16 @@
     ]
 
 
-def point_stress(deform, stiffness, stiffness_four):
+def point_stress(deform):
     cofactors = cofactor_rows(deform)
     jacobian = (
         deform[0][0] * cofactors[0][0]
         + deform[0][1] * cofactors[0][1]
         + deform[0][2] * cofactors[0][2]
     )
-    pressure = stiffness_four * (jacobian - rest_ratio)
+    pressure = lame_ratio * (jacobian - rest_ratio)
     return [
-        [stiffness * deform[i][d] + pressure * cofactors[i][d] for d in range(3)] for i in range(3)
+        [deform[i][d] + pressure * cofactors[i][d] for d in range(3)] for i in range(3)
     ]
 
 
@@ -535,34 +535,54 @@
         )
 
     def gradient(self, u, spread, pairs):
-        blocks = [self.gather(u[i, pair], u[i, pair + 1]) for i in range(3) for pair in pairs]
-        high, low = high_low(jnp.concatenate(blocks, 1))
+        parts = [
+            high_low(self.gather(u[i, pair], u[i, pair + 1])) for i in range(3) for pair in pairs
+        ]
         return jnp.dot(
             spread[...],
-            jnp.concatenate([high, low, high], 0),
+            jnp.concatenate([jnp.concatenate([h, l, h], 0) for h, l in parts], 1),
             preferred_element_type=jnp.float32,
         )
 
     def force(self, gradient, stiff, collect, pairs):
-        width = len(pairs) * self.width
-        stiffness = jnp.concatenate([stiff[pair : pair + 1, :] for pair in pairs], 1)
-        deform = [
-            [
-                gradient[64 * e : 64 * e + 64, width * i : width * (i + 1)]
-                + (1.0 if i == e else 0.0)
-                for e in range(3)
-            ]
-            for i in range(3)
-        ]
-        stress = point_stress(deform, stiffness, lame_ratio * stiffness)
-        stress = jnp.concatenate(
-            [jnp.concatenate([stress[i][e] for i in range(3)], 1) for e in range(3)], 0
+        width, count = self.width, len(pairs)
+        rows = 16
+        high, low = {}, {}
+        for q in range(count):
+            for r in range(64 // rows):
+                deform = [
+                    [
+                        gradient[
+                            64 * e + rows * r : 64 * e + rows * (r + 1),
+                            width * (count * i + q) : width * (count * i + q + 1),
+                        ]
+                        + (1.0 if i == e else 0.0)
+                        for e in range(3)
+                    ]
+                    for i in range(3)
+                ]
+                stress = point_stress(deform)
+                for i in range(3):
+                    for e in range(3):
+                        high[e, r, i, q], low[e, r, i, q] = high_low(stress[i][e])
+
+        def whole(part):
+            return jnp.concatenate(
+                [
+                    jnp.concatenate([part[e, r, i, q] for i in range(3) for q in range(count)], 1)
+                    for e in range(3)
+                    for r in range(64 // rows)
+                ],
+                0,
+            )
+
+        force = jnp.dot(collect[...], whole(high), preferred_element_type=jnp.float32)
+        force = force[0:ROWS] + (
+            force[ROWS:]
+            + jnp.dot(collect[0:ROWS], whole(low), preferred_element_type=jnp.float32)
         )
-        high, low = high_low(stress)
-        force = jnp.dot(collect[...], high, preferred_element_type=jnp.float32)
-        return force[0:ROWS] + (
-            force[ROWS:] + jnp.dot(collect[0:ROWS], low, preferred_element_type=jnp.float32)
-        )
+        stiffness = [stiff[pair : pair + 1, :] for pair in pairs]
+        return force * jnp.concatenate(stiffness * 3, 1)
 
     def run(self, u, stiff, spread, collect, jobs, given=None):
         plan = plan_steps([job[:2] for job in jobs])
@@ -672,7 +692,6 @@
             grads.append((dx, dy, dz))
         weight = element_span**2 / 8.0
         scaled = weight * stiffness
-        scaled_four = lame_ratio * scaled
         sums = [({}, {}, {}) for i in range(3)]
 
         def add(table, key, value):
@@ -687,7 +706,7 @@
                     ]
                     for i in range(3):
                         deform[i][i] = deform[i][i] + 1.0
-                    stress = point_stress(deform, scaled, scaled_four)
+                    stress = point_stress(deform)
                     for i in range(3):
                         add(sums[i][0], (j, k), stress[i][0])
                         add(sums[i][1], (h, k), stress[i][1])
@@ -715,7 +734,7 @@
                 for a in two:
                     part[a, b, 0] = part[a, b, 0] - line[a]
                     part[a, b, 1] = part[a, b, 1] + line[a]
-            forces.append(self.assemble(part))
+            forces.append(self.assemble({key: scaled * value for key, value in part.items()}))
         return forces
 
 

time: 50.4 us -> 50.2 us (level)
  no operation moved by 1% of the time
where the time goes in v12:
time: 50.2 us; the launch traced here: 50 us
  blocking collectives  26.8 us (53%)
  Pallas kernels  14.3 us (28%)
  waiting for transfers between devices  7 us (14%)
  starting transfers between devices  1.16 us (2%)
  between operations  0.69 us (1%)
    all_to_all x1, blocking collectives, body(): lax.all_to_all(sent, everyone, 0, 0, tiled=True).reshape(devices * 12, 128)  16.2 us
    all_to_all x1, blocking collectives, body(): lax.all_to_all(result.reshape(devices, 8, 128), everyone, 0, 0, tiled=True)  10.6 us
    ppermute x4, waiting for transfers between devices, from_device(): return lax.ppermute(block, ('gx', 'gy'), route)  7 us
    pallas_call x1, Pallas kernels, body(): first(*blocks, jnp.asarray(spread), jnp.asarray(collect), jnp.asarray(tra...  5.43 us
    pallas_call x1, Pallas kernels, body(): second(*messages, load, jnp.asarray(spread), jnp.asarray(collect), jnp.as...  4.4 us
    pallas_call x1, Pallas kernels, body(): pack(initial, forcing, modulus, solid_list, jnp.asarray(pack_table()))  2.42 us
    ppermute x4, starting transfers between devices, from_device(): return lax.ppermute(block, ('gx', 'gy'), route)  1.16 us
    pallas_call x1, Pallas kernels, body(): return unpack(back, jnp.asarray(unpack_table()))  1.02 us
  transfers between devices with their start and end apart: 4, of which 3 were waited for; matrix products, arithmetic and copies ran while one was open for 0% of the time, Pallas kernels for 2%

profile of v12, /device:TPU:0, one launch (start us, length us, event | category | flops | bytes accessed | tf_op | source)
XLA Modules:
  0.0 50.0 jit_solution(1596509301966820942)
XLA Ops:
  0.6 2.4 %shard_map.113 = f32[384,128]{1,0:T(8,128)} custom-call(f32[3,6,3,384]{3,2,1,0:T(4,128)} %initial_at.1, f32[3,6,3,384]{3,2,1,0:T(4,128)} %forcing_at.1, f32[2,1,128]{2,1,0:T(1,128)} %modulus_at.1, s32[1,1,192]{2,1,0:T(1,128)} %listing_at.1, bf16[384,512]{1,0:T(8,128)(2,1)} %constant.12.clone.table_at), custom_call_target="tpu_custom_call" | custom-call | tf_op jit(solution)/shard_map/pallas_call | solution.py:1194
  3.1 0.0 copy-start
  3.1 0.0 copy-start.1
  3.1 16.2 %all_to_all.10 = f32[32,3,4,128]{3,2,1,0:T(4,128)S(1)} all-to-all(f32[32,3,4,128]{3,2,1,0:T(4,128)} %bitcast.7), channel_id=1, replica_groups=mesh['gx'=4,'gy'=8] {'gy','gx'}, dimensions={0} | all-to-all | bytes 393216 | tf_op jit(solution)/shard_map/all_to_all | solution.py:1196
  19.3 0.2 collective-permute-start.1
  19.5 0.4 collective-permute-start
  19.9 0.0 copy-done
  19.9 0.0 copy-done.1
  19.9 0.0 copy-start.3
  19.9 1.0 %shard_map.114 = (f32[3,3,32,128]{3,2,1,0:T(8,128)S(1)}, f32[3,2,32,128]{3,2,1,0:T(8,128)S(1)}, f32[2,128]{1,0:T(2,128)S(1)}, f32[3,2,32,128]{3,2,1,0:T(8,128)S(1)}, f32[3,2,8,128]{3,2,1,0:T(8,128)S(1)}) custom-call(f32[384,128]{1,0:T(8,128)S(1)} %bitcast.6, bf16[192,240]{1,0:T(8,128)(2,1)S(1)} %copy-done, bf16[144,192]{1,0:T(8,128)(2,1)S(1)} %copy-done.1), custom_call_target="tpu_custom_call" | custom-call | flops 400000000 | bytes 1000000 | tf_op jit(solution)/shard_map/pallas_call | solution.py:1200
  20.9 1.8 %collective-permute-done.1.refs_1_ = f32[384,128]{1,0:T(8,128)S(1)} collective-permute-done((f32[384,128]{1,0:T(8,128)S(1)}, f32[384,128]{1,0:T(8,128)S(1)}, u32[]{:S(2)}, u32[]{:S(2)}) %collective-permute-start.1) | collective-permute-done | bytes 196640 | tf_op jit(solution)/shard_map/ppermute | solution.py:1191
  22.7 1.9 %collective-permute-done.refs_0_ = f32[384,128]{1,0:T(8,128)S(1)} collective-permute-done((f32[384,128]{1,0:T(8,128)S(1)}, f32[384,128]{1,0:T(8,128)S(1)}, u32[]{:S(2)}, u32[]{:S(2)}) %collective-permute-start) | collective-permute-done | bytes 196640 | tf_op jit(solution)/shard_map/ppermute | solution.py:1191
  24.6 0.0 copy-done.3
  24.6 0.0 copy-start.4
  24.6 5.4 %shard_map.115 = (f32[3,2,32,128]{3,2,1,0:T(8,128)S(1)}, f32[3,48,128]{2,1,0:T(8,128)S(1)}, f32[3,32,128]{2,1,0:T(8,128)S(1)}, f32[3,6,32,128]{3,2,1,0:T(8,128)S(1)}) custom-call(f32[384,128]{1,0:T(8,128)S(1)} %collective-permute-done.refs_0_, f32[384,128]{1,0:T(8,128)S(1)} %collective-permute-done.1.refs_1_, ...), custom_call_target="tpu_custom_call" | custom-call | tf_op jit(solution)/shard_map/pallas_call | solution.py:1201
  30.0 0.3 collective-permute-start.3
  30.4 0.2 collective-permute-start.2
  30.6 3.3 %collective-permute-done.2.refs_0_ = f32[3,32,128]{2,1,0:T(8,128)S(1)} collective-permute-done((f32[3,32,128]{2,1,0:T(8,128)S(1)}, f32[3,32,128]{2,1,0:T(8,128)S(1)}, u32[]{:S(2)}, u32[]{:S(2)}) %collective-permute-start.2) | collective-permute-done | bytes 49184 | tf_op jit(solution)/shard_map/ppermute | solution.py:1191
  33.9 0.0 collective-permute-done.3.refs_2_
  33.9 0.0 copy-done.4
  33.9 4.4 %shard_map.116 = f32[16,2,8,128]{3,2,1,0:T(8,128)S(1)} custom-call(f32[3,32,128]{2,1,0:T(8,128)S(1)} %collective-permute-done.2.refs_0_, f32[3,2,32,128]{3,2,1,0:T(8,128)S(1)} %get-tuple-element.17.refs_1_, f32[3,48,128]{2,1,0:T(8,128)S(1)} %collective-permute-done.3.refs_2_, f32[3,6,32,128]{3,2,1,0:T(8,128)S(1)} %get-tuple-element.19.refs_3_, ...), custom_call_target="tpu_custom_call" | custom-call | tf_op jit(solution)/shard_map/pallas_call | solution.py:1213
  38.3 0.0 copy-start.2
  38.3 10.6 %all_to_all.11.arrived = f32[32,8,128]{2,1,0:T(8,128)S(1)} all-to-all(f32[32,8,128]{2,1,0:T(8,128)S(1)} %bitcast.3), channel_id=1, replica_groups=mesh['gx'=4,'gy'=8] {'gy','gx'}, dimensions={0} | all-to-all | bytes 262144 | tf_op jit(solution)/shard_map/all_to_all | solution.py:1220
  48.9 0.0 copy-done.2
  48.9 1.0 %shard_map.117 = (f32[3,6,3,384]{3,2,1,0:T(4,128)}, f32[3,2,1,128]{3,2,1,0:T(1,128)}) custom-call(f32[32,8,128]{2,1,0:T(8,128)S(1)} %all_to_all.11.arrived, bf16[256,512]{1,0:T(8,128)(2,1)S(1)} %copy-done.2), custom_call_target="tpu_custom_call" | custom-call | tf_op jit(solution)/shard_map/pallas_call | solution.py:1221
Async XLA Ops:
  3.1 16.8 %copy-start = (bf16[192,240]{1,0:T(8,128)(2,1)S(1)}, bf16[192,240]{1,0:T(8,128)(2,1)}, u32[]{:S(2)}) copy-start(bf16[192,240]{1,0:T(8,128)(2,1)} %constant.13.clone.spread.refs_7_.refs_4_) | copy-start | bytes 276484
  3.1 16.8 %copy-start.1 = (bf16[144,192]{1,0:T(8,128)(2,1)S(1)}, bf16[144,192]{1,0:T(8,128)(2,1)}, u32[]{:S(2)}) copy-start(bf16[144,192]{1,0:T(8,128)(2,1)} %constant.14.clone.collect.refs_8_.refs_5_) | copy-start | bytes 165892
  19.3 3.4 %collective-permute-start.1 = (f32[384,128]{1,0:T(8,128)S(1)}, f32[384,128]{1,0:T(8,128)S(1)}, u32[]{:S(2)}, u32[]{:S(2)}) collective-permute-start(f32[384,128]{1,0:T(8,128)S(1)} %bitcast.4), channel_id=1, source_target_pairs={{8,0},{2,8},{10,2},{4,10},{12,4},{6,12},{14,6},{22,14},{30,22},{20... | collective-permute-start | bytes 589832 | tf_op jit(solution)/shard_map/ppermute | solution.py:1191
  19.5 5.1 %collective-permute-start = (f32[384,128]{1,0:T(8,128)S(1)}, f32[384,128]{1,0:T(8,128)S(1)}, u32[]{:S(2)}, u32[]{:S(2)}) collective-permute-start(f32[384,128]{1,0:T(8,128)S(1)} %bitcast.5), channel_id=1, source_target_pairs={{9,0},{0,8},{8,2},{2,10},{10,4},{4,12},{12,6},{6,14},{14,22},{22,3... | collective-permute-start | bytes 589832 | tf_op jit(solution)/shard_map/ppermute | solution.py:1191
  19.9 4.7 %copy-start.3 = (f32[32,8]{1,0:T(8,128)S(1)}, f32[32,8]{1,0:T(8,128)}, u32[]{:S(2)}) copy-start(f32[32,8]{1,0:T(8,128)} %constant.15.clone.refs_9_) | copy-start | bytes 3076
  24.6 9.3 %copy-start.4 = (f32[32,8]{1,0:T(8,128)S(1)}, f32[32,8]{1,0:T(8,128)}, u32[]{:S(2)}) copy-start(f32[32,8]{1,0:T(8,128)} %constant.16.clone.refs_6_) | copy-start | bytes 3076
  30.0 3.9 %collective-permute-start.3 = (f32[3,48,128]{2,1,0:T(8,128)S(1)}, f32[3,48,128]{2,1,0:T(8,128)S(1)}, u32[]{:S(2)}, u32[]{:S(2)}) collective-permute-start(f32[3,48,128]{2,1,0:T(8,128)S(1)} %get-tuple-element.18), channel_id=1, source_target_pairs={{8,0},{2,8},{10,2},{4,10},{12,4},{6,12},{14,6},{22,14},{30,22},{20... | collective-permute-start | bytes 221192 | tf_op jit(solution)/shard_map/ppermute | solution.py:1191
  30.4 3.5 %collective-permute-start.2 = (f32[3,32,128]{2,1,0:T(8,128)S(1)}, f32[3,32,128]{2,1,0:T(8,128)S(1)}, u32[]{:S(2)}, u32[]{:S(2)}) collective-permute-start(f32[3,32,128]{2,1,0:T(8,128)S(1)} %get-tuple-element.16), channel_id=1, source_target_pairs={{9,0},{0,8},{8,2},{2,10},{10,4},{4,12},{12,6},{6,14},{14,22},{22,3... | collective-permute-start | bytes 147464 | tf_op jit(solution)/shard_map/ppermute | solution.py:1191
  38.3 10.6 %copy-start.2 = (bf16[256,512]{1,0:T(8,128)(2,1)S(1)}, bf16[256,512]{1,0:T(8,128)(2,1)}, u32[]{:S(2)}) copy-start(bf16[256,512]{1,0:T(8,128)(2,1)} %constant.17.clone.table) | copy-start | bytes 786436

commit v13 on v12

--- a/solution.py
+++ b/solution.py
@@ -1111,7 +1111,7 @@
 
     pack = pl.pallas_call(
         functools.partial(pack_kernel, order),
-        out_shape=jax.ShapeDtypeStruct((devices * 12, 128), f32),
+        out_shape=pltpu.VMEM((devices * 12, 128), f32),
         in_specs=[pl.BlockSpec(memory_space=pl.ANY)] * 5,
         out_specs=pl.BlockSpec(memory_space=pltpu.VMEM),
         scratch_shapes=[

time: 50.2 us -> 49.3 us (0.982)
  Pallas kernels: 14.3 us -> 13.6 us
    pallas_call x1, Pallas kernels: 2.42 us -> 1.74 us  [body(): pack(initial, forcing, modulus, solid_list, jnp.asarray(pack_table()))]
where the time goes in v13:
time: 49.3 us; the launch traced here: 49.1 us
  blocking collectives  26.6 us (54%)
  Pallas kernels  13.6 us (28%)
  waiting for transfers between devices  7 us (14%)
  starting transfers between devices  1.16 us (2%)
  between operations  0.69 us (1%)
    all_to_all x1, blocking collectives, body(): lax.all_to_all(sent, everyone, 0, 0, tiled=True).reshape(devices * 12, 128)  16 us
    all_to_all x1, blocking collectives, body(): lax.all_to_all(result.reshape(devices, 8, 128), everyone, 0, 0, tiled=True)  10.6 us
    ppermute x4, waiting for transfers between devices, from_device(): return lax.ppermute(block, ('gx', 'gy'), route)  7 us
    pallas_call x1, Pallas kernels, body(): first(*blocks, jnp.asarray(spread), jnp.asarray(collect), jnp.asarray(tra...  5.43 us
    pallas_call x1, Pallas kernels, body(): second(*messages, load, jnp.asarray(spread), jnp.asarray(collect), jnp.as...  4.4 us
    pallas_call x1, Pallas kernels, body(): pack(initial, forcing, modulus, solid_list, jnp.asarray(pack_table()))  1.74 us
    ppermute x4, starting transfers between devices, from_device(): return lax.ppermute(block, ('gx', 'gy'), route)  1.16 us
    pallas_call x1, Pallas kernels, body(): return unpack(back, jnp.asarray(unpack_table()))  1.02 us
  transfers between devices with their start and end apart: 4, of which 3 were waited for; matrix products, arithmetic and copies ran while one was open for 0% of the time, Pallas kernels for 2%

profile of v13, /device:TPU:0, one launch (start us, length us, event | category | flops | bytes accessed | tf_op | source)
XLA Modules:
  0.0 49.1 jit_solution(5990659346456105950)
XLA Ops:
  0.6 1.7 %shard_map.113 = f32[384,128]{1,0:T(8,128)S(1)} custom-call(f32[3,6,3,384]{3,2,1,0:T(4,128)} %initial_at.1, f32[3,6,3,384]{3,2,1,0:T(4,128)} %forcing_at.1, f32[2,1,128]{2,1,0:T(1,128)} %modulus_at.1, s32[1,1,192]{2,1,0:T(1,128)} %listing_at.1, bf16[384,512]{1,0:T(8,128)(2,1)} %constant.12.clone.table_at), custom_call_target="tpu_custom_call" | custom-call | tf_op jit(solution)/shard_map/pallas_call | solution.py:1194
  2.4 0.0 copy-start
  2.4 0.0 copy-start.1
  2.4 16.0 %all_to_all.10 = f32[32,3,4,128]{3,2,1,0:T(4,128)S(1)} all-to-all(f32[32,3,4,128]{3,2,1,0:T(4,128)S(1)} %bitcast.3), channel_id=1, replica_groups=mesh['gx'=4,'gy'=8] {'gy','gx'}, dimensions={0} | all-to-all | bytes 393216 | tf_op jit(solution)/shard_map/all_to_all | solution.py:1196
  18.4 0.2 collective-permute-start.1
  18.6 0.4 collective-permute-start
  19.0 0.0 copy-done
  19.0 0.0 copy-done.1
  19.0 0.0 copy-start.3
  19.0 1.0 %shard_map.114 = (f32[3,3,32,128]{3,2,1,0:T(8,128)S(1)}, f32[3,2,32,128]{3,2,1,0:T(8,128)S(1)}, f32[2,128]{1,0:T(2,128)S(1)}, f32[3,2,32,128]{3,2,1,0:T(8,128)S(1)}, f32[3,2,8,128]{3,2,1,0:T(8,128)S(1)}) custom-call(f32[384,128]{1,0:T(8,128)S(1)} %bitcast.7, bf16[192,240]{1,0:T(8,128)(2,1)S(1)} %copy-done, bf16[144,192]{1,0:T(8,128)(2,1)S(1)} %copy-done.1), custom_call_target="tpu_custom_call" | custom-call | flops 400000000 | bytes 1000000 | tf_op jit(solution)/shard_map/pallas_call | solution.py:1200
  20.0 1.8 %collective-permute-done.1.refs_1_ = f32[384,128]{1,0:T(8,128)S(1)} collective-permute-done((f32[384,128]{1,0:T(8,128)S(1)}, f32[384,128]{1,0:T(8,128)S(1)}, u32[]{:S(2)}, u32[]{:S(2)}) %collective-permute-start.1) | collective-permute-done | bytes 196640 | tf_op jit(solution)/shard_map/ppermute | solution.py:1191
  21.8 1.9 %collective-permute-done.refs_0_ = f32[384,128]{1,0:T(8,128)S(1)} collective-permute-done((f32[384,128]{1,0:T(8,128)S(1)}, f32[384,128]{1,0:T(8,128)S(1)}, u32[]{:S(2)}, u32[]{:S(2)}) %collective-permute-start) | collective-permute-done | bytes 196640 | tf_op jit(solution)/shard_map/ppermute | solution.py:1191
  23.7 0.0 copy-done.3
  23.7 0.0 copy-start.4
  23.7 5.4 %shard_map.115 = (f32[3,2,32,128]{3,2,1,0:T(8,128)S(1)}, f32[3,48,128]{2,1,0:T(8,128)S(1)}, f32[3,32,128]{2,1,0:T(8,128)S(1)}, f32[3,6,32,128]{3,2,1,0:T(8,128)S(1)}) custom-call(f32[384,128]{1,0:T(8,128)S(1)} %collective-permute-done.refs_0_, f32[384,128]{1,0:T(8,128)S(1)} %collective-permute-done.1.refs_1_, ...), custom_call_target="tpu_custom_call" | custom-call | tf_op jit(solution)/shard_map/pallas_call | solution.py:1201
  29.1 0.3 collective-permute-start.3
  29.5 0.2 collective-permute-start.2
  29.7 3.3 %collective-permute-done.2.refs_0_ = f32[3,32,128]{2,1,0:T(8,128)S(1)} collective-permute-done((f32[3,32,128]{2,1,0:T(8,128)S(1)}, f32[3,32,128]{2,1,0:T(8,128)S(1)}, u32[]{:S(2)}, u32[]{:S(2)}) %collective-permute-start.2) | collective-permute-done | bytes 49184 | tf_op jit(solution)/shard_map/ppermute | solution.py:1191
  33.0 0.0 collective-permute-done.3.refs_2_
  33.0 0.0 copy-done.4
  33.0 4.4 %shard_map.116 = f32[16,2,8,128]{3,2,1,0:T(8,128)S(1)} custom-call(f32[3,32,128]{2,1,0:T(8,128)S(1)} %collective-permute-done.2.refs_0_, f32[3,2,32,128]{3,2,1,0:T(8,128)S(1)} %get-tuple-element.17.refs_1_, f32[3,48,128]{2,1,0:T(8,128)S(1)} %collective-permute-done.3.refs_2_, f32[3,6,32,128]{3,2,1,0:T(8,128)S(1)} %get-tuple-element.19.refs_3_, ...), custom_call_target="tpu_custom_call" | custom-call | tf_op jit(solution)/shard_map/pallas_call | solution.py:1213
  37.4 0.0 copy-start.2
  37.4 10.6 %all_to_all.11.arrived = f32[32,8,128]{2,1,0:T(8,128)S(1)} all-to-all(f32[32,8,128]{2,1,0:T(8,128)S(1)} %bitcast.4), channel_id=1, replica_groups=mesh['gx'=4,'gy'=8] {'gy','gx'}, dimensions={0} | all-to-all | bytes 262144 | tf_op jit(solution)/shard_map/all_to_all | solution.py:1220
  48.1 0.0 copy-done.2
  48.1 1.0 %shard_map.117 = (f32[3,6,3,384]{3,2,1,0:T(4,128)}, f32[3,2,1,128]{3,2,1,0:T(1,128)}) custom-call(f32[32,8,128]{2,1,0:T(8,128)S(1)} %all_to_all.11.arrived, bf16[256,512]{1,0:T(8,128)(2,1)S(1)} %copy-done.2), custom_call_target="tpu_custom_call" | custom-call | tf_op jit(solution)/shard_map/pallas_call | solution.py:1221
Async XLA Ops:
  2.4 16.6 %copy-start = (bf16[192,240]{1,0:T(8,128)(2,1)S(1)}, bf16[192,240]{1,0:T(8,128)(2,1)}, u32[]{:S(2)}) copy-start(bf16[192,240]{1,0:T(8,128)(2,1)} %constant.13.clone.spread.refs_7_.refs_4_) | copy-start | bytes 276484
  2.4 16.6 %copy-start.1 = (bf16[144,192]{1,0:T(8,128)(2,1)S(1)}, bf16[144,192]{1,0:T(8,128)(2,1)}, u32[]{:S(2)}) copy-start(bf16[144,192]{1,0:T(8,128)(2,1)} %constant.14.clone.collect.refs_8_.refs_5_) | copy-start | bytes 165892
  18.4 3.4 %collective-permute-start.1 = (f32[384,128]{1,0:T(8,128)S(1)}, f32[384,128]{1,0:T(8,128)S(1)}, u32[]{:S(2)}, u32[]{:S(2)}) collective-permute-start(f32[384,128]{1,0:T(8,128)S(1)} %bitcast.5), channel_id=1, source_target_pairs={{8,0},{2,8},{10,2},{4,10},{12,4},{6,12},{14,6},{22,14},{30,22},{20... | collective-permute-start | bytes 589832 | tf_op jit(solution)/shard_map/ppermute | solution.py:1191
  18.6 5.1 %collective-permute-start = (f32[384,128]{1,0:T(8,128)S(1)}, f32[384,128]{1,0:T(8,128)S(1)}, u32[]{:S(2)}, u32[]{:S(2)}) collective-permute-start(f32[384,128]{1,0:T(8,128)S(1)} %bitcast.6), channel_id=1, source_target_pairs={{9,0},{0,8},{8,2},{2,10},{10,4},{4,12},{12,6},{6,14},{14,22},{22,3... | collective-permute-start | bytes 589832 | tf_op jit(solution)/shard_map/ppermute | solution.py:1191
  19.0 4.7 %copy-start.3 = (f32[32,8]{1,0:T(8,128)S(1)}, f32[32,8]{1,0:T(8,128)}, u32[]{:S(2)}) copy-start(f32[32,8]{1,0:T(8,128)} %constant.15.clone.refs_9_) | copy-start | bytes 3076
  23.7 9.3 %copy-start.4 = (f32[32,8]{1,0:T(8,128)S(1)}, f32[32,8]{1,0:T(8,128)}, u32[]{:S(2)}) copy-start(f32[32,8]{1,0:T(8,128)} %constant.16.clone.refs_6_) | copy-start | bytes 3076
  29.1 3.9 %collective-permute-start.3 = (f32[3,48,128]{2,1,0:T(8,128)S(1)}, f32[3,48,128]{2,1,0:T(8,128)S(1)}, u32[]{:S(2)}, u32[]{:S(2)}) collective-permute-start(f32[3,48,128]{2,1,0:T(8,128)S(1)} %get-tuple-element.18), channel_id=1, source_target_pairs={{8,0},{2,8},{10,2},{4,10},{12,4},{6,12},{14,6},{22,14},{30,22},{20... | collective-permute-start | bytes 221192 | tf_op jit(solution)/shard_map/ppermute | solution.py:1191
  29.5 3.5 %collective-permute-start.2 = (f32[3,32,128]{2,1,0:T(8,128)S(1)}, f32[3,32,128]{2,1,0:T(8,128)S(1)}, u32[]{:S(2)}, u32[]{:S(2)}) collective-permute-start(f32[3,32,128]{2,1,0:T(8,128)S(1)} %get-tuple-element.16), channel_id=1, source_target_pairs={{9,0},{0,8},{8,2},{2,10},{10,4},{4,12},{12,6},{6,14},{14,22},{22,3... | collective-permute-start | bytes 147464 | tf_op jit(solution)/shard_map/ppermute | solution.py:1191
  37.4 10.6 %copy-start.2 = (bf16[256,512]{1,0:T(8,128)(2,1)S(1)}, bf16[256,512]{1,0:T(8,128)(2,1)}, u32[]{:S(2)}) copy-start(bf16[256,512]{1,0:T(8,128)(2,1)} %constant.17.clone.table) | copy-start | bytes 786436

commit v14 on v13

--- a/solution.py
+++ b/solution.py
@@ -431,11 +431,6 @@
     for first, count in spans:
         pairs = list(range(first, first + count))
         plan.append([pairs[n : n + 2] for n in range(0, count, 2)])
-    for now, later in zip(plan, plan[1:]):
-        if reads(later[0]) & set(now[-1]) and len(now[-1]) == 2:
-            now[-1:] = [now[-1][:1], now[-1][1:]]
-        if reads(later[0]) & set(now[-1]) and len(later[0]) == 2:
-            later[:1] = [later[0][:1], later[0][1:]]
     return plan
 
 
@@ -848,8 +843,8 @@
             refs = refs[5:]
         spread, collect, transfer, message, *sent, f, u, d, stiff, shares, mixed, turned = refs
         slab = Slab(width, across)
-        u[...] = jnp.zeros(u.shape, jnp.float32)
         if not prepared:
+            u[...] = jnp.zeros(u.shape, jnp.float32)
             f[...] = jnp.zeros(f.shape, jnp.float32)
         shares[...] = jnp.zeros(shares.shape, jnp.float32)
         stiff[...] = jnp.zeros(stiff.shape, jnp.float32)
@@ -1032,14 +1027,11 @@
         def pair_of(pair, fetch):
             return window_pair(slab, 2 * pair - BEFORE_B, own_layers, fetch)
 
-        u[...] = jnp.zeros(u.shape, jnp.float32)
         coarse[...] = jnp.zeros(coarse.shape, jnp.float32)
-        d[...] = jnp.zeros(d.shape, jnp.float32)
         for pair in range(PAIRS_B):
             for i in range(3):
                 block = pair_of(pair, lambda device, q: block_of(device, q, i))
-                if block is not None:
-                    u[i, pair] = block
+                u[i, pair] = jnp.zeros((32, width), jnp.float32) if block is None else block
             for n in range(7):
                 line = pair_of(pair, lambda device, q: line_of(device, q, n))
                 if line is not None:
@@ -1167,7 +1159,7 @@
         make_second_kernel(width, across, own_layers, fine_bound, coarse_bound),
         out_shape=jax.ShapeDtypeStruct((devices // 2, 2, 8, 128), f32),
         scratch_shapes=[
-            pltpu.VMEM((3, PAIRS_B + 2, 32, width), f32),
+            pltpu.VMEM((3, PAIRS_B, 32, width), f32),
             pltpu.VMEM((3, PAIRS_B, 32, width), f32),
             pltpu.VMEM((PAIRS_B, width), f32),
             pltpu.VMEM((7, PAIRS_B, width), f32),

time: 49.3 us -> 48.9 us (level)
  no operation moved by 1% of the time
where the time goes in v14:
time: 48.9 us; the launch traced here: 48.7 us
  blocking collectives  26.6 us (54%)
  Pallas kernels  13.2 us (27%)
  waiting for transfers between devices  7 us (14%)
  starting transfers between devices  1.16 us (2%)
  between operations  0.69 us (1%)
    all_to_all x1, blocking collectives, body(): lax.all_to_all(sent, everyone, 0, 0, tiled=True).reshape(devices * 12, 128)  16 us
    all_to_all x1, blocking collectives, body(): lax.all_to_all(result.reshape(devices, 8, 128), everyone, 0, 0, tiled=True)  10.6 us
    ppermute x4, waiting for transfers between devices, from_device(): return lax.ppermute(block, ('gx', 'gy'), route)  7 us
    pallas_call x1, Pallas kernels, body(): first(*blocks, jnp.asarray(spread), jnp.asarray(collect), jnp.asarray(tra...  5.35 us
    pallas_call x1, Pallas kernels, body(): second(*messages, load, jnp.asarray(spread), jnp.asarray(collect), jnp.as...  4.1 us
    pallas_call x1, Pallas kernels, body(): pack(initial, forcing, modulus, solid_list, jnp.asarray(pack_table()))  1.74 us
    ppermute x4, starting transfers between devices, from_device(): return lax.ppermute(block, ('gx', 'gy'), route)  1.16 us
    pallas_call x1, Pallas kernels, body(): return unpack(back, jnp.asarray(unpack_table()))  1.02 us
  transfers between devices with their start and end apart: 4, of which 3 were waited for; matrix products, arithmetic and copies ran while one was open for 0% of the time, Pallas kernels for 2%

profile of v14, /device:TPU:0, one launch (start us, length us, event | category | flops | bytes accessed | tf_op | source)
XLA Modules:
  0.0 48.7 jit_solution(13400658669016928631)
XLA Ops:
  0.6 1.7 %shard_map.113 = f32[384,128]{1,0:T(8,128)S(1)} custom-call(f32[3,6,3,384]{3,2,1,0:T(4,128)} %initial_at.1, f32[3,6,3,384]{3,2,1,0:T(4,128)} %forcing_at.1, f32[2,1,128]{2,1,0:T(1,128)} %modulus_at.1, s32[1,1,192]{2,1,0:T(1,128)} %listing_at.1, bf16[384,512]{1,0:T(8,128)(2,1)} %constant.12.clone.table_at), custom_call_target="tpu_custom_call" | custom-call | tf_op jit(solution)/shard_map/pallas_call | solution.py:1186
  2.4 0.0 copy-start
  2.4 0.0 copy-start.1
  2.4 16.0 %all_to_all.10 = f32[32,3,4,128]{3,2,1,0:T(4,128)S(1)} all-to-all(f32[32,3,4,128]{3,2,1,0:T(4,128)S(1)} %bitcast.3), channel_id=1, replica_groups=mesh['gx'=4,'gy'=8] {'gy','gx'}, dimensions={0} | all-to-all | bytes 393216 | tf_op jit(solution)/shard_map/all_to_all | solution.py:1188
  18.4 0.2 collective-permute-start.1
  18.6 0.4 collective-permute-start
  19.0 0.0 copy-done
  19.0 0.0 copy-done.1
  19.0 0.0 copy-start.3
  19.0 1.0 %shard_map.114 = (f32[3,3,32,128]{3,2,1,0:T(8,128)S(1)}, f32[3,2,32,128]{3,2,1,0:T(8,128)S(1)}, f32[2,128]{1,0:T(2,128)S(1)}, f32[3,2,32,128]{3,2,1,0:T(8,128)S(1)}, f32[3,2,8,128]{3,2,1,0:T(8,128)S(1)}) custom-call(f32[384,128]{1,0:T(8,128)S(1)} %bitcast.7, bf16[192,240]{1,0:T(8,128)(2,1)S(1)} %copy-done, bf16[144,192]{1,0:T(8,128)(2,1)S(1)} %copy-done.1), custom_call_target="tpu_custom_call" | custom-call | flops 400000000 | bytes 1000000 | tf_op jit(solution)/shard_map/pallas_call | solution.py:1192
  20.0 1.8 %collective-permute-done.1.refs_1_ = f32[384,128]{1,0:T(8,128)S(1)} collective-permute-done((f32[384,128]{1,0:T(8,128)S(1)}, f32[384,128]{1,0:T(8,128)S(1)}, u32[]{:S(2)}, u32[]{:S(2)}) %collective-permute-start.1) | collective-permute-done | bytes 196640 | tf_op jit(solution)/shard_map/ppermute | solution.py:1183
  21.8 1.9 %collective-permute-done.refs_0_ = f32[384,128]{1,0:T(8,128)S(1)} collective-permute-done((f32[384,128]{1,0:T(8,128)S(1)}, f32[384,128]{1,0:T(8,128)S(1)}, u32[]{:S(2)}, u32[]{:S(2)}) %collective-permute-start) | collective-permute-done | bytes 196640 | tf_op jit(solution)/shard_map/ppermute | solution.py:1183
  23.7 0.0 copy-done.3
  23.7 0.0 copy-start.4
  23.7 5.3 %shard_map.115 = (f32[3,2,32,128]{3,2,1,0:T(8,128)S(1)}, f32[3,48,128]{2,1,0:T(8,128)S(1)}, f32[3,32,128]{2,1,0:T(8,128)S(1)}, f32[3,6,32,128]{3,2,1,0:T(8,128)S(1)}) custom-call(f32[384,128]{1,0:T(8,128)S(1)} %collective-permute-done.refs_0_, f32[384,128]{1,0:T(8,128)S(1)} %collective-permute-done.1.refs_1_, ...), custom_call_target="tpu_custom_call" | custom-call | tf_op jit(solution)/shard_map/pallas_call | solution.py:1193
  29.1 0.3 collective-permute-start.3
  29.4 0.2 collective-permute-start.2
  29.6 3.3 %collective-permute-done.2.refs_0_ = f32[3,32,128]{2,1,0:T(8,128)S(1)} collective-permute-done((f32[3,32,128]{2,1,0:T(8,128)S(1)}, f32[3,32,128]{2,1,0:T(8,128)S(1)}, u32[]{:S(2)}, u32[]{:S(2)}) %collective-permute-start.2) | collective-permute-done | bytes 49184 | tf_op jit(solution)/shard_map/ppermute | solution.py:1183
  32.9 0.0 collective-permute-done.3.refs_2_
  32.9 0.0 copy-done.4
  32.9 4.1 %shard_map.116 = f32[16,2,8,128]{3,2,1,0:T(8,128)S(1)} custom-call(f32[3,32,128]{2,1,0:T(8,128)S(1)} %collective-permute-done.2.refs_0_, f32[3,2,32,128]{3,2,1,0:T(8,128)S(1)} %get-tuple-element.17.refs_1_, f32[3,48,128]{2,1,0:T(8,128)S(1)} %collective-permute-done.3.refs_2_, f32[3,6,32,128]{3,2,1,0:T(8,128)S(1)} %get-tuple-element.19.refs_3_, ...), custom_call_target="tpu_custom_call" | custom-call | tf_op jit(solution)/shard_map/pallas_call | solution.py:1205
  37.0 0.0 copy-start.2
  37.0 10.6 %all_to_all.11.arrived = f32[32,8,128]{2,1,0:T(8,128)S(1)} all-to-all(f32[32,8,128]{2,1,0:T(8,128)S(1)} %bitcast.4), channel_id=1, replica_groups=mesh['gx'=4,'gy'=8] {'gy','gx'}, dimensions={0} | all-to-all | bytes 262144 | tf_op jit(solution)/shard_map/all_to_all | solution.py:1212
  47.7 0.0 copy-done.2
  47.7 1.0 %shard_map.117 = (f32[3,6,3,384]{3,2,1,0:T(4,128)}, f32[3,2,1,128]{3,2,1,0:T(1,128)}) custom-call(f32[32,8,128]{2,1,0:T(8,128)S(1)} %all_to_all.11.arrived, bf16[256,512]{1,0:T(8,128)(2,1)S(1)} %copy-done.2), custom_call_target="tpu_custom_call" | custom-call | tf_op jit(solution)/shard_map/pallas_call | solution.py:1213
Async XLA Ops:
  2.4 16.6 %copy-start = (bf16[192,240]{1,0:T(8,128)(2,1)S(1)}, bf16[192,240]{1,0:T(8,128)(2,1)}, u32[]{:S(2)}) copy-start(bf16[192,240]{1,0:T(8,128)(2,1)} %constant.13.clone.spread.refs_7_.refs_4_) | copy-start | bytes 276484
  2.4 16.6 %copy-start.1 = (bf16[144,192]{1,0:T(8,128)(2,1)S(1)}, bf16[144,192]{1,0:T(8,128)(2,1)}, u32[]{:S(2)}) copy-start(bf16[144,192]{1,0:T(8,128)(2,1)} %constant.14.clone.collect.refs_8_.refs_5_) | copy-start | bytes 165892
  18.4 3.4 %collective-permute-start.1 = (f32[384,128]{1,0:T(8,128)S(1)}, f32[384,128]{1,0:T(8,128)S(1)}, u32[]{:S(2)}, u32[]{:S(2)}) collective-permute-start(f32[384,128]{1,0:T(8,128)S(1)} %bitcast.5), channel_id=1, source_target_pairs={{8,0},{2,8},{10,2},{4,10},{12,4},{6,12},{14,6},{22,14},{30,22},{20... | collective-permute-start | bytes 589832 | tf_op jit(solution)/shard_map/ppermute | solution.py:1183
  18.6 5.1 %collective-permute-start = (f32[384,128]{1,0:T(8,128)S(1)}, f32[384,128]{1,0:T(8,128)S(1)}, u32[]{:S(2)}, u32[]{:S(2)}) collective-permute-start(f32[384,128]{1,0:T(8,128)S(1)} %bitcast.6), channel_id=1, source_target_pairs={{9,0},{0,8},{8,2},{2,10},{10,4},{4,12},{12,6},{6,14},{14,22},{22,3... | collective-permute-start | bytes 589832 | tf_op jit(solution)/shard_map/ppermute | solution.py:1183
  19.0 4.7 %copy-start.3 = (f32[32,8]{1,0:T(8,128)S(1)}, f32[32,8]{1,0:T(8,128)}, u32[]{:S(2)}) copy-start(f32[32,8]{1,0:T(8,128)} %constant.15.clone.refs_9_) | copy-start | bytes 3076
  23.7 9.2 %copy-start.4 = (f32[32,8]{1,0:T(8,128)S(1)}, f32[32,8]{1,0:T(8,128)}, u32[]{:S(2)}) copy-start(f32[32,8]{1,0:T(8,128)} %constant.16.clone.refs_6_) | copy-start | bytes 3076
  29.1 3.9 %collective-permute-start.3 = (f32[3,48,128]{2,1,0:T(8,128)S(1)}, f32[3,48,128]{2,1,0:T(8,128)S(1)}, u32[]{:S(2)}, u32[]{:S(2)}) collective-permute-start(f32[3,48,128]{2,1,0:T(8,128)S(1)} %get-tuple-element.18), channel_id=1, source_target_pairs={{8,0},{2,8},{10,2},{4,10},{12,4},{6,12},{14,6},{22,14},{30,22},{20... | collective-permute-start | bytes 221192 | tf_op jit(solution)/shard_map/ppermute | solution.py:1183
  29.4 3.5 %collective-permute-start.2 = (f32[3,32,128]{2,1,0:T(8,128)S(1)}, f32[3,32,128]{2,1,0:T(8,128)S(1)}, u32[]{:S(2)}, u32[]{:S(2)}) collective-permute-start(f32[3,32,128]{2,1,0:T(8,128)S(1)} %get-tuple-element.16), channel_id=1, source_target_pairs={{9,0},{0,8},{8,2},{2,10},{10,4},{4,12},{12,6},{6,14},{14,22},{22,3... | collective-permute-start | bytes 147464 | tf_op jit(solution)/shard_map/ppermute | solution.py:1183
  37.0 10.6 %copy-start.2 = (bf16[256,512]{1,0:T(8,128)(2,1)S(1)}, bf16[256,512]{1,0:T(8,128)(2,1)}, u32[]{:S(2)}) copy-start(bf16[256,512]{1,0:T(8,128)(2,1)} %constant.17.clone.table) | copy-start | bytes 786436

commit v15 on v14

--- a/solution.py
+++ b/solution.py
@@ -176,6 +176,8 @@
         if node is not None:
             spread[:, row] = forward[:, node]
             collect[row, :] = backward[node, :]
+    for column in range(3):
+        spread[64 * column : 64 * column + 64, ROWS + column] = 1.0
     spread_high, spread_low = halves(spread)
     collect_high, collect_low = halves(collect)
     return (
@@ -350,15 +352,16 @@
 def unpack_kernel(order, arrived, table, out, coarse_out, layers, turned):
     devices = arrived.shape[0]
     own_layers = EZ // devices
+    together = min(own_layers, 2)
     for x in range(2):
-        for layer in range(own_layers):
-            row = (layer // 2) * 4 + x * 2 + layer % 2
+        for layer in range(0, own_layers, 2):
+            row = (layer // 2) * 4 + x * 2
             if order == sorted(order):
                 layers[x, pl.ds(layer, devices, stride=own_layers), :] = arrived[:, row, :]
                 continue
             for device, k in enumerate(order):
                 at = own_layers * k + layer
-                layers[x, at : at + 1, :] = arrived[device, row : row + 1, :]
+                layers[x, at : at + together, :] = arrived[device, row : row + together, :]
     wide = pick(jnp.concatenate([layers[0], layers[1]], 1), table[...])
     shares = pltpu.roll(wide[:, 384:512], own_layers, 0)
     turned[pl.ds(0, 128, stride=3), :] = wide[:, 0:128] + shares
@@ -465,7 +468,7 @@
             v = self.lanes(v, 2 * x + self.y_step * y + z)
         return jnp.where(self.bottom, 0.0, v) if x else v
 
-    def gather(self, here, ahead):
+    def gather(self, component, here, ahead):
         row = self.row
         g0, g1, g2, g3 = here[0:8], here[8:16], here[16:24], here[24:32]
         a0 = ahead[0:8]
@@ -485,7 +488,7 @@
                 jnp.where(row == 7, xz, z0),
                 jnp.where(row < 4, self.from_next(g1, 1, 0), self.from_next(g1, 0, 1)),
                 edges,
-                jnp.zeros_like(g0),
+                jnp.where(row == component, 1.0, 0.0),
             ],
             0,
         )
@@ -514,9 +517,8 @@
         own1 = g1 + jnp.where(row < 4, self.onto_next(sides, 1, 0), self.onto_next(sides, 0, 1))
         share2 = jnp.where(self.even, behind[1], self.onto_next(g3, 0, 0, 1))
         own2 = g2 + jnp.where(row < 4, share2, 0.0)
-        own3 = jnp.where(row < 4, 0.0, g3)
         moved = (above(-1), self.onto_next(g3, 0, 0, -1))
-        return jnp.concatenate([self.twinned(own0), own1, own2, own3], 0), moved
+        return jnp.concatenate([self.twinned(own0), own1, own2, g3], 0), moved
 
     def twinned(self, v):
         twins = jnp.where(self.row == 7, pltpu.roll(v, 7, 0), 0.0)
@@ -531,7 +533,9 @@
 
     def gradient(self, u, spread, pairs):
         parts = [
-            high_low(self.gather(u[i, pair], u[i, pair + 1])) for i in range(3) for pair in pairs
+            high_low(self.gather(i, u[i, pair], u[i, pair + 1]))
+            for i in range(3)
+            for pair in pairs
         ]
         return jnp.dot(
             spread[...],
@@ -551,7 +555,6 @@
                             64 * e + rows * r : 64 * e + rows * (r + 1),
                             width * (count * i + q) : width * (count * i + q + 1),
                         ]
-                        + (1.0 if i == e else 0.0)
                         for e in range(3)
                     ]
                     for i in range(3)

time: 48.9 us -> 48.6 us (level)
  no operation moved by 1% of the time
where the time goes in v15:
time: 48.6 us; the launch traced here: 48.4 us
  blocking collectives  26.6 us (55%)
  Pallas kernels  12.9 us (27%)
  waiting for transfers between devices  7.03 us (14%)
  starting transfers between devices  1.16 us (2%)
  between operations  0.69 us (1%)
    all_to_all x1, blocking collectives, body(): lax.all_to_all(sent, everyone, 0, 0, tiled=True).reshape(devices * 12, 128)  16 us
    all_to_all x1, blocking collectives, body(): lax.all_to_all(result.reshape(devices, 8, 128), everyone, 0, 0, tiled=True)  10.6 us
    ppermute x4, waiting for transfers between devices, from_device(): return lax.ppermute(block, ('gx', 'gy'), route)  7.03 us
    pallas_call x1, Pallas kernels, body(): first(*blocks, jnp.asarray(spread), jnp.asarray(collect), jnp.asarray(tra...  5.21 us
    pallas_call x1, Pallas kernels, body(): second(*messages, load, jnp.asarray(spread), jnp.asarray(collect), jnp.as...  3.98 us
    pallas_call x1, Pallas kernels, body(): pack(initial, forcing, modulus, solid_list, jnp.asarray(pack_table()))  1.74 us
    ppermute x4, starting transfers between devices, from_device(): return lax.ppermute(block, ('gx', 'gy'), route)  1.16 us
    pallas_call x1, Pallas kernels, body(): return unpack(back, jnp.asarray(unpack_table()))  1.02 us
  transfers between devices with their start and end apart: 4, of which 3 were waited for; matrix products, arithmetic and copies ran while one was open for 0% of the time, Pallas kernels for 2%

profile of v15, /device:TPU:0, one launch (start us, length us, event | category | flops | bytes accessed | tf_op | source)
XLA Modules:
  0.0 48.4 jit_solution(7440677140123009819)
XLA Ops:
  0.6 1.7 %shard_map.113 = f32[384,128]{1,0:T(8,128)S(1)} custom-call(f32[3,6,3,384]{3,2,1,0:T(4,128)} %initial_at.1, f32[3,6,3,384]{3,2,1,0:T(4,128)} %forcing_at.1, f32[2,1,128]{2,1,0:T(1,128)} %modulus_at.1, s32[1,1,192]{2,1,0:T(1,128)} %listing_at.1, bf16[384,512]{1,0:T(8,128)(2,1)} %constant.12.clone.table_at), custom_call_target="tpu_custom_call" | custom-call | tf_op jit(solution)/shard_map/pallas_call | solution.py:1189
  2.4 0.0 copy-start
  2.4 0.0 copy-start.1
  2.4 16.0 %all_to_all.10 = f32[32,3,4,128]{3,2,1,0:T(4,128)S(1)} all-to-all(f32[32,3,4,128]{3,2,1,0:T(4,128)S(1)} %bitcast.3), channel_id=1, replica_groups=mesh['gx'=4,'gy'=8] {'gy','gx'}, dimensions={0} | all-to-all | bytes 393216 | tf_op jit(solution)/shard_map/all_to_all | solution.py:1191
  18.4 0.2 collective-permute-start.1
  18.6 0.4 collective-permute-start
  19.0 0.0 copy-done
  19.0 0.0 copy-done.1
  19.0 0.0 copy-start.3
  19.0 1.0 %shard_map.114 = (f32[3,3,32,128]{3,2,1,0:T(8,128)S(1)}, f32[3,2,32,128]{3,2,1,0:T(8,128)S(1)}, f32[2,128]{1,0:T(2,128)S(1)}, f32[3,2,32,128]{3,2,1,0:T(8,128)S(1)}, f32[3,2,8,128]{3,2,1,0:T(8,128)S(1)}) custom-call(f32[384,128]{1,0:T(8,128)S(1)} %bitcast.7, bf16[192,240]{1,0:T(8,128)(2,1)S(1)} %copy-done, bf16[144,192]{1,0:T(8,128)(2,1)S(1)} %copy-done.1), custom_call_target="tpu_custom_call" | custom-call | flops 400000000 | bytes 1000000 | tf_op jit(solution)/shard_map/pallas_call | solution.py:1195
  20.0 1.8 %collective-permute-done.1.refs_1_ = f32[384,128]{1,0:T(8,128)S(1)} collective-permute-done((f32[384,128]{1,0:T(8,128)S(1)}, f32[384,128]{1,0:T(8,128)S(1)}, u32[]{:S(2)}, u32[]{:S(2)}) %collective-permute-start.1) | collective-permute-done | bytes 196640 | tf_op jit(solution)/shard_map/ppermute | solution.py:1186
  21.8 1.9 %collective-permute-done.refs_0_ = f32[384,128]{1,0:T(8,128)S(1)} collective-permute-done((f32[384,128]{1,0:T(8,128)S(1)}, f32[384,128]{1,0:T(8,128)S(1)}, u32[]{:S(2)}, u32[]{:S(2)}) %collective-permute-start) | collective-permute-done | bytes 196640 | tf_op jit(solution)/shard_map/ppermute | solution.py:1186
  23.7 0.0 copy-done.3
  23.7 0.0 copy-start.4
  23.7 5.2 %shard_map.115 = (f32[3,2,32,128]{3,2,1,0:T(8,128)S(1)}, f32[3,48,128]{2,1,0:T(8,128)S(1)}, f32[3,32,128]{2,1,0:T(8,128)S(1)}, f32[3,6,32,128]{3,2,1,0:T(8,128)S(1)}) custom-call(f32[384,128]{1,0:T(8,128)S(1)} %collective-permute-done.refs_0_, f32[384,128]{1,0:T(8,128)S(1)} %collective-permute-done.1.refs_1_, ...), custom_call_target="tpu_custom_call" | custom-call | tf_op jit(solution)/shard_map/pallas_call | solution.py:1196
  28.9 0.4 collective-permute-start.3
  29.3 0.2 collective-permute-start.2
  29.5 3.3 %collective-permute-done.2.refs_0_ = f32[3,32,128]{2,1,0:T(8,128)S(1)} collective-permute-done((f32[3,32,128]{2,1,0:T(8,128)S(1)}, f32[3,32,128]{2,1,0:T(8,128)S(1)}, u32[]{:S(2)}, u32[]{:S(2)}) %collective-permute-start.2) | collective-permute-done | bytes 49184 | tf_op jit(solution)/shard_map/ppermute | solution.py:1186
  32.8 0.0 collective-permute-done.3.refs_2_
  32.8 0.0 copy-done.4
  32.8 4.0 %shard_map.116 = f32[16,2,8,128]{3,2,1,0:T(8,128)S(1)} custom-call(f32[3,32,128]{2,1,0:T(8,128)S(1)} %collective-permute-done.2.refs_0_, f32[3,2,32,128]{3,2,1,0:T(8,128)S(1)} %get-tuple-element.17.refs_1_, f32[3,48,128]{2,1,0:T(8,128)S(1)} %collective-permute-done.3.refs_2_, f32[3,6,32,128]{3,2,1,0:T(8,128)S(1)} %get-tuple-element.19.refs_3_, ...), custom_call_target="tpu_custom_call" | custom-call | tf_op jit(solution)/shard_map/pallas_call | solution.py:1208
  36.8 0.0 copy-start.2
  36.8 10.6 %all_to_all.11.arrived = f32[32,8,128]{2,1,0:T(8,128)S(1)} all-to-all(f32[32,8,128]{2,1,0:T(8,128)S(1)} %bitcast.4), channel_id=1, replica_groups=mesh['gx'=4,'gy'=8] {'gy','gx'}, dimensions={0} | all-to-all | bytes 262144 | tf_op jit(solution)/shard_map/all_to_all | solution.py:1215
  47.4 0.0 copy-done.2
  47.4 1.0 %shard_map.117 = (f32[3,6,3,384]{3,2,1,0:T(4,128)}, f32[3,2,1,128]{3,2,1,0:T(1,128)}) custom-call(f32[32,8,128]{2,1,0:T(8,128)S(1)} %all_to_all.11.arrived, bf16[256,512]{1,0:T(8,128)(2,1)S(1)} %copy-done.2), custom_call_target="tpu_custom_call" | custom-call | tf_op jit(solution)/shard_map/pallas_call | solution.py:1216
Async XLA Ops:
  2.4 16.6 %copy-start = (bf16[192,240]{1,0:T(8,128)(2,1)S(1)}, bf16[192,240]{1,0:T(8,128)(2,1)}, u32[]{:S(2)}) copy-start(bf16[192,240]{1,0:T(8,128)(2,1)} %constant.13.clone.spread.refs_7_.refs_4_) | copy-start | bytes 276484
  2.4 16.6 %copy-start.1 = (bf16[144,192]{1,0:T(8,128)(2,1)S(1)}, bf16[144,192]{1,0:T(8,128)(2,1)}, u32[]{:S(2)}) copy-start(bf16[144,192]{1,0:T(8,128)(2,1)} %constant.14.clone.collect.refs_8_.refs_5_) | copy-start | bytes 165892
  18.4 3.4 %collective-permute-start.1 = (f32[384,128]{1,0:T(8,128)S(1)}, f32[384,128]{1,0:T(8,128)S(1)}, u32[]{:S(2)}, u32[]{:S(2)}) collective-permute-start(f32[384,128]{1,0:T(8,128)S(1)} %bitcast.5), channel_id=1, source_target_pairs={{8,0},{2,8},{10,2},{4,10},{12,4},{6,12},{14,6},{22,14},{30,22},{20... | collective-permute-start | bytes 589832 | tf_op jit(solution)/shard_map/ppermute | solution.py:1186
  18.6 5.1 %collective-permute-start = (f32[384,128]{1,0:T(8,128)S(1)}, f32[384,128]{1,0:T(8,128)S(1)}, u32[]{:S(2)}, u32[]{:S(2)}) collective-permute-start(f32[384,128]{1,0:T(8,128)S(1)} %bitcast.6), channel_id=1, source_target_pairs={{9,0},{0,8},{8,2},{2,10},{10,4},{4,12},{12,6},{6,14},{14,22},{22,3... | collective-permute-start | bytes 589832 | tf_op jit(solution)/shard_map/ppermute | solution.py:1186
  19.0 4.7 %copy-start.3 = (f32[32,8]{1,0:T(8,128)S(1)}, f32[32,8]{1,0:T(8,128)}, u32[]{:S(2)}) copy-start(f32[32,8]{1,0:T(8,128)} %constant.15.clone.refs_9_) | copy-start | bytes 3076
  23.7 9.1 %copy-start.4 = (f32[32,8]{1,0:T(8,128)S(1)}, f32[32,8]{1,0:T(8,128)}, u32[]{:S(2)}) copy-start(f32[32,8]{1,0:T(8,128)} %constant.16.clone.refs_6_) | copy-start | bytes 3076
  28.9 3.9 %collective-permute-start.3 = (f32[3,48,128]{2,1,0:T(8,128)S(1)}, f32[3,48,128]{2,1,0:T(8,128)S(1)}, u32[]{:S(2)}, u32[]{:S(2)}) collective-permute-start(f32[3,48,128]{2,1,0:T(8,128)S(1)} %get-tuple-element.18), channel_id=1, source_target_pairs={{8,0},{2,8},{10,2},{4,10},{12,4},{6,12},{14,6},{22,14},{30,22},{20... | collective-permute-start | bytes 221192 | tf_op jit(solution)/shard_map/ppermute | solution.py:1186
  29.3 3.5 %collective-permute-start.2 = (f32[3,32,128]{2,1,0:T(8,128)S(1)}, f32[3,32,128]{2,1,0:T(8,128)S(1)}, u32[]{:S(2)}, u32[]{:S(2)}) collective-permute-start(f32[3,32,128]{2,1,0:T(8,128)S(1)} %get-tuple-element.16), channel_id=1, source_target_pairs={{9,0},{0,8},{8,2},{2,10},{10,4},{4,12},{12,6},{6,14},{14,22},{22,3... | collective-permute-start | bytes 147464 | tf_op jit(solution)/shard_map/ppermute | solution.py:1186
  36.8 10.6 %copy-start.2 = (bf16[256,512]{1,0:T(8,128)(2,1)S(1)}, bf16[256,512]{1,0:T(8,128)(2,1)}, u32[]{:S(2)}) copy-start(bf16[256,512]{1,0:T(8,128)(2,1)} %constant.17.clone.table) | copy-start | bytes 786436

commit v16 on v15

--- a/solution.py
+++ b/solution.py
@@ -184,6 +184,22 @@
         np.concatenate([spread_high, spread_high, spread_low], 1),
         np.concatenate([collect_high, collect_low], 0),
         bound,
+    )
+
+
+def corner_tables():
+    anchors = [0.0, inner_anchors[0], inner_anchors[1], 1.0]
+    backward = build_tables(anchors, 4)[1]
+    reach = np.stack([1.0 - np.array(anchors), np.array(anchors)])
+    weights = outer_three(reach, reach, reach).reshape(8, 64)
+    held = np.arange(64) < 16
+    from_stress = np.concatenate([weights @ backward, np.where(held, 0.0, weights) @ backward], 0)
+    from_loads = np.zeros((16, 32))
+    from_loads[:8] = transfer_table()[0].T
+    loads_high, loads_low = halves(from_loads)
+    return (
+        np.concatenate(halves(from_stress), 0),
+        np.concatenate([loads_high, loads_high, loads_low], 1),
     )
 
 
@@ -357,7 +373,9 @@
         for layer in range(0, own_layers, 2):
             row = (layer // 2) * 4 + x * 2
             if order == sorted(order):
-                layers[x, pl.ds(layer, devices, stride=own_layers), :] = arrived[:, row, :]
+                for n in range(together):
+                    at = pl.ds(layer + n, devices, stride=own_layers)
+                    layers[x, at, :] = arrived[:, row + n, :]
                 continue
             for device, k in enumerate(order):
                 at = own_layers * k + layer
@@ -543,8 +561,8 @@
             preferred_element_type=jnp.float32,
         )
 
-    def force(self, gradient, stiff, collect, pairs):
-        width, count = self.width, len(pairs)
+    def stresses(self, gradient, count):
+        width = self.width
         rows = 16
         high, low = {}, {}
         for q in range(count):
@@ -574,10 +592,14 @@
                 0,
             )
 
-        force = jnp.dot(collect[...], whole(high), preferred_element_type=jnp.float32)
-        force = force[0:ROWS] + (
-            force[ROWS:]
-            + jnp.dot(collect[0:ROWS], whole(low), preferred_element_type=jnp.float32)
+        return whole(high), whole(low)
+
+    def force(self, gradient, stiff, collect, pairs):
+        high, low = self.stresses(gradient, len(pairs))
+        rows = collect.shape[0] // 2
+        force = jnp.dot(collect[...], high, preferred_element_type=jnp.float32)
+        force = force[0:rows] + (
+            force[rows:] + jnp.dot(collect[0:rows], low, preferred_element_type=jnp.float32)
         )
         stiffness = [stiff[pair : pair + 1, :] for pair in pairs]
         return force * jnp.concatenate(stiffness * 3, 1)
@@ -844,7 +866,8 @@
         if prepared:
             own_u, own_f, own_stiff, own_forces, own_moved = refs[:5]
             refs = refs[5:]
-        spread, collect, transfer, message, *sent, f, u, d, stiff, shares, mixed, turned = refs
+        spread, collect, corners, from_loads, message, *sent, f = refs[: -6]
+        u, d, stiff, shares, mixed, turned = refs[-6:]
         slab = Slab(width, across)
         if not prepared:
             u[...] = jnp.zeros(u.shape, jnp.float32)
@@ -887,21 +910,31 @@
                 [(own_moved[i, 0], own_moved[i, 1]) for i in range(3)],
             )
 
-        weights = [jnp.broadcast_to(transfer[:, n : n + 1], (32, width)) for n in range(8)]
-
-        def restrict(pair, forces):
-            for i in range(3):
-                rest = slab.keep * (f[i, pair] - forces[i])
-                for n in range(8):
-                    part = rest * weights[n]
-                    part = (part[0:8] + part[8:16]) + (part[16:24] + part[24:32])
-                    shares[i, n, pl.ds(pair, 1), :] = jnp.sum(part, axis=0, keepdims=True)
-
+        first, count = spans[3]
+        blocks = [
+            high_low(slab.keep * f[i, pair]) for pair in range(first, first + count) for i in range(3)
+        ]
+        loads = jnp.dot(
+            from_loads[...],
+            jnp.concatenate([jnp.concatenate([h, l, h], 0) for h, l in blocks], 1),
+            preferred_element_type=jnp.float32,
+        )
         jobs = slab.smoothing(u, f, 0, d, spans[0:3], fine_bound)
-        slab.run(u, stiff, spread, collect, jobs + [(*spans[3], restrict)], given)
+        slab.run(u, stiff, spread, collect, jobs, given)
+        steps = plan_steps([spans[3]])[0]
+        gradients = [slab.gradient(u, spread, pairs) for pairs in steps]
+        for pairs, gradient in zip(steps, gradients):
+            force = slab.force(gradient, stiff, corners, pairs)
+            for q, pair in enumerate(pairs):
+                for i in range(3):
+                    at = (len(pairs) * i + q) * width
+                    load_at = (3 * (pair - first) + i) * width
+                    part = force[:, at : at + width]
+                    part = jnp.where(slab.bottom, part[8:16], part[0:8])
+                    shares[i, pair] = loads[0:8, load_at : load_at + width] - part
 
         restricted = [
-            slab.assemble({corner: shares[i, n] for n, corner in enumerate(CORNERS)})
+            slab.assemble({corner: shares[i, :, n, :] for n, corner in enumerate(CORNERS)})
             for i in range(3)
         ]
         def line(rows, q):
@@ -1099,7 +1132,8 @@
     whole, outer = sources_of(own_layers)
     spread, collect, fine_bound = element_tables()
     coarse_bound = build_tables([0.0, 1.0], 2)[2]
-    transfer, transfer_back = transfer_table()
+    transfer_back = transfer_table()[1]
+    corners, from_loads = corner_tables()
     wide = pltpu.CompilerParams(vmem_limit_bytes=60 * 1024 * 1024)
     limit = pltpu.CompilerParams(vmem_limit_bytes=48 * 1024 * 1024)
     f32 = jnp.float32
@@ -1197,7 +1231,8 @@
             *blocks,
             jnp.asarray(spread),
             jnp.asarray(collect),
-            jnp.asarray(transfer),
+            jnp.asarray(corners),
+            jnp.asarray(from_loads),
         )
         if prepared:
             down, up = edges

time: 48.6 us -> 48.9 us (level)
  local copies, waits for them, and re-layouts: 0.03 us -> 0.71 us
  Pallas kernels: 12.9 us -> 12.4 us
    unnamed x10 -> x12, local copies, waits for them, and re-layouts: 0.03 us -> 0.71 us
where the time goes in v16:
time: 48.9 us; the launch traced here: 48.6 us
  blocking collectives  26.6 us (54%)
  Pallas kernels  12.4 us (25%)
  waiting for transfers between devices  7.02 us (14%)
  starting transfers between devices  1.16 us (2%)
  local copies, waits for them, and re-layouts  0.71 us (1%)
  between operations  0.69 us (1%)
    all_to_all x1, blocking collectives, body(): lax.all_to_all(sent, everyone, 0, 0, tiled=True).reshape(devices * 12, 128)  16 us
    all_to_all x1, blocking collectives, body(): lax.all_to_all(result.reshape(devices, 8, 128), everyone, 0, 0, tiled=True)  10.6 us
    ppermute x4, waiting for transfers between devices, from_device(): return lax.ppermute(block, ('gx', 'gy'), route)  7.02 us
    pallas_call x1, Pallas kernels, body(): first(*blocks, jnp.asarray(spread), jnp.asarray(collect), jnp.asarray(cor...  4.78 us
    pallas_call x1, Pallas kernels, body(): second(*messages, load, jnp.asarray(spread), jnp.asarray(collect), jnp.as...  3.92 us
    pallas_call x1, Pallas kernels, body(): pack(initial, forcing, modulus, solid_list, jnp.asarray(pack_table()))  1.74 us
    ppermute x4, starting transfers between devices, from_device(): return lax.ppermute(block, ('gx', 'gy'), route)  1.16 us
    pallas_call x1, Pallas kernels, body(): return unpack(back, jnp.asarray(unpack_table()))  1.02 us
  transfers between devices with their start and end apart: 4, of which 3 were waited for; matrix products, arithmetic and copies ran while one was open for 0% of the time, Pallas kernels for 2%

profile of v16, /device:TPU:0, one launch (start us, length us, event | category | flops | bytes accessed | tf_op | source)
XLA Modules:
  0.0 48.6 jit_solution(8771624303051292060)
XLA Ops:
  0.6 1.7 %shard_map.122 = f32[384,128]{1,0:T(8,128)S(1)} custom-call(f32[3,6,3,384]{3,2,1,0:T(4,128)} %initial_at.1, f32[3,6,3,384]{3,2,1,0:T(4,128)} %forcing_at.1, f32[2,1,128]{2,1,0:T(1,128)} %modulus_at.1, s32[1,1,192]{2,1,0:T(1,128)} %listing_at.1, bf16[384,512]{1,0:T(8,128)(2,1)} %constant.14.clone.table_at), custom_call_target="tpu_custom_call" | custom-call | tf_op jit(solution)/shard_map/pallas_call | solution.py:1223
  2.4 0.0 copy-start
  2.4 0.0 copy-start.1
  2.4 16.0 %all_to_all.10 = f32[32,3,4,128]{3,2,1,0:T(4,128)S(1)} all-to-all(f32[32,3,4,128]{3,2,1,0:T(4,128)S(1)} %bitcast.3), channel_id=1, replica_groups=mesh['gx'=4,'gy'=8] {'gy','gx'}, dimensions={0} | all-to-all | bytes 393216 | tf_op jit(solution)/shard_map/all_to_all | solution.py:1225
  18.4 0.2 collective-permute-start.1
  18.6 0.4 collective-permute-start
  19.0 0.0 copy-done
  19.0 0.0 copy-done.1
  19.0 0.0 copy-start.3
  19.0 1.0 %shard_map.123 = (f32[3,3,32,128]{3,2,1,0:T(8,128)S(1)}, f32[3,2,32,128]{3,2,1,0:T(8,128)S(1)}, f32[2,128]{1,0:T(2,128)S(1)}, f32[3,2,32,128]{3,2,1,0:T(8,128)S(1)}, f32[3,2,8,128]{3,2,1,0:T(8,128)S(1)}) custom-call(f32[384,128]{1,0:T(8,128)S(1)} %bitcast.7, bf16[192,240]{1,0:T(8,128)(2,1)S(1)} %copy-done, bf16[144,192]{1,0:T(8,128)(2,1)S(1)} %copy-done.1), custom_call_target="tpu_custom_call" | custom-call | flops 400000000 | bytes 1000000 | tf_op jit(solution)/shard_map/pallas_call | solution.py:1229
  20.0 1.8 %collective-permute-done.1.refs_1_ = f32[384,128]{1,0:T(8,128)S(1)} collective-permute-done((f32[384,128]{1,0:T(8,128)S(1)}, f32[384,128]{1,0:T(8,128)S(1)}, u32[]{:S(2)}, u32[]{:S(2)}) %collective-permute-start.1) | collective-permute-done | bytes 196640 | tf_op jit(solution)/shard_map/ppermute | solution.py:1220
  21.8 1.9 %collective-permute-done.refs_0_ = f32[384,128]{1,0:T(8,128)S(1)} collective-permute-done((f32[384,128]{1,0:T(8,128)S(1)}, f32[384,128]{1,0:T(8,128)S(1)}, u32[]{:S(2)}, u32[]{:S(2)}) %collective-permute-start) | collective-permute-done | bytes 196640 | tf_op jit(solution)/shard_map/ppermute | solution.py:1220
  23.7 0.0 copy-start.5
  23.7 0.0 copy-done.3
  23.7 0.7 %copy-done.5 = bf16[16,96]{1,0:T(8,128)(2,1)S(1)} copy-done((bf16[16,96]{1,0:T(8,128)(2,1)S(1)}, bf16[16,96]{1,0:T(8,128)(2,1)}, u32[]{:S(2)}) %copy-start.5) | copy-done | bytes 3096
  24.4 0.0 copy-start.4
  24.4 4.8 %shard_map.124 = (f32[3,2,32,128]{3,2,1,0:T(8,128)S(1)}, f32[3,48,128]{2,1,0:T(8,128)S(1)}, f32[3,32,128]{2,1,0:T(8,128)S(1)}, f32[3,6,32,128]{3,2,1,0:T(8,128)S(1)}) custom-call(f32[384,128]{1,0:T(8,128)S(1)} %collective-permute-done.refs_0_, f32[384,128]{1,0:T(8,128)S(1)} %collective-permute-done.1.refs_1_, ...), custom_call_target="tpu_custom_call" | custom-call | tf_op jit(solution)/shard_map/pallas_call | solution.py:1230
  29.2 0.3 collective-permute-start.3
  29.5 0.2 collective-permute-start.2
  29.7 3.3 %collective-permute-done.2.refs_0_ = f32[3,32,128]{2,1,0:T(8,128)S(1)} collective-permute-done((f32[3,32,128]{2,1,0:T(8,128)S(1)}, f32[3,32,128]{2,1,0:T(8,128)S(1)}, u32[]{:S(2)}, u32[]{:S(2)}) %collective-permute-start.2) | collective-permute-done | bytes 49184 | tf_op jit(solution)/shard_map/ppermute | solution.py:1220
  33.0 0.0 collective-permute-done.3.refs_2_
  33.0 0.0 copy-done.4
  33.0 3.9 %shard_map.125 = f32[16,2,8,128]{3,2,1,0:T(8,128)S(1)} custom-call(f32[3,32,128]{2,1,0:T(8,128)S(1)} %collective-permute-done.2.refs_0_, f32[3,2,32,128]{3,2,1,0:T(8,128)S(1)} %get-tuple-element.17.refs_1_, f32[3,48,128]{2,1,0:T(8,128)S(1)} %collective-permute-done.3.refs_2_, f32[3,6,32,128]{3,2,1,0:T(8,128)S(1)} %get-tuple-element.19.refs_3_, ...), custom_call_target="tpu_custom_call" | custom-call | tf_op jit(solution)/shard_map/pallas_call | solution.py:1243
  37.0 0.0 copy-start.2
  37.0 10.6 %all_to_all.11.arrived = f32[32,8,128]{2,1,0:T(8,128)S(1)} all-to-all(f32[32,8,128]{2,1,0:T(8,128)S(1)} %bitcast.4), channel_id=1, replica_groups=mesh['gx'=4,'gy'=8] {'gy','gx'}, dimensions={0} | all-to-all | bytes 262144 | tf_op jit(solution)/shard_map/all_to_all | solution.py:1250
  47.6 0.0 copy-done.2
  47.6 1.0 %shard_map.126 = (f32[3,6,3,384]{3,2,1,0:T(4,128)}, f32[3,2,1,128]{3,2,1,0:T(1,128)}) custom-call(f32[32,8,128]{2,1,0:T(8,128)S(1)} %all_to_all.11.arrived, bf16[256,512]{1,0:T(8,128)(2,1)S(1)} %copy-done.2), custom_call_target="tpu_custom_call" | custom-call | tf_op jit(solution)/shard_map/pallas_call | solution.py:1251
Async XLA Ops:
  2.4 16.6 %copy-start = (bf16[192,240]{1,0:T(8,128)(2,1)S(1)}, bf16[192,240]{1,0:T(8,128)(2,1)}, u32[]{:S(2)}) copy-start(bf16[192,240]{1,0:T(8,128)(2,1)} %constant.15.clone.spread.refs_7_.refs_4_) | copy-start | bytes 276484
  2.4 16.6 %copy-start.1 = (bf16[144,192]{1,0:T(8,128)(2,1)S(1)}, bf16[144,192]{1,0:T(8,128)(2,1)}, u32[]{:S(2)}) copy-start(bf16[144,192]{1,0:T(8,128)(2,1)} %constant.16.clone.collect.refs_8_.refs_5_) | copy-start | bytes 165892
  18.4 3.4 %collective-permute-start.1 = (f32[384,128]{1,0:T(8,128)S(1)}, f32[384,128]{1,0:T(8,128)S(1)}, u32[]{:S(2)}, u32[]{:S(2)}) collective-permute-start(f32[384,128]{1,0:T(8,128)S(1)} %bitcast.5), channel_id=1, source_target_pairs={{8,0},{2,8},{10,2},{4,10},{12,4},{6,12},{14,6},{22,14},{30,22},{20... | collective-permute-start | bytes 589832 | tf_op jit(solution)/shard_map/ppermute | solution.py:1220
  18.6 5.1 %collective-permute-start = (f32[384,128]{1,0:T(8,128)S(1)}, f32[384,128]{1,0:T(8,128)S(1)}, u32[]{:S(2)}, u32[]{:S(2)}) collective-permute-start(f32[384,128]{1,0:T(8,128)S(1)} %bitcast.6), channel_id=1, source_target_pairs={{9,0},{0,8},{8,2},{2,10},{10,4},{4,12},{12,6},{6,14},{14,22},{22,3... | collective-permute-start | bytes 589832 | tf_op jit(solution)/shard_map/ppermute | solution.py:1220
  19.0 4.7 %copy-start.3 = (bf16[32,192]{1,0:T(8,128)(2,1)S(1)}, bf16[32,192]{1,0:T(8,128)(2,1)}, u32[]{:S(2)}) copy-start(bf16[32,192]{1,0:T(8,128)(2,1)} %constant.17.clone.refs_9_) | copy-start | bytes 36868
  23.7 0.7 %copy-start.5 = (bf16[16,96]{1,0:T(8,128)(2,1)S(1)}, bf16[16,96]{1,0:T(8,128)(2,1)}, u32[]{:S(2)}) copy-start(bf16[16,96]{1,0:T(8,128)(2,1)} %constant.18.clone.refs_10_) | copy-start | bytes 9220
  24.4 8.7 %copy-start.4 = (f32[32,8]{1,0:T(8,128)S(1)}, f32[32,8]{1,0:T(8,128)}, u32[]{:S(2)}) copy-start(f32[32,8]{1,0:T(8,128)} %constant.19.clone.refs_6_) | copy-start | bytes 3076
  29.2 3.9 %collective-permute-start.3 = (f32[3,48,128]{2,1,0:T(8,128)S(1)}, f32[3,48,128]{2,1,0:T(8,128)S(1)}, u32[]{:S(2)}, u32[]{:S(2)}) collective-permute-start(f32[3,48,128]{2,1,0:T(8,128)S(1)} %get-tuple-element.18), channel_id=1, source_target_pairs={{8,0},{2,8},{10,2},{4,10},{12,4},{6,12},{14,6},{22,14},{30,22},{20... | collective-permute-start | bytes 221192 | tf_op jit(solution)/shard_map/ppermute | solution.py:1220
  29.5 3.5 %collective-permute-start.2 = (f32[3,32,128]{2,1,0:T(8,128)S(1)}, f32[3,32,128]{2,1,0:T(8,128)S(1)}, u32[]{:S(2)}, u32[]{:S(2)}) collective-permute-start(f32[3,32,128]{2,1,0:T(8,128)S(1)} %get-tuple-element.16), channel_id=1, source_target_pairs={{9,0},{0,8},{8,2},{2,10},{10,4},{4,12},{12,6},{6,14},{14,22},{22,3... | collective-permute-start | bytes 147464 | tf_op jit(solution)/shard_map/ppermute | solution.py:1220
  37.0 10.6 %copy-start.2 = (bf16[256,512]{1,0:T(8,128)(2,1)S(1)}, bf16[256,512]{1,0:T(8,128)(2,1)}, u32[]{:S(2)}) copy-start(bf16[256,512]{1,0:T(8,128)(2,1)} %constant.20.clone.table) | copy-start | bytes 786436

commit v17 on v16

--- a/solution.py
+++ b/solution.py
@@ -54,6 +54,7 @@
 )
 ROWS = len(ELEMENT_ROWS)
 DEPTH = 80
+POINT_ROWS = 192
 CORNERS = [(a, b, c) for a in range(2) for b in range(2) for c in range(2)]
 
 
@@ -556,7 +557,7 @@
             for pair in pairs
         ]
         return jnp.dot(
-            spread[...],
+            spread[0:POINT_ROWS, :],
             jnp.concatenate([jnp.concatenate([h, l, h], 0) for h, l in parts], 1),
             preferred_element_type=jnp.float32,
         )
@@ -594,12 +595,12 @@
 
         return whole(high), whole(low)
 
-    def force(self, gradient, stiff, collect, pairs):
+    def force(self, gradient, stiff, collect, pairs, first=0, rows=ROWS):
         high, low = self.stresses(gradient, len(pairs))
-        rows = collect.shape[0] // 2
-        force = jnp.dot(collect[...], high, preferred_element_type=jnp.float32)
+        both = collect[first : first + 2 * rows, :]
+        force = jnp.dot(both, high, preferred_element_type=jnp.float32)
         force = force[0:rows] + (
-            force[rows:] + jnp.dot(collect[0:rows], low, preferred_element_type=jnp.float32)
+            force[rows:] + jnp.dot(both[0:rows], low, preferred_element_type=jnp.float32)
         )
         stiffness = [stiff[pair : pair + 1, :] for pair in pairs]
         return force * jnp.concatenate(stiffness * 3, 1)
@@ -866,7 +867,7 @@
         if prepared:
             own_u, own_f, own_stiff, own_forces, own_moved = refs[:5]
             refs = refs[5:]
-        spread, collect, corners, from_loads, message, *sent, f = refs[: -6]
+        spread, collect, message, *sent, f = refs[:-6]
         u, d, stiff, shares, mixed, turned = refs[-6:]
         slab = Slab(width, across)
         if not prepared:
@@ -915,7 +916,7 @@
             high_low(slab.keep * f[i, pair]) for pair in range(first, first + count) for i in range(3)
         ]
         loads = jnp.dot(
-            from_loads[...],
+            spread[POINT_ROWS:, 0:96],
             jnp.concatenate([jnp.concatenate([h, l, h], 0) for h, l in blocks], 1),
             preferred_element_type=jnp.float32,
         )
@@ -924,7 +925,7 @@
         steps = plan_steps([spans[3]])[0]
         gradients = [slab.gradient(u, spread, pairs) for pairs in steps]
         for pairs, gradient in zip(steps, gradients):
-            force = slab.force(gradient, stiff, corners, pairs)
+            force = slab.force(gradient, stiff, collect, pairs, 2 * ROWS, 16)
             for q, pair in enumerate(pairs):
                 for i in range(3):
                     at = (len(pairs) * i + q) * width
@@ -1134,6 +1135,9 @@
     coarse_bound = build_tables([0.0, 1.0], 2)[2]
     transfer_back = transfer_table()[1]
     corners, from_loads = corner_tables()
+    from_loads = np.pad(from_loads, ((0, 0), (0, spread.shape[1] - from_loads.shape[1])))
+    spread = np.concatenate([spread, from_loads], 0)
+    collect = np.concatenate([collect, corners], 0)
     wide = pltpu.CompilerParams(vmem_limit_bytes=60 * 1024 * 1024)
     limit = pltpu.CompilerParams(vmem_limit_bytes=48 * 1024 * 1024)
     f32 = jnp.float32
@@ -1231,8 +1235,6 @@
             *blocks,
             jnp.asarray(spread),
             jnp.asarray(collect),
-            jnp.asarray(corners),
-            jnp.asarray(from_loads),
         )
         if prepared:
             down, up = edges

time: 48.9 us -> 48.3 us (0.988)
  local copies, waits for them, and re-layouts: 0.71 us -> 0.02 us
    unnamed x12 -> x8, local copies, waits for them, and re-layouts: 0.71 us -> 0.02 us
where the time goes in v17:
time: 48.3 us; the launch traced here: 48.1 us
  blocking collectives  26.6 us (55%)
  Pallas kernels  12.6 us (26%)
  waiting for transfers between devices  7.02 us (15%)
  starting transfers between devices  1.16 us (2%)
  between operations  0.69 us (1%)
    all_to_all x1, blocking collectives, body(): lax.all_to_all(sent, everyone, 0, 0, tiled=True).reshape(devices * 12, 128)  16 us
    all_to_all x1, blocking collectives, body(): lax.all_to_all(result.reshape(devices, 8, 128), everyone, 0, 0, tiled=True)  10.6 us
    ppermute x4, waiting for transfers between devices, from_device(): return lax.ppermute(block, ('gx', 'gy'), route)  7.02 us
    pallas_call x1, Pallas kernels, body(): first(*blocks, jnp.asarray(spread), jnp.asarray(collect))  4.86 us
    pallas_call x1, Pallas kernels, body(): second(*messages, load, jnp.asarray(spread), jnp.asarray(collect), jnp.as...  3.95 us
    pallas_call x1, Pallas kernels, body(): pack(initial, forcing, modulus, solid_list, jnp.asarray(pack_table()))  1.74 us
    ppermute x4, starting transfers between devices, from_device(): return lax.ppermute(block, ('gx', 'gy'), route)  1.16 us
    pallas_call x1, Pallas kernels, body(): return unpack(back, jnp.asarray(unpack_table()))  1.02 us
  transfers between devices with their start and end apart: 4, of which 3 were waited for; matrix products, arithmetic and copies ran while one was open for 0% of the time, Pallas kernels for 2%

profile of v17, /device:TPU:0, one launch (start us, length us, event | category | flops | bytes accessed | tf_op | source)
XLA Modules:
  0.0 48.1 jit_solution(17875009908211474211)
XLA Ops:
  0.6 1.7 %shard_map.104 = f32[384,128]{1,0:T(8,128)S(1)} custom-call(f32[3,6,3,384]{3,2,1,0:T(4,128)} %initial_at.1, f32[3,6,3,384]{3,2,1,0:T(4,128)} %forcing_at.1, f32[2,1,128]{2,1,0:T(1,128)} %modulus_at.1, s32[1,1,192]{2,1,0:T(1,128)} %listing_at.1, bf16[384,512]{1,0:T(8,128)(2,1)} %constant.10.clone.table_at), custom_call_target="tpu_custom_call" | custom-call | tf_op jit(solution)/shard_map/pallas_call | solution.py:1227
  2.4 0.0 copy-start
  2.4 0.0 copy-start.1
  2.4 16.0 %all_to_all.10 = f32[32,3,4,128]{3,2,1,0:T(4,128)S(1)} all-to-all(f32[32,3,4,128]{3,2,1,0:T(4,128)S(1)} %bitcast.3), channel_id=1, replica_groups=mesh['gx'=4,'gy'=8] {'gy','gx'}, dimensions={0} | all-to-all | bytes 393216 | tf_op jit(solution)/shard_map/all_to_all | solution.py:1229
  18.4 0.2 collective-permute-start.1
  18.6 0.4 collective-permute-start
  19.0 0.0 copy-done
  19.0 0.0 copy-done.1
  19.0 1.0 %shard_map.105 = (f32[3,3,32,128]{3,2,1,0:T(8,128)S(1)}, f32[3,2,32,128]{3,2,1,0:T(8,128)S(1)}, f32[2,128]{1,0:T(2,128)S(1)}, f32[3,2,32,128]{3,2,1,0:T(8,128)S(1)}, f32[3,2,8,128]{3,2,1,0:T(8,128)S(1)}) custom-call(f32[384,128]{1,0:T(8,128)S(1)} %bitcast.7, bf16[208,240]{1,0:T(8,128)(2,1)S(1)} %copy-done, bf16[176,192]{1,0:T(8,128)(2,1)S(1)} %copy-done.1), custom_call_target="tpu_custom_call" | custom-call | flops 400000000 | bytes 1000000 | tf_op jit(solution)/shard_map/pallas_call | solution.py:1233
  20.0 1.8 %collective-permute-done.1.refs_1_ = f32[384,128]{1,0:T(8,128)S(1)} collective-permute-done((f32[384,128]{1,0:T(8,128)S(1)}, f32[384,128]{1,0:T(8,128)S(1)}, u32[]{:S(2)}, u32[]{:S(2)}) %collective-permute-start.1) | collective-permute-done | bytes 196640 | tf_op jit(solution)/shard_map/ppermute | solution.py:1224
  21.8 1.9 %collective-permute-done.refs_0_ = f32[384,128]{1,0:T(8,128)S(1)} collective-permute-done((f32[384,128]{1,0:T(8,128)S(1)}, f32[384,128]{1,0:T(8,128)S(1)}, u32[]{:S(2)}, u32[]{:S(2)}) %collective-permute-start) | collective-permute-done | bytes 196640 | tf_op jit(solution)/shard_map/ppermute | solution.py:1224
  23.7 0.0 copy-start.3
  23.7 4.9 %shard_map.106 = (f32[3,2,32,128]{3,2,1,0:T(8,128)S(1)}, f32[3,48,128]{2,1,0:T(8,128)S(1)}, f32[3,32,128]{2,1,0:T(8,128)S(1)}, f32[3,6,32,128]{3,2,1,0:T(8,128)S(1)}) custom-call(f32[384,128]{1,0:T(8,128)S(1)} %collective-permute-done.refs_0_, f32[384,128]{1,0:T(8,128)S(1)} %collective-permute-done.1.refs_1_, ...), custom_call_target="tpu_custom_call" | custom-call | tf_op jit(solution)/shard_map/pallas_call | solution.py:1234
  28.6 0.3 collective-permute-start.3
  28.9 0.2 collective-permute-start.2
  29.1 3.3 %collective-permute-done.2.refs_0_ = f32[3,32,128]{2,1,0:T(8,128)S(1)} collective-permute-done((f32[3,32,128]{2,1,0:T(8,128)S(1)}, f32[3,32,128]{2,1,0:T(8,128)S(1)}, u32[]{:S(2)}, u32[]{:S(2)}) %collective-permute-start.2) | collective-permute-done | bytes 49184 | tf_op jit(solution)/shard_map/ppermute | solution.py:1224
  32.4 0.0 collective-permute-done.3.refs_2_
  32.4 0.0 copy-done.3
  32.4 4.0 %shard_map.107 = f32[16,2,8,128]{3,2,1,0:T(8,128)S(1)} custom-call(f32[3,32,128]{2,1,0:T(8,128)S(1)} %collective-permute-done.2.refs_0_, f32[3,2,32,128]{3,2,1,0:T(8,128)S(1)} %get-tuple-element.17.refs_1_, f32[3,48,128]{2,1,0:T(8,128)S(1)} %collective-permute-done.3.refs_2_, f32[3,6,32,128]{3,2,1,0:T(8,128)S(1)} %get-tuple-element.19.refs_3_, ...), custom_call_target="tpu_custom_call" | custom-call | tf_op jit(solution)/shard_map/pallas_call | solution.py:1245
  36.4 0.0 copy-start.2
  36.4 10.6 %all_to_all.11.arrived = f32[32,8,128]{2,1,0:T(8,128)S(1)} all-to-all(f32[32,8,128]{2,1,0:T(8,128)S(1)} %bitcast.4), channel_id=1, replica_groups=mesh['gx'=4,'gy'=8] {'gy','gx'}, dimensions={0} | all-to-all | bytes 262144 | tf_op jit(solution)/shard_map/all_to_all | solution.py:1252
  47.0 0.0 copy-done.2
  47.0 1.0 %shard_map.108 = (f32[3,6,3,384]{3,2,1,0:T(4,128)}, f32[3,2,1,128]{3,2,1,0:T(1,128)}) custom-call(f32[32,8,128]{2,1,0:T(8,128)S(1)} %all_to_all.11.arrived, bf16[256,512]{1,0:T(8,128)(2,1)S(1)} %copy-done.2), custom_call_target="tpu_custom_call" | custom-call | tf_op jit(solution)/shard_map/pallas_call | solution.py:1253
Async XLA Ops:
  2.4 16.6 %copy-start = (bf16[208,240]{1,0:T(8,128)(2,1)S(1)}, bf16[208,240]{1,0:T(8,128)(2,1)}, u32[]{:S(2)}) copy-start(bf16[208,240]{1,0:T(8,128)(2,1)} %constant.11.clone.spread.refs_7_.refs_4_) | copy-start | bytes 299524
  2.4 16.6 %copy-start.1 = (bf16[176,192]{1,0:T(8,128)(2,1)S(1)}, bf16[176,192]{1,0:T(8,128)(2,1)}, u32[]{:S(2)}) copy-start(bf16[176,192]{1,0:T(8,128)(2,1)} %constant.12.clone.collect.refs_8_.refs_5_) | copy-start | bytes 202756
  18.4 3.4 %collective-permute-start.1 = (f32[384,128]{1,0:T(8,128)S(1)}, f32[384,128]{1,0:T(8,128)S(1)}, u32[]{:S(2)}, u32[]{:S(2)}) collective-permute-start(f32[384,128]{1,0:T(8,128)S(1)} %bitcast.5), channel_id=1, source_target_pairs={{8,0},{2,8},{10,2},{4,10},{12,4},{6,12},{14,6},{22,14},{30,22},{20... | collective-permute-start | bytes 589832 | tf_op jit(solution)/shard_map/ppermute | solution.py:1224
  18.6 5.1 %collective-permute-start = (f32[384,128]{1,0:T(8,128)S(1)}, f32[384,128]{1,0:T(8,128)S(1)}, u32[]{:S(2)}, u32[]{:S(2)}) collective-permute-start(f32[384,128]{1,0:T(8,128)S(1)} %bitcast.6), channel_id=1, source_target_pairs={{9,0},{0,8},{8,2},{2,10},{10,4},{4,12},{12,6},{6,14},{14,22},{22,3... | collective-permute-start | bytes 589832 | tf_op jit(solution)/shard_map/ppermute | solution.py:1224
  23.7 8.7 %copy-start.3 = (f32[32,8]{1,0:T(8,128)S(1)}, f32[32,8]{1,0:T(8,128)}, u32[]{:S(2)}) copy-start(f32[32,8]{1,0:T(8,128)} %constant.13.clone.refs_6_) | copy-start | bytes 3076
  28.6 3.9 %collective-permute-start.3 = (f32[3,48,128]{2,1,0:T(8,128)S(1)}, f32[3,48,128]{2,1,0:T(8,128)S(1)}, u32[]{:S(2)}, u32[]{:S(2)}) collective-permute-start(f32[3,48,128]{2,1,0:T(8,128)S(1)} %get-tuple-element.18), channel_id=1, source_target_pairs={{8,0},{2,8},{10,2},{4,10},{12,4},{6,12},{14,6},{22,14},{30,22},{20... | collective-permute-start | bytes 221192 | tf_op jit(solution)/shard_map/ppermute | solution.py:1224
  28.9 3.5 %collective-permute-start.2 = (f32[3,32,128]{2,1,0:T(8,128)S(1)}, f32[3,32,128]{2,1,0:T(8,128)S(1)}, u32[]{:S(2)}, u32[]{:S(2)}) collective-permute-start(f32[3,32,128]{2,1,0:T(8,128)S(1)} %get-tuple-element.16), channel_id=1, source_target_pairs={{9,0},{0,8},{8,2},{2,10},{10,4},{4,12},{12,6},{6,14},{14,22},{22,3... | collective-permute-start | bytes 147464 | tf_op jit(solution)/shard_map/ppermute | solution.py:1224
  36.4 10.6 %copy-start.2 = (bf16[256,512]{1,0:T(8,128)(2,1)S(1)}, bf16[256,512]{1,0:T(8,128)(2,1)}, u32[]{:S(2)}) copy-start(bf16[256,512]{1,0:T(8,128)(2,1)} %constant.14.clone.table) | copy-start | bytes 786436

commit v18 on v17

--- a/solution.py
+++ b/solution.py
@@ -551,11 +551,14 @@
         )
 
     def gradient(self, u, spread, pairs):
-        parts = [
-            high_low(self.gather(i, u[i, pair], u[i, pair + 1]))
-            for i in range(3)
-            for pair in pairs
-        ]
+        def block(i, pair):
+            if isinstance(pair, tuple):
+                halves_of = [block(i, each) for each in pair]
+                lane = lax.broadcasted_iota(jnp.int32, halves_of[0].shape, 1)
+                return jnp.where(lane % 2 == 0, *halves_of)
+            return self.gather(i, u[i, pair], u[i, pair + 1])
+
+        parts = [high_low(block(i, pair)) for i in range(3) for pair in pairs]
         return jnp.dot(
             spread[0:POINT_ROWS, :],
             jnp.concatenate([jnp.concatenate([h, l, h], 0) for h, l in parts], 1),
@@ -602,7 +605,13 @@
         force = force[0:rows] + (
             force[rows:] + jnp.dot(both[0:rows], low, preferred_element_type=jnp.float32)
         )
-        stiffness = [stiff[pair : pair + 1, :] for pair in pairs]
+        stiffness = []
+        for pair in pairs:
+            if isinstance(pair, tuple):
+                rows = [stiff[each : each + 1, :] for each in pair]
+                stiffness.append(jnp.where(self.even[0:1], *rows))
+            else:
+                stiffness.append(stiff[pair : pair + 1, :])
         return force * jnp.concatenate(stiffness * 3, 1)
 
     def run(self, u, stiff, spread, collect, jobs, given=None):
@@ -923,16 +932,25 @@
         jobs = slab.smoothing(u, f, 0, d, spans[0:3], fine_bound)
         slab.run(u, stiff, spread, collect, jobs, given)
         steps = plan_steps([spans[3]])[0]
+        if prepared:
+            steps = [list(range(own, own + own_pairs)), [(own + own_pairs, own - 1)]]
         gradients = [slab.gradient(u, spread, pairs) for pairs in steps]
         for pairs, gradient in zip(steps, gradients):
             force = slab.force(gradient, stiff, collect, pairs, 2 * ROWS, 16)
             for q, pair in enumerate(pairs):
                 for i in range(3):
                     at = (len(pairs) * i + q) * width
-                    load_at = (3 * (pair - first) + i) * width
                     part = force[:, at : at + width]
                     part = jnp.where(slab.bottom, part[8:16], part[0:8])
-                    shares[i, pair] = loads[0:8, load_at : load_at + width] - part
+                    owners = {pair: part}
+                    if isinstance(pair, tuple):
+                        owners = {
+                            pair[0]: jnp.where(slab.even, part, 0.0),
+                            pair[1]: jnp.where(slab.even, 0.0, part),
+                        }
+                    for each, share in owners.items():
+                        load_at = (3 * (each - first) + i) * width
+                        shares[i, each] = loads[0:8, load_at : load_at + width] - share
 
         restricted = [
             slab.assemble({corner: shares[i, :, n, :] for n, corner in enumerate(CORNERS)})

time: 48.3 us -> 48.2 us (level)
  no operation moved by 1% of the time
where the time goes in v18:
time: 48.2 us; the launch traced here: 48 us
  blocking collectives  26.6 us (55%)
  Pallas kernels  12.5 us (26%)
  waiting for transfers between devices  7.02 us (15%)
  starting transfers between devices  1.16 us (2%)
  between operations  0.69 us (1%)
    all_to_all x1, blocking collectives, body(): lax.all_to_all(sent, everyone, 0, 0, tiled=True).reshape(devices * 12, 128)  16 us
    all_to_all x1, blocking collectives, body(): lax.all_to_all(result.reshape(devices, 8, 128), everyone, 0, 0, tiled=True)  10.6 us
    ppermute x4, waiting for transfers between devices, from_device(): return lax.ppermute(block, ('gx', 'gy'), route)  7.02 us
    pallas_call x1, Pallas kernels, body(): first(*blocks, jnp.asarray(spread), jnp.asarray(collect))  4.84 us
    pallas_call x1, Pallas kernels, body(): second(*messages, load, jnp.asarray(spread), jnp.asarray(collect), jnp.as...  3.95 us
    pallas_call x1, Pallas kernels, body(): pack(initial, forcing, modulus, solid_list, jnp.asarray(pack_table()))  1.74 us
    ppermute x4, starting transfers between devices, from_device(): return lax.ppermute(block, ('gx', 'gy'), route)  1.16 us
    pallas_call x1, Pallas kernels, body(): return unpack(back, jnp.asarray(unpack_table()))  1.02 us
  transfers between devices with their start and end apart: 4, of which 3 were waited for; matrix products, arithmetic and copies ran while one was open for 0% of the time, Pallas kernels for 2%

profile of v18, /device:TPU:0, one launch (start us, length us, event | category | flops | bytes accessed | tf_op | source)
XLA Modules:
  0.0 48.0 jit_solution(6392373254211745980)
XLA Ops:
  0.6 1.7 %shard_map.104 = f32[384,128]{1,0:T(8,128)S(1)} custom-call(f32[3,6,3,384]{3,2,1,0:T(4,128)} %initial_at.1, f32[3,6,3,384]{3,2,1,0:T(4,128)} %forcing_at.1, f32[2,1,128]{2,1,0:T(1,128)} %modulus_at.1, s32[1,1,192]{2,1,0:T(1,128)} %listing_at.1, bf16[384,512]{1,0:T(8,128)(2,1)} %constant.10.clone.table_at), custom_call_target="tpu_custom_call" | custom-call | tf_op jit(solution)/shard_map/pallas_call | solution.py:1245
  2.4 0.0 copy-start
  2.4 0.0 copy-start.1
  2.4 16.0 %all_to_all.10 = f32[32,3,4,128]{3,2,1,0:T(4,128)S(1)} all-to-all(f32[32,3,4,128]{3,2,1,0:T(4,128)S(1)} %bitcast.3), channel_id=1, replica_groups=mesh['gx'=4,'gy'=8] {'gy','gx'}, dimensions={0} | all-to-all | bytes 393216 | tf_op jit(solution)/shard_map/all_to_all | solution.py:1247
  18.4 0.2 collective-permute-start.1
  18.6 0.4 collective-permute-start
  19.0 0.0 copy-done
  19.0 0.0 copy-done.1
  19.0 1.0 %shard_map.105 = (f32[3,3,32,128]{3,2,1,0:T(8,128)S(1)}, f32[3,2,32,128]{3,2,1,0:T(8,128)S(1)}, f32[2,128]{1,0:T(2,128)S(1)}, f32[3,2,32,128]{3,2,1,0:T(8,128)S(1)}, f32[3,2,8,128]{3,2,1,0:T(8,128)S(1)}) custom-call(f32[384,128]{1,0:T(8,128)S(1)} %bitcast.7, bf16[208,240]{1,0:T(8,128)(2,1)S(1)} %copy-done, bf16[176,192]{1,0:T(8,128)(2,1)S(1)} %copy-done.1), custom_call_target="tpu_custom_call" | custom-call | flops 400000000 | bytes 1000000 | tf_op jit(solution)/shard_map/pallas_call | solution.py:1251
  20.0 1.8 %collective-permute-done.1.refs_1_ = f32[384,128]{1,0:T(8,128)S(1)} collective-permute-done((f32[384,128]{1,0:T(8,128)S(1)}, f32[384,128]{1,0:T(8,128)S(1)}, u32[]{:S(2)}, u32[]{:S(2)}) %collective-permute-start.1) | collective-permute-done | bytes 196640 | tf_op jit(solution)/shard_map/ppermute | solution.py:1242
  21.8 1.9 %collective-permute-done.refs_0_ = f32[384,128]{1,0:T(8,128)S(1)} collective-permute-done((f32[384,128]{1,0:T(8,128)S(1)}, f32[384,128]{1,0:T(8,128)S(1)}, u32[]{:S(2)}, u32[]{:S(2)}) %collective-permute-start) | collective-permute-done | bytes 196640 | tf_op jit(solution)/shard_map/ppermute | solution.py:1242
  23.7 0.0 copy-start.3
  23.7 4.8 %shard_map.106 = (f32[3,2,32,128]{3,2,1,0:T(8,128)S(1)}, f32[3,48,128]{2,1,0:T(8,128)S(1)}, f32[3,32,128]{2,1,0:T(8,128)S(1)}, f32[3,6,32,128]{3,2,1,0:T(8,128)S(1)}) custom-call(f32[384,128]{1,0:T(8,128)S(1)} %collective-permute-done.refs_0_, f32[384,128]{1,0:T(8,128)S(1)} %collective-permute-done.1.refs_1_, ...), custom_call_target="tpu_custom_call" | custom-call | tf_op jit(solution)/shard_map/pallas_call | solution.py:1252
  28.6 0.3 collective-permute-start.3
  28.9 0.2 collective-permute-start.2
  29.1 3.3 %collective-permute-done.2.refs_0_ = f32[3,32,128]{2,1,0:T(8,128)S(1)} collective-permute-done((f32[3,32,128]{2,1,0:T(8,128)S(1)}, f32[3,32,128]{2,1,0:T(8,128)S(1)}, u32[]{:S(2)}, u32[]{:S(2)}) %collective-permute-start.2) | collective-permute-done | bytes 49184 | tf_op jit(solution)/shard_map/ppermute | solution.py:1242
  32.4 0.0 collective-permute-done.3.refs_2_
  32.4 0.0 copy-done.3
  32.4 4.0 %shard_map.107 = f32[16,2,8,128]{3,2,1,0:T(8,128)S(1)} custom-call(f32[3,32,128]{2,1,0:T(8,128)S(1)} %collective-permute-done.2.refs_0_, f32[3,2,32,128]{3,2,1,0:T(8,128)S(1)} %get-tuple-element.17.refs_1_, f32[3,48,128]{2,1,0:T(8,128)S(1)} %collective-permute-done.3.refs_2_, f32[3,6,32,128]{3,2,1,0:T(8,128)S(1)} %get-tuple-element.19.refs_3_, ...), custom_call_target="tpu_custom_call" | custom-call | tf_op jit(solution)/shard_map/pallas_call | solution.py:1263
  36.4 0.0 copy-start.2
  36.4 10.6 %all_to_all.11.arrived = f32[32,8,128]{2,1,0:T(8,128)S(1)} all-to-all(f32[32,8,128]{2,1,0:T(8,128)S(1)} %bitcast.4), channel_id=1, replica_groups=mesh['gx'=4,'gy'=8] {'gy','gx'}, dimensions={0} | all-to-all | bytes 262144 | tf_op jit(solution)/shard_map/all_to_all | solution.py:1270
  47.0 0.0 copy-done.2
  47.0 1.0 %shard_map.108 = (f32[3,6,3,384]{3,2,1,0:T(4,128)}, f32[3,2,1,128]{3,2,1,0:T(1,128)}) custom-call(f32[32,8,128]{2,1,0:T(8,128)S(1)} %all_to_all.11.arrived, bf16[256,512]{1,0:T(8,128)(2,1)S(1)} %copy-done.2), custom_call_target="tpu_custom_call" | custom-call | tf_op jit(solution)/shard_map/pallas_call | solution.py:1271
Async XLA Ops:
  2.4 16.6 %copy-start = (bf16[208,240]{1,0:T(8,128)(2,1)S(1)}, bf16[208,240]{1,0:T(8,128)(2,1)}, u32[]{:S(2)}) copy-start(bf16[208,240]{1,0:T(8,128)(2,1)} %constant.11.clone.spread.refs_7_.refs_4_) | copy-start | bytes 299524
  2.4 16.6 %copy-start.1 = (bf16[176,192]{1,0:T(8,128)(2,1)S(1)}, bf16[176,192]{1,0:T(8,128)(2,1)}, u32[]{:S(2)}) copy-start(bf16[176,192]{1,0:T(8,128)(2,1)} %constant.12.clone.collect.refs_8_.refs_5_) | copy-start | bytes 202756
  18.4 3.4 %collective-permute-start.1 = (f32[384,128]{1,0:T(8,128)S(1)}, f32[384,128]{1,0:T(8,128)S(1)}, u32[]{:S(2)}, u32[]{:S(2)}) collective-permute-start(f32[384,128]{1,0:T(8,128)S(1)} %bitcast.5), channel_id=1, source_target_pairs={{8,0},{2,8},{10,2},{4,10},{12,4},{6,12},{14,6},{22,14},{30,22},{20... | collective-permute-start | bytes 589832 | tf_op jit(solution)/shard_map/ppermute | solution.py:1242
  18.6 5.1 %collective-permute-start = (f32[384,128]{1,0:T(8,128)S(1)}, f32[384,128]{1,0:T(8,128)S(1)}, u32[]{:S(2)}, u32[]{:S(2)}) collective-permute-start(f32[384,128]{1,0:T(8,128)S(1)} %bitcast.6), channel_id=1, source_target_pairs={{9,0},{0,8},{8,2},{2,10},{10,4},{4,12},{12,6},{6,14},{14,22},{22,3... | collective-permute-start | bytes 589832 | tf_op jit(solution)/shard_map/ppermute | solution.py:1242
  23.7 8.7 %copy-start.3 = (f32[32,8]{1,0:T(8,128)S(1)}, f32[32,8]{1,0:T(8,128)}, u32[]{:S(2)}) copy-start(f32[32,8]{1,0:T(8,128)} %constant.13.clone.refs_6_) | copy-start | bytes 3076
  28.6 3.9 %collective-permute-start.3 = (f32[3,48,128]{2,1,0:T(8,128)S(1)}, f32[3,48,128]{2,1,0:T(8,128)S(1)}, u32[]{:S(2)}, u32[]{:S(2)}) collective-permute-start(f32[3,48,128]{2,1,0:T(8,128)S(1)} %get-tuple-element.18), channel_id=1, source_target_pairs={{8,0},{2,8},{10,2},{4,10},{12,4},{6,12},{14,6},{22,14},{30,22},{20... | collective-permute-start | bytes 221192 | tf_op jit(solution)/shard_map/ppermute | solution.py:1242
  28.9 3.5 %collective-permute-start.2 = (f32[3,32,128]{2,1,0:T(8,128)S(1)}, f32[3,32,128]{2,1,0:T(8,128)S(1)}, u32[]{:S(2)}, u32[]{:S(2)}) collective-permute-start(f32[3,32,128]{2,1,0:T(8,128)S(1)} %get-tuple-element.16), channel_id=1, source_target_pairs={{9,0},{0,8},{8,2},{2,10},{10,4},{4,12},{12,6},{6,14},{14,22},{22,3... | collective-permute-start | bytes 147464 | tf_op jit(solution)/shard_map/ppermute | solution.py:1242
  36.4 10.6 %copy-start.2 = (bf16[256,512]{1,0:T(8,128)(2,1)S(1)}, bf16[256,512]{1,0:T(8,128)(2,1)}, u32[]{:S(2)}) copy-start(bf16[256,512]{1,0:T(8,128)(2,1)} %constant.14.clone.table) | copy-start | bytes 786436

commit v19 on v18

--- a/solution.py
+++ b/solution.py
@@ -299,18 +299,18 @@
     initial, forcing, modulus, listing, table, rows, turned, places, ready,
 ):
     own_layers = EZ // len(order)
-    sources = (listing_at, modulus_at, initial_at, forcing_at, table_at)
+    sources = (initial_at, forcing_at, listing_at, modulus_at, table_at)
     copies = [
         pltpu.make_async_copy(source, here, ready.at[n])
         for n, (source, here) in enumerate(
-            zip(sources, (listing, modulus, initial, forcing, table))
+            zip(sources, (initial, forcing, listing, modulus, table))
         )
     ]
     for copy in copies:
         copy.start()
     rows[108:128, :] = jnp.zeros((20, 384), jnp.float32)
-    copies[0].wait()
-    copies[1].wait()
+    copies[2].wait()
+    copies[3].wait()
     listed = listing[0].astype(jnp.float32)
     listed = jnp.concatenate([listed, jnp.full((1, 64), 256.0, jnp.float32)], 1)
     listed = jnp.broadcast_to(listed, (128, 256)).T
@@ -320,9 +320,8 @@
     for x in range(2):
         hit = jnp.max(jnp.where(listed == lanes + 128.0 * x, 1.0, 0.0), axis=0, keepdims=True)
         stiff = jnp.where(row_at == 108 + x, hit * modulus[x], stiff)
-    copies[2].wait()
-    copies[3].wait()
     for field, source in enumerate((initial, forcing)):
+        copies[field].wait()
         for component in range(3):
             for layer in range(6):
                 at = stack_row(field, component, layer, 0)

time: 48.2 us -> 48.2 us (level)
  no operation moved by 1% of the time
where the time goes in v19:
time: 48.2 us; the launch traced here: 48 us
  blocking collectives  26.6 us (55%)
  Pallas kernels  12.5 us (26%)
  waiting for transfers between devices  7.02 us (15%)
  starting transfers between devices  1.16 us (2%)
  between operations  0.69 us (1%)
    all_to_all x1, blocking collectives, body(): lax.all_to_all(sent, everyone, 0, 0, tiled=True).reshape(devices * 12, 128)  16 us
    all_to_all x1, blocking collectives, body(): lax.all_to_all(result.reshape(devices, 8, 128), everyone, 0, 0, tiled=True)  10.6 us
    ppermute x4, waiting for transfers between devices, from_device(): return lax.ppermute(block, ('gx', 'gy'), route)  7.02 us
    pallas_call x1, Pallas kernels, body(): first(*blocks, jnp.asarray(spread), jnp.asarray(collect))  4.84 us
    pallas_call x1, Pallas kernels, body(): second(*messages, load, jnp.asarray(spread), jnp.asarray(collect), jnp.as...  3.95 us
    pallas_call x1, Pallas kernels, body(): pack(initial, forcing, modulus, solid_list, jnp.asarray(pack_table()))  1.72 us
    ppermute x4, starting transfers between devices, from_device(): return lax.ppermute(block, ('gx', 'gy'), route)  1.16 us
    pallas_call x1, Pallas kernels, body(): return unpack(back, jnp.asarray(unpack_table()))  1.02 us
  transfers between devices with their start and end apart: 4, of which 3 were waited for; matrix products, arithmetic and copies ran while one was open for 0% of the time, Pallas kernels for 2%

profile of v19, /device:TPU:0, one launch (start us, length us, event | category | flops | bytes accessed | tf_op | source)
XLA Modules:
  0.0 48.0 jit_solution(17464352053401872544)
XLA Ops:
  0.6 1.7 %shard_map.104 = f32[384,128]{1,0:T(8,128)S(1)} custom-call(f32[3,6,3,384]{3,2,1,0:T(4,128)} %initial_at.1, f32[3,6,3,384]{3,2,1,0:T(4,128)} %forcing_at.1, f32[2,1,128]{2,1,0:T(1,128)} %modulus_at.1, s32[1,1,192]{2,1,0:T(1,128)} %listing_at.1, bf16[384,512]{1,0:T(8,128)(2,1)} %constant.10.clone.table_at), custom_call_target="tpu_custom_call" | custom-call | tf_op jit(solution)/shard_map/pallas_call | solution.py:1244
  2.4 0.0 copy-start
  2.4 0.0 copy-start.1
  2.4 16.0 %all_to_all.10 = f32[32,3,4,128]{3,2,1,0:T(4,128)S(1)} all-to-all(f32[32,3,4,128]{3,2,1,0:T(4,128)S(1)} %bitcast.3), channel_id=1, replica_groups=mesh['gx'=4,'gy'=8] {'gy','gx'}, dimensions={0} | all-to-all | bytes 393216 | tf_op jit(solution)/shard_map/all_to_all | solution.py:1246
  18.4 0.2 collective-permute-start.1
  18.6 0.4 collective-permute-start
  19.0 0.0 copy-done
  19.0 0.0 copy-done.1
  19.0 1.0 %shard_map.105 = (f32[3,3,32,128]{3,2,1,0:T(8,128)S(1)}, f32[3,2,32,128]{3,2,1,0:T(8,128)S(1)}, f32[2,128]{1,0:T(2,128)S(1)}, f32[3,2,32,128]{3,2,1,0:T(8,128)S(1)}, f32[3,2,8,128]{3,2,1,0:T(8,128)S(1)}) custom-call(f32[384,128]{1,0:T(8,128)S(1)} %bitcast.7, bf16[208,240]{1,0:T(8,128)(2,1)S(1)} %copy-done, bf16[176,192]{1,0:T(8,128)(2,1)S(1)} %copy-done.1), custom_call_target="tpu_custom_call" | custom-call | flops 400000000 | bytes 1000000 | tf_op jit(solution)/shard_map/pallas_call | solution.py:1250
  20.0 1.8 %collective-permute-done.1.refs_1_ = f32[384,128]{1,0:T(8,128)S(1)} collective-permute-done((f32[384,128]{1,0:T(8,128)S(1)}, f32[384,128]{1,0:T(8,128)S(1)}, u32[]{:S(2)}, u32[]{:S(2)}) %collective-permute-start.1) | collective-permute-done | bytes 196640 | tf_op jit(solution)/shard_map/ppermute | solution.py:1241
  21.8 1.9 %collective-permute-done.refs_0_ = f32[384,128]{1,0:T(8,128)S(1)} collective-permute-done((f32[384,128]{1,0:T(8,128)S(1)}, f32[384,128]{1,0:T(8,128)S(1)}, u32[]{:S(2)}, u32[]{:S(2)}) %collective-permute-start) | collective-permute-done | bytes 196640 | tf_op jit(solution)/shard_map/ppermute | solution.py:1241
  23.7 0.0 copy-start.3
  23.7 4.8 %shard_map.106 = (f32[3,2,32,128]{3,2,1,0:T(8,128)S(1)}, f32[3,48,128]{2,1,0:T(8,128)S(1)}, f32[3,32,128]{2,1,0:T(8,128)S(1)}, f32[3,6,32,128]{3,2,1,0:T(8,128)S(1)}) custom-call(f32[384,128]{1,0:T(8,128)S(1)} %collective-permute-done.refs_0_, f32[384,128]{1,0:T(8,128)S(1)} %collective-permute-done.1.refs_1_, ...), custom_call_target="tpu_custom_call" | custom-call | tf_op jit(solution)/shard_map/pallas_call | solution.py:1251
  28.5 0.3 collective-permute-start.3
  28.9 0.2 collective-permute-start.2
  29.1 3.3 %collective-permute-done.2.refs_0_ = f32[3,32,128]{2,1,0:T(8,128)S(1)} collective-permute-done((f32[3,32,128]{2,1,0:T(8,128)S(1)}, f32[3,32,128]{2,1,0:T(8,128)S(1)}, u32[]{:S(2)}, u32[]{:S(2)}) %collective-permute-start.2) | collective-permute-done | bytes 49184 | tf_op jit(solution)/shard_map/ppermute | solution.py:1241
  32.4 0.0 collective-permute-done.3.refs_2_
  32.4 0.0 copy-done.3
  32.4 4.0 %shard_map.107 = f32[16,2,8,128]{3,2,1,0:T(8,128)S(1)} custom-call(f32[3,32,128]{2,1,0:T(8,128)S(1)} %collective-permute-done.2.refs_0_, f32[3,2,32,128]{3,2,1,0:T(8,128)S(1)} %get-tuple-element.17.refs_1_, f32[3,48,128]{2,1,0:T(8,128)S(1)} %collective-permute-done.3.refs_2_, f32[3,6,32,128]{3,2,1,0:T(8,128)S(1)} %get-tuple-element.19.refs_3_, ...), custom_call_target="tpu_custom_call" | custom-call | tf_op jit(solution)/shard_map/pallas_call | solution.py:1262
  36.4 0.0 copy-start.2
  36.4 10.6 %all_to_all.11.arrived = f32[32,8,128]{2,1,0:T(8,128)S(1)} all-to-all(f32[32,8,128]{2,1,0:T(8,128)S(1)} %bitcast.4), channel_id=1, replica_groups=mesh['gx'=4,'gy'=8] {'gy','gx'}, dimensions={0} | all-to-all | bytes 262144 | tf_op jit(solution)/shard_map/all_to_all | solution.py:1269
  47.0 0.0 copy-done.2
  47.0 1.0 %shard_map.108 = (f32[3,6,3,384]{3,2,1,0:T(4,128)}, f32[3,2,1,128]{3,2,1,0:T(1,128)}) custom-call(f32[32,8,128]{2,1,0:T(8,128)S(1)} %all_to_all.11.arrived, bf16[256,512]{1,0:T(8,128)(2,1)S(1)} %copy-done.2), custom_call_target="tpu_custom_call" | custom-call | tf_op jit(solution)/shard_map/pallas_call | solution.py:1270
Async XLA Ops:
  2.4 16.6 %copy-start = (bf16[208,240]{1,0:T(8,128)(2,1)S(1)}, bf16[208,240]{1,0:T(8,128)(2,1)}, u32[]{:S(2)}) copy-start(bf16[208,240]{1,0:T(8,128)(2,1)} %constant.11.clone.spread.refs_7_.refs_4_) | copy-start | bytes 299524
  2.4 16.6 %copy-start.1 = (bf16[176,192]{1,0:T(8,128)(2,1)S(1)}, bf16[176,192]{1,0:T(8,128)(2,1)}, u32[]{:S(2)}) copy-start(bf16[176,192]{1,0:T(8,128)(2,1)} %constant.12.clone.collect.refs_8_.refs_5_) | copy-start | bytes 202756
  18.4 3.4 %collective-permute-start.1 = (f32[384,128]{1,0:T(8,128)S(1)}, f32[384,128]{1,0:T(8,128)S(1)}, u32[]{:S(2)}, u32[]{:S(2)}) collective-permute-start(f32[384,128]{1,0:T(8,128)S(1)} %bitcast.5), channel_id=1, source_target_pairs={{8,0},{2,8},{10,2},{4,10},{12,4},{6,12},{14,6},{22,14},{30,22},{20... | collective-permute-start | bytes 589832 | tf_op jit(solution)/shard_map/ppermute | solution.py:1241
  18.6 5.1 %collective-permute-start = (f32[384,128]{1,0:T(8,128)S(1)}, f32[384,128]{1,0:T(8,128)S(1)}, u32[]{:S(2)}, u32[]{:S(2)}) collective-permute-start(f32[384,128]{1,0:T(8,128)S(1)} %bitcast.6), channel_id=1, source_target_pairs={{9,0},{0,8},{8,2},{2,10},{10,4},{4,12},{12,6},{6,14},{14,22},{22,3... | collective-permute-start | bytes 589832 | tf_op jit(solution)/shard_map/ppermute | solution.py:1241
  23.7 8.7 %copy-start.3 = (f32[32,8]{1,0:T(8,128)S(1)}, f32[32,8]{1,0:T(8,128)}, u32[]{:S(2)}) copy-start(f32[32,8]{1,0:T(8,128)} %constant.13.clone.refs_6_) | copy-start | bytes 3076
  28.5 3.9 %collective-permute-start.3 = (f32[3,48,128]{2,1,0:T(8,128)S(1)}, f32[3,48,128]{2,1,0:T(8,128)S(1)}, u32[]{:S(2)}, u32[]{:S(2)}) collective-permute-start(f32[3,48,128]{2,1,0:T(8,128)S(1)} %get-tuple-element.18), channel_id=1, source_target_pairs={{8,0},{2,8},{10,2},{4,10},{12,4},{6,12},{14,6},{22,14},{30,22},{20... | collective-permute-start | bytes 221192 | tf_op jit(solution)/shard_map/ppermute | solution.py:1241
  28.9 3.5 %collective-permute-start.2 = (f32[3,32,128]{2,1,0:T(8,128)S(1)}, f32[3,32,128]{2,1,0:T(8,128)S(1)}, u32[]{:S(2)}, u32[]{:S(2)}) collective-permute-start(f32[3,32,128]{2,1,0:T(8,128)S(1)} %get-tuple-element.16), channel_id=1, source_target_pairs={{9,0},{0,8},{8,2},{2,10},{10,4},{4,12},{12,6},{6,14},{14,22},{22,3... | collective-permute-start | bytes 147464 | tf_op jit(solution)/shard_map/ppermute | solution.py:1241
  36.4 10.6 %copy-start.2 = (bf16[256,512]{1,0:T(8,128)(2,1)S(1)}, bf16[256,512]{1,0:T(8,128)(2,1)}, u32[]{:S(2)}) copy-start(bf16[256,512]{1,0:T(8,128)(2,1)} %constant.14.clone.table) | copy-start | bytes 786436
